TPU v7x, 32 devices: a whole 2x2x4 slice. The times are simulated.
32 devices in a mesh: wide: 4 (over y, core), narrow: 8 (over z, x).
Axes of the slice: x: 2, y: 2, z: 4, core: 2. Of those that a mesh axis runs over, the one named last changes fastest.
Arguments:
- positions: float32 [3, 4, 8, 1, 128], P(None, 'wide', 'narrow'), may hold values from 0.08 to 0.92
- species: int32 [4, 8, 1, 128], P('wide', 'narrow'), may hold values 0 or 1
- neighbours: int32 [4, 8, 1, 128, 128], P('wide', 'narrow'), may hold values from 0 to 3455
- embed_one_w: float32 [2, 25], replicated, may hold values from -12 to 12
- embed_one_b: float32 [2, 25], replicated, may hold values from -6 to 6
- embed_two_w: float32 [25, 50], replicated, may hold values from -1.25 to 1.25
- embed_two_b: float32 [50], replicated, may hold values from -3 to 3
- embed_three_w: float32 [50, 100], replicated, may hold values from -0.875 to 0.875
- embed_three_b: float32 [100], replicated, may hold values from -3 to 3
- fit_one_w: float32 [1600, 240], replicated, may hold values from -0.15625 to 0.15625
- fit_one_b: float32 [240], replicated, may hold values from -6 to 6
- fit_two_w: float32 [240, 240], replicated, may hold values from -0.375 to 0.375
- fit_two_b: float32 [240], replicated, may hold values from -3 to 3
- fit_three_w: float32 [240, 240], replicated, may hold values from -0.375 to 0.375
- fit_three_b: float32 [240], replicated, may hold values from -3 to 3
- fit_out_w: float32 [240, 100], replicated, may hold values from -0.375 to 0.375
Outputs:
- dipole: float32 [3, 4, 8, 1, 128], P(None, 'wide', 'narrow')
- atom_field: float32 [4, 4, 8, 1, 128], P(None, 'wide', 'narrow')
- centroid_field: float32 [4, 4, 8, 1, 128], P(None, 'wide', 'narrow')
- energy: float32 [], replicated
Inputs may be any that keep to these rules, and one draw needn't show every extreme that they name: `species`: 1 marks a hydrogen, 0 an oxygen. `neighbours`: entry c names slot c % 128 of the brick offset by (q // 9 - 1, q % 3 - 1, (q // 3) % 3 - 1) bricks along x, y, z from the atom's own, q = c // 128, periodically; an entry may name the atom itself.
All inputs are finite; a program needn't handle non-finite values. No bound on the sum of `species` on one device may be relied on, other than what follows from the above.
Results may differ from a plain program's by a relative error of at most 0.0003.
Values sent between devices are 32-bit elements; how exact they have to be, the bound alone decides.
No kernel may reach another device: no remote copies, remote signals or barrier semaphores. Data moves between devices by JAX's collectives and lax.ppermute only.
A program may use at most 128 MiB of HBM per device.

v0:
```python
import math

import jax
import jax.numpy as jnp
from jax import lax
from jax.sharding import PartitionSpec as P

GRID_X = 256
GRID_Y = 256
GRID_Z = 256
AXIS_COLUMNS = 16


radius_scale = 24.0
wannier_reach = 0.5
ewald_beta = 0.9
coulomb = 0.25
atom_block = 64
largest_value = lax.Precision.HIGHEST


def extended(x, sides, width):
    for axis, dim in sides:
        size, length = (lax.axis_size(axis), x.shape[dim])
        up = [(i, (i + 1) % size) for i in range(size)]
        down = [(j, i) for i, j in up]
        last = lax.slice_in_dim(x, length - width, length, axis=dim)
        leading = lax.slice_in_dim(x, 0, width, axis=dim)
        before = lax.ppermute(last, axis, up)
        after = lax.ppermute(leading, axis, down)
        x = jnp.concatenate([before, x, after], axis=dim)
    return x


def shifted(x, axis, by):
    length = lax.axis_size(axis)
    return lax.ppermute(x, axis, [(i, (i + by) % length) for i in range(length)])


def spline(offset):
    square = offset * offset
    offset_cube = square * offset
    remain = 4.0 - offset
    piece_one = offset_cube / 6.0
    piece_two = (-3.0 * offset_cube + 12.0 * square - 12.0 * offset + 4.0) / 6.0
    piece_three = (3.0 * offset_cube - 24.0 * square + 60.0 * offset - 44.0) / 6.0
    piece_four = remain * remain * remain / 6.0
    result_value = jnp.where(
        offset < 1.0,
        piece_one,
        jnp.where(offset < 2.0, piece_two, jnp.where(offset < 3.0, piece_three, piece_four)),
    )
    inside = (offset >= 0.0) & (offset < 4.0)
    return jnp.where(inside, result_value, jnp.zeros_like(offset))


def slope(offset):
    square = offset * offset
    remain = 4.0 - offset
    piece_one = square / 2.0
    piece_two = (-9.0 * square + 24.0 * offset - 12.0) / 6.0
    piece_three = (9.0 * square - 48.0 * offset + 60.0) / 6.0
    piece_four = -remain * remain / 2.0
    result_value = jnp.where(
        offset < 1.0,
        piece_one,
        jnp.where(offset < 2.0, piece_two, jnp.where(offset < 3.0, piece_three, piece_four)),
    )
    inside = (offset >= 0.0) & (offset < 4.0)
    return jnp.where(inside, result_value, jnp.zeros_like(offset))


def environment(
    relative, hydrogen, one_w, one_b, second_weight, second_bias, third_weight, third_bias
):
    scaled = relative / radius_scale
    square = jnp.sum(scaled * scaled, axis=0)
    smooth = 1.0 / (1.0 + square)
    radial = jnp.concatenate([smooth[None], smooth[None] * scaled], axis=0)
    is_hydrogen = hydrogen[None] > 0.5
    weight = jnp.where(is_hydrogen, one_w[1][:, None, None], one_w[0][:, None, None])
    offset_b = jnp.where(is_hydrogen, one_b[1][:, None, None], one_b[0][:, None, None])
    first_layer = jnp.tanh(weight * smooth[None] + offset_b)
    second_layer = jnp.tanh(
        jnp.einsum("tky,ti->iky", first_layer, second_weight, precision=largest_value)
        + second_bias[:, None, None]
    ) + jnp.concatenate([first_layer, first_layer], axis=0)
    third_layer = jnp.tanh(
        jnp.einsum("tky,ti->iky", second_layer, third_weight, precision=largest_value)
        + third_bias[:, None, None]
    ) + jnp.concatenate([second_layer, second_layer], axis=0)
    return (
        jnp.einsum("pbn,dbn->pdb", radial, third_layer, precision=largest_value) / relative.shape[2]
    )


def fitting(matrix, one_w, one_b, second_weight, second_bias, third_weight, third_bias, out_w):
    descriptor = jnp.einsum(
        "pda,pea->dea", matrix, matrix[:, :AXIS_COLUMNS], precision=largest_value
    )
    descriptor = descriptor.reshape(-1, matrix.shape[2])
    hidden = jnp.tanh(
        jnp.einsum("fh,fa->ha", one_w, descriptor, precision=largest_value) + one_b[:, None]
    )
    hidden = hidden + jnp.tanh(
        jnp.einsum("gh,ga->ha", second_weight, hidden, precision=largest_value)
        + second_bias[:, None]
    )
    hidden = hidden + jnp.tanh(
        jnp.einsum("gh,ga->ha", third_weight, hidden, precision=largest_value) + third_bias[:, None]
    )
    coeffs = jnp.einsum("hk,ha->ka", out_w, hidden, precision=largest_value)
    return jnp.einsum("ka,cka->ca", coeffs, matrix[1:], precision=largest_value)


def folded(mode_index, length):
    wrapped = mode_index % length
    return jnp.where(2 * wrapped >= length, wrapped - length, wrapped)


def modulus(mode_index, length):
    phase_angle = (mode_index % length).astype(jnp.float32) * (2.0 * math.pi / length)
    divisor = (4.0 + 2.0 * jnp.cos(phase_angle)) / 6.0
    return 1.0 / (divisor * divisor)


def influence(index_x, index_y, index_z):
    fold_x = folded(index_x, GRID_X)
    fold_y = folded(index_y, GRID_Y)
    fold_z = folded(index_z, GRID_Z)
    freq_x = fold_x.astype(jnp.float32) / GRID_X
    freq_y = fold_y.astype(jnp.float32) / GRID_Y
    freq_z = fold_z.astype(jnp.float32) / GRID_Z
    square = freq_x * freq_x + freq_y * freq_y + freq_z * freq_z
    is_zero = (fold_x == 0) & (fold_y == 0) & (fold_z == 0)
    safe_square = jnp.where(is_zero, 1.0, square)
    result_value = jnp.exp(-(math.pi * math.pi) * square / (ewald_beta * ewald_beta)) / safe_square
    result_value = (
        result_value
        * modulus(index_x, GRID_X)
        * modulus(index_y, GRID_Y)
        * modulus(index_z, GRID_Z)
    )
    return jnp.where(is_zero, 0.0, result_value) * (coulomb / (math.pi * GRID_X * GRID_Y * GRID_Z))


def phases(length):
    counter = jnp.arange(length, dtype=jnp.int32)
    product = counter[:, None] * counter[None, :] % length
    phase_angle = product.astype(jnp.float32) * (2.0 * math.pi / length)
    return (jnp.cos(phase_angle), jnp.sin(phase_angle))


def rotate(real_part, imag_part, cos_table, sin_table, pattern, direction):
    real_cos = jnp.einsum(pattern, real_part, cos_table, precision=largest_value)
    real_sin = jnp.einsum(pattern, real_part, sin_table, precision=largest_value)
    imag_cos = jnp.einsum(pattern, imag_part, cos_table, precision=largest_value)
    imag_sin = jnp.einsum(pattern, imag_part, sin_table, precision=largest_value)
    return (real_cos - direction * imag_sin, imag_cos + direction * real_sin)


def spline_rows(coordinate, lowest, cell_count):
    grid_cells = jnp.arange(cell_count, dtype=jnp.int32).astype(jnp.float32) + lowest
    offset = coordinate[None, :] - grid_cells[:, None]
    return (spline(offset), slope(offset))


def mirrored(plane):
    return jnp.roll(jnp.flip(plane, (0, 1)), 1, (0, 1))


def local(
    positions,
    species,
    neighbours,
    embed_one_w,
    embed_one_b,
    embed_two_w,
    embed_two_b,
    embed_three_w,
    embed_three_b,
    fit_one_w,
    fit_one_b,
    fit_two_w,
    fit_two_b,
    fit_three_w,
    fit_three_b,
    fit_out_w,
):
    wide_count = lax.axis_size("wide")
    narrow_count = lax.axis_size("narrow")
    pieces = wide_count * narrow_count
    bricks = positions.shape[3]
    per_brick = positions.shape[4]
    atom_count = bricks * per_brick
    listed = neighbours.shape[4]
    cells_x = GRID_X // wide_count
    cells_z = GRID_Z // narrow_count
    brick_y = GRID_Y // bricks
    hydrogen = species.reshape(atom_count).astype(jnp.float32)
    packed = jnp.concatenate([positions, species.astype(jnp.float32)[None]], axis=0)
    ghosts = extended(packed, (("wide", 1), ("narrow", 2)), 1)
    own_atoms = positions.reshape(3, atom_count)
    code_table = neighbours.reshape(atom_count, listed)
    slot_index = code_table % per_brick
    offset = code_table // per_brick
    step_x = offset // 9
    step_z = offset // 3 % 3
    step_y = offset % 3
    home_brick = (jnp.arange(atom_count, dtype=jnp.int32) // per_brick)[:, None]
    source = (
        (step_x * 3 + step_z) * bricks + (home_brick + step_y - 1) % bricks
    ) * per_brick + slot_index
    ghost_table = ghosts.reshape(4, 9 * atom_count)
    nearby = jnp.take(ghost_table, source, axis=1)
    extent = jnp.array([cells_x, brick_y, cells_z], jnp.float32)[:, None, None]
    steps_all = jnp.stack([step_x, step_y, step_z]) - 1
    relative = (
        steps_all.astype(jnp.float32) * extent + (nearby[:3] - own_atoms[:, :, None]) * extent
    )
    block_size = min(atom_block, atom_count)
    block_count = atom_count // block_size
    rel_blocks = relative.reshape(3, block_count, block_size, listed).transpose(1, 0, 2, 3)
    kind_blocks = nearby[3].reshape(block_count, block_size, listed)

    def one_block(operands):
        return environment(
            operands[0],
            operands[1],
            embed_one_w,
            embed_one_b,
            embed_two_w,
            embed_two_b,
            embed_three_w,
            embed_three_b,
        )

    matrix = lax.map(one_block, (rel_blocks, kind_blocks))
    matrix = matrix.transpose(1, 2, 0, 3).reshape(4, matrix.shape[2], atom_count)
    dipole = fitting(
        matrix, fit_one_w, fit_one_b, fit_two_w, fit_two_b, fit_three_w, fit_three_b, fit_out_w
    )
    oxygen = 1.0 - hydrogen
    home_y = (jnp.arange(atom_count, dtype=jnp.int32) // per_brick).astype(jnp.float32)
    atom_x = own_atoms[0] * cells_x
    atom_y = home_y * brick_y + own_atoms[1] * brick_y
    atom_z = own_atoms[2] * cells_z
    displace = wannier_reach * jnp.tanh(dipole)
    site_x = jnp.concatenate([atom_x, atom_x + displace[0]])
    site_y = jnp.concatenate([atom_y, atom_y + displace[1]])
    site_z = jnp.concatenate([atom_z, atom_z + displace[2]])
    charge = jnp.concatenate([6.0 * oxygen + hydrogen, -8.0 * oxygen])
    site_count = 2 * atom_count
    weight_x, slope_x = spline_rows(site_x, -3.0, cells_x + 3)
    weight_z, slope_z = spline_rows(site_z, -3.0, cells_z + 3)
    cells_y = jnp.arange(GRID_Y, dtype=jnp.int32).astype(jnp.float32)
    offset_y = jnp.mod(site_y[None, :] - cells_y[:, None], float(GRID_Y))
    weight_y = spline(offset_y)
    slope_y = slope(offset_y)
    mixed_rows = (weight_z[:, None, :] * weight_x[None, :, :] * charge[None, None, :]).reshape(
        -1, site_count
    )
    spread = lax.dot_general(
        mixed_rows, weight_y, (((1,), (1,)), ((), ())), precision=largest_value
    )
    spread = spread.reshape(cells_z + 3, cells_x + 3, GRID_Y)
    rim_x = shifted(spread[:, :3], "wide", -1)
    inner_rows = spread[:, 3:]
    inner_rows = jnp.concatenate(
        [inner_rows[:, : cells_x - 3], inner_rows[:, cells_x - 3 :] + rim_x], axis=1
    )
    rim_z = shifted(inner_rows[:3], "narrow", -1)
    inner_rows = inner_rows[3:]
    charge_grid = jnp.concatenate(
        [inner_rows[: cells_z - 3], inner_rows[cells_z - 3 :] + rim_z], axis=0
    )
    cos_y, sin_y = phases(GRID_Y)
    mode_count = GRID_Y // 2
    counter = jnp.arange(GRID_Y, dtype=jnp.int32)
    alternate = (1 - 2 * (counter % 2)).astype(jnp.float32)
    first_mode = jnp.arange(mode_count, dtype=jnp.int32) == 0
    cos_fwd = cos_y[:, :mode_count]
    sin_fwd = jnp.where(first_mode[None, :], -alternate[:, None], sin_y[:, :mode_count])
    doubled = jnp.where(first_mode, 1.0, 2.0)[:, None]
    cos_back = cos_y[:mode_count] * doubled
    sin_back = jnp.where(first_mode[:, None], -alternate[None, :], 2.0 * sin_y[:mode_count])
    fine_modes = mode_count // pieces
    wide_modes = mode_count // wide_count
    cos_x, sin_x = phases(GRID_X)
    cos_z, sin_z = phases(GRID_Z)
    table_xc = cos_x.reshape(wide_count, cells_x, GRID_X)
    table_xs = sin_x.reshape(wide_count, cells_x, GRID_X)
    table_zc = cos_z.reshape(narrow_count, cells_z, GRID_Z)
    table_zs = sin_z.reshape(narrow_count, cells_z, GRID_Z)
    real_part = jnp.einsum(
        "zxy,ywj->zwxj",
        charge_grid,
        cos_fwd.reshape(GRID_Y, wide_count, wide_modes),
        precision=largest_value,
    )
    imag_part = -jnp.einsum(
        "zxy,ywj->zwxj",
        charge_grid,
        sin_fwd.reshape(GRID_Y, wide_count, wide_modes),
        precision=largest_value,
    )
    outgoing = jnp.stack([real_part, imag_part]).reshape(
        2, cells_z, wide_count, cells_x * wide_modes
    )
    arrived = lax.all_to_all(outgoing, "wide", split_axis=2, concat_axis=2, tiled=True)
    arrived = arrived.reshape(2, cells_z, wide_count, cells_x, narrow_count, fine_modes)
    real_part, imag_part = rotate(
        arrived[0], arrived[1], table_xc, table_xs, "zwxnj,wxm->nzmj", -1.0
    )
    outgoing = jnp.stack([real_part, imag_part]).reshape(
        2, narrow_count, cells_z * GRID_X * fine_modes
    )
    arrived = lax.all_to_all(outgoing, "narrow", split_axis=1, concat_axis=1, tiled=True)
    arrived = arrived.reshape(2, narrow_count, cells_z, GRID_X, fine_modes)
    real_part, imag_part = rotate(arrived[0], arrived[1], table_zc, table_zs, "nzmj,nzk->jmk", -1.0)
    piece_index = lax.axis_index("wide") * narrow_count + lax.axis_index("narrow")
    index_y = (piece_index * fine_modes + jnp.arange(fine_modes, dtype=jnp.int32))[:, None, None]
    index_x = jnp.arange(GRID_X, dtype=jnp.int32)[None, :, None]
    index_z = jnp.arange(GRID_Z, dtype=jnp.int32)[None, None, :]
    green_table = influence(index_x, index_y, index_z)
    is_first = piece_index == 0
    first_real = real_part[0]
    first_imag = imag_part[0]
    mirror_real = mirrored(first_real)
    mirror_imag = mirrored(first_imag)
    zero_real = 0.5 * (first_real + mirror_real)
    zero_imag = 0.5 * (first_imag - mirror_imag)
    top_real = 0.5 * (first_imag + mirror_imag)
    top_imag = 0.5 * (mirror_real - first_real)
    green_zero = green_table[0]
    green_top = influence(index_x[0], jnp.full((1, 1), GRID_Y // 2, jnp.int32), index_z[0])
    ordinary = green_table * (real_part * real_part + imag_part * imag_part)
    special = 0.5 * (
        green_zero * (zero_real * zero_real + zero_imag * zero_imag)
        + green_top * (top_real * top_real + top_imag * top_imag)
    )
    first_terms = jnp.where(is_first, special, ordinary[0])
    partial_modes = jnp.sum(ordinary[1:]) + jnp.sum(first_terms)
    packed_real = green_zero * zero_real - green_top * top_imag
    packed_imag = green_zero * zero_imag + green_top * top_real
    row_real = jnp.where(is_first, packed_real, green_zero * first_real)
    row_imag = jnp.where(is_first, packed_imag, green_zero * first_imag)
    real_part = jnp.concatenate([row_real[None], real_part[1:] * green_table[1:]], axis=0)
    imag_part = jnp.concatenate([row_imag[None], imag_part[1:] * green_table[1:]], axis=0)
    energy = lax.psum(partial_modes, ("wide", "narrow")) / (atom_count * pieces)
    real_part, imag_part = rotate(real_part, imag_part, table_zc, table_zs, "jmk,nzk->nzmj", 1.0)
    outgoing = jnp.stack([real_part, imag_part]).reshape(
        2, narrow_count, cells_z * GRID_X * fine_modes
    )
    arrived = lax.all_to_all(outgoing, "narrow", split_axis=1, concat_axis=1, tiled=True)
    arrived = arrived.reshape(2, narrow_count, cells_z, GRID_X, fine_modes)
    real_part, imag_part = rotate(
        arrived[0], arrived[1], table_xc, table_xs, "nzmj,wxm->zwxnj", 1.0
    )
    outgoing = jnp.stack([real_part, imag_part]).reshape(
        2, cells_z, wide_count, cells_x * wide_modes
    )
    arrived = lax.all_to_all(outgoing, "wide", split_axis=2, concat_axis=2, tiled=True)
    arrived = arrived.reshape(2, cells_z, wide_count, cells_x, wide_modes)
    potential_grid = jnp.einsum(
        "zwxq,wqy->zxy",
        arrived[0],
        cos_back.reshape(wide_count, wide_modes, GRID_Y),
        precision=largest_value,
    ) - jnp.einsum(
        "zwxq,wqy->zxy",
        arrived[1],
        sin_back.reshape(wide_count, wide_modes, GRID_Y),
        precision=largest_value,
    )
    lower_z = shifted(potential_grid[cells_z - 3 :], "narrow", 1)
    grid_z = jnp.concatenate([lower_z, potential_grid], axis=0)
    lower_x = shifted(grid_z[:, cells_x - 3 :], "wide", 1)
    grid_ext = jnp.concatenate([lower_x, grid_z], axis=1)
    flat_rows = grid_ext.reshape(-1, GRID_Y)
    value_rows = jnp.dot(flat_rows, weight_y, precision=largest_value).reshape(
        cells_z + 3, cells_x + 3, site_count
    )
    slope_rows = jnp.dot(flat_rows, slope_y, precision=largest_value).reshape(
        cells_z + 3, cells_x + 3, site_count
    )
    potential = jnp.einsum("zxs,zs,xs->s", value_rows, weight_z, weight_x, precision=largest_value)
    field_x = -jnp.einsum("zxs,zs,xs->s", value_rows, weight_z, slope_x, precision=largest_value)
    field_y = -jnp.einsum("zxs,zs,xs->s", slope_rows, weight_z, weight_x, precision=largest_value)
    field_z = -jnp.einsum("zxs,zs,xs->s", value_rows, slope_z, weight_x, precision=largest_value)
    fields = jnp.stack([potential, field_x, field_y, field_z])
    atom_field = fields[:, :atom_count].reshape(4, 1, 1, bricks, per_brick)
    centroid_field = (fields[:, atom_count:] * oxygen[None]).reshape(4, 1, 1, bricks, per_brick)
    dipole_out = (dipole * oxygen[None]).reshape(3, 1, 1, bricks, per_brick)
    return (dipole_out, atom_field, centroid_field, energy)


def solution(mesh):
    in_specs = (
        P(None, "wide", "narrow", None, None),
        P("wide", "narrow", None, None),
        P("wide", "narrow", None, None, None),
        P(),
        P(),
        P(),
        P(),
        P(),
        P(),
        P(),
        P(),
        P(),
        P(),
        P(),
        P(),
        P(),
    )
    out_specs = (
        P(None, "wide", "narrow", None, None),
        P(None, "wide", "narrow", None, None),
        P(None, "wide", "narrow", None, None),
        P(),
    )
    return jax.shard_map(local, mesh=mesh, in_specs=in_specs, out_specs=out_specs, check_vma=False)
```

profile of v0, /device:TPU:0, one launch (start us, length us, event | category | flops | bytes accessed | tf_op | source)
XLA Modules:
  0.0 699.7 jit_solution(8341442674070345907)
XLA Ops:
  23.2 54.8 %gather_fusion = f32[16384,4]{1,0:T(8,128)} fusion(f32[4,1152]{0,1:T(8,128)S(1)} %bitcast.523, s32[16384]{0:T(1024)S(1)} %fusion.310), kind=kCustom, calls=%fused_computation | custom fusion | bytes 589824 | tf_op jit(solution)/shard_map/jit(_take)/gather | solution.py:215
  83.8 22.5 %while.10 = (s32[]{:T(128)}, f32[2,4,100,64]{2,1,3,0:T(4,128)S(1)}, f32[2,64,128]{2,1,0:T(8,128)S(1)}, f32[2,25]{1,0:T(2,128)S(1)}, f32[2,3,64,128]{3,1,2,0:T(4,...) while((s32[]{:T(128)}, f32[2,4,100,64]{2,1,3,0:T(4,128)S(1)}, ...), condition=%wide.region_2.3_spmd, body=%wide.region_0.2_spmd.sunk | while | flops 658408448 | bytes 14297509 | solution.py:238
  89.2 5.8 fusion.522
  100.3 5.8 fusion.522
  124.3 5.6 collective-permute-done.5
  160.4 25.7 %all-to-all-done = f32[2,32,4,2048]{3,1,0,2:T(8,128)} async-done(((f32[2,32,4,2048]{3,1,0,2:T(8,128)}), f32[2,32,4,2048]{3,1,0,2:T(8,128)}, u32[]{:S(2)}, u32[]{:S(2)}) %all-to-all-start) | async-done | bytes 2097184 | tf_op jit(solution)/shard_map/all_to_all | solution.py:310
  216.0 8.6 %copy.116 = f32[8,32,256,4]{0,3,2,1:T(4,128)} copy(f32[8,32,256,4]{2,1,3,0:T(8,128)S(1)} %fusion.31) | data formatting | bytes 2097152 | tf_op jit(solution)/shard_map/add | solution.py:159
  224.6 8.6 %copy.113 = f32[8,32,256,4]{0,3,2,1:T(4,128)} copy(f32[8,32,256,4]{2,1,3,0:T(8,128)S(1)} %fusion.34) | data formatting | bytes 2097152 | tf_op jit(solution)/shard_map/sub | solution.py:159
  233.2 22.4 %pad_maximum_fusion = f32[2,8,32768]{1,2,0:T(8,128)} fusion(f32[1,8,32768]{1,2,0:T(8,128)} %bitcast.515, f32[1,8,32768]{1,2,0:T(8,128)} %bitcast.517), kind=kLoop, calls=%fused_computation.33 | loop fusion | flops 524288 | bytes 4194304 | tf_op jit(solution)/shard_map/stack | solution.py:315
  255.6 19.1 %copy.117 = f32[2,8,32768]{2,0,1:T(2,128)} copy(f32[2,8,32768]{1,2,0:T(8,128)} %pad_maximum_fusion) | data formatting | bytes 4194304 | tf_op jit(solution)/shard_map/stack | solution.py:315
  279.4 47.9 %all-to-all-done.1 = f32[2,8,32768]{2,0,1:T(2,128)} async-done(((f32[2,8,32768]{2,0,1:T(2,128)}), f32[2,8,32768]{2,0,1:T(2,128)}, u32[]{:S(2)}, u32[]{:S(2)}) %all-to-all-start.1) | async-done | bytes 2097184 | tf_op jit(solution)/shard_map/all_to_all | solution.py:318
  331.6 8.6 %copy.118 = f32[1,8,32768]{1,2,0:T(8,128)} copy(f32[1,8,32768]{2,0,1:T(1,128)S(1)} %get-tuple-element.97) | data formatting | bytes 2097152 | tf_op jit(solution)/shard_map/slice | solution.py:320
  340.2 9.8 %copy.119 = f32[8,32,256,4]{2,1,0,3:T(8,128)S(1)} copy(f32[8,32,256,4]{0,3,2,1:T(4,128)} %bitcast.511) | data formatting | bytes 2097152 | tf_op jit(solution)/shard_map/squeeze | solution.py:320
  350.0 8.6 %copy.120 = f32[1,8,32768]{1,2,0:T(8,128)} copy(f32[1,8,32768]{2,0,1:T(1,128)S(1)} %get-tuple-element.98) | data formatting | bytes 2097152 | tf_op jit(solution)/shard_map/slice | solution.py:320
  358.6 10.2 %copy.121 = f32[8,32,256,4]{2,1,0,3:T(8,128)S(1)} copy(f32[8,32,256,4]{0,3,2,1:T(4,128)} %bitcast.512) | data formatting | bytes 2097152 | tf_op jit(solution)/shard_map/squeeze | solution.py:320
  379.8 6.3 add_multiply_fusion.1
  399.7 9.8 %copy.125 = f32[8,32,256,4]{0,3,2,1:T(4,128)} copy(f32[8,32,256,4]{2,1,3,0:T(8,128)} %fusion.35) | data formatting | bytes 2097152 | tf_op jit(solution)/shard_map/add | solution.py:159
  409.5 8.6 %copy.124 = f32[8,32,256,4]{0,3,2,1:T(4,128)} copy(f32[8,32,256,4]{2,1,3,0:T(8,128)S(1)} %fusion.36) | data formatting | bytes 2097152 | tf_op jit(solution)/shard_map/sub | solution.py:159
  418.1 22.4 %pad_maximum_fusion.1 = f32[2,8,32768]{1,2,0:T(8,128)} fusion(f32[1,8,32768]{1,2,0:T(8,128)} %bitcast.516, f32[1,8,32768]{1,2,0:T(8,128)} %bitcast.518), kind=kLoop, calls=%fused_computation.34 | loop fusion | flops 524288 | bytes 4194304 | tf_op jit(solution)/shard_map/stack | solution.py:352
  440.6 19.1 %copy.126 = f32[2,8,32768]{2,0,1:T(2,128)} copy(f32[2,8,32768]{1,2,0:T(8,128)} %pad_maximum_fusion.1) | data formatting | bytes 4194304 | tf_op jit(solution)/shard_map/stack | solution.py:352
  459.6 52.0 %all_to_all.20 = f32[2,8,32768]{2,0,1:T(2,128)S(1)} all-to-all(f32[2,8,32768]{2,0,1:T(2,128)} %copy.126), channel_id=1, replica_groups=mesh['wide'=4,'narrow'=8] {'narrow'}, dimensions={1} | all-to-all | bytes 4194304 | tf_op jit(solution)/shard_map/all_to_all | solution.py:355
  513.2 8.6 %copy.127 = f32[1,8,32768]{1,2,0:T(8,128)} copy(f32[1,8,32768]{2,0,1:T(1,128)S(1)} %get-tuple-element.95) | data formatting | bytes 2097152 | tf_op jit(solution)/shard_map/slice | solution.py:358
  521.8 9.8 %copy.128 = f32[8,32,256,4]{2,1,3,0:T(8,128)S(1)} copy(f32[8,32,256,4]{0,3,2,1:T(4,128)} %bitcast.513) | data formatting | bytes 2097152 | tf_op jit(solution)/shard_map/squeeze | solution.py:358
  535.8 8.6 %copy.129 = f32[1,8,32768]{1,2,0:T(8,128)} copy(f32[1,8,32768]{2,0,1:T(1,128)S(1)} %get-tuple-element.96) | data formatting | bytes 2097152 | tf_op jit(solution)/shard_map/slice | solution.py:358
  544.4 10.1 %copy.130 = f32[8,32,256,4]{2,1,3,0:T(8,128)S(1)} copy(f32[8,32,256,4]{0,3,2,1:T(4,128)} %bitcast.514) | data formatting | bytes 2097152 | tf_op jit(solution)/shard_map/squeeze | solution.py:358
  565.8 5.9 copy.134
  571.7 5.9 copy.131
  577.5 7.3 %pad_maximum_fusion.2 = f32[2,32,4,2048]{1,3,2,0:T(8,128)} fusion(f32[1,32,4,2048]{1,3,2,0:T(8,128)} %bitcast.521, f32[1,32,4,2048]{1,3,2,0:T(8,128)} %bitcast.522), kind=kLoop, calls=%fused_computation.35 | loop fusion | flops 524288 | bytes 4194304 | tf_op jit(solution)/shard_map/stack | solution.py:360
  584.8 6.3 copy.135
  597.9 24.0 %all-to-all-done.3 = f32[2,32,4,2048]{3,1,0,2:T(8,128)} async-done(((f32[2,32,4,2048]{3,1,0,2:T(8,128)}), f32[2,32,4,2048]{3,1,0,2:T(8,128)}, u32[]{:S(2)}, u32[]{:S(2)}) %all-to-all-start.3) | async-done | bytes 2097184 | tf_op jit(solution)/shard_map/all_to_all | solution.py:363
  629.1 5.8 fusion.477
  650.3 37.3 %psum.7 = f32[]{:T(128)} all-reduce(f32[]{:T(128)S(6)} %add.1002), channel_id=1, replica_groups=mesh['wide'=4,'narrow'=8] {'wide','narrow'}, use_global_device_ids=true, to_apply=%region_5.6 | all-reduce | flops 1 | bytes 8 | tf_op jit(solution)/shard_map/psum | solution.py:350
  (259 shorter events, 205.3 us)
Async XLA Ops:
  0.6 109.1 %copy-start = (f32[1600,240]{0,1:T(8,128)S(1)}, f32[1600,240]{0,1:T(8,128)}, u32[]{:S(2)}) copy-start(f32[1600,240]{0,1:T(8,128)} %param.28) | copy-start | bytes 4608004
  2.1 8.6 %collective-permute-start.1 = (f32[4,1,1,1,128]{4,3,2,1,0:T(1,128)S(1)}, f32[4,1,1,1,128]{4,3,2,1,0:T(1,128)S(1)}, u32[]{:S(2)}, u32[]{:S(2)}) collective-permute-start(f32[4,1,1,1,128]{4,3,2,1,0:T(1,128)S(1)} %pad_maximum_fusion.15), channel_id=1, source_target_pairs={{8,0},{16,8},{24,16},{0,24},{9,1},{17,9},{25,17},{1,25},{10,2},{18... | collective-permute-start | bytes 6152 | tf_op jit(solution)/shard_map/ppermute | solution.py:30
  4.5 6.2 collective-permute-start
  4.5 114.4 %copy-start.36 = (pred[128]{0:T(512)(128)(4,1)}, pred[128]{0:T(512)(128)(4,1)S(1)}, u32[]{:S(2)}) copy-start(pred[128]{0:T(512)(128)(4,1)S(1)} %iota_compare_fusion) | copy-start | bytes 388
  4.5 110.8 %copy-start.45 = (f32[256]{0:T(256)}, f32[256]{0:T(256)S(1)}, u32[]{:S(2)}) copy-start(f32[256]{0:T(256)S(1)} %iota_convert_fusion) | copy-start | bytes 3076
  4.6 114.4 %copy-start.34 = (f32[256]{0:T(256)}, f32[256]{0:T(256)S(1)}, u32[]{:S(2)}) copy-start(f32[256]{0:T(256)S(1)} %fusion.356) | copy-start | bytes 3076
  5.9 107.2 %copy-start.32 = (f32[128]{0:T(128)}, f32[128]{0:T(128)S(1)}, u32[]{:S(2)}) copy-start(f32[128]{0:T(128)S(1)} %get-tuple-element.126) | copy-start | bytes 1540
  11.4 5.9 collective-permute-start.3
  15.9 6.4 collective-permute-start.2
  78.0 5.7 copy-start.17
  78.0 5.7 copy-start.19
  78.0 5.7 copy-start.28
  78.1 5.7 copy-start.29
  78.1 5.7 copy-start.30
  78.1 5.7 copy-start.44
  118.6 3.0 collective-permute-start.4
  121.7 8.2 %collective-permute-start.5 = (f32[3,64,256]{2,1,0:T(8,128)S(1)}, f32[3,64,256]{2,1,0:T(8,128)S(1)}, u32[]{:S(2)}, u32[]{:S(2)}) collective-permute-start(f32[3,64,256]{2,1,0:T(8,128)S(1)} %pad_maximum_fusion.10), channel_id=1, source_target_pairs={{0,7},{1,0},{2,1},{3,2},{4,3},{5,4},{6,5},{7,6},{8,15},{9,8},{10,9... | collective-permute-start | bytes 589832 | tf_op jit(solution)/shard_map/ppermute | solution.py:37
  155.9 30.2 %all-to-all-start = ((f32[2,32,4,2048]{3,1,0,2:T(8,128)}), f32[2,32,4,2048]{3,1,0,2:T(8,128)}, u32[]{:S(2)}, u32[]{:S(2)}) async-start(f32[2,32,4,2048]{3,1,0,2:T(8,128)} %copy.108), calls=%async_computation | async-start | bytes 4194304 | tf_op jit(solution)/shard_map/all_to_all | solution.py:310
  274.7 52.7 %all-to-all-start.1 = ((f32[2,8,32768]{2,0,1:T(2,128)}), f32[2,8,32768]{2,0,1:T(2,128)}, u32[]{:S(2)}, u32[]{:S(2)}) async-start(f32[2,8,32768]{2,0,1:T(2,128)} %copy.117), calls=%async_computation.1 | async-start | bytes 4194304 | tf_op jit(solution)/shard_map/all_to_all | solution.py:318
  350.0 18.8 %copy-start.8 = (f32[8,32,256,4]{2,1,0,3:T(8,128)}, f32[8,32,256,4]{2,1,0,3:T(8,128)S(1)}, u32[]{:S(2)}) copy-start(f32[8,32,256,4]{2,1,0,3:T(8,128)S(1)} %copy.119) | copy-start | bytes 3145732
  378.0 11.1 %copy-start.7 = (f32[4,256,256]{2,1,0:T(8,128)}, f32[4,256,256]{2,1,0:T(8,128)S(1)}, u32[]{:S(2)}) copy-start(f32[4,256,256]{2,1,0:T(8,128)S(1)} %fusion.39) | copy-start | bytes 3145732
  591.1 6.0 copy-start.23
  591.1 30.7 %all-to-all-start.3 = ((f32[2,32,4,2048]{3,1,0,2:T(8,128)}), f32[2,32,4,2048]{3,1,0,2:T(8,128)}, u32[]{:S(2)}, u32[]{:S(2)}) async-start(f32[2,32,4,2048]{3,1,0,2:T(8,128)} %copy.135), calls=%async_computation.3 | async-start | bytes 4194304 | tf_op jit(solution)/shard_map/all_to_all | solution.py:363
  629.1 5.8 copy-start.4
  638.7 9.3 %copy-start.5 = (f32[32,64,256]{2,1,0:T(8,128)}, f32[32,64,256]{2,1,0:T(8,128)S(1)}, u32[]{:S(2)}) copy-start(f32[32,64,256]{2,1,0:T(8,128)S(1)} %bitcast_subtract_fusion) | copy-start | bytes 6291460
  638.8 9.2 %collective-permute-start.6 = (f32[3,64,256]{2,1,0:T(8,128)S(1)}, f32[3,64,256]{2,1,0:T(8,128)S(1)}, u32[]{:S(2)}, u32[]{:S(2)}) collective-permute-start(f32[3,64,256]{2,1,0:T(8,128)S(1)} %slice.305), channel_id=1, source_target_pairs={{0,1},{1,2},{2,3},{3,4},{4,5},{5,6},{6,7},{7,0},{8,9},{9,10},{10,1... | collective-permute-start | bytes 589832 | tf_op jit(solution)/shard_map/ppermute | solution.py:37
  640.3 9.9 %copy-start.22 = (f32[256,35]{0,1:T(8,128)S(1)}, f32[256,35]{0,1:T(8,128)}, u32[]{:S(2)}) copy-start(f32[256,35]{0,1:T(8,128)} %get-tuple-element.117) | copy-start | bytes 107524
  640.3 48.0 %copy-start.25 = (f32[256,67]{0,1:T(8,128)S(1)}, f32[256,67]{0,1:T(8,128)}, u32[]{:S(2)}) copy-start(f32[256,67]{0,1:T(8,128)} %get-tuple-element.119) | copy-start | bytes 205828
  640.3 48.0 %copy-start.26 = (f32[256,67]{0,1:T(8,128)S(1)}, f32[256,67]{0,1:T(8,128)}, u32[]{:S(2)}) copy-start(f32[256,67]{0,1:T(8,128)} %get-tuple-element.121) | copy-start | bytes 205828
  640.3 48.0 %copy-start.42 = (f32[256]{0:T(256)S(1)}, f32[256]{0:T(256)}, u32[]{:S(2)}) copy-start(f32[256]{0:T(256)} %copy-done.41) | copy-start | bytes 3076
  640.3 48.0 %copy-start.46 = (f32[256]{0:T(256)S(1)}, f32[256]{0:T(256)}, u32[]{:S(2)}) copy-start(f32[256]{0:T(256)} %copy-done.45) | copy-start | bytes 3076
  648.0 40.3 %collective-permute-start.7 = (f32[35,3,256]{2,1,0:T(4,128)S(1)}, f32[35,3,256]{2,1,0:T(4,128)S(1)}, u32[]{:S(2)}, u32[]{:S(2)}) collective-permute-start(f32[35,3,256]{2,1,0:T(4,128)S(1)} %pad_maximum_fusion.11), channel_id=1, source_target_pairs={{0,8},{8,16},{16,24},{24,0},{1,9},{9,17},{17,25},{25,1},{2,10},{10... | collective-permute-start | bytes 322568 | tf_op jit(solution)/shard_map/ppermute | solution.py:37
  (27 other events, 96.2 us)
where the time goes:
time: 712 us; the launch traced here: 700 us
  local copies, waits for them, and re-layouts  281 us (39%)
  waiting for transfers between devices  117 us (16%)
  matrix products  110 us (15%)
  blocking collectives  89.3 us (13%)
  other arithmetic  74.5 us (10%)
  starting transfers between devices  23.7 us (3%)
    gather x2, local copies, waits for them, and re-layouts, local(): nearby = jnp.take(ghost_table, source, axis=1)  60.1 us
    another operation x6, local copies, waits for them, and re-layouts, local(): jnp.stack([real_part, imag_part])  53.1 us
    another operation x4, other arithmetic, local(): jnp.stack([real_part, imag_part])  52.3 us
    all_to_all x1, blocking collectives, local(): lax.all_to_all(outgoing, 'narrow', split_axis=1, concat_axis=1, tiled=True)  52 us
    all_to_all x2, waiting for transfers between devices, local(): lax.all_to_all(outgoing, 'wide', split_axis=2, concat_axis=2, tiled=True)  49.7 us
    all_to_all x1, waiting for transfers between devices, local(): lax.all_to_all(outgoing, 'narrow', split_axis=1, concat_axis=1, tiled=True)  47.9 us
    psum x1, blocking collectives, local(): energy = lax.psum(partial_modes, ('wide', 'narrow')) / (atom_count * pieces)  37.3 us
    squeeze x4, local copies, waits for them, and re-layouts, local(): arrived[1]  28.1 us
  transfers between devices with their start and end apart: 11, of which 8 were waited for; matrix products, arithmetic and copies ran while one was open for 2% of the time, Pallas kernels for 0%

commit v1 on v0

v1 whole, which is shorter than its diff:
```python
import math

import jax
import jax.numpy as jnp
import numpy as np
from jax import lax
from jax.experimental import pallas as pl
from jax.experimental.pallas import tpu as pltpu
from jax.sharding import PartitionSpec as P

GRID_X = 256
GRID_Y = 256
GRID_Z = 256
AXIS_COLUMNS = 16

radius_scale = 24.0
wannier_reach = 0.5
ewald_beta = 0.9
coulomb = 0.25

ROW_PAD = 32
SLOT_CHUNK = 16
HALO_X = 16
HALO_Z = 8

NN = (((1,), (0,)), ((), ()))
NT = (((1,), (1,)), ((), ()))


def split(value):
    high = value.astype(jnp.bfloat16)
    low = (value - high.astype(jnp.float32)).astype(jnp.bfloat16)
    return high, low


def multiply(left, right, dims=NN):
    def one(a, b):
        return lax.dot_general(a, b, dims, preferred_element_type=jnp.float32)

    return one(left[0], right[0]) + (one(left[1], right[0]) + one(left[0], right[1]))


def spline_pair(offset):
    centred = offset - 2.0
    away = jnp.abs(centred)
    outer = jnp.maximum(2.0 - away, 0.0)
    inner = jnp.maximum(1.0 - away, 0.0)
    outer_square = outer * outer
    inner_square = inner * inner
    value = (outer_square * outer - 4.0 * (inner_square * inner)) * (1.0 / 6.0)
    slope = jnp.where(centred < 0.0, 0.5, -0.5) * (outer_square - 4.0 * inner_square)
    return value, slope


def centroid_kernel(
    place,
    table,
    codes,
    columns,
    second,
    third,
    fit_one_w,
    fit_one_b,
    fit_two_w,
    fit_two_b,
    fit_three_w,
    fit_three_b,
    fit_out_w,
    dipole_ref,
    shift_ref,
    matrix,
    descriptor,
):
    wide_count, narrow_count, _, atoms = table.shape
    listed = codes.shape[0]
    width_one = fit_out_w.shape[1] // 4
    width_three = fit_out_w.shape[1]
    cells = (GRID_X // wide_count, GRID_Y, GRID_Z // narrow_count)
    at_wide = place[0]
    at_narrow = place[1]
    own = table[at_wide, at_narrow]
    nearby = []
    for step in range(9):
        wide_at = lax.rem(at_wide + (step // 3 - 1) + wide_count, wide_count)
        narrow_at = lax.rem(at_narrow + (step % 3 - 1) + narrow_count, narrow_count)
        nearby.append(table[wide_at, narrow_at])

    second_high, second_low = split(second[...])
    second_all = jnp.concatenate([second_high, second_high, second_low], axis=1)
    third_high, third_low = split(third[...])
    third_all = jnp.concatenate([third_high, third_high, third_low], axis=1)
    weight_oxygen = columns[0:ROW_PAD, 0:1]
    weight_hydrogen = columns[0:ROW_PAD, 1:2]
    bias_oxygen = columns[0:ROW_PAD, 2:3]
    bias_hydrogen = columns[0:ROW_PAD, 3:4]
    second_bias = columns[0 : 2 * ROW_PAD, 4:5]
    third_bias = columns[0 : 4 * ROW_PAD, 5:6]
    matrix[...] = jnp.zeros_like(matrix)

    def chunk(index, carry):
        first = pl.multiple_of(index * SLOT_CHUNK, SLOT_CHUNK)
        code = codes[pl.ds(first, SLOT_CHUNK), :]
        offset = code // atoms
        slot = code - offset * atoms
        step_x = jnp.where(offset >= 9, 1, 0) + jnp.where(offset >= 18, 1, 0)
        rest = offset - 9 * step_x
        step_z = jnp.where(rest >= 3, 1, 0) + jnp.where(rest >= 6, 1, 0)
        step_y = rest - 3 * step_z
        brick = step_x * 3 + step_z
        found = []
        for component in range(4):
            picked = jnp.zeros((SLOT_CHUNK, atoms), jnp.float32)
            for step in range(9):
                row = jnp.broadcast_to(
                    nearby[step][component : component + 1], (SLOT_CHUNK, atoms)
                )
                here = jnp.take_along_axis(row, slot, axis=1, mode="promise_in_bounds")
                picked = jnp.where(brick == step, here, picked)
            found.append(picked)
        scaled = []
        for component, step in enumerate((step_x, step_y, step_z)):
            extent = float(cells[component])
            relative = (step - 1).astype(jnp.float32) * extent + (
                found[component] - own[component : component + 1]
            ) * extent
            scaled.append(relative * (1.0 / radius_scale))
        smooth = 1.0 / (
            1.0 + (scaled[0] * scaled[0] + scaled[1] * scaled[1] + scaled[2] * scaled[2])
        )
        radial = [smooth] + [smooth * part for part in scaled]
        hydrogen = found[3] > 0.5
        first_layers = []
        for k in range(SLOT_CHUNK):
            row = smooth[k : k + 1]
            kind = hydrogen[k : k + 1]
            weight = jnp.where(kind, weight_hydrogen, weight_oxygen)
            bias = jnp.where(kind, bias_hydrogen, bias_oxygen)
            first_layers.append(jnp.tanh(weight * row + bias))
        layer_one = jnp.concatenate(first_layers, axis=1)
        high, low = split(layer_one)
        layer_two = lax.dot_general(
            second_all,
            jnp.concatenate([high, low, high], axis=0),
            NN,
            preferred_element_type=jnp.float32,
        )
        layer_two = jnp.tanh(layer_two + second_bias) + jnp.concatenate(
            [layer_one, layer_one], axis=0
        )
        high, low = split(layer_two)
        layer_three = lax.dot_general(
            third_all,
            jnp.concatenate([high, low, high], axis=0),
            NN,
            preferred_element_type=jnp.float32,
        )
        layer_three = jnp.tanh(layer_three + third_bias) + jnp.concatenate(
            [layer_two, layer_two], axis=0
        )
        for part in range(4):
            total = matrix[part]
            for k in range(SLOT_CHUNK):
                total = total + layer_three[:, k * atoms : (k + 1) * atoms] * radial[part][k : k + 1]
            matrix[part] = total
        return carry

    lax.fori_loop(0, listed // SLOT_CHUNK, chunk, 0)

    parts = []
    for part in range(4):
        padded = matrix[part] * (1.0 / listed)
        parts.append(
            jnp.concatenate(
                [padded[k * ROW_PAD : k * ROW_PAD + width_one] for k in range(4)], axis=0
            )
        )
    leading = [part[0:AXIS_COLUMNS] for part in parts]
    for row in range(width_three):
        total = parts[0][row : row + 1] * leading[0]
        for part in range(1, 4):
            total = total + parts[part][row : row + 1] * leading[part]
        descriptor[row * AXIS_COLUMNS : (row + 1) * AXIS_COLUMNS, :] = total
    entries = width_three * AXIS_COLUMNS
    descriptor[entries:, :] = jnp.zeros((descriptor.shape[0] - entries, atoms), jnp.float32)
    turned = jnp.transpose(descriptor[...])
    hidden = jnp.tanh(
        multiply(split(turned[:, :entries]), split(fit_one_w[...])) + fit_one_b[...]
    )
    hidden = hidden + jnp.tanh(multiply(split(hidden), split(fit_two_w[...])) + fit_two_b[...])
    hidden = hidden + jnp.tanh(multiply(split(hidden), split(fit_three_w[...])) + fit_three_b[...])
    coeffs = multiply(split(hidden), split(fit_out_w[...]))
    coeffs = jnp.concatenate(
        [coeffs, jnp.zeros((atoms, 128 - width_three), jnp.float32)], axis=1
    )
    coeffs = jnp.transpose(coeffs)[:width_three]
    vector = jnp.concatenate(
        [jnp.sum(coeffs * parts[1 + c], axis=0, keepdims=True) for c in range(3)], axis=0
    )
    dipole_ref[...] = vector * (1.0 - own[3:4])
    moved = wannier_reach * jnp.tanh(vector)
    moved = jnp.concatenate([moved, jnp.zeros((1, atoms), jnp.float32)], axis=0)
    for target in range(shift_ref.shape[0]):
        shift_ref[target] = moved


def mesh_kernel(
    place,
    factors,
    table,
    shifts,
    phase,
    factor_row,
    factor_column,
    ahead_high,
    ahead_low,
    back_high,
    back_low,
    out_ref,
    grid,
    modes,
    weight_high,
    weight_low,
    slope_high,
    slope_low,
    waves,
    wave_slopes,
):
    wide_count, narrow_count, _, atoms = table.shape
    cells_x = GRID_X // wide_count
    cells_z = GRID_Z // narrow_count
    window = cells_z + HALO_Z
    pair = 2 * atoms
    length = wide_count * pair
    channels = 2 * (grid.shape[0] - 1)
    fine = channels // 2
    piece = place[0] * narrow_count + place[1]
    ahead = (ahead_high, ahead_low)
    back = (back_high, back_low)

    def read(pair_of_refs):
        return (pair_of_refs[0][...], pair_of_refs[1][...])

    def sites(at_wide, at_narrow):
        atom = table[at_wide, at_narrow]
        moved = shifts[at_wide, at_narrow]
        rows = []
        for component, extent in enumerate((cells_x, GRID_Y, cells_z)):
            start = atom[component : component + 1] * float(extent)
            rows.append(jnp.concatenate([start, start + moved[component : component + 1]], axis=1))
        oxygen = 1.0 - atom[3:4]
        rows.append(jnp.concatenate([6.0 * oxygen + atom[3:4], -8.0 * oxygen], axis=1))
        return rows

    def line(at_narrow):
        groups = [sites(at_wide, at_narrow) for at_wide in range(wide_count)]
        return [jnp.concatenate([g[k] for g in groups], axis=1) for k in range(4)]

    def weights_z(row):
        counter = lax.broadcasted_iota(jnp.int32, (window, 1), 0).astype(jnp.float32)
        return spline_pair(row - (counter - float(HALO_Z)))

    def fill_x(row, targets):
        counter = lax.broadcasted_iota(jnp.int32, (cells_x + HALO_X, 1), 0).astype(jnp.float32)
        for at_wide in range(wide_count):
            lanes = slice(at_wide * pair, (at_wide + 1) * pair)
            both = spline_pair(row[:, lanes] - (counter - float(HALO_X)))
            for values, (high_ref, low_ref) in zip(both, targets):
                high, low = split(values)
                below = (at_wide * cells_x - HALO_X) % GRID_X
                start = at_wide * cells_x
                for ref, half in ((high_ref, high), (low_ref, low)):
                    ref[below : below + HALO_X, lanes] = half[:HALO_X]
                    ref[start : start + cells_x, lanes] = half[HALO_X:]

    for ref in (weight_high, weight_low, slope_high, slope_low):
        ref[...] = jnp.zeros_like(ref)
    grid[...] = jnp.zeros_like(grid)
    weights = (weight_high, weight_low)
    slopes = (slope_high, slope_low)

    def spread(at_narrow, carry):
        row_x, row_y, row_z, charge = line(at_narrow)
        lower = jnp.floor(row_y)
        share = row_y - lower
        cell = lower.astype(jnp.int32)
        rows = phase.shape[0]
        wave_blocks = []
        slope_blocks = []
        for block in range(length // 128):
            lanes = slice(block * 128, (block + 1) * 128)
            wave = jnp.zeros((rows, 128), jnp.float32)
            wave_slope = jnp.zeros((rows, 128), jnp.float32)
            for back_by in range(4):
                where = lax.rem(cell[:, lanes] + (GRID_Y - back_by), GRID_Y)
                value, slope = spline_pair(share[:, lanes] + float(back_by))
                found = jnp.zeros((rows, 128), jnp.float32)
                for part in range(GRID_Y // 128):
                    spot = jnp.broadcast_to(where - part * 128, (rows, 128))
                    inside = (spot >= 0) & (spot < 128)
                    here = jnp.take_along_axis(
                        phase[:, part * 128 : (part + 1) * 128],
                        jnp.where(inside, spot, 0),
                        axis=1,
                        mode="promise_in_bounds",
                    )
                    found = jnp.where(inside, here, found)
                wave = wave + value * found
                wave_slope = wave_slope + slope * found
            wave_blocks.append(wave)
            slope_blocks.append(wave_slope)
        wave = jnp.concatenate(wave_blocks, axis=1)
        waves[at_narrow] = wave
        wave_slopes[at_narrow] = jnp.concatenate(slope_blocks, axis=1)
        fill_x(row_x, (weights,))
        value_z, _ = weights_z(row_z)
        charged = wave * charge
        left = jnp.concatenate([value_z * charged[c : c + 1] for c in range(channels)], axis=0)
        total = multiply(split(left), read(weights), NT)
        first = pl.multiple_of(at_narrow * cells_z, HALO_Z)
        for c in range(channels):
            lanes = slice((c % 2) * GRID_X, (c % 2 + 1) * GRID_X)
            grid[c // 2, pl.ds(first, window), lanes] += total[c * window : (c + 1) * window]
        return carry

    lax.fori_loop(0, narrow_count, spread, 0)
    for j in range(fine):
        grid[j, GRID_Z : GRID_Z + HALO_Z, :] += grid[j, 0:HALO_Z, :]
    is_first = piece == 0
    second_plane = grid[0, :, GRID_X:]
    empty = jnp.zeros_like(second_plane)
    grid[fine, :, 0:GRID_X] = jnp.where(is_first, second_plane, empty)
    grid[0, :, GRID_X:] = jnp.where(is_first, empty, second_plane)

    def to_modes(j, energy):
        plane = multiply(split(grid[j, HALO_Z:, :]), read(ahead))
        plane = jnp.concatenate([plane[:, :GRID_X], plane[:, GRID_X:]], axis=0)
        spectrum = multiply(read(back), split(plane))
        real = spectrum[:GRID_Z]
        imag = spectrum[GRID_Z:]
        mode = jnp.where(j == fine, GRID_Y // 2, piece * fine + j)
        square = factors[1, mode] + factor_row[1:2, :] + factor_column[:, 1:2]
        top = factors[0, mode] * (factor_row[0:1, :] * factor_column[:, 0:1])
        green = jnp.where(square == 0.0, 0.0, top / jnp.where(square == 0.0, 1.0, square))
        share = jnp.where((mode == 0) | (mode == GRID_Y // 2), 0.5, 1.0)
        energy = energy + share * jnp.sum(green * (real * real + imag * imag))
        modes[j, 0:GRID_Z, :] = green * real
        modes[j, GRID_Z:, :] = green * imag
        return energy

    energy = lax.fori_loop(0, fine + 1, to_modes, jnp.float32(0.0))
    modes[0, 0:GRID_Z, :] -= modes[fine, GRID_Z:, :]
    modes[0, GRID_Z:, :] += modes[fine, 0:GRID_Z, :]

    def to_grid(j, carry):
        plane = multiply(read(ahead), split(modes[j]))
        plane = jnp.concatenate([plane[:GRID_Z], plane[GRID_Z:]], axis=1)
        plane = multiply(split(plane), read(back))
        mode = piece * fine + j
        plane = plane * jnp.where(mode == 0, 1.0, 2.0)
        grid[j, HALO_Z:, :] = plane
        grid[j, 0:HALO_Z, :] = plane[GRID_Z - HALO_Z :]
        return carry

    lax.fori_loop(0, fine, to_grid, 0)

    def collect(at_narrow, carry):
        row_x, _, row_z, _ = line(at_narrow)
        fill_x(row_x, (weights, slopes))
        value_z, slope_z = weights_z(row_z)
        first = pl.multiple_of(at_narrow * cells_z, HALO_Z)
        left = jnp.concatenate(
            [
                grid[c // 2, pl.ds(first, window), (c % 2) * GRID_X : (c % 2 + 1) * GRID_X]
                for c in range(channels)
            ],
            axis=0,
        )
        left = split(left)
        wave = waves[at_narrow]
        wave_slope = wave_slopes[at_narrow]
        for at_wide in range(wide_count):
            lanes = slice(at_wide * pair, (at_wide + 1) * pair)
            value = multiply(left, (weight_high[:, lanes], weight_low[:, lanes]))
            slope = multiply(left, (slope_high[:, lanes], slope_low[:, lanes]))
            plain = jnp.zeros((window, pair), jnp.float32)
            along_x = plain
            along_y = plain
            for c in range(channels):
                rows = slice(c * window, (c + 1) * window)
                plain = plain + value[rows] * wave[c : c + 1, lanes]
                along_x = along_x + slope[rows] * wave[c : c + 1, lanes]
                along_y = along_y + value[rows] * wave_slope[c : c + 1, lanes]
            near = value_z[:, lanes]
            near_slope = slope_z[:, lanes]
            results = [
                jnp.sum(near * plain, axis=0, keepdims=True),
                -jnp.sum(near * along_x, axis=0, keepdims=True),
                -jnp.sum(near * along_y, axis=0, keepdims=True),
                -jnp.sum(near_slope * plain, axis=0, keepdims=True),
            ]
            for k, row in enumerate(results):
                out_ref[at_wide, at_narrow, :, k * pair : (k + 1) * pair] = row
            out_ref[at_wide, at_narrow, :, 4 * pair :] = jnp.full((1, 128), energy, jnp.float32)
        return carry

    lax.fori_loop(0, narrow_count, collect, 0)


def mode_factors(length):
    counter = np.arange(length)
    wrapped = np.where(2 * counter >= length, counter - length, counter)
    square = (wrapped / length) ** 2
    ratio = (4.0 + 2.0 * np.cos(2.0 * math.pi * counter / length)) / 6.0
    return np.stack([np.exp(-(math.pi**2) * square / ewald_beta**2) / ratio**2, square])


def halves(table):
    high = table.astype(jnp.bfloat16)
    low = (table - high.astype(np.float64)).astype(jnp.bfloat16)
    return high, low


def grouped(array, width):
    parts = array.reshape((-1, width) + array.shape[1:])
    pads = ((0, 0), (0, ROW_PAD - width)) + ((0, 0),) * (array.ndim - 1)
    parts = jnp.pad(parts, pads)
    return parts.reshape((-1,) + array.shape[1:])


def vmem(count):
    return [pl.BlockSpec(memory_space=pltpu.VMEM)] * count


def smem(count):
    return [pl.BlockSpec(memory_space=pltpu.SMEM)] * count


def local(
    positions,
    species,
    neighbours,
    embed_one_w,
    embed_one_b,
    embed_two_w,
    embed_two_b,
    embed_three_w,
    embed_three_b,
    fit_one_w,
    fit_one_b,
    fit_two_w,
    fit_two_b,
    fit_three_w,
    fit_three_b,
    fit_out_w,
):
    axes = ("wide", "narrow")
    wide_count = lax.axis_size("wide")
    narrow_count = lax.axis_size("narrow")
    pieces = wide_count * narrow_count
    atoms = positions.shape[4]
    listed = neighbours.shape[4]
    place = jnp.stack([lax.axis_index("wide"), lax.axis_index("narrow")]).astype(jnp.int32)
    piece = place[0] * narrow_count + place[1]

    kinds = species.reshape(1, atoms).astype(jnp.float32)
    packed = jnp.concatenate([positions.reshape(3, atoms), kinds], axis=0)
    table = lax.all_to_all(
        jnp.broadcast_to(packed[None], (pieces, 4, atoms)), axes, 0, 0, tiled=True
    )
    table = table.reshape(wide_count, narrow_count, 4, atoms)

    width_one = embed_one_w.shape[1]
    tall = 4 * ROW_PAD
    column_list = [
        embed_one_w[0],
        embed_one_w[1],
        embed_one_b[0],
        embed_one_b[1],
        embed_two_b,
        embed_three_b,
    ]
    columns = []
    for column in column_list:
        rows = grouped(column, width_one)
        columns.append(jnp.pad(rows, (0, tall - rows.shape[0])))
    columns = jnp.stack(columns, axis=1)
    second = grouped(jnp.pad(embed_two_w.T, ((0, 0), (0, ROW_PAD - width_one))), width_one)
    third = grouped(grouped(embed_three_w, width_one).T, width_one)
    codes = neighbours.reshape(atoms, listed).T
    entries = fit_one_w.shape[0]
    dipole, shifts = pl.pallas_call(
        centroid_kernel,
        out_shape=(
            jax.ShapeDtypeStruct((3, atoms), jnp.float32),
            jax.ShapeDtypeStruct((pieces, 4, atoms), jnp.float32),
        ),
        in_specs=smem(1) + vmem(12),
        out_specs=tuple(vmem(2)),
        scratch_shapes=[
            pltpu.VMEM((4, tall, atoms), jnp.float32),
            pltpu.VMEM((-(-entries // 128) * 128, atoms), jnp.float32),
        ],
        compiler_params=pltpu.CompilerParams(vmem_limit_bytes=32 * 1024 * 1024),
        name="centroids",
    )(
        place,
        table,
        codes,
        columns,
        second,
        third,
        fit_one_w,
        fit_one_b[None],
        fit_two_w,
        fit_two_b[None],
        fit_three_w,
        fit_three_b[None],
        fit_out_w,
    )
    shifts = lax.all_to_all(shifts, axes, 0, 0, tiled=True)
    shifts = shifts.reshape(wide_count, narrow_count, 4, atoms)

    fine = GRID_Y // 2 // pieces
    mode = piece * fine + jnp.arange(fine, dtype=jnp.int32)
    counter = jnp.arange(GRID_Y, dtype=jnp.int32)
    angle = (mode[:, None] * counter[None, :] % GRID_Y).astype(jnp.float32) * (
        2.0 * math.pi / GRID_Y
    )
    alternate = (1 - 2 * (counter % 2)).astype(jnp.float32)
    sine = jnp.where(mode[:, None] == 0, alternate[None, :], -jnp.sin(angle))
    phase = jnp.stack([jnp.cos(angle), sine], axis=1).reshape(2 * fine, GRID_Y)
    phase = jnp.pad(phase, ((0, -2 * fine % 8), (0, 0)))

    turns = np.outer(np.arange(GRID_X), np.arange(GRID_X)) % GRID_X * (2.0 * math.pi / GRID_X)
    cosine = np.cos(turns)
    sines = np.sin(turns)
    ahead = np.block([[cosine, -sines], [sines, cosine]])
    scale = coulomb / (math.pi * GRID_X * GRID_Y * GRID_Z)
    factors = mode_factors(GRID_Y)
    factors[0] *= scale
    window = GRID_Z // narrow_count + HALO_Z
    length = wide_count * 2 * atoms
    out_width = 8 * atoms + 128
    partial = pl.pallas_call(
        mesh_kernel,
        out_shape=jax.ShapeDtypeStruct((wide_count, narrow_count, 1, out_width), jnp.float32),
        in_specs=smem(2) + vmem(9),
        out_specs=vmem(1)[0],
        scratch_shapes=[
            pltpu.VMEM((fine + 1, HALO_Z + GRID_Z, 2 * GRID_X), jnp.float32),
            pltpu.VMEM((fine + 1, 2 * GRID_Z, GRID_X), jnp.float32),
        ]
        + [pltpu.VMEM((GRID_X, length), jnp.bfloat16)] * 4
        + [pltpu.VMEM((narrow_count, phase.shape[0], length), jnp.float32)] * 2,
        compiler_params=pltpu.CompilerParams(vmem_limit_bytes=48 * 1024 * 1024),
        name="mesh",
    )(
        place,
        jnp.asarray(factors, jnp.float32),
        table,
        shifts,
        phase,
        jnp.asarray(mode_factors(GRID_X), jnp.float32),
        jnp.asarray(mode_factors(GRID_Z).T, jnp.float32),
        *[jnp.asarray(half) for half in halves(ahead)],
        *[jnp.asarray(half) for half in halves(ahead.T)],
    )
    arrived = lax.all_to_all(
        partial.reshape(pieces, 1, out_width), axes, 0, 0, tiled=True
    )
    total = jnp.sum(arrived, axis=(0, 1))
    fields = total[: 8 * atoms].reshape(4, 2, atoms)
    energy = total[8 * atoms] / (atoms * pieces)
    atom_field = fields[:, 0].reshape(4, 1, 1, 1, atoms)
    centroid_field = (fields[:, 1] * (1.0 - kinds)).reshape(4, 1, 1, 1, atoms)
    return (dipole.reshape(3, 1, 1, 1, atoms), atom_field, centroid_field, energy)


def solution(mesh):
    column = P(None, "wide", "narrow", None, None)
    in_specs = (column, P("wide", "narrow", None, None), P("wide", "narrow", None, None, None))
    in_specs = in_specs + (P(),) * 13
    out_specs = (column, column, column, P())
    return jax.shard_map(local, mesh=mesh, in_specs=in_specs, out_specs=out_specs, check_vma=False)
```

time: 712 us -> 101 us (0.14); the launches traced: 700 us -> 99.9 us
  local copies, waits for them, and re-layouts: 281 us -> 20 us
  matrix products: 110 us -> 0 us
  waiting for transfers between devices: 117 us -> 13.6 us
  blocking collectives: 89.3 us -> 0 us
  other arithmetic: 74.5 us -> 3.95 us
  Pallas kernels: 0 us -> 44 us
  starting transfers between devices: 23.7 us -> 15.7 us
    dot_general x33 -> x0, matrix products: 109 us -> none  [the longest x4 16.4 us: rotate(): jnp.einsum(pattern, real_part, sin_table, precision=largest_value)]
    all_to_all x3, waiting for transfers between devices: 97.6 us -> 13.6 us  [the longest x1 7.24 us: local(): lax.all_to_all(partial.reshape(pieces, 1, out_width), axes, 0, 0, tiled=T...]
    gather x2 -> x0, local copies, waits for them, and re-layouts: 60.1 us -> none  [local(): nearby = jnp.take(ghost_table, source, axis=1)]
    squeeze x8 -> x0, local copies, waits for them, and re-layouts: 55.3 us -> none  [the longest x4 28.1 us: local(): arrived[1]]
    another operation x6 -> x8, local copies, waits for them, and re-layouts: 53.1 us -> 0.25 us  [local(): columns = jnp.stack(columns, axis=1)]
    another operation x5 -> x2, other arithmetic: 52.3 us -> 0.09 us  [the longest x1 0.07 us: local(): jnp.stack([lax.axis_index('wide'), lax.axis_index('narrow')])]
    all_to_all x1 -> x0, blocking collectives: 52 us -> none  [local(): lax.all_to_all(outgoing, 'narrow', split_axis=1, concat_axis=1, tiled=True)]
    slice x25 -> x5, local copies, waits for them, and re-layouts: 52.1 us -> 2.61 us  [the longest x1 0.76 us: local(): embed_one_b[1]]
  transfers between devices with their start and end apart: 11 -> 3, of which waited for: 8 -> 2; matrix products, arithmetic and copies ran while one was open for 2% -> 13% of each run, Pallas kernels for 0% -> 0%
where the time goes in v1:
time: 101 us; the launch traced here: 99.9 us
  Pallas kernels  44 us (44%)
  local copies, waits for them, and re-layouts  20 us (20%)
  starting transfers between devices  15.7 us (16%)
  waiting for transfers between devices  13.6 us (13%)
  other arithmetic  3.95 us (4%)
  between operations  2.63 us (3%)
    pallas_call x1, Pallas kernels, local(): pl.pallas_call(mesh_kernel, out_shape=jax.ShapeDtypeStruct((wide_count, n...  34.6 us
    unnamed x38, local copies, waits for them, and re-layouts  11.9 us
    pallas_call x1, Pallas kernels, local(): pl.pallas_call(centroid_kernel, out_shape=(jax.ShapeDtypeStruct((3, atoms...  9.41 us
    all_to_all x1, starting transfers between devices, local(): lax.all_to_all(jnp.broadcast_to(packed[None], (pieces, 4, atoms)), axes,...  7.3 us
    all_to_all x1, waiting for transfers between devices, local(): lax.all_to_all(partial.reshape(pieces, 1, out_width), axes, 0, 0, tiled=T...  7.24 us
    all_to_all x1, waiting for transfers between devices, local(): shifts = lax.all_to_all(shifts, axes, 0, 0, tiled=True)  6.34 us
    all_to_all x1, starting transfers between devices, local(): shifts = lax.all_to_all(shifts, axes, 0, 0, tiled=True)  5.83 us
    all_to_all x1, starting transfers between devices, local(): lax.all_to_all(partial.reshape(pieces, 1, out_width), axes, 0, 0, tiled=T...  2.58 us
  transfers between devices with their start and end apart: 3, of which 2 were waited for; matrix products, arithmetic and copies ran while one was open for 13% of the time, Pallas kernels for 0%

profile of v1, /device:TPU:0, one launch (start us, length us, event | category | flops | bytes accessed | tf_op | source)
XLA Modules:
  0.0 99.9 jit_solution(9832401671655109512)
XLA Ops:
  0.6 0.7 convert_bitcast_fusion
  1.3 0.7 copy.65
  2.0 0.6 broadcast_in_dim.35
  2.6 7.3 %all-to-all-start = ((f32[32,4,128]{2,1,0:T(4,128)}), f32[32,4,128]{2,1,0:T(4,128)S(1)}, u32[]{:S(2)}, u32[]{:S(2)}) async-start(f32[32,4,128]{2,1,0:T(4,128)} %broadcast_in_dim.35), calls=%async_computation | async-start | bytes 131072 | tf_op jit(solution)/shard_map/all_to_all | solution.py:467
  11.0 0.8 fusion.9
  11.7 0.8 fusion.8
  12.5 0.7 reshape.289
  13.4 0.9 copy.53
  14.4 0.7 reshape.291
  15.4 0.7 pad.65
  16.3 0.6 pad.66.clone
  16.9 0.8 reshape.294
  17.8 0.6 pad.68
  18.4 1.8 %copy.57.fit_one_w = f32[1600,240]{1,0:T(8,128)S(1)} copy(f32[1600,240]{0,1:T(8,128)} %param.32) | data formatting | bytes 3072000 | tf_op args[9]
  20.3 1.1 %copy.58.fit_out_w = f32[240,100]{1,0:T(8,128)S(1)} copy(f32[240,100]{0,1:T(8,128)} %param.38) | data formatting | bytes 192000 | tf_op args[15]
  22.0 0.8 copy-done.4
  22.8 0.9 copy-done.5
  23.7 0.9 copy-done.6
  24.7 0.8 copy-done.7
  25.4 0.7 copy-done.14
  26.1 9.4 %centroids.1 = (f32[3,128]{1,0:T(4,128)S(1)}, f32[32,4,128]{2,1,0:T(4,128)S(1)}) custom-call(s32[2]{0:T(128)S(1)} %pad_add_fusion.place, f32[4,8,4,128]{3,2,1,0:T(4,128)S(1)} %bitcast.52, s32[128,128]{1,0:T(8,128)S(1)} %bitcast.54, f32[128,6]{1,0:T(8,128)S(1)} %copy.56.columns, f32[64,32]{1,0:T(8,128)S(1)} %bitcast.57, f32[128,64]{1,0:T(8,128)S(1)} %bitcast.56, ...), custom_call_target="tpu_custom_call" | custom-call | tf_op jit(solution)/shard_map/centroids/pallas_call | solution.py:491
  35.5 0.6 copy-done.9
  36.2 5.8 %all-to-all-start.1 = ((f32[32,4,128]{2,1,0:T(4,128)}), f32[32,4,128]{2,1,0:T(4,128)S(1)}, u32[]{:S(2)}, u32[]{:S(2)}) async-start(f32[32,4,128]{2,1,0:T(4,128)} %copy-done.9), calls=%async_computation.1 | async-start | bytes 131072 | tf_op jit(solution)/shard_map/all_to_all | solution.py:520
  42.0 0.9 fusion.3
  42.9 6.3 %all-to-all-done.1 = f32[32,4,128]{2,1,0:T(4,128)S(1)} async-done(((f32[32,4,128]{2,1,0:T(4,128)}), f32[32,4,128]{2,1,0:T(4,128)S(1)}, u32[]{:S(2)}, u32[]{:S(2)}) %all-to-all-start.1) | async-done | bytes 65568 | tf_op jit(solution)/shard_map/all_to_all | solution.py:520
  49.3 1.0 %copy-done.3 = bf16[512,512]{1,0:T(8,128)(2,1)S(1)} copy-done((bf16[512,512]{1,0:T(8,128)(2,1)S(1)}, bf16[512,512]{1,0:T(8,128)(2,1)}, u32[]{:S(2)}) %copy-start.3) | copy-done | bytes 524312
  50.4 0.9 copy-done.8
  51.3 34.6 %mesh.1 = f32[4,8,1,1152]{3,2,1,0:T(1,128)} custom-call(s32[2]{0:T(128)S(1)} %pad_add_fusion.place, f32[2,256]{1,0:T(2,128)S(1)} %copy-done.10, f32[4,8,4,128]{3,2,1,0:T(4,128)S(1)} %bitcast.53, f32[4,8,4,128]{3,2,1,0:T(4,128)S(1)} %bitcast.55, f32[8,256]{1,0:T(8,128)S(1)} %reshape.300.phase, f32[2,256]{1,0:T(2,128)S(1)} %copy-done.11, ...), custom_call_target="tpu_custom_call" | custom-call | tf_op jit(solution)/shard_map/mesh/pallas_call | solution.py:544
  85.9 2.6 %all-to-all-start.2 = ((f32[32,1,1152]{2,1,0:T(1,128)}), f32[32,1,1152]{2,1,0:T(1,128)S(1)}, u32[]{:S(2)}, u32[]{:S(2)}) async-start(f32[32,1,1152]{2,1,0:T(1,128)} %bitcast.25), calls=%async_computation.2 | async-start | bytes 294912 | tf_op jit(solution)/shard_map/all_to_all | solution.py:568
  89.1 7.2 %all-to-all-done.2 = f32[32,1,1152]{2,1,0:T(1,128)S(1)} async-done(((f32[32,1,1152]{2,1,0:T(1,128)}), f32[32,1,1152]{2,1,0:T(1,128)S(1)}, u32[]{:S(2)}, u32[]{:S(2)}) %all-to-all-start.2) | async-done | bytes 147488 | tf_op jit(solution)/shard_map/all_to_all | solution.py:568
  96.9 0.6 fusion.7
  97.5 0.6 broadcast_multiply_fusion
  (55 shorter events, 3.6 us)
Async XLA Ops:
  2.6 19.3 %all-to-all-start = ((f32[32,4,128]{2,1,0:T(4,128)}), f32[32,4,128]{2,1,0:T(4,128)S(1)}, u32[]{:S(2)}, u32[]{:S(2)}) async-start(f32[32,4,128]{2,1,0:T(4,128)} %broadcast_in_dim.35), calls=%async_computation | async-start | bytes 131072 | tf_op jit(solution)/shard_map/all_to_all | solution.py:467
  18.4 3.5 %copy-start.12 = (f32[240]{0:T(256)S(1)}, f32[240]{0:T(256)}, u32[]{:S(2)}) copy-start(f32[240]{0:T(256)} %param.33) | copy-start | bytes 2884
  18.4 3.5 %copy-start.13 = (f32[240]{0:T(256)S(1)}, f32[240]{0:T(256)}, u32[]{:S(2)}) copy-start(f32[240]{0:T(256)} %param.35) | copy-start | bytes 2884
  18.4 30.9 %copy-start.10 = (f32[2,256]{1,0:T(2,128)S(1)}, f32[2,256]{1,0:T(2,128)}, u32[]{:S(2)}) copy-start(f32[2,256]{1,0:T(2,128)} %constant.71.clone.factors) | copy-start | bytes 6148
  18.4 30.9 %copy-start.11 = (f32[2,256]{1,0:T(2,128)S(1)}, f32[2,256]{1,0:T(2,128)}, u32[]{:S(2)}) copy-start(f32[2,256]{1,0:T(2,128)} %constant.72.clone.factor_row) | copy-start | bytes 6148
  20.2 29.1 %copy-start = (bf16[512,512]{1,0:T(8,128)(2,1)S(1)}, bf16[512,512]{1,0:T(8,128)(2,1)}, u32[]{:S(2)}) copy-start(bf16[512,512]{1,0:T(8,128)(2,1)} %constant.74.clone.ahead_high) | copy-start | bytes 1572868
  20.2 29.1 %copy-start.1 = (bf16[512,512]{1,0:T(8,128)(2,1)S(1)}, bf16[512,512]{1,0:T(8,128)(2,1)}, u32[]{:S(2)}) copy-start(bf16[512,512]{1,0:T(8,128)(2,1)} %constant.75.clone.ahead_low) | copy-start | bytes 1572868
  20.2 29.1 %copy-start.2 = (bf16[512,512]{1,0:T(8,128)(2,1)S(1)}, bf16[512,512]{1,0:T(8,128)(2,1)}, u32[]{:S(2)}) copy-start(bf16[512,512]{1,0:T(8,128)(2,1)} %constant.76.clone.back_high) | copy-start | bytes 1572868
  21.9 0.8 copy-start.4
  22.8 0.9 copy-start.5
  23.7 0.9 copy-start.6
  24.7 0.8 copy-start.7
  25.4 0.7 copy-start.14
  35.5 0.6 copy-start.9
  36.2 52.3 %copy-start.15 = (s32[1,1,1,128]{3,2,1,0:T(1,128)S(1)}, s32[1,1,1,128]{3,2,1,0:T(1,128)}, u32[]{:S(2)}) copy-start(s32[1,1,1,128]{3,2,1,0:T(1,128)} %param.24) | copy-start | bytes 1540
  36.2 13.1 %all-to-all-start.1 = ((f32[32,4,128]{2,1,0:T(4,128)}), f32[32,4,128]{2,1,0:T(4,128)S(1)}, u32[]{:S(2)}, u32[]{:S(2)}) async-start(f32[32,4,128]{2,1,0:T(4,128)} %copy-done.9), calls=%async_computation.1 | async-start | bytes 131072 | tf_op jit(solution)/shard_map/all_to_all | solution.py:520
  49.3 1.0 %copy-start.3 = (bf16[512,512]{1,0:T(8,128)(2,1)S(1)}, bf16[512,512]{1,0:T(8,128)(2,1)}, u32[]{:S(2)}) copy-start(bf16[512,512]{1,0:T(8,128)(2,1)} %constant.77.clone.back_low) | copy-start | bytes 1572868
  50.4 0.9 copy-start.8
  85.9 10.4 %all-to-all-start.2 = ((f32[32,1,1152]{2,1,0:T(1,128)}), f32[32,1,1152]{2,1,0:T(1,128)S(1)}, u32[]{:S(2)}, u32[]{:S(2)}) async-start(f32[32,1,1152]{2,1,0:T(1,128)} %bitcast.25), calls=%async_computation.2 | async-start | bytes 294912 | tf_op jit(solution)/shard_map/all_to_all | solution.py:568

commit v2 on v1

v2 whole, which is shorter than its diff:
```python
import math

import jax
import jax.numpy as jnp
import numpy as np
from jax import lax
from jax.experimental import pallas as pl
from jax.experimental.pallas import tpu as pltpu
from jax.sharding import PartitionSpec as P

GRID_X = 256
GRID_Y = 256
GRID_Z = 256
AXIS_COLUMNS = 16

radius_scale = 24.0
wannier_reach = 0.5
ewald_beta = 0.9
coulomb = 0.25

ROW_PAD = 32
SLOT_CHUNK = 16
HALO_X = 16
HALO_Z = 8

NN = (((1,), (0,)), ((), ()))
NT = (((1,), (1,)), ((), ()))


def split(value):
    high = value.astype(jnp.bfloat16)
    low = (value - high.astype(jnp.float32)).astype(jnp.bfloat16)
    return high, low


def multiply(left, right, dims=NN):
    def one(a, b):
        return lax.dot_general(a, b, dims, preferred_element_type=jnp.float32)

    return one(left[0], right[0]) + (one(left[1], right[0]) + one(left[0], right[1]))


def spline_pair(offset):
    centred = offset - 2.0
    away = jnp.abs(centred)
    outer = jnp.maximum(2.0 - away, 0.0)
    inner = jnp.maximum(1.0 - away, 0.0)
    outer_square = outer * outer
    inner_square = inner * inner
    value = (outer_square * outer - 4.0 * (inner_square * inner)) * (1.0 / 6.0)
    slope = jnp.where(centred < 0.0, 0.5, -0.5) * (outer_square - 4.0 * inner_square)
    return value, slope


def lookup(row_table, spot):
    found = None
    for part in range(row_table.shape[1] // 128):
        inside = spot // 128 == part
        here = jnp.take_along_axis(
            jnp.broadcast_to(row_table[:, part * 128 : (part + 1) * 128], spot.shape),
            lax.rem(spot, 128),
            axis=1,
            mode="promise_in_bounds",
        )
        found = here if found is None else jnp.where(inside, here, found)
    return found


def pack_kernel(positions, species, out_ref):
    rows = [positions[component] for component in range(3)]
    rows.append(species[...].astype(jnp.float32))
    rows = jnp.concatenate(rows, axis=0)
    for target in range(out_ref.shape[0]):
        out_ref[target] = rows


def prepare_kernel(
    neighbours,
    embed_one_w,
    embed_one_b,
    embed_two_w,
    embed_two_b,
    embed_three_w,
    embed_three_b,
    fit_one_w,
    fit_one_b,
    fit_two_w,
    fit_two_b,
    fit_three_w,
    fit_three_b,
    circle,
    codes_ref,
    columns_ref,
    second_ref,
    third_ref,
    one_high_ref,
    one_low_ref,
    two_high_ref,
    two_low_ref,
    three_high_ref,
    three_low_ref,
    phase_ref,
    rows,
    square,
):
    pieces = lax.axis_size("wide") * lax.axis_size("narrow")
    piece = lax.axis_index("wide") * lax.axis_size("narrow") + lax.axis_index("narrow")
    width_one = embed_one_w.shape[1]
    hidden = fit_two_w.shape[0]
    codes_ref[...] = jnp.transpose(neighbours[...].astype(jnp.float32)).astype(jnp.int32)
    rows[...] = jnp.zeros_like(rows)
    for kind in range(2):
        rows[kind : kind + 1, 0:width_one] = embed_one_w[kind : kind + 1, :]
        rows[2 + kind : 3 + kind, 0:width_one] = embed_one_b[kind : kind + 1, :]
    for row, source, groups in ((4, embed_two_b, 2), (5, embed_three_b, 4)):
        for k in range(groups):
            rows[row : row + 1, k * ROW_PAD : k * ROW_PAD + width_one] = source[
                :, k * width_one : (k + 1) * width_one
            ]
    for row, source in ((6, fit_one_b), (7, fit_two_b), (8, fit_three_b)):
        rows[row : row + 1, 0:hidden] = source[...]
    columns_ref[...] = jnp.transpose(rows[...])

    square[...] = jnp.zeros_like(square)
    for k in range(2):
        square[0:width_one, k * ROW_PAD : k * ROW_PAD + width_one] = embed_two_w[
            :, k * width_one : (k + 1) * width_one
        ]
    high, low = split(jnp.transpose(square[0:128, 0:128])[0 : 2 * ROW_PAD, 0:ROW_PAD])
    second_ref[...] = jnp.concatenate([high, high, low], axis=1)
    square[0:128, 0:128] = jnp.zeros((128, 128), jnp.float32)
    for g in range(2):
        for k in range(4):
            square[
                g * ROW_PAD : g * ROW_PAD + width_one, k * ROW_PAD : k * ROW_PAD + width_one
            ] = embed_three_w[
                g * width_one : (g + 1) * width_one, k * width_one : (k + 1) * width_one
            ]
    high, low = split(jnp.transpose(square[0:128, 0:128])[:, 0 : 2 * ROW_PAD])
    third_ref[...] = jnp.concatenate([high, high, low], axis=1)
    one_high_ref[...], one_low_ref[...] = split(fit_one_w[...])
    for source, high_ref, low_ref in (
        (fit_two_w, two_high_ref, two_low_ref),
        (fit_three_w, three_high_ref, three_low_ref),
    ):
        square[0:hidden, 0:hidden] = source[...]
        high_ref[...], low_ref[...] = split(jnp.transpose(square[...])[0:hidden, 0:hidden])

    fine = GRID_Y // 2 // pieces
    shape = (phase_ref.shape[0], 128)
    row = lax.broadcasted_iota(jnp.int32, shape, 0)
    mode = piece * fine + row // 2
    for part in range(GRID_Y // 128):
        cell = lax.broadcasted_iota(jnp.int32, shape, 1) + part * 128
        spot = lax.rem(mode * cell, GRID_Y)
        cosine = lookup(circle[0:1, :], spot)
        sine = lookup(circle[1:2, :], spot)
        alternate = (1 - 2 * lax.rem(cell, 2)).astype(jnp.float32)
        odd = jnp.where(mode == 0, alternate, -sine)
        value = jnp.where(lax.rem(row, 2) == 0, cosine, odd)
        phase_ref[:, part * 128 : (part + 1) * 128] = jnp.where(row < 2 * fine, value, 0.0)


def centroid_kernel(
    table,
    codes,
    columns,
    second,
    third,
    one_high,
    one_low,
    two_high,
    two_low,
    three_high,
    three_low,
    fit_out_w,
    dipole_ref,
    shift_ref,
    matrix,
    descriptor,
):
    wide_count, narrow_count, _, atoms = table.shape
    listed = codes.shape[0]
    width_three = fit_out_w.shape[0]
    width_one = width_three // 4
    hidden_width = two_high.shape[0]
    cells = (GRID_X // wide_count, GRID_Y, GRID_Z // narrow_count)
    at_wide = lax.axis_index("wide")
    at_narrow = lax.axis_index("narrow")
    own = table[at_wide, at_narrow]
    nearby = []
    for step in range(9):
        wide_at = lax.rem(at_wide + (step // 3 - 1) + wide_count, wide_count)
        narrow_at = lax.rem(at_narrow + (step % 3 - 1) + narrow_count, narrow_count)
        nearby.append(table[wide_at, narrow_at])

    second_all = second[...]
    third_all = third[...]
    weight_oxygen = jnp.broadcast_to(columns[0:ROW_PAD, 0:1], (ROW_PAD, atoms))
    weight_hydrogen = jnp.broadcast_to(columns[0:ROW_PAD, 1:2], (ROW_PAD, atoms))
    bias_oxygen = jnp.broadcast_to(columns[0:ROW_PAD, 2:3], (ROW_PAD, atoms))
    bias_hydrogen = jnp.broadcast_to(columns[0:ROW_PAD, 3:4], (ROW_PAD, atoms))
    second_bias = columns[0 : 2 * ROW_PAD, 4:5]
    third_bias = columns[0 : 4 * ROW_PAD, 5:6]
    matrix[...] = jnp.zeros_like(matrix)

    def chunk(index, carry):
        first = pl.multiple_of(index * SLOT_CHUNK, SLOT_CHUNK)
        code = codes[pl.ds(first, SLOT_CHUNK), :]
        offset = code // atoms
        slot = code - offset * atoms
        step_x = jnp.where(offset >= 9, 1, 0) + jnp.where(offset >= 18, 1, 0)
        rest = offset - 9 * step_x
        step_z = jnp.where(rest >= 3, 1, 0) + jnp.where(rest >= 6, 1, 0)
        step_y = rest - 3 * step_z
        brick = step_x * 3 + step_z
        found = []
        for component in range(4):
            picked = jnp.zeros((SLOT_CHUNK, atoms), jnp.float32)
            for step in range(9):
                row = jnp.broadcast_to(
                    nearby[step][component : component + 1], (SLOT_CHUNK, atoms)
                )
                here = jnp.take_along_axis(row, slot, axis=1, mode="promise_in_bounds")
                picked = jnp.where(brick == step, here, picked)
            found.append(picked)
        scaled = []
        for component, step in enumerate((step_x, step_y, step_z)):
            extent = float(cells[component])
            relative = (step - 1).astype(jnp.float32) * extent + (
                found[component] - own[component : component + 1]
            ) * extent
            scaled.append(relative * (1.0 / radius_scale))
        smooth = 1.0 / (
            1.0 + (scaled[0] * scaled[0] + scaled[1] * scaled[1] + scaled[2] * scaled[2])
        )
        radial = [smooth] + [smooth * part for part in scaled]
        hydrogen = found[3] > 0.5
        first_layers = []
        for k in range(SLOT_CHUNK):
            row = smooth[k : k + 1]
            kind = hydrogen[k : k + 1]
            weight = jnp.where(kind, weight_hydrogen, weight_oxygen)
            bias = jnp.where(kind, bias_hydrogen, bias_oxygen)
            first_layers.append(jnp.tanh(weight * row + bias))
        layer_one = jnp.concatenate(first_layers, axis=1)
        high, low = split(layer_one)
        layer_two = lax.dot_general(
            second_all,
            jnp.concatenate([high, low, high], axis=0),
            NN,
            preferred_element_type=jnp.float32,
        )
        layer_two = jnp.tanh(layer_two + second_bias) + jnp.concatenate(
            [layer_one, layer_one], axis=0
        )
        high, low = split(layer_two)
        layer_three = lax.dot_general(
            third_all,
            jnp.concatenate([high, low, high], axis=0),
            NN,
            preferred_element_type=jnp.float32,
        )
        layer_three = jnp.tanh(layer_three + third_bias) + jnp.concatenate(
            [layer_two, layer_two], axis=0
        )
        for part in range(4):
            total = matrix[part]
            for k in range(SLOT_CHUNK):
                total = total + layer_three[:, k * atoms : (k + 1) * atoms] * radial[part][k : k + 1]
            matrix[part] = total
        return carry

    lax.fori_loop(0, listed // SLOT_CHUNK, chunk, 0)

    parts = []
    for part in range(4):
        padded = matrix[part] * (1.0 / listed)
        parts.append(
            jnp.concatenate(
                [padded[k * ROW_PAD : k * ROW_PAD + width_one] for k in range(4)], axis=0
            )
        )
    leading = [part[0:AXIS_COLUMNS] for part in parts]
    for row in range(width_three):
        total = parts[0][row : row + 1] * leading[0]
        for part in range(1, 4):
            total = total + parts[part][row : row + 1] * leading[part]
        descriptor[row * AXIS_COLUMNS : (row + 1) * AXIS_COLUMNS, :] = total
    def layer(high_ref, low_ref, given, column):
        weights = (high_ref[...], low_ref[...])
        return jnp.tanh(multiply(weights, split(given)) + columns[0:hidden_width, column : column + 1])

    hidden = layer(one_high, one_low, descriptor[...], 6)
    hidden = hidden + layer(two_high, two_low, hidden, 7)
    hidden = hidden + layer(three_high, three_low, hidden, 8)
    coeffs = multiply(split(fit_out_w[...]), split(hidden))
    vector = jnp.concatenate(
        [jnp.sum(coeffs * parts[1 + c], axis=0, keepdims=True) for c in range(3)], axis=0
    )
    oxygen = 1.0 - own[3:4]
    for c in range(3):
        dipole_ref[c] = vector[c : c + 1] * oxygen
    moved = wannier_reach * jnp.tanh(vector)
    moved = jnp.concatenate([moved, jnp.zeros((1, atoms), jnp.float32)], axis=0)
    for target in range(shift_ref.shape[0]):
        shift_ref[target] = moved


def mesh_kernel(
    factors,
    table,
    shifts,
    phase,
    factor_row,
    factor_column,
    fold_high,
    fold_low,
    unfold_high,
    unfold_low,
    out_ref,
    grid,
    planes,
    weights,
    slopes,
    waves,
    wave_slopes,
):
    wide_count, narrow_count, _, atoms = table.shape
    cells_x = GRID_X // wide_count
    cells_z = GRID_Z // narrow_count
    window = cells_z + HALO_Z
    reach = cells_x + HALO_X
    pair = 2 * atoms
    length = wide_count * pair
    copies = grid.shape[0]
    fine = grid.shape[1]
    channels = 2 * fine
    rows = phase.shape[0]
    half_x = GRID_X // 2
    half_z = GRID_Z // 2
    piece = lax.axis_index("wide") * narrow_count + lax.axis_index("narrow")
    lane_zero = lax.broadcasted_iota(jnp.int32, (1, half_x), 1) == 0
    row_zero = lax.broadcasted_iota(jnp.int32, (half_z, 1), 0) == 0

    def fold():
        return (fold_high[...], fold_low[...])

    def unfold():
        return (unfold_high[...], unfold_low[...])

    def sites(at_wide, at_narrow):
        atom = table[at_wide, at_narrow]
        moved = shifts[at_wide, at_narrow]
        found = []
        for component, extent in enumerate((cells_x, GRID_Y, cells_z)):
            start = atom[component : component + 1] * float(extent)
            found.append(jnp.concatenate([start, start + moved[component : component + 1]], axis=1))
        oxygen = 1.0 - atom[3:4]
        found.append(jnp.concatenate([6.0 * oxygen + atom[3:4], -8.0 * oxygen], axis=1))
        return found

    def line(at_narrow):
        groups = [sites(at_wide, at_narrow) for at_wide in range(wide_count)]
        return [jnp.concatenate([g[k] for g in groups], axis=1) for k in range(4)]

    def weights_z(row):
        counter = lax.broadcasted_iota(jnp.int32, (window, 1), 0).astype(jnp.float32)
        return spline_pair(row - (counter - float(HALO_Z)))

    def fill_x(row, targets):
        counter = lax.broadcasted_iota(jnp.int32, (reach, 1), 0).astype(jnp.float32)
        both = spline_pair(row - (counter - float(HALO_X)))
        for values, ref in zip(both, targets):
            high, low = split(values)
            ref[0:reach, :] = high
            ref[128 : 128 + reach, :] = low

    weights[...] = jnp.zeros_like(weights)
    slopes[...] = jnp.zeros_like(slopes)
    grid[...] = jnp.zeros_like(grid)

    def spread(at_narrow, carry):
        row_x, row_y, row_z, charge = line(at_narrow)
        lower = jnp.floor(row_y)
        back = lax.broadcasted_iota(jnp.int32, (8, 1), 0)
        value_y, slope_y = spline_pair((row_y - lower) + back.astype(jnp.float32))
        cell = lax.rem(lower.astype(jnp.int32) - back + GRID_Y, GRID_Y)
        wave_blocks = []
        slope_blocks = []
        for block in range(length // 128):
            lanes = slice(block * 128, (block + 1) * 128)
            wave = jnp.zeros((rows, 128), jnp.float32)
            wave_slope = jnp.zeros((rows, 128), jnp.float32)
            for k in range(4):
                spot = jnp.broadcast_to(cell[k : k + 1, lanes], (rows, 128))
                found = lookup(phase[...], spot)
                wave = wave + value_y[k : k + 1, lanes] * found
                wave_slope = wave_slope + slope_y[k : k + 1, lanes] * found
            wave_blocks.append(wave)
            slope_blocks.append(wave_slope)
        wave = jnp.concatenate(wave_blocks, axis=1)
        waves[at_narrow] = wave
        wave_slopes[at_narrow] = jnp.concatenate(slope_blocks, axis=1)
        fill_x(row_x, (weights,))
        value_z, _ = weights_z(row_z)
        charged = wave * charge
        first = pl.multiple_of(at_narrow * cells_z, HALO_Z)
        for at_wide in range(wide_count):
            lanes = slice(at_wide * pair, (at_wide + 1) * pair)
            near = value_z[:, lanes]
            left = jnp.concatenate(
                [near * charged[c : c + 1, lanes] for c in range(channels)], axis=0
            )
            high, low = split(left)
            total = lax.dot_general(high, weights[:, lanes], NT, preferred_element_type=jnp.float32)
            total = total[:, 0:128] + (
                total[:, 128:256]
                + lax.dot_general(low, weights[0:128, lanes], NT, preferred_element_type=jnp.float32)
            )
            start = at_wide // copies * 128
            for c in range(channels):
                spot = c % 2 * GRID_X + start
                grid[
                    at_wide % copies, c // 2, pl.ds(first, window), spot : spot + 128
                ] += total[c * window : (c + 1) * window]
        return carry

    lax.fori_loop(0, narrow_count, spread, 0)

    def gather(j, carry):
        for lanes in (slice(0, GRID_X), slice(GRID_X, 2 * GRID_X)):
            total = None
            for k in range(copies):
                moved = pltpu.roll(grid[k, j, :, lanes], (k * cells_x - HALO_X) % GRID_X, 1)
                total = moved if total is None else total + moved
            planes[j, :, lanes] = total[HALO_Z:]
            planes[j, GRID_Z - HALO_Z :, lanes] += total[:HALO_Z]
        return carry

    lax.fori_loop(0, fine, gather, 0)
    is_first = piece == 0
    second_plane = planes[0, :, GRID_X:]
    empty = jnp.zeros_like(second_plane)
    planes[fine, :, 0:GRID_X] = jnp.where(is_first, second_plane, empty)
    planes[fine, :, GRID_X:] = empty
    planes[0, :, GRID_X:] = jnp.where(is_first, empty, second_plane)

    def to_modes(j, energy):
        real = multiply(split(planes[j, :, 0:GRID_X]), fold())
        imag = multiply(split(planes[j, :, GRID_X:]), fold())
        real_c, real_s = real[:, :half_x], real[:, half_x:]
        imag_c, imag_s = imag[:, :half_x], imag[:, half_x:]
        plane = jnp.concatenate(
            [
                real_c + jnp.where(lane_zero, 0.0, imag_s),
                jnp.where(lane_zero, real_s, real_c - imag_s),
                imag_c - jnp.where(lane_zero, 0.0, real_s),
                jnp.where(lane_zero, imag_s, imag_c + real_s),
            ],
            axis=1,
        )
        plane = multiply(unfold(), split(plane))
        real_c, real_s = plane[:half_z, :GRID_X], plane[half_z:, :GRID_X]
        imag_c, imag_s = plane[:half_z, GRID_X:], plane[half_z:, GRID_X:]
        real = jnp.concatenate(
            [
                real_c + jnp.where(row_zero, 0.0, imag_s),
                jnp.where(row_zero, real_s, real_c - imag_s),
            ],
            axis=0,
        )
        imag = jnp.concatenate(
            [
                imag_c - jnp.where(row_zero, 0.0, real_s),
                jnp.where(row_zero, imag_s, imag_c + real_s),
            ],
            axis=0,
        )
        mode = jnp.where(j == fine, GRID_Y // 2, piece * fine + j)
        square = (factors[1, mode] + factor_row[1:2, :]) + factor_column[:, 1:2]
        top = (factors[0, mode] * factor_row[0:1, :]) * factor_column[:, 0:1]
        green = jnp.where(square == 0.0, 0.0, top / jnp.where(square == 0.0, 1.0, square))
        share = jnp.where((mode == 0) | (mode == GRID_Y // 2), 0.5, 1.0)
        energy = energy + share * jnp.sum(green * (real * real + imag * imag))
        planes[j, :, 0:GRID_X] = green * real
        planes[j, :, GRID_X:] = green * imag
        return energy

    energy = lax.fori_loop(0, fine + 1, to_modes, jnp.float32(0.0))
    planes[0, :, 0:GRID_X] -= planes[fine, :, GRID_X:]
    planes[0, :, GRID_X:] += planes[fine, :, 0:GRID_X]

    def to_grid(j, carry):
        real_a, real_b = planes[j, :half_z, :GRID_X], planes[j, half_z:, :GRID_X]
        imag_a, imag_b = planes[j, :half_z, GRID_X:], planes[j, half_z:, GRID_X:]
        real = jnp.concatenate(
            [
                real_a + jnp.where(row_zero, 0.0, real_b),
                jnp.where(row_zero, real_b, imag_b - imag_a),
            ],
            axis=0,
        )
        imag = jnp.concatenate(
            [
                imag_a + jnp.where(row_zero, 0.0, imag_b),
                jnp.where(row_zero, imag_b, real_a - real_b),
            ],
            axis=0,
        )
        real = multiply(fold(), split(real))
        imag = multiply(fold(), split(imag))
        real_a, real_b = real[:, :half_x], real[:, half_x:]
        imag_a, imag_b = imag[:, :half_x], imag[:, half_x:]
        scale = jnp.where(piece * fine + j == 0, 1.0, 2.0)
        real = jnp.concatenate(
            [
                real_a + jnp.where(lane_zero, 0.0, real_b),
                jnp.where(lane_zero, real_b, imag_b - imag_a),
            ],
            axis=1,
        )
        imag = jnp.concatenate(
            [
                imag_a + jnp.where(lane_zero, 0.0, imag_b),
                jnp.where(lane_zero, imag_b, real_a - real_b),
            ],
            axis=1,
        )
        for part, lanes in ((real, slice(0, GRID_X)), (imag, slice(GRID_X, 2 * GRID_X))):
            part = multiply(split(part * scale), unfold())
            for k in range(copies):
                moved = pltpu.roll(part, (HALO_X - k * cells_x) % GRID_X, 1)
                grid[k, j, HALO_Z:, lanes] = moved
                grid[k, j, 0:HALO_Z, lanes] = moved[GRID_Z - HALO_Z :]
        return carry

    lax.fori_loop(0, fine, to_grid, 0)

    def collect(at_narrow, carry):
        row_x, _, row_z, _ = line(at_narrow)
        fill_x(row_x, (weights, slopes))
        value_z, slope_z = weights_z(row_z)
        first = pl.multiple_of(at_narrow * cells_z, HALO_Z)
        lefts = []
        for k in range(copies):
            left = jnp.concatenate(
                [
                    grid[k, c // 2, pl.ds(first, window), c % 2 * GRID_X : (c % 2 + 1) * GRID_X]
                    for c in range(channels)
                ],
                axis=0,
            )
            lefts.append(split(left))
        wave = waves[at_narrow]
        wave_slope = wave_slopes[at_narrow]
        for at_wide in range(wide_count):
            lanes = slice(at_wide * pair, (at_wide + 1) * pair)
            start = at_wide // copies * 128
            high = lefts[at_wide % copies][0][:, start : start + 128]
            low = lefts[at_wide % copies][1][:, start : start + 128]
            twice = jnp.concatenate([high, high], axis=1)

            def across(ref):
                return lax.dot_general(
                    twice, ref[:, lanes], NN, preferred_element_type=jnp.float32
                ) + lax.dot_general(
                    low, ref[0:128, lanes], NN, preferred_element_type=jnp.float32
                )

            value = across(weights)
            slope = across(slopes)
            plain = jnp.zeros((window, pair), jnp.float32)
            along_x = plain
            along_y = plain
            for c in range(channels):
                block = slice(c * window, (c + 1) * window)
                plain = plain + value[block] * wave[c : c + 1, lanes]
                along_x = along_x + slope[block] * wave[c : c + 1, lanes]
                along_y = along_y + value[block] * wave_slope[c : c + 1, lanes]
            near = value_z[:, lanes]
            near_slope = slope_z[:, lanes]
            results = [
                jnp.sum(near * plain, axis=0, keepdims=True),
                -jnp.sum(near * along_x, axis=0, keepdims=True),
                -jnp.sum(near * along_y, axis=0, keepdims=True),
                -jnp.sum(near_slope * plain, axis=0, keepdims=True),
            ]
            for k, row in enumerate(results):
                out_ref[at_wide, at_narrow, :, k * pair : (k + 1) * pair] = row
            out_ref[at_wide, at_narrow, :, 4 * pair :] = jnp.full((1, 128), energy, jnp.float32)
        return carry

    lax.fori_loop(0, narrow_count, collect, 0)


def finish_kernel(arrived, species, atom_ref, centroid_ref, energy_ref):
    atoms = species.shape[1]
    total = arrived[0]
    for k in range(1, arrived.shape[0]):
        total = total + arrived[k]
    oxygen = 1.0 - species[...].astype(jnp.float32)
    for k in range(4):
        atom_ref[k] = total[:, 2 * k * atoms : (2 * k + 1) * atoms]
        centroid_ref[k] = total[:, (2 * k + 1) * atoms : (2 * k + 2) * atoms] * oxygen
    energy_ref[...] = total[:, 8 * atoms :] * (1.0 / (atoms * arrived.shape[0]))


def mode_factors(length, order):
    wrapped = np.where(2 * order >= length, order - length, order)
    square = (wrapped / length) ** 2
    ratio = (4.0 + 2.0 * np.cos(2.0 * math.pi * order / length)) / 6.0
    return np.stack([np.exp(-(math.pi**2) * square / ewald_beta**2) / ratio**2, square])


def folded_order(length):
    half = length // 2
    counter = np.arange(half)
    return np.concatenate([counter, np.where(counter == 0, half, length - counter)])


def fold_table(length):
    half = length // 2
    turns = np.outer(np.arange(length), np.arange(half)) % length * (2.0 * math.pi / length)
    sines = np.sin(turns)
    sines[:, 0] = 1.0 - 2.0 * (np.arange(length) % 2)
    return np.concatenate([np.cos(turns), sines], axis=1)


def halves(table):
    high = table.astype(jnp.bfloat16)
    low = (table - high.astype(np.float64)).astype(jnp.bfloat16)
    return high, low


def vmem(count):
    return [pl.BlockSpec(memory_space=pltpu.VMEM)] * count


def smem(count):
    return [pl.BlockSpec(memory_space=pltpu.SMEM)] * count


def shaped(shape, dtype=jnp.float32):
    return jax.ShapeDtypeStruct(shape, dtype)


def limits(mebibytes):
    return pltpu.CompilerParams(vmem_limit_bytes=mebibytes * 1024 * 1024)


def local(
    positions,
    species,
    neighbours,
    embed_one_w,
    embed_one_b,
    embed_two_w,
    embed_two_b,
    embed_three_w,
    embed_three_b,
    fit_one_w,
    fit_one_b,
    fit_two_w,
    fit_two_b,
    fit_three_w,
    fit_three_b,
    fit_out_w,
):
    axes = ("wide", "narrow")
    wide_count = lax.axis_size("wide")
    narrow_count = lax.axis_size("narrow")
    pieces = wide_count * narrow_count
    atoms = positions.shape[4]
    listed = neighbours.shape[4]
    fine = GRID_Y // 2 // pieces
    width_three = embed_three_w.shape[1]
    entries, hidden = fit_one_w.shape
    kinds = species.reshape(1, atoms)

    packed = pl.pallas_call(
        pack_kernel,
        out_shape=shaped((pieces, 4, atoms)),
        in_specs=vmem(2),
        out_specs=vmem(1)[0],
        name="pack",
    )(positions.reshape(3, 1, atoms), kinds)
    table = lax.all_to_all(packed, axes, 0, 0, tiled=True)
    table = table.reshape(wide_count, narrow_count, 4, atoms)

    tall = 4 * ROW_PAD
    bf16 = jnp.bfloat16
    wave_rows = -(-2 * fine // 8) * 8
    angle = np.arange(GRID_Y) * (2.0 * math.pi / GRID_Y)
    circle = jnp.asarray(np.stack([np.cos(angle), np.sin(angle)]), jnp.float32)
    prepared = pl.pallas_call(
        prepare_kernel,
        out_shape=(
            shaped((listed, atoms), jnp.int32),
            shaped((256, 16)),
            shaped((2 * ROW_PAD, 3 * ROW_PAD), bf16),
            shaped((tall, 6 * ROW_PAD), bf16),
            shaped((hidden, entries), bf16),
            shaped((hidden, entries), bf16),
        )
        + (shaped((hidden, hidden), bf16),) * 4
        + (shaped((wave_rows, GRID_Y)),),
        in_specs=vmem(14),
        out_specs=tuple(vmem(11)),
        scratch_shapes=[pltpu.VMEM((16, 256), jnp.float32), pltpu.VMEM((256, 256), jnp.float32)],
        compiler_params=limits(32),
        cost_estimate=pl.CostEstimate(
            flops=1000000, bytes_accessed=8 * entries * hidden, transcendentals=0
        ),
        name="prepare",
    )(
        neighbours.reshape(atoms, listed),
        embed_one_w,
        embed_one_b,
        embed_two_w,
        embed_two_b[None],
        embed_three_w,
        embed_three_b[None],
        fit_one_w.T,
        fit_one_b[None],
        fit_two_w,
        fit_two_b[None],
        fit_three_w,
        fit_three_b[None],
        circle,
    )
    phase = prepared[10]
    dipole, shifts = pl.pallas_call(
        centroid_kernel,
        out_shape=(shaped((3, 1, atoms)), shaped((pieces, 4, atoms))),
        in_specs=vmem(12),
        out_specs=tuple(vmem(2)),
        scratch_shapes=[
            pltpu.VMEM((4, tall, atoms), jnp.float32),
            pltpu.VMEM((width_three * AXIS_COLUMNS, atoms), jnp.float32),
        ],
        compiler_params=limits(32),
        name="centroids",
    )(table, *prepared[:10], fit_out_w.T)
    shifts = lax.all_to_all(shifts, axes, 0, 0, tiled=True)
    shifts = shifts.reshape(wide_count, narrow_count, 4, atoms)

    factors = mode_factors(GRID_Y, np.arange(GRID_Y))
    factors[0] *= coulomb / (math.pi * GRID_X * GRID_Y * GRID_Z)
    cells_x = GRID_X // wide_count
    copies = 128 // cells_x
    length = wide_count * 2 * atoms
    out_width = 8 * atoms + 128
    partial = pl.pallas_call(
        mesh_kernel,
        out_shape=shaped((wide_count, narrow_count, 1, out_width)),
        in_specs=smem(1) + vmem(9),
        out_specs=vmem(1)[0],
        scratch_shapes=[
            pltpu.VMEM((copies, fine, HALO_Z + GRID_Z, 2 * GRID_X), jnp.float32),
            pltpu.VMEM((fine + 1, GRID_Z, 2 * GRID_X), jnp.float32),
        ]
        + [pltpu.VMEM((256, length), bf16)] * 2
        + [pltpu.VMEM((narrow_count, wave_rows, length), jnp.float32)] * 2,
        compiler_params=limits(48),
        name="mesh",
    )(
        jnp.asarray(factors, jnp.float32),
        table,
        shifts,
        phase,
        jnp.asarray(mode_factors(GRID_X, folded_order(GRID_X)), jnp.float32),
        jnp.asarray(mode_factors(GRID_Z, folded_order(GRID_Z)).T, jnp.float32),
        *[jnp.asarray(half) for half in halves(fold_table(GRID_X))],
        *[jnp.asarray(half) for half in halves(fold_table(GRID_X).T)],
    )
    arrived = lax.all_to_all(partial.reshape(pieces, 1, out_width), axes, 0, 0, tiled=True)
    atom_field, centroid_field, energy = pl.pallas_call(
        finish_kernel,
        out_shape=(shaped((4, 1, atoms)), shaped((4, 1, atoms)), shaped((1, 128))),
        in_specs=vmem(2),
        out_specs=tuple(vmem(3)),
        name="finish",
    )(arrived, kinds)
    atom_field = atom_field.reshape(4, 1, 1, 1, atoms)
    centroid_field = centroid_field.reshape(4, 1, 1, 1, atoms)
    return (dipole.reshape(3, 1, 1, 1, atoms), atom_field, centroid_field, energy[0, 0])


def solution(mesh):
    column = P(None, "wide", "narrow", None, None)
    in_specs = (column, P("wide", "narrow", None, None), P("wide", "narrow", None, None, None))
    in_specs = in_specs + (P(),) * 13
    out_specs = (column, column, column, P())
    return jax.shard_map(local, mesh=mesh, in_specs=in_specs, out_specs=out_specs, check_vma=False)
```

time: 101 us -> 83.1 us (0.82)
  blocking collectives: 0 us -> 23.1 us
  waiting for transfers between devices: 13.6 us -> 0.01 us
  local copies, waits for them, and re-layouts: 20 us -> 11 us
  starting transfers between devices: 15.7 us -> 7.3 us
  other arithmetic: 3.95 us -> 0 us
  Pallas kernels: 44 us -> 40.2 us
  between operations: 2.63 us -> 0.79 us
    all_to_all x0 -> x2, blocking collectives: none -> 23.1 us  [the longest x1 12.9 us: local(): shifts = lax.all_to_all(shifts, axes, 0, 0, tiled=True)]
    all_to_all x3 -> x1, waiting for transfers between devices: 13.6 us -> 0.01 us  [local(): table = lax.all_to_all(packed, axes, 0, 0, tiled=True)]
    all_to_all x3 -> x1, starting transfers between devices: 15.7 us -> 7.3 us  [local(): table = lax.all_to_all(packed, axes, 0, 0, tiled=True)]
    pallas_call x2 -> x5, Pallas kernels: 44 us -> 40.2 us  [the longest x1 26.8 us: local(): pl.pallas_call(mesh_kernel, out_shape=shaped((wide_count, narrow_count, 1...]
    slice x5 -> x0, local copies, waits for them, and re-layouts: 2.61 us -> none  [the longest x1 0.76 us: local(): embed_one_b[1]]
    reshape x10 -> x0, local copies, waits for them, and re-layouts: 2.53 us -> none  [the longest x5 2.32 us: grouped(): parts = array.reshape((-1, width) + array.shape[1:])]
    pad x6 -> x0, local copies, waits for them, and re-layouts: 2.01 us -> none  [the longest x5 1.29 us: grouped(): parts = jnp.pad(parts, pads)]
    convert_element_type x2 -> x0, other arithmetic: 1.23 us -> none  [the longest x1 0.66 us: local(): kinds = species.reshape(1, atoms).astype(jnp.float32)]
  transfers between devices with their start and end apart: 3 -> 1, of which waited for: 2 -> 0; matrix products, arithmetic and copies ran while one was open for 13% -> 0% of each run, Pallas kernels for 0% -> 1%
where the time goes in v2:
time: 83.1 us; the launch traced here: 82.5 us
  Pallas kernels  40.2 us (48%)
  blocking collectives  23.1 us (28%)
  local copies, waits for them, and re-layouts  11 us (13%)
  starting transfers between devices  7.3 us (9%)
    pallas_call x1, Pallas kernels, local(): pl.pallas_call(mesh_kernel, out_shape=shaped((wide_count, narrow_count, 1...  26.8 us
    all_to_all x1, blocking collectives, local(): shifts = lax.all_to_all(shifts, axes, 0, 0, tiled=True)  12.9 us
    unnamed x44, local copies, waits for them, and re-layouts  11 us
    all_to_all x1, blocking collectives, local(): lax.all_to_all(partial.reshape(pieces, 1, out_width), axes, 0, 0, tiled=T...  10.2 us
    pallas_call x1, Pallas kernels, local(): pl.pallas_call(centroid_kernel, out_shape=(shaped((3, 1, atoms)), shaped(...  9.68 us
    all_to_all x1, starting transfers between devices, local(): table = lax.all_to_all(packed, axes, 0, 0, tiled=True)  7.3 us
  transfers between devices with their start and end apart: 1, of which 0 were waited for; matrix products, arithmetic and copies ran while one was open for 0% of the time, Pallas kernels for 1%

profile of v2, /device:TPU:0, one launch (start us, length us, event | category | flops | bytes accessed | tf_op | source)
XLA Modules:
  0.0 82.5 jit_solution(14529504859655411988)
XLA Ops:
  0.6 0.0 copy-start.8
  0.6 1.4 %pack.1 = f32[32,4,128]{2,1,0:T(4,128)} custom-call(f32[3,1,128]{2,1,0:T(1,128)} %bitcast.38, s32[1,128]{1,0:T(1,128)} %bitcast.36), custom_call_target="tpu_custom_call" | custom-call | tf_op jit(solution)/shard_map/pack/pallas_call | solution.py:681
  2.0 7.3 %all-to-all-start = ((f32[32,4,128]{2,1,0:T(4,128)}), f32[32,4,128]{2,1,0:T(4,128)S(1)}, u32[]{:S(2)}, u32[]{:S(2)}) async-start(f32[32,4,128]{2,1,0:T(4,128)} %pack.1), calls=%async_computation | async-start | bytes 131072 | tf_op jit(solution)/shard_map/all_to_all | solution.py:688
  9.3 0.0 copy-start
  9.3 1.4 %copy-done = f32[1600,240]{0,1:T(8,128)S(1)} copy-done((f32[1600,240]{0,1:T(8,128)S(1)}, f32[1600,240]{0,1:T(8,128)}, u32[]{:S(2)}) %copy-start) | copy-done | bytes 1536024
  10.7 0.9 %copy-done.1 = f32[240,240]{1,0:T(8,128)S(1)} copy-done((f32[240,240]{1,0:T(8,128)S(1)}, f32[240,240]{1,0:T(8,128)}, u32[]{:S(2)}) %copy-start.1) | copy-done | bytes 230424
  11.7 0.9 %copy-done.2 = f32[240,240]{1,0:T(8,128)S(1)} copy-done((f32[240,240]{1,0:T(8,128)S(1)}, f32[240,240]{1,0:T(8,128)}, u32[]{:S(2)}) %copy-start.2) | copy-done | bytes 230424
  12.6 0.8 %copy-done.9 = s32[1,1,1,128,128]{4,3,2,1,0:T(8,128)S(1)} copy-done((s32[1,1,1,128,128]{4,3,2,1,0:T(8,128)S(1)}, s32[1,1,1,128,128]{4,3,2,1,0:T(8,128)}, u32[]{:S(2)}) %copy-start.9) | copy-done | bytes 65560
  13.5 0.7 copy-done.10
  14.2 0.7 copy-done.11
  14.9 0.7 copy-done.14
  15.6 0.7 copy-done.15
  16.3 0.7 copy-done.16
  17.0 0.7 copy-done.17
  17.6 0.7 copy-done.18
  18.3 0.7 copy-done.19
  19.0 0.7 copy-done.20
  19.7 0.7 copy-done.21
  20.3 0.9 %prepare.1 = (s32[128,128]{1,0:T(8,128)S(1)}, f32[256,16]{1,0:T(8,128)S(1)}, bf16[64,96]{1,0:T(8,128)(2,1)S(1)}, bf16[128,192]{1,0:T(8,128)(2,1)S(1)}, bf16[240,...) custom-call(s32[128,128]{1,0:T(8,128)S(1)} %bitcast.30, ...), custom_call_target="tpu_custom_call" | custom-call | flops 1000000 | bytes 3072000 | tf_op jit(solution)/shard_map/prepare/pallas_call | solution.py:696
  21.2 0.0 copy-start.3
  21.2 0.0 copy-start.4
  21.2 0.0 copy-start.5
  21.2 0.0 copy-start.6
  21.3 0.0 copy-start.7
  21.3 0.0 copy-start.12
  21.3 0.0 copy-start.13
  21.3 0.0 all-to-all-done
  21.3 9.7 %centroids.1 = (f32[3,1,128]{2,1,0:T(1,128)}, f32[32,4,128]{2,1,0:T(4,128)S(1)}) custom-call(f32[4,8,4,128]{3,2,1,0:T(4,128)S(1)} %bitcast.26, s32[128,128]{1,0:T(8,128)S(1)} %get-tuple-element.20.codes, f32[256,16]{1,0:T(8,128)S(1)} %get-tuple-element.21.columns, bf16[64,96]{1,0:T(8,128)(2,1)S(1)} %get-tuple-element.22.second, ...), custom_call_target="tpu_custom_call" | custom-call | tf_op jit(solution)/shard_map/centroids/pallas_call | solution.py:733
  31.0 12.9 %all_to_all.15 = f32[32,4,128]{2,1,0:T(4,128)S(1)} all-to-all(f32[32,4,128]{2,1,0:T(4,128)S(1)} %get-tuple-element.31), channel_id=1, replica_groups=mesh['wide'=4,'narrow'=8] {'wide','narrow'}, dimensions={0} | all-to-all | bytes 131072 | tf_op jit(solution)/shard_map/all_to_all | solution.py:745
  44.0 26.8 %mesh.1 = f32[4,8,1,1152]{3,2,1,0:T(1,128)S(1)} custom-call(f32[2,256]{1,0:T(2,128)S(1)} %copy-done.13, f32[4,8,4,128]{3,2,1,0:T(4,128)S(1)} %bitcast.27, f32[4,8,4,128]{3,2,1,0:T(4,128)S(1)} %bitcast.28, f32[8,256]{1,0:T(8,128)S(1)} %get-tuple-element.32.phase, f32[2,256]{1,0:T(2,128)S(1)} %copy-done.12, f32[256,2]{1,0:T(8,128)S(1)} %copy-done.7, ...), custom_call_target="tpu_custom_call" | custom-call | tf_op jit(solution)/shard_map/mesh/pallas_call | solution.py:754
  70.7 10.2 %all_to_all.16.arrived = f32[32,1,1152]{2,1,0:T(1,128)} all-to-all(f32[32,1,1152]{2,1,0:T(1,128)S(1)} %bitcast.25), channel_id=1, replica_groups=mesh['wide'=4,'narrow'=8] {'wide','narrow'}, dimensions={0} | all-to-all | bytes 294912 | tf_op jit(solution)/shard_map/all_to_all | solution.py:777
  80.9 1.5 %finish.1 = (f32[4,1,128]{2,1,0:T(1,128)}, f32[4,1,128]{2,1,0:T(1,128)}, f32[1,128]{1,0:T(1,128)}) custom-call(f32[32,1,1152]{2,1,0:T(1,128)} %all_to_all.16.arrived, s32[1,128]{1,0:T(1,128)} %bitcast.37), custom_call_target="tpu_custom_call" | custom-call | tf_op jit(solution)/shard_map/finish/pallas_call | solution.py:778
  (21 shorter events, 0.0 us)
Async XLA Ops:
  0.6 20.7 %copy-start.8 = (f32[240,100]{0,1:T(8,128)S(1)}, f32[240,100]{0,1:T(8,128)}, u32[]{:S(2)}) copy-start(f32[240,100]{0,1:T(8,128)} %param.39) | copy-start | bytes 288004
  2.0 19.3 %all-to-all-start = ((f32[32,4,128]{2,1,0:T(4,128)}), f32[32,4,128]{2,1,0:T(4,128)S(1)}, u32[]{:S(2)}, u32[]{:S(2)}) async-start(f32[32,4,128]{2,1,0:T(4,128)} %pack.1), calls=%async_computation | async-start | bytes 131072 | tf_op jit(solution)/shard_map/all_to_all | solution.py:688
  9.3 1.4 %copy-start = (f32[1600,240]{0,1:T(8,128)S(1)}, f32[1600,240]{0,1:T(8,128)}, u32[]{:S(2)}) copy-start(f32[1600,240]{0,1:T(8,128)} %param.33) | copy-start | bytes 4608004
  10.7 0.9 %copy-start.1 = (f32[240,240]{1,0:T(8,128)S(1)}, f32[240,240]{1,0:T(8,128)}, u32[]{:S(2)}) copy-start(f32[240,240]{1,0:T(8,128)} %fit_two_w.1) | copy-start | bytes 691204
  11.7 0.9 %copy-start.2 = (f32[240,240]{1,0:T(8,128)S(1)}, f32[240,240]{1,0:T(8,128)}, u32[]{:S(2)}) copy-start(f32[240,240]{1,0:T(8,128)} %fit_three_w.1) | copy-start | bytes 691204
  12.6 0.8 %copy-start.9 = (s32[1,1,1,128,128]{4,3,2,1,0:T(8,128)S(1)}, s32[1,1,1,128,128]{4,3,2,1,0:T(8,128)}, u32[]{:S(2)}) copy-start(s32[1,1,1,128,128]{4,3,2,1,0:T(8,128)} %param.26) | copy-start | bytes 196612
  13.5 0.7 copy-start.10
  14.2 0.7 copy-start.11
  14.9 0.7 copy-start.14
  15.6 0.7 copy-start.15
  16.3 0.7 copy-start.16
  17.0 0.7 copy-start.17
  17.6 0.7 copy-start.18
  18.3 0.7 copy-start.19
  19.0 0.7 copy-start.20
  19.7 0.7 copy-start.21
  21.2 22.7 %copy-start.3 = (bf16[256,256]{1,0:T(8,128)(2,1)S(1)}, bf16[256,256]{1,0:T(8,128)(2,1)}, u32[]{:S(2)}) copy-start(bf16[256,256]{1,0:T(8,128)(2,1)} %constant.23.clone.unfold_low) | copy-start | bytes 393220
  21.2 22.7 %copy-start.4 = (bf16[256,256]{1,0:T(8,128)(2,1)S(1)}, bf16[256,256]{1,0:T(8,128)(2,1)}, u32[]{:S(2)}) copy-start(bf16[256,256]{1,0:T(8,128)(2,1)} %constant.22.clone.unfold_high) | copy-start | bytes 393220
  21.2 22.7 %copy-start.5 = (bf16[256,256]{1,0:T(8,128)(2,1)S(1)}, bf16[256,256]{1,0:T(8,128)(2,1)}, u32[]{:S(2)}) copy-start(bf16[256,256]{1,0:T(8,128)(2,1)} %constant.21.clone.fold_low) | copy-start | bytes 393220
  21.2 22.7 %copy-start.6 = (bf16[256,256]{1,0:T(8,128)(2,1)S(1)}, bf16[256,256]{1,0:T(8,128)(2,1)}, u32[]{:S(2)}) copy-start(bf16[256,256]{1,0:T(8,128)(2,1)} %constant.20.clone.fold_high) | copy-start | bytes 393220
  21.3 22.7 %copy-start.7 = (f32[256,2]{1,0:T(8,128)S(1)}, f32[256,2]{1,0:T(8,128)}, u32[]{:S(2)}) copy-start(f32[256,2]{1,0:T(8,128)} %constant.19.clone.factor_column) | copy-start | bytes 6148
  21.3 22.7 %copy-start.12 = (f32[2,256]{1,0:T(2,128)S(1)}, f32[2,256]{1,0:T(2,128)}, u32[]{:S(2)}) copy-start(f32[2,256]{1,0:T(2,128)} %constant.18.clone.factor_row) | copy-start | bytes 6148
  21.3 22.7 %copy-start.13 = (f32[2,256]{1,0:T(2,128)S(1)}, f32[2,256]{1,0:T(2,128)}, u32[]{:S(2)}) copy-start(f32[2,256]{1,0:T(2,128)} %constant.17.clone.factors) | copy-start | bytes 6148

commit v3 on v2

--- a/solution.py
+++ b/solution.py
@@ -88,7 +88,7 @@
     fit_two_b,
     fit_three_w,
     fit_three_b,
-    circle,
+    constants,
     codes_ref,
     columns_ref,
     second_ref,
@@ -100,9 +100,52 @@
     three_high_ref,
     three_low_ref,
     phase_ref,
+    green_ref,
     rows,
     square,
+    arrivals,
+    *held,
 ):
+    sources = (
+        neighbours,
+        embed_one_w,
+        embed_one_b,
+        embed_two_w,
+        embed_two_b,
+        embed_three_w,
+        embed_three_b,
+        fit_one_b,
+        fit_two_b,
+        fit_three_b,
+        constants,
+        fit_two_w,
+        fit_three_w,
+        fit_one_w,
+    )
+    copies = [
+        pltpu.make_async_copy(source, target, arrivals.at[k])
+        for k, (source, target) in enumerate(zip(sources, held))
+    ]
+    for copy in copies:
+        copy.start()
+    (
+        neighbours,
+        embed_one_w,
+        embed_one_b,
+        embed_two_w,
+        embed_two_b,
+        embed_three_w,
+        embed_three_b,
+        fit_one_b,
+        fit_two_b,
+        fit_three_b,
+        constants,
+        fit_two_w,
+        fit_three_w,
+        fit_one_w,
+    ) = held
+    for copy in copies[:11]:
+        copy.wait()
     pieces = lax.axis_size("wide") * lax.axis_size("narrow")
     piece = lax.axis_index("wide") * lax.axis_size("narrow") + lax.axis_index("narrow")
     width_one = embed_one_w.shape[1]
@@ -138,7 +181,8 @@
             ]
     high, low = split(jnp.transpose(square[0:128, 0:128])[:, 0 : 2 * ROW_PAD])
     third_ref[...] = jnp.concatenate([high, high, low], axis=1)
-    one_high_ref[...], one_low_ref[...] = split(fit_one_w[...])
+    for copy in copies[11:13]:
+        copy.wait()
     for source, high_ref, low_ref in (
         (fit_two_w, two_high_ref, two_low_ref),
         (fit_three_w, three_high_ref, three_low_ref),
@@ -153,12 +197,25 @@
     for part in range(GRID_Y // 128):
         cell = lax.broadcasted_iota(jnp.int32, shape, 1) + part * 128
         spot = lax.rem(mode * cell, GRID_Y)
-        cosine = lookup(circle[0:1, :], spot)
-        sine = lookup(circle[1:2, :], spot)
+        cosine = lookup(constants[0:1, :], spot)
+        sine = lookup(constants[1:2, :], spot)
         alternate = (1 - 2 * lax.rem(cell, 2)).astype(jnp.float32)
         odd = jnp.where(mode == 0, alternate, -sine)
         value = jnp.where(lax.rem(row, 2) == 0, cosine, odd)
         phase_ref[:, part * 128 : (part + 1) * 128] = jnp.where(row < 2 * fine, value, 0.0)
+
+    column = jnp.transpose(constants[...])
+    lane = lax.broadcasted_iota(jnp.int32, (1, GRID_Y), 1)
+    for j in range(fine + 1):
+        here = lane == (GRID_Y // 2 if j == fine else piece * fine + j)
+        factor = jnp.sum(jnp.where(here, constants[2:3, :], 0.0), axis=1, keepdims=True)
+        part = jnp.sum(jnp.where(here, constants[3:4, :], 0.0), axis=1, keepdims=True)
+        wave = (part + constants[5:6, :]) + column[:, 7:8]
+        top = (factor * constants[4:5, :]) * column[:, 6:7]
+        green_ref[j] = jnp.where(wave == 0.0, 0.0, top / jnp.where(wave == 0.0, 1.0, wave))
+
+    copies[13].wait()
+    one_high_ref[...], one_low_ref[...] = split(fit_one_w[...])
 
 
 def centroid_kernel(
@@ -308,12 +365,10 @@
 
 
 def mesh_kernel(
-    factors,
     table,
     shifts,
     phase,
-    factor_row,
-    factor_column,
+    green_ref,
     fold_high,
     fold_low,
     unfold_high,
@@ -323,6 +378,7 @@
     planes,
     weights,
     slopes,
+    weights_z,
     waves,
     wave_slopes,
 ):
@@ -364,23 +420,25 @@
         groups = [sites(at_wide, at_narrow) for at_wide in range(wide_count)]
         return [jnp.concatenate([g[k] for g in groups], axis=1) for k in range(4)]
 
-    def weights_z(row):
+    def splines_z(row):
         counter = lax.broadcasted_iota(jnp.int32, (window, 1), 0).astype(jnp.float32)
         return spline_pair(row - (counter - float(HALO_Z)))
 
     def fill_x(row, targets):
         counter = lax.broadcasted_iota(jnp.int32, (reach, 1), 0).astype(jnp.float32)
         both = spline_pair(row - (counter - float(HALO_X)))
+        rest = jnp.zeros((128 - reach, length), jnp.bfloat16)
         for values, ref in zip(both, targets):
-            high, low = split(values)
-            ref[0:reach, :] = high
-            ref[128 : 128 + reach, :] = low
-
-    weights[...] = jnp.zeros_like(weights)
-    slopes[...] = jnp.zeros_like(slopes)
-    grid[...] = jnp.zeros_like(grid)
-
-    def spread(at_narrow, carry):
+            if ref is not None:
+                high, low = split(values)
+                ref[0:reach, :] = high
+                ref[reach:128, :] = rest
+                ref[128 : 128 + reach, :] = low
+                ref[128 + reach : 256, :] = rest
+
+    grid[:, :, 0:HALO_Z, :] = jnp.zeros((copies, fine, HALO_Z, 2 * GRID_X), jnp.float32)
+
+    def spread(at_narrow):
         row_x, row_y, row_z, charge = line(at_narrow)
         lower = jnp.floor(row_y)
         back = lax.broadcasted_iota(jnp.int32, (8, 1), 0)
@@ -402,8 +460,9 @@
         wave = jnp.concatenate(wave_blocks, axis=1)
         waves[at_narrow] = wave
         wave_slopes[at_narrow] = jnp.concatenate(slope_blocks, axis=1)
-        fill_x(row_x, (weights,))
-        value_z, _ = weights_z(row_z)
+        fill_x(row_x, (weights.at[at_narrow], None))
+        value_z, _ = splines_z(row_z)
+        weights_z[at_narrow] = value_z
         charged = wave * charge
         first = pl.multiple_of(at_narrow * cells_z, HALO_Z)
         for at_wide in range(wide_count):
@@ -413,20 +472,29 @@
                 [near * charged[c : c + 1, lanes] for c in range(channels)], axis=0
             )
             high, low = split(left)
-            total = lax.dot_general(high, weights[:, lanes], NT, preferred_element_type=jnp.float32)
+            across = weights[at_narrow, :, lanes]
+            total = lax.dot_general(high, across, NT, preferred_element_type=jnp.float32)
             total = total[:, 0:128] + (
                 total[:, 128:256]
-                + lax.dot_general(low, weights[0:128, lanes], NT, preferred_element_type=jnp.float32)
+                + lax.dot_general(low, across[0:128], NT, preferred_element_type=jnp.float32)
             )
             start = at_wide // copies * 128
             for c in range(channels):
-                spot = c % 2 * GRID_X + start
-                grid[
-                    at_wide % copies, c // 2, pl.ds(first, window), spot : spot + 128
-                ] += total[c * window : (c + 1) * window]
-        return carry
-
-    lax.fori_loop(0, narrow_count, spread, 0)
+                spot = slice(c % 2 * GRID_X + start, c % 2 * GRID_X + start + 128)
+                k = at_wide % copies
+                part = total[c * window : (c + 1) * window]
+                grid[k, c // 2, pl.ds(first, HALO_Z), spot] += part[:HALO_Z]
+                grid[k, c // 2, pl.ds(first + HALO_Z, cells_z), spot] = part[HALO_Z:]
+
+    def in_pairs(step):
+        def both(index, carry):
+            step(2 * index, 0)
+            step(2 * index + 1, 1)
+            return carry
+
+        lax.fori_loop(0, narrow_count // 2, both, 0)
+
+    in_pairs(lambda at_narrow, _: spread(at_narrow))
 
     def gather(j, carry):
         for lanes in (slice(0, GRID_X), slice(GRID_X, 2 * GRID_X)):
@@ -440,107 +508,86 @@
 
     lax.fori_loop(0, fine, gather, 0)
     is_first = piece == 0
-    second_plane = planes[0, :, GRID_X:]
-    empty = jnp.zeros_like(second_plane)
-    planes[fine, :, 0:GRID_X] = jnp.where(is_first, second_plane, empty)
-    planes[fine, :, GRID_X:] = empty
-    planes[0, :, GRID_X:] = jnp.where(is_first, empty, second_plane)
-
-    def to_modes(j, energy):
-        real = multiply(split(planes[j, :, 0:GRID_X]), fold())
-        imag = multiply(split(planes[j, :, GRID_X:]), fold())
-        real_c, real_s = real[:, :half_x], real[:, half_x:]
-        imag_c, imag_s = imag[:, :half_x], imag[:, half_x:]
-        plane = jnp.concatenate(
-            [
-                real_c + jnp.where(lane_zero, 0.0, imag_s),
-                jnp.where(lane_zero, real_s, real_c - imag_s),
-                imag_c - jnp.where(lane_zero, 0.0, real_s),
-                jnp.where(lane_zero, imag_s, imag_c + real_s),
-            ],
-            axis=1,
-        )
-        plane = multiply(unfold(), split(plane))
-        real_c, real_s = plane[:half_z, :GRID_X], plane[half_z:, :GRID_X]
-        imag_c, imag_s = plane[:half_z, GRID_X:], plane[half_z:, GRID_X:]
-        real = jnp.concatenate(
-            [
-                real_c + jnp.where(row_zero, 0.0, imag_s),
-                jnp.where(row_zero, real_s, real_c - imag_s),
-            ],
-            axis=0,
-        )
-        imag = jnp.concatenate(
-            [
-                imag_c - jnp.where(row_zero, 0.0, real_s),
-                jnp.where(row_zero, imag_s, imag_c + real_s),
-            ],
-            axis=0,
-        )
-        mode = jnp.where(j == fine, GRID_Y // 2, piece * fine + j)
-        square = (factors[1, mode] + factor_row[1:2, :]) + factor_column[:, 1:2]
-        top = (factors[0, mode] * factor_row[0:1, :]) * factor_column[:, 0:1]
-        green = jnp.where(square == 0.0, 0.0, top / jnp.where(square == 0.0, 1.0, square))
+
+    def paired(real, imag, zero, axis):
+        half = real.shape[axis] // 2
+        first = (slice(None),) * axis + (slice(0, half),)
+        second = (slice(None),) * axis + (slice(half, 2 * half),)
+        real_c, real_s = real[first], real[second]
+        if imag is None:
+            none = jnp.zeros_like(real_s)
+            real_all = [real_c, jnp.where(zero, real_s, real_c)]
+            imag_all = [jnp.where(zero, none, -real_s), jnp.where(zero, none, real_s)]
+        else:
+            imag_c, imag_s = imag[first], imag[second]
+            real_all = [
+                real_c + jnp.where(zero, 0.0, imag_s),
+                jnp.where(zero, real_s, real_c - imag_s),
+            ]
+            imag_all = [
+                imag_c - jnp.where(zero, 0.0, real_s),
+                jnp.where(zero, imag_s, imag_c + real_s),
+            ]
+        return jnp.concatenate(real_all, axis=axis), jnp.concatenate(imag_all, axis=axis)
+
+    def merged(real, imag, zero, axis):
+        half = real.shape[axis] // 2
+        first = (slice(None),) * axis + (slice(0, half),)
+        second = (slice(None),) * axis + (slice(half, 2 * half),)
+        real_a, real_b = real[first], real[second]
+        imag_a, imag_b = imag[first], imag[second]
+        real = [
+            real_a + jnp.where(zero, 0.0, real_b),
+            jnp.where(zero, real_b, imag_b - imag_a),
+        ]
+        imag = [
+            imag_a + jnp.where(zero, 0.0, imag_b),
+            jnp.where(zero, imag_b, real_a - real_b),
+        ]
+        return jnp.concatenate(real, axis=axis), jnp.concatenate(imag, axis=axis)
+
+    def to_modes(real, imag, j):
+        real = multiply(split(real), fold())
+        if imag is not None:
+            imag = multiply(split(imag), fold())
+        real, imag = paired(real, imag, lane_zero, 1)
+        real = multiply(unfold(), split(real))
+        imag = multiply(unfold(), split(imag))
+        real, imag = paired(real, imag, row_zero, 0)
+        green = green_ref[j]
+        mode = GRID_Y // 2 if j == fine else piece * fine + j
         share = jnp.where((mode == 0) | (mode == GRID_Y // 2), 0.5, 1.0)
-        energy = energy + share * jnp.sum(green * (real * real + imag * imag))
-        planes[j, :, 0:GRID_X] = green * real
-        planes[j, :, GRID_X:] = green * imag
-        return energy
-
-    energy = lax.fori_loop(0, fine + 1, to_modes, jnp.float32(0.0))
-    planes[0, :, 0:GRID_X] -= planes[fine, :, GRID_X:]
-    planes[0, :, GRID_X:] += planes[fine, :, 0:GRID_X]
-
-    def to_grid(j, carry):
-        real_a, real_b = planes[j, :half_z, :GRID_X], planes[j, half_z:, :GRID_X]
-        imag_a, imag_b = planes[j, :half_z, GRID_X:], planes[j, half_z:, GRID_X:]
-        real = jnp.concatenate(
-            [
-                real_a + jnp.where(row_zero, 0.0, real_b),
-                jnp.where(row_zero, real_b, imag_b - imag_a),
-            ],
-            axis=0,
-        )
-        imag = jnp.concatenate(
-            [
-                imag_a + jnp.where(row_zero, 0.0, imag_b),
-                jnp.where(row_zero, imag_b, real_a - real_b),
-            ],
-            axis=0,
-        )
+        part = jnp.sum(green * (real * real + imag * imag), axis=0, keepdims=True)
+        return green * real, green * imag, share * part
+
+    second_plane = jnp.where(is_first, planes[0, :, GRID_X:], 0.0)
+    last_real, last_imag, energy = to_modes(second_plane, None, fine)
+    for j in range(fine):
+        imag = planes[j, :, GRID_X:]
+        if j == 0:
+            imag = jnp.where(is_first, 0.0, imag)
+        real, imag, part = to_modes(planes[j, :, 0:GRID_X], imag, j)
+        energy = energy + part
+        if j == 0:
+            real, imag = real - last_imag, imag + last_real
+        real, imag = merged(real, imag, row_zero, 0)
         real = multiply(fold(), split(real))
         imag = multiply(fold(), split(imag))
-        real_a, real_b = real[:, :half_x], real[:, half_x:]
-        imag_a, imag_b = imag[:, :half_x], imag[:, half_x:]
+        real, imag = merged(real, imag, lane_zero, 1)
         scale = jnp.where(piece * fine + j == 0, 1.0, 2.0)
-        real = jnp.concatenate(
-            [
-                real_a + jnp.where(lane_zero, 0.0, real_b),
-                jnp.where(lane_zero, real_b, imag_b - imag_a),
-            ],
-            axis=1,
-        )
-        imag = jnp.concatenate(
-            [
-                imag_a + jnp.where(lane_zero, 0.0, imag_b),
-                jnp.where(lane_zero, imag_b, real_a - real_b),
-            ],
-            axis=1,
-        )
         for part, lanes in ((real, slice(0, GRID_X)), (imag, slice(GRID_X, 2 * GRID_X))):
             part = multiply(split(part * scale), unfold())
             for k in range(copies):
                 moved = pltpu.roll(part, (HALO_X - k * cells_x) % GRID_X, 1)
                 grid[k, j, HALO_Z:, lanes] = moved
                 grid[k, j, 0:HALO_Z, lanes] = moved[GRID_Z - HALO_Z :]
-        return carry
-
-    lax.fori_loop(0, fine, to_grid, 0)
-
-    def collect(at_narrow, carry):
+    energy = jnp.broadcast_to(jnp.sum(energy, axis=1, keepdims=True), (1, 128))
+
+    def collect(at_narrow, buffer):
         row_x, _, row_z, _ = line(at_narrow)
-        fill_x(row_x, (weights, slopes))
-        value_z, slope_z = weights_z(row_z)
+        fill_x(row_x, (None, slopes.at[buffer]))
+        value_z = weights_z[at_narrow]
+        _, slope_z = splines_z(row_z)
         first = pl.multiple_of(at_narrow * cells_z, HALO_Z)
         lefts = []
         for k in range(copies):
@@ -561,15 +608,13 @@
             low = lefts[at_wide % copies][1][:, start : start + 128]
             twice = jnp.concatenate([high, high], axis=1)
 
-            def across(ref):
+            def across(right):
                 return lax.dot_general(
-                    twice, ref[:, lanes], NN, preferred_element_type=jnp.float32
-                ) + lax.dot_general(
-                    low, ref[0:128, lanes], NN, preferred_element_type=jnp.float32
-                )
-
-            value = across(weights)
-            slope = across(slopes)
+                    twice, right, NN, preferred_element_type=jnp.float32
+                ) + lax.dot_general(low, right[0:128], NN, preferred_element_type=jnp.float32)
+
+            value = across(weights[at_narrow, :, lanes])
+            slope = across(slopes[buffer, :, lanes])
             plain = jnp.zeros((window, pair), jnp.float32)
             along_x = plain
             along_y = plain
@@ -588,10 +633,9 @@
             ]
             for k, row in enumerate(results):
                 out_ref[at_wide, at_narrow, :, k * pair : (k + 1) * pair] = row
-            out_ref[at_wide, at_narrow, :, 4 * pair :] = jnp.full((1, 128), energy, jnp.float32)
-        return carry
-
-    lax.fori_loop(0, narrow_count, collect, 0)
+            out_ref[at_wide, at_narrow, :, 4 * pair :] = energy
+
+    in_pairs(collect)
 
 
 def finish_kernel(arrived, species, atom_ref, centroid_ref, energy_ref):
@@ -635,10 +679,6 @@
 
 def vmem(count):
     return [pl.BlockSpec(memory_space=pltpu.VMEM)] * count
-
-
-def smem(count):
-    return [pl.BlockSpec(memory_space=pltpu.SMEM)] * count
 
 
 def shaped(shape, dtype=jnp.float32):
@@ -692,28 +732,16 @@
     bf16 = jnp.bfloat16
     wave_rows = -(-2 * fine // 8) * 8
     angle = np.arange(GRID_Y) * (2.0 * math.pi / GRID_Y)
-    circle = jnp.asarray(np.stack([np.cos(angle), np.sin(angle)]), jnp.float32)
-    prepared = pl.pallas_call(
-        prepare_kernel,
-        out_shape=(
-            shaped((listed, atoms), jnp.int32),
-            shaped((256, 16)),
-            shaped((2 * ROW_PAD, 3 * ROW_PAD), bf16),
-            shaped((tall, 6 * ROW_PAD), bf16),
-            shaped((hidden, entries), bf16),
-            shaped((hidden, entries), bf16),
-        )
-        + (shaped((hidden, hidden), bf16),) * 4
-        + (shaped((wave_rows, GRID_Y)),),
-        in_specs=vmem(14),
-        out_specs=tuple(vmem(11)),
-        scratch_shapes=[pltpu.VMEM((16, 256), jnp.float32), pltpu.VMEM((256, 256), jnp.float32)],
-        compiler_params=limits(32),
-        cost_estimate=pl.CostEstimate(
-            flops=1000000, bytes_accessed=8 * entries * hidden, transcendentals=0
-        ),
-        name="prepare",
-    )(
+    constants = np.concatenate(
+        [
+            np.stack([np.cos(angle), np.sin(angle)]),
+            mode_factors(GRID_Y, np.arange(GRID_Y)),
+            mode_factors(GRID_X, folded_order(GRID_X)),
+            mode_factors(GRID_Z, folded_order(GRID_Z)),
+        ]
+    )
+    constants[2] *= coulomb / (math.pi * GRID_X * GRID_Y * GRID_Z)
+    arguments = (
         neighbours.reshape(atoms, listed),
         embed_one_w,
         embed_one_b,
@@ -727,9 +755,36 @@
         fit_two_b[None],
         fit_three_w,
         fit_three_b[None],
-        circle,
+        jnp.asarray(constants, jnp.float32),
     )
-    phase = prepared[10]
+    held = [arguments[k] for k in (0, 1, 2, 3, 4, 5, 6, 8, 10, 12, 13, 9, 11, 7)]
+    prepared = pl.pallas_call(
+        prepare_kernel,
+        out_shape=(
+            shaped((listed, atoms), jnp.int32),
+            shaped((256, 16)),
+            shaped((2 * ROW_PAD, 3 * ROW_PAD), bf16),
+            shaped((tall, 6 * ROW_PAD), bf16),
+            shaped((hidden, entries), bf16),
+            shaped((hidden, entries), bf16),
+        )
+        + (shaped((hidden, hidden), bf16),) * 4
+        + (shaped((wave_rows, GRID_Y)), shaped((fine + 1, GRID_Z, GRID_X))),
+        in_specs=[pl.BlockSpec(memory_space=pltpu.HBM)] * len(arguments),
+        out_specs=tuple(vmem(12)),
+        scratch_shapes=[
+            pltpu.VMEM((16, 256), jnp.float32),
+            pltpu.VMEM((256, 256), jnp.float32),
+            pltpu.SemaphoreType.DMA((len(held),)),
+        ]
+        + [pltpu.VMEM(array.shape, array.dtype) for array in held],
+        compiler_params=limits(32),
+        cost_estimate=pl.CostEstimate(
+            flops=1000000, bytes_accessed=8 * entries * hidden, transcendentals=0
+        ),
+        name="prepare",
+    )(*arguments)
+    phase, green = prepared[10:]
     dipole, shifts = pl.pallas_call(
         centroid_kernel,
         out_shape=(shaped((3, 1, atoms)), shaped((pieces, 4, atoms))),
@@ -745,8 +800,6 @@
     shifts = lax.all_to_all(shifts, axes, 0, 0, tiled=True)
     shifts = shifts.reshape(wide_count, narrow_count, 4, atoms)
 
-    factors = mode_factors(GRID_Y, np.arange(GRID_Y))
-    factors[0] *= coulomb / (math.pi * GRID_X * GRID_Y * GRID_Z)
     cells_x = GRID_X // wide_count
     copies = 128 // cells_x
     length = wide_count * 2 * atoms
@@ -754,23 +807,22 @@
     partial = pl.pallas_call(
         mesh_kernel,
         out_shape=shaped((wide_count, narrow_count, 1, out_width)),
-        in_specs=smem(1) + vmem(9),
+        in_specs=vmem(8),
         out_specs=vmem(1)[0],
         scratch_shapes=[
             pltpu.VMEM((copies, fine, HALO_Z + GRID_Z, 2 * GRID_X), jnp.float32),
             pltpu.VMEM((fine + 1, GRID_Z, 2 * GRID_X), jnp.float32),
         ]
-        + [pltpu.VMEM((256, length), bf16)] * 2
+        + [pltpu.VMEM((narrow_count, 256, length), bf16), pltpu.VMEM((2, 256, length), bf16)]
+        + [pltpu.VMEM((narrow_count, GRID_Z // narrow_count + HALO_Z, length), jnp.float32)]
         + [pltpu.VMEM((narrow_count, wave_rows, length), jnp.float32)] * 2,
         compiler_params=limits(48),
         name="mesh",
     )(
-        jnp.asarray(factors, jnp.float32),
         table,
         shifts,
         phase,
-        jnp.asarray(mode_factors(GRID_X, folded_order(GRID_X)), jnp.float32),
-        jnp.asarray(mode_factors(GRID_Z, folded_order(GRID_Z)).T, jnp.float32),
+        green,
         *[jnp.asarray(half) for half in halves(fold_table(GRID_X))],
         *[jnp.asarray(half) for half in halves(fold_table(GRID_X).T)],
     )

time: 83.1 us -> 90.3 us (1.087)
  local copies, waits for them, and re-layouts: 11 us -> 22.6 us
  Pallas kernels: 40.2 us -> 35.7 us
    unnamed x44 -> x66, local copies, waits for them, and re-layouts: 11 us -> 22.6 us
    pallas_call x1, Pallas kernels: 26.8 us -> 20.8 us  [local(): pl.pallas_call(mesh_kernel, out_shape=shaped((wide_count, narrow_count, 1...]
    pallas_call x1, Pallas kernels: 0.89 us -> 2.43 us  [local(): pl.pallas_call(prepare_kernel, out_shape=(shaped((listed, atoms), jnp.int...]
  transfers between devices with their start and end apart: 1 -> 1, of which waited for: 0 -> 0; matrix products, arithmetic and copies ran while one was open for 0% -> 0% of each run, Pallas kernels for 1% -> 3%
where the time goes in v3:
time: 90.3 us; the launch traced here: 89.5 us
  Pallas kernels  35.7 us (40%)
  blocking collectives  23.1 us (26%)
  local copies, waits for them, and re-layouts  22.6 us (25%)
  starting transfers between devices  7.3 us (8%)
    unnamed x66, local copies, waits for them, and re-layouts  22.6 us
    pallas_call x1, Pallas kernels, local(): pl.pallas_call(mesh_kernel, out_shape=shaped((wide_count, narrow_count, 1...  20.8 us
    all_to_all x1, blocking collectives, local(): shifts = lax.all_to_all(shifts, axes, 0, 0, tiled=True)  12.9 us
    all_to_all x1, blocking collectives, local(): lax.all_to_all(partial.reshape(pieces, 1, out_width), axes, 0, 0, tiled=T...  10.2 us
    pallas_call x1, Pallas kernels, local(): pl.pallas_call(centroid_kernel, out_shape=(shaped((3, 1, atoms)), shaped(...  9.67 us
    all_to_all x1, starting transfers between devices, local(): table = lax.all_to_all(packed, axes, 0, 0, tiled=True)  7.3 us
    pallas_call x1, Pallas kernels, local(): pl.pallas_call(prepare_kernel, out_shape=(shaped((listed, atoms), jnp.int...  2.43 us
  transfers between devices with their start and end apart: 1, of which 0 were waited for; matrix products, arithmetic and copies ran while one was open for 0% of the time, Pallas kernels for 3%

profile of v3, /device:TPU:0, one launch (start us, length us, event | category | flops | bytes accessed | tf_op | source)
XLA Modules:
  0.0 89.5 jit_solution(11803587854101801222)
XLA Ops:
  0.6 1.3 %pack.1 = f32[32,4,128]{2,1,0:T(4,128)} custom-call(f32[3,1,128]{2,1,0:T(1,128)} %bitcast.38, s32[1,128]{1,0:T(1,128)} %bitcast.36), custom_call_target="tpu_custom_call" | custom-call | tf_op jit(solution)/shard_map/pack/pallas_call | solution.py:721
  2.0 7.3 %all-to-all-start = ((f32[32,4,128]{2,1,0:T(4,128)}), f32[32,4,128]{2,1,0:T(4,128)S(1)}, u32[]{:S(2)}, u32[]{:S(2)}) async-start(f32[32,4,128]{2,1,0:T(4,128)} %pack.1), calls=%async_computation | async-start | bytes 131072 | tf_op jit(solution)/shard_map/all_to_all | solution.py:728
  9.3 1.4 %copy-done = f32[1600,240]{0,1:T(8,128)S(1)} copy-done((f32[1600,240]{0,1:T(8,128)S(1)}, f32[1600,240]{0,1:T(8,128)}, u32[]{:S(2)}) %copy-start) | copy-done | bytes 1536024
  10.7 0.9 %copy-done.1 = f32[240,240]{1,0:T(8,128)S(1)} copy-done((f32[240,240]{1,0:T(8,128)S(1)}, f32[240,240]{1,0:T(8,128)}, u32[]{:S(2)}) %copy-start.1) | copy-done | bytes 230424
  11.6 0.9 %copy-done.2 = f32[240,240]{1,0:T(8,128)S(1)} copy-done((f32[240,240]{1,0:T(8,128)S(1)}, f32[240,240]{1,0:T(8,128)}, u32[]{:S(2)}) %copy-start.2) | copy-done | bytes 230424
  12.6 0.8 copy-done.18
  13.4 0.7 copy-done.23
  14.2 0.7 copy-done.24
  14.9 0.7 copy-done.25
  15.6 0.7 copy-done.26
  16.3 0.7 copy-done.27
  16.9 0.7 copy-done.28
  17.6 0.7 copy-done.29
  18.3 0.7 copy-done.30
  19.0 0.7 copy-done.31
  19.6 0.7 copy-done.32
  20.3 2.4 %prepare.1 = (s32[128,128]{1,0:T(8,128)S(1)}, f32[256,16]{1,0:T(8,128)S(1)}, bf16[64,96]{1,0:T(8,128)(2,1)S(1)}, bf16[128,192]{1,0:T(8,128)(2,1)S(1)}, bf16[240,...) custom-call(s32[128,128]{1,0:T(8,128)S(1)} %bitcast.30, ...), custom_call_target="tpu_custom_call" | custom-call | flops 1000000 | bytes 3072000 | tf_op jit(solution)/shard_map/prepare/pallas_call | solution.py:761
  24.0 0.6 copy-done.11
  24.7 0.7 copy-done.13
  27.2 1.0 %copy-done.8 = f32[256,16]{1,0:T(8,128)S(1)} copy-done((f32[256,16]{1,0:T(8,128)S(1)}, f32[256,16]{1,0:T(8,128)}, u32[]{:S(2)}) %copy-start.8) | copy-done | bytes 16408
  28.2 0.9 %copy-done.10 = bf16[240,240]{1,0:T(8,128)(2,1)S(1)} copy-done((bf16[240,240]{1,0:T(8,128)(2,1)S(1)}, bf16[240,240]{1,0:T(8,128)(2,1)}, u32[]{:S(2)}) %copy-start.10) | copy-done | bytes 115224
  29.1 0.9 %copy-done.12 = bf16[240,240]{1,0:T(8,128)(2,1)S(1)} copy-done((bf16[240,240]{1,0:T(8,128)(2,1)S(1)}, bf16[240,240]{1,0:T(8,128)(2,1)}, u32[]{:S(2)}) %copy-start.12) | copy-done | bytes 115224
  30.0 0.9 %copy-done.14 = bf16[240,240]{1,0:T(8,128)(2,1)S(1)} copy-done((bf16[240,240]{1,0:T(8,128)(2,1)S(1)}, bf16[240,240]{1,0:T(8,128)(2,1)}, u32[]{:S(2)}) %copy-start.14) | copy-done | bytes 115224
  30.9 0.9 %copy-done.16 = bf16[240,240]{1,0:T(8,128)(2,1)S(1)} copy-done((bf16[240,240]{1,0:T(8,128)(2,1)S(1)}, bf16[240,240]{1,0:T(8,128)(2,1)}, u32[]{:S(2)}) %copy-start.16) | copy-done | bytes 115224
  31.8 0.9 copy-done.17
  32.7 0.8 copy-done.20
  33.5 0.8 copy-done.22
  34.4 9.7 %centroids.1 = (f32[3,1,128]{2,1,0:T(1,128)}, f32[32,4,128]{2,1,0:T(4,128)S(1)}) custom-call(f32[4,8,4,128]{3,2,1,0:T(4,128)S(1)} %bitcast.26, s32[128,128]{1,0:T(8,128)S(1)} %copy-done.20, f32[256,16]{1,0:T(8,128)S(1)} %copy-done.8, bf16[64,96]{1,0:T(8,128)(2,1)S(1)} %get-tuple-element.23.second, bf16[128,192]{1,0:T(8,128)(2,1)S(1)} %copy-done.22, ...), custom_call_target="tpu_custom_call" | custom-call | tf_op jit(solution)/shard_map/centroids/pallas_call | solution.py:788
  44.0 12.9 %all_to_all.15 = f32[32,4,128]{2,1,0:T(4,128)S(1)} all-to-all(f32[32,4,128]{2,1,0:T(4,128)S(1)} %get-tuple-element.32), channel_id=1, replica_groups=mesh['wide'=4,'narrow'=8] {'wide','narrow'}, dimensions={0} | all-to-all | bytes 131072 | tf_op jit(solution)/shard_map/all_to_all | solution.py:800
  57.0 20.8 %mesh.1 = f32[4,8,1,1152]{3,2,1,0:T(1,128)S(1)} custom-call(f32[4,8,4,128]{3,2,1,0:T(4,128)S(1)} %bitcast.27, f32[4,8,4,128]{3,2,1,0:T(4,128)S(1)} %bitcast.28, f32[8,256]{1,0:T(8,128)S(1)} %get-tuple-element.33.phase, f32[5,256,256]{2,1,0:T(8,128)S(1)} %get-tuple-element.34.green_ref, bf16[256,256]{1,0:T(8,128)(2,1)S(1)} %copy-done.6, ...), custom_call_target="tpu_custom_call" | custom-call | tf_op jit(solution)/shard_map/mesh/pallas_call | solution.py:807
  77.7 10.2 %all_to_all.16.arrived = f32[32,1,1152]{2,1,0:T(1,128)} all-to-all(f32[32,1,1152]{2,1,0:T(1,128)S(1)} %bitcast.25), channel_id=1, replica_groups=mesh['wide'=4,'narrow'=8] {'wide','narrow'}, dimensions={0} | all-to-all | bytes 294912 | tf_op jit(solution)/shard_map/all_to_all | solution.py:829
  87.9 1.5 %finish.1 = (f32[4,1,128]{2,1,0:T(1,128)}, f32[4,1,128]{2,1,0:T(1,128)}, f32[1,128]{1,0:T(1,128)}) custom-call(f32[32,1,1152]{2,1,0:T(1,128)} %all_to_all.16.arrived, s32[1,128]{1,0:T(1,128)} %bitcast.37), custom_call_target="tpu_custom_call" | custom-call | tf_op jit(solution)/shard_map/finish/pallas_call | solution.py:830
  (43 shorter events, 3.2 us)
Async XLA Ops:
  2.0 25.2 %all-to-all-start = ((f32[32,4,128]{2,1,0:T(4,128)}), f32[32,4,128]{2,1,0:T(4,128)S(1)}, u32[]{:S(2)}, u32[]{:S(2)}) async-start(f32[32,4,128]{2,1,0:T(4,128)} %pack.1), calls=%async_computation | async-start | bytes 131072 | tf_op jit(solution)/shard_map/all_to_all | solution.py:728
  9.3 1.4 %copy-start = (f32[1600,240]{0,1:T(8,128)S(1)}, f32[1600,240]{0,1:T(8,128)}, u32[]{:S(2)}) copy-start(f32[1600,240]{0,1:T(8,128)} %param.30) | copy-start | bytes 4608004
  10.7 0.9 %copy-start.1 = (f32[240,240]{1,0:T(8,128)S(1)}, f32[240,240]{1,0:T(8,128)}, u32[]{:S(2)}) copy-start(f32[240,240]{1,0:T(8,128)} %fit_two_w.1) | copy-start | bytes 691204
  11.6 0.9 %copy-start.2 = (f32[240,240]{1,0:T(8,128)S(1)}, f32[240,240]{1,0:T(8,128)}, u32[]{:S(2)}) copy-start(f32[240,240]{1,0:T(8,128)} %fit_three_w.1) | copy-start | bytes 691204
  12.6 0.8 copy-start.18
  13.4 0.7 copy-start.23
  14.2 0.7 copy-start.24
  14.9 0.7 copy-start.25
  15.6 0.7 copy-start.26
  16.3 0.7 copy-start.27
  16.9 0.7 copy-start.28
  17.6 0.7 copy-start.29
  18.3 0.7 copy-start.30
  19.0 0.7 copy-start.31
  19.6 0.7 copy-start.32
  22.7 0.6 copy-start.7
  23.4 0.6 copy-start.9
  24.0 0.6 copy-start.11
  24.6 0.7 copy-start.13
  25.3 0.6 copy-start.15
  27.2 29.8 %copy-start.3 = (bf16[256,256]{1,0:T(8,128)(2,1)S(1)}, bf16[256,256]{1,0:T(8,128)(2,1)}, u32[]{:S(2)}) copy-start(bf16[256,256]{1,0:T(8,128)(2,1)} %constant.14.clone.unfold_low) | copy-start | bytes 393220
  27.2 29.8 %copy-start.4 = (bf16[256,256]{1,0:T(8,128)(2,1)S(1)}, bf16[256,256]{1,0:T(8,128)(2,1)}, u32[]{:S(2)}) copy-start(bf16[256,256]{1,0:T(8,128)(2,1)} %constant.13.clone.unfold_high) | copy-start | bytes 393220
  27.2 29.8 %copy-start.5 = (bf16[256,256]{1,0:T(8,128)(2,1)S(1)}, bf16[256,256]{1,0:T(8,128)(2,1)}, u32[]{:S(2)}) copy-start(bf16[256,256]{1,0:T(8,128)(2,1)} %constant.12.clone.fold_low) | copy-start | bytes 393220
  27.2 29.8 %copy-start.6 = (bf16[256,256]{1,0:T(8,128)(2,1)S(1)}, bf16[256,256]{1,0:T(8,128)(2,1)}, u32[]{:S(2)}) copy-start(bf16[256,256]{1,0:T(8,128)(2,1)} %constant.11.clone.fold_high) | copy-start | bytes 393220
  27.2 1.0 %copy-start.8 = (f32[256,16]{1,0:T(8,128)S(1)}, f32[256,16]{1,0:T(8,128)}, u32[]{:S(2)}) copy-start(f32[256,16]{1,0:T(8,128)} %copy-done.7) | copy-start | bytes 49156
  28.2 0.9 %copy-start.10 = (bf16[240,240]{1,0:T(8,128)(2,1)S(1)}, bf16[240,240]{1,0:T(8,128)(2,1)}, u32[]{:S(2)}) copy-start(bf16[240,240]{1,0:T(8,128)(2,1)} %copy-done.9) | copy-start | bytes 345604
  29.1 0.9 %copy-start.12 = (bf16[240,240]{1,0:T(8,128)(2,1)S(1)}, bf16[240,240]{1,0:T(8,128)(2,1)}, u32[]{:S(2)}) copy-start(bf16[240,240]{1,0:T(8,128)(2,1)} %copy-done.11) | copy-start | bytes 345604
  30.0 0.9 %copy-start.14 = (bf16[240,240]{1,0:T(8,128)(2,1)S(1)}, bf16[240,240]{1,0:T(8,128)(2,1)}, u32[]{:S(2)}) copy-start(bf16[240,240]{1,0:T(8,128)(2,1)} %copy-done.13) | copy-start | bytes 345604
  30.9 0.9 %copy-start.16 = (bf16[240,240]{1,0:T(8,128)(2,1)S(1)}, bf16[240,240]{1,0:T(8,128)(2,1)}, u32[]{:S(2)}) copy-start(bf16[240,240]{1,0:T(8,128)(2,1)} %copy-done.15) | copy-start | bytes 345604
  31.8 0.9 %copy-start.17 = (f32[240,100]{0,1:T(8,128)S(1)}, f32[240,100]{0,1:T(8,128)}, u32[]{:S(2)}) copy-start(f32[240,100]{0,1:T(8,128)} %param.36) | copy-start | bytes 288004
  32.7 0.8 copy-start.20
  33.5 0.8 copy-start.22
  (2 other events, 1.2 us)

commit v4 on v3

--- a/solution.py
+++ b/solution.py
@@ -235,7 +235,17 @@
     shift_ref,
     matrix,
     descriptor,
+    arrivals,
+    *held,
 ):
+    sources = (one_high, one_low, two_high, two_low, three_high, three_low, fit_out_w)
+    copies = [
+        pltpu.make_async_copy(source, target, arrivals.at[k])
+        for k, (source, target) in enumerate(zip(sources, held))
+    ]
+    for copy in copies:
+        copy.start()
+    one_high, one_low, two_high, two_low, three_high, three_low, fit_out_w = held
     wide_count, narrow_count, _, atoms = table.shape
     listed = codes.shape[0]
     width_three = fit_out_w.shape[0]
@@ -344,6 +354,9 @@
         for part in range(1, 4):
             total = total + parts[part][row : row + 1] * leading[part]
         descriptor[row * AXIS_COLUMNS : (row + 1) * AXIS_COLUMNS, :] = total
+    for copy in copies:
+        copy.wait()
+
     def layer(high_ref, low_ref, given, column):
         weights = (high_ref[...], low_ref[...])
         return jnp.tanh(multiply(weights, split(given)) + columns[0:hidden_width, column : column + 1])
@@ -681,6 +694,10 @@
     return [pl.BlockSpec(memory_space=pltpu.VMEM)] * count
 
 
+def hbm(count):
+    return [pl.BlockSpec(memory_space=pltpu.HBM)] * count
+
+
 def shaped(shape, dtype=jnp.float32):
     return jax.ShapeDtypeStruct(shape, dtype)
 
@@ -770,7 +787,7 @@
         )
         + (shaped((hidden, hidden), bf16),) * 4
         + (shaped((wave_rows, GRID_Y)), shaped((fine + 1, GRID_Z, GRID_X))),
-        in_specs=[pl.BlockSpec(memory_space=pltpu.HBM)] * len(arguments),
+        in_specs=hbm(len(arguments)),
         out_specs=tuple(vmem(12)),
         scratch_shapes=[
             pltpu.VMEM((16, 256), jnp.float32),
@@ -778,25 +795,28 @@
             pltpu.SemaphoreType.DMA((len(held),)),
         ]
         + [pltpu.VMEM(array.shape, array.dtype) for array in held],
-        compiler_params=limits(32),
+        compiler_params=limits(62),
         cost_estimate=pl.CostEstimate(
             flops=1000000, bytes_accessed=8 * entries * hidden, transcendentals=0
         ),
         name="prepare",
     )(*arguments)
     phase, green = prepared[10:]
+    fitted = (*prepared[4:10], fit_out_w.T)
     dipole, shifts = pl.pallas_call(
         centroid_kernel,
         out_shape=(shaped((3, 1, atoms)), shaped((pieces, 4, atoms))),
-        in_specs=vmem(12),
+        in_specs=vmem(5) + hbm(7),
         out_specs=tuple(vmem(2)),
         scratch_shapes=[
             pltpu.VMEM((4, tall, atoms), jnp.float32),
             pltpu.VMEM((width_three * AXIS_COLUMNS, atoms), jnp.float32),
-        ],
-        compiler_params=limits(32),
+            pltpu.SemaphoreType.DMA((len(fitted),)),
+        ]
+        + [pltpu.VMEM(array.shape, array.dtype) for array in fitted],
+        compiler_params=limits(62),
         name="centroids",
-    )(table, *prepared[:10], fit_out_w.T)
+    )(table, *prepared[:4], *fitted)
     shifts = lax.all_to_all(shifts, axes, 0, 0, tiled=True)
     shifts = shifts.reshape(wide_count, narrow_count, 4, atoms)
 

time: 90.3 us -> 71.6 us (0.79)
  local copies, waits for them, and re-layouts: 22.6 us -> 1.5 us
  waiting for transfers between devices: 0.01 us -> 3.25 us
  blocking collectives: 23.1 us -> 20.1 us
  Pallas kernels: 35.7 us -> 38.3 us
    unnamed x66 -> x16, local copies, waits for them, and re-layouts: 22.6 us -> 1.5 us
    all_to_all x1, waiting for transfers between devices: 0.01 us -> 3.25 us  [local(): table = lax.all_to_all(packed, axes, 0, 0, tiled=True)]
    all_to_all x1, blocking collectives: 12.9 us -> 9.89 us  [local(): shifts = lax.all_to_all(shifts, axes, 0, 0, tiled=True)]
    pallas_call x1, Pallas kernels: 2.43 us -> 3.95 us  [local(): pl.pallas_call(prepare_kernel, out_shape=(shaped((listed, atoms), jnp.int...]
    pallas_call x1, Pallas kernels: 9.67 us -> 10.9 us  [local(): pl.pallas_call(centroid_kernel, out_shape=(shaped((3, 1, atoms)), shaped(...]
  transfers between devices with their start and end apart: 1 -> 1, of which waited for: 0 -> 1; matrix products, arithmetic and copies ran while one was open for 0% -> 0% of each run, Pallas kernels for 3% -> 6%
where the time goes in v4:
time: 71.6 us; the launch traced here: 71.2 us
  Pallas kernels  38.3 us (53%)
  blocking collectives  20.1 us (28%)
  starting transfers between devices  7.3 us (10%)
  waiting for transfers between devices  3.25 us (5%)
  local copies, waits for them, and re-layouts  1.5 us (2%)
  between operations  0.75 us (1%)
    pallas_call x1, Pallas kernels, local(): pl.pallas_call(mesh_kernel, out_shape=shaped((wide_count, narrow_count, 1...  20.6 us
    pallas_call x1, Pallas kernels, local(): pl.pallas_call(centroid_kernel, out_shape=(shaped((3, 1, atoms)), shaped(...  10.9 us
    all_to_all x1, blocking collectives, local(): lax.all_to_all(partial.reshape(pieces, 1, out_width), axes, 0, 0, tiled=T...  10.2 us
    all_to_all x1, blocking collectives, local(): shifts = lax.all_to_all(shifts, axes, 0, 0, tiled=True)  9.89 us
    all_to_all x1, starting transfers between devices, local(): table = lax.all_to_all(packed, axes, 0, 0, tiled=True)  7.3 us
    pallas_call x1, Pallas kernels, local(): pl.pallas_call(prepare_kernel, out_shape=(shaped((listed, atoms), jnp.int...  3.95 us
    all_to_all x1, waiting for transfers between devices, local(): table = lax.all_to_all(packed, axes, 0, 0, tiled=True)  3.25 us
    pallas_call x1, Pallas kernels, local(): pl.pallas_call(finish_kernel, out_shape=(shaped((4, 1, atoms)), shaped((4...  1.53 us
  transfers between devices with their start and end apart: 1, of which 1 were waited for; matrix products, arithmetic and copies ran while one was open for 0% of the time, Pallas kernels for 6%

profile of v4, /device:TPU:0, one launch (start us, length us, event | category | flops | bytes accessed | tf_op | source)
XLA Modules:
  0.0 71.2 jit_solution(16354058510773543740)
XLA Ops:
  0.6 1.3 %pack.1 = f32[32,4,128]{2,1,0:T(4,128)} custom-call(f32[3,1,128]{2,1,0:T(1,128)} %bitcast.33, s32[1,128]{1,0:T(1,128)} %bitcast.31), custom_call_target="tpu_custom_call" | custom-call | tf_op jit(solution)/shard_map/pack/pallas_call | solution.py:738
  2.0 7.3 %all-to-all-start = ((f32[32,4,128]{2,1,0:T(4,128)}), f32[32,4,128]{2,1,0:T(4,128)S(1)}, u32[]{:S(2)}, u32[]{:S(2)}) async-start(f32[32,4,128]{2,1,0:T(4,128)} %pack.1), calls=%async_computation | async-start | bytes 131072 | tf_op jit(solution)/shard_map/all_to_all | solution.py:745
  9.3 3.9 %prepare.1 = (s32[128,128]{1,0:T(8,128)}, f32[256,16]{1,0:T(8,128)}, bf16[64,96]{1,0:T(8,128)(2,1)}, bf16[128,192]{1,0:T(8,128)(2,1)}, bf16[240,1600]{1,0:T(8,12...) custom-call(s32[128,128]{1,0:T(8,128)} %bitcast.30, ...), custom_call_target="tpu_custom_call" | custom-call | flops 1000000 | bytes 3072000 | tf_op jit(solution)/shard_map/prepare/pallas_call | solution.py:778
  13.2 0.0 copy-start
  13.2 0.0 copy-start.3
  13.2 0.0 copy-start.4
  13.2 0.0 copy-start.5
  13.3 0.0 copy-start.6
  13.3 0.0 copy-start.7
  13.3 3.3 %all-to-all-done = f32[32,4,128]{2,1,0:T(4,128)S(1)} async-done(((f32[32,4,128]{2,1,0:T(4,128)}), f32[32,4,128]{2,1,0:T(4,128)S(1)}, u32[]{:S(2)}, u32[]{:S(2)}) %all-to-all-start) | async-done | bytes 65568 | tf_op jit(solution)/shard_map/all_to_all | solution.py:745
  16.5 0.0 copy-start.1
  16.5 0.6 copy-done.1
  17.2 10.9 %centroids.1 = (f32[3,1,128]{2,1,0:T(1,128)}, f32[32,4,128]{2,1,0:T(4,128)}) custom-call(f32[4,8,4,128]{3,2,1,0:T(4,128)} %bitcast.25, s32[128,128]{1,0:T(8,128)} %get-tuple-element.21.codes, f32[256,16]{1,0:T(8,128)} %get-tuple-element.22.columns, bf16[64,96]{1,0:T(8,128)(2,1)} %get-tuple-element.23.second, bf16[128,192]{1,0:T(8,128)(2,1)} %get-tuple-element.24.third, ...), custom_call_target="tpu_custom_call" | custom-call | tf_op jit(solution)/shard_map/centroids/pallas_call | solution.py:806
  28.1 9.9 %all_to_all.15 = f32[32,4,128]{2,1,0:T(4,128)S(1)} all-to-all(f32[32,4,128]{2,1,0:T(4,128)} %get-tuple-element.32), channel_id=1, replica_groups=mesh['wide'=4,'narrow'=8] {'wide','narrow'}, dimensions={0} | all-to-all | bytes 131072 | tf_op jit(solution)/shard_map/all_to_all | solution.py:820
  38.0 0.0 copy-done
  38.0 0.0 copy-done.3
  38.0 0.0 copy-done.4
  38.0 0.0 copy-done.5
  38.0 0.0 copy-done.6
  38.0 0.0 copy-done.7
  38.0 0.0 copy-start.2
  38.0 0.8 %copy-done.2 = f32[32,4,128]{2,1,0:T(4,128)S(1)} copy-done((f32[32,4,128]{2,1,0:T(4,128)S(1)}, f32[32,4,128]{2,1,0:T(4,128)}, u32[]{:S(2)}) %copy-start.2) | copy-done | bytes 65560
  38.9 20.6 %mesh.1 = f32[4,8,1,1152]{3,2,1,0:T(1,128)S(1)} custom-call(f32[4,8,4,128]{3,2,1,0:T(4,128)S(1)} %bitcast.26, f32[4,8,4,128]{3,2,1,0:T(4,128)S(1)} %bitcast.27, f32[8,256]{1,0:T(8,128)S(1)} %copy-done.7, f32[5,256,256]{2,1,0:T(8,128)S(1)} %copy-done, bf16[256,256]{1,0:T(8,128)(2,1)S(1)} %copy-done.6, bf16[256,256]{1,0:T(8,128)(2,1)S(1)} %copy-done.5, ...), custom_call_target="tpu_custom_call" | custom-call | tf_op jit(solution)/shard_map/mesh/pallas_call | solution.py:827
  59.5 10.2 %all_to_all.16.arrived = f32[32,1,1152]{2,1,0:T(1,128)} all-to-all(f32[32,1,1152]{2,1,0:T(1,128)S(1)} %bitcast.24), channel_id=1, replica_groups=mesh['wide'=4,'narrow'=8] {'wide','narrow'}, dimensions={0} | all-to-all | bytes 294912 | tf_op jit(solution)/shard_map/all_to_all | solution.py:849
  69.7 1.5 %finish.1 = (f32[4,1,128]{2,1,0:T(1,128)}, f32[4,1,128]{2,1,0:T(1,128)}, f32[1,128]{1,0:T(1,128)}) custom-call(f32[32,1,1152]{2,1,0:T(1,128)} %all_to_all.16.arrived, s32[1,128]{1,0:T(1,128)} %bitcast.32), custom_call_target="tpu_custom_call" | custom-call | tf_op jit(solution)/shard_map/finish/pallas_call | solution.py:850
Async XLA Ops:
  2.0 14.6 %all-to-all-start = ((f32[32,4,128]{2,1,0:T(4,128)}), f32[32,4,128]{2,1,0:T(4,128)S(1)}, u32[]{:S(2)}, u32[]{:S(2)}) async-start(f32[32,4,128]{2,1,0:T(4,128)} %pack.1), calls=%async_computation | async-start | bytes 131072 | tf_op jit(solution)/shard_map/all_to_all | solution.py:745
  13.2 24.8 %copy-start = (f32[5,256,256]{2,1,0:T(8,128)S(1)}, f32[5,256,256]{2,1,0:T(8,128)}, u32[]{:S(2)}) copy-start(f32[5,256,256]{2,1,0:T(8,128)} %get-tuple-element.34.green_ref) | copy-start | bytes 3932164
  13.2 24.8 %copy-start.3 = (bf16[256,256]{1,0:T(8,128)(2,1)S(1)}, bf16[256,256]{1,0:T(8,128)(2,1)}, u32[]{:S(2)}) copy-start(bf16[256,256]{1,0:T(8,128)(2,1)} %constant.14.clone.unfold_low) | copy-start | bytes 393220
  13.2 24.8 %copy-start.4 = (bf16[256,256]{1,0:T(8,128)(2,1)S(1)}, bf16[256,256]{1,0:T(8,128)(2,1)}, u32[]{:S(2)}) copy-start(bf16[256,256]{1,0:T(8,128)(2,1)} %constant.13.clone.unfold_high) | copy-start | bytes 393220
  13.2 24.8 %copy-start.5 = (bf16[256,256]{1,0:T(8,128)(2,1)S(1)}, bf16[256,256]{1,0:T(8,128)(2,1)}, u32[]{:S(2)}) copy-start(bf16[256,256]{1,0:T(8,128)(2,1)} %constant.12.clone.fold_low) | copy-start | bytes 393220
  13.3 24.7 %copy-start.6 = (bf16[256,256]{1,0:T(8,128)(2,1)S(1)}, bf16[256,256]{1,0:T(8,128)(2,1)}, u32[]{:S(2)}) copy-start(bf16[256,256]{1,0:T(8,128)(2,1)} %constant.11.clone.fold_high) | copy-start | bytes 393220
  13.3 24.7 %copy-start.7 = (f32[8,256]{1,0:T(8,128)S(1)}, f32[8,256]{1,0:T(8,128)}, u32[]{:S(2)}) copy-start(f32[8,256]{1,0:T(8,128)} %get-tuple-element.33.phase) | copy-start | bytes 24580
  16.5 0.6 copy-start.1
  38.0 0.8 %copy-start.2 = (f32[32,4,128]{2,1,0:T(4,128)S(1)}, f32[32,4,128]{2,1,0:T(4,128)}, u32[]{:S(2)}) copy-start(f32[32,4,128]{2,1,0:T(4,128)} %copy-done.1) | copy-start | bytes 196612

commit v5 on v4

--- a/solution.py
+++ b/solution.py
@@ -155,12 +155,8 @@
     for kind in range(2):
         rows[kind : kind + 1, 0:width_one] = embed_one_w[kind : kind + 1, :]
         rows[2 + kind : 3 + kind, 0:width_one] = embed_one_b[kind : kind + 1, :]
-    for row, source, groups in ((4, embed_two_b, 2), (5, embed_three_b, 4)):
-        for k in range(groups):
-            rows[row : row + 1, k * ROW_PAD : k * ROW_PAD + width_one] = source[
-                :, k * width_one : (k + 1) * width_one
-            ]
-    for row, source in ((6, fit_one_b), (7, fit_two_b), (8, fit_three_b)):
+        rows[2 + kind : 3 + kind, width_one : width_one + 1] = jnp.full((1, 1), 40.0, jnp.float32)
+    for row, source in ((4, fit_one_b), (5, fit_two_b), (6, fit_three_b)):
         rows[row : row + 1, 0:hidden] = source[...]
     columns_ref[...] = jnp.transpose(rows[...])
 
@@ -169,6 +165,9 @@
         square[0:width_one, k * ROW_PAD : k * ROW_PAD + width_one] = embed_two_w[
             :, k * width_one : (k + 1) * width_one
         ]
+        square[
+            width_one : width_one + 1, k * ROW_PAD : k * ROW_PAD + width_one
+        ] = embed_two_b[:, k * width_one : (k + 1) * width_one]
     high, low = split(jnp.transpose(square[0:128, 0:128])[0 : 2 * ROW_PAD, 0:ROW_PAD])
     second_ref[...] = jnp.concatenate([high, high, low], axis=1)
     square[0:128, 0:128] = jnp.zeros((128, 128), jnp.float32)
@@ -179,6 +178,10 @@
             ] = embed_three_w[
                 g * width_one : (g + 1) * width_one, k * width_one : (k + 1) * width_one
             ]
+    for k in range(4):
+        square[
+            width_one : width_one + 1, k * ROW_PAD : k * ROW_PAD + width_one
+        ] = embed_three_b[:, k * width_one : (k + 1) * width_one]
     high, low = split(jnp.transpose(square[0:128, 0:128])[:, 0 : 2 * ROW_PAD])
     third_ref[...] = jnp.concatenate([high, high, low], axis=1)
     for copy in copies[11:13]:
@@ -267,12 +270,9 @@
     weight_hydrogen = jnp.broadcast_to(columns[0:ROW_PAD, 1:2], (ROW_PAD, atoms))
     bias_oxygen = jnp.broadcast_to(columns[0:ROW_PAD, 2:3], (ROW_PAD, atoms))
     bias_hydrogen = jnp.broadcast_to(columns[0:ROW_PAD, 3:4], (ROW_PAD, atoms))
-    second_bias = columns[0 : 2 * ROW_PAD, 4:5]
-    third_bias = columns[0 : 4 * ROW_PAD, 5:6]
     matrix[...] = jnp.zeros_like(matrix)
 
-    def chunk(index, carry):
-        first = pl.multiple_of(index * SLOT_CHUNK, SLOT_CHUNK)
+    def chunk(first):
         code = codes[pl.ds(first, SLOT_CHUNK), :]
         offset = code // atoms
         slot = code - offset * atoms
@@ -318,7 +318,7 @@
             NN,
             preferred_element_type=jnp.float32,
         )
-        layer_two = jnp.tanh(layer_two + second_bias) + jnp.concatenate(
+        layer_two = jnp.tanh(layer_two) + jnp.concatenate(
             [layer_one, layer_one], axis=0
         )
         high, low = split(layer_two)
@@ -328,7 +328,7 @@
             NN,
             preferred_element_type=jnp.float32,
         )
-        layer_three = jnp.tanh(layer_three + third_bias) + jnp.concatenate(
+        layer_three = jnp.tanh(layer_three) + jnp.concatenate(
             [layer_two, layer_two], axis=0
         )
         for part in range(4):
@@ -336,9 +336,14 @@
             for k in range(SLOT_CHUNK):
                 total = total + layer_three[:, k * atoms : (k + 1) * atoms] * radial[part][k : k + 1]
             matrix[part] = total
+
+    def two_chunks(index, carry):
+        first = pl.multiple_of(index * (2 * SLOT_CHUNK), 2 * SLOT_CHUNK)
+        chunk(first)
+        chunk(pl.multiple_of(first + SLOT_CHUNK, SLOT_CHUNK))
         return carry
 
-    lax.fori_loop(0, listed // SLOT_CHUNK, chunk, 0)
+    lax.fori_loop(0, listed // (2 * SLOT_CHUNK), two_chunks, 0)
 
     parts = []
     for part in range(4):
@@ -361,9 +366,9 @@
         weights = (high_ref[...], low_ref[...])
         return jnp.tanh(multiply(weights, split(given)) + columns[0:hidden_width, column : column + 1])
 
-    hidden = layer(one_high, one_low, descriptor[...], 6)
-    hidden = hidden + layer(two_high, two_low, hidden, 7)
-    hidden = hidden + layer(three_high, three_low, hidden, 8)
+    hidden = layer(one_high, one_low, descriptor[...], 4)
+    hidden = hidden + layer(two_high, two_low, hidden, 5)
+    hidden = hidden + layer(three_high, three_low, hidden, 6)
     coeffs = multiply(split(fit_out_w[...]), split(hidden))
     vector = jnp.concatenate(
         [jnp.sum(coeffs * parts[1 + c], axis=0, keepdims=True) for c in range(3)], axis=0
@@ -377,6 +382,132 @@
         shift_ref[target] = moved
 
 
+def splines_z(row, window):
+    counter = lax.broadcasted_iota(jnp.int32, (window, 1), 0).astype(jnp.float32)
+    return spline_pair(row - (counter - float(HALO_Z)))
+
+
+def splines_x(row, reach, value_ref, slope_ref):
+    counter = lax.broadcasted_iota(jnp.int32, (reach, 1), 0).astype(jnp.float32)
+    both = spline_pair(row - (counter - float(HALO_X)))
+    rest = jnp.zeros((128 - reach, row.shape[1]), jnp.bfloat16)
+    for values, ref in zip(both, (value_ref, slope_ref)):
+        if ref is not None:
+            high, low = split(values)
+            ref[0:reach, :] = high
+            ref[reach:128, :] = rest
+            ref[128 : 128 + reach, :] = low
+            ref[128 + reach : 256, :] = rest
+
+
+def in_pairs(count, step):
+    def both(index, carry):
+        step(2 * index, 0)
+        step(2 * index + 1, 1)
+        return carry
+
+    lax.fori_loop(0, count // 2, both, 0)
+
+
+def site_rows(table, shifts, at_narrow):
+    wide_count, narrow_count, _, _ = table.shape
+    extents = (GRID_X // wide_count, GRID_Y, GRID_Z // narrow_count)
+    rows = [[], [], [], []]
+    for at_wide in range(wide_count):
+        atom = table[at_wide, at_narrow]
+        for component, extent in enumerate(extents):
+            row = atom[component : component + 1] * float(extent)
+            if shifts is not None:
+                row = row + shifts[at_wide, at_narrow, component : component + 1, :]
+            rows[component].append(row)
+        hydrogen = atom[3:4]
+        oxygen = 1.0 - hydrogen
+        rows[3].append(6.0 * oxygen + hydrogen if shifts is None else -8.0 * oxygen)
+    return [jnp.concatenate(row, axis=1) for row in rows]
+
+
+def spread_sites(table, shifts, phase, grid, weights, weights_z, waves, wave_slopes):
+    wide_count, narrow_count, _, atoms = table.shape
+    cells_x = GRID_X // wide_count
+    cells_z = GRID_Z // narrow_count
+    window = cells_z + HALO_Z
+    copies, fine = grid.shape[:2]
+    rows = phase.shape[0]
+    grid[:, :, 0:HALO_Z, :] = jnp.zeros((copies, fine, HALO_Z, 2 * GRID_X), jnp.float32)
+
+    def spread(at_narrow, _):
+        row_x, row_y, row_z, charge = site_rows(table, shifts, at_narrow)
+        lower = jnp.floor(row_y)
+        back = lax.broadcasted_iota(jnp.int32, (8, 1), 0)
+        value_y, slope_y = spline_pair((row_y - lower) + back.astype(jnp.float32))
+        cell = lax.rem(lower.astype(jnp.int32) - back + GRID_Y, GRID_Y)
+        wave_blocks = []
+        slope_blocks = []
+        for at_wide in range(wide_count):
+            lanes = slice(at_wide * atoms, (at_wide + 1) * atoms)
+            wave = jnp.zeros((rows, atoms), jnp.float32)
+            wave_slope = jnp.zeros((rows, atoms), jnp.float32)
+            for k in range(4):
+                spot = jnp.broadcast_to(cell[k : k + 1, lanes], (rows, atoms))
+                found = lookup(phase[...], spot)
+                wave = wave + value_y[k : k + 1, lanes] * found
+                wave_slope = wave_slope + slope_y[k : k + 1, lanes] * found
+            wave_blocks.append(wave)
+            slope_blocks.append(wave_slope)
+        wave = jnp.concatenate(wave_blocks, axis=1)
+        waves[at_narrow] = wave
+        wave_slopes[at_narrow] = jnp.concatenate(slope_blocks, axis=1)
+        splines_x(row_x, cells_x + HALO_X, weights.at[at_narrow], None)
+        value_z, _ = splines_z(row_z, window)
+        weights_z[at_narrow] = value_z
+        charged = wave * charge
+        first = pl.multiple_of(at_narrow * cells_z, HALO_Z)
+        for at_wide in range(wide_count):
+            lanes = slice(at_wide * atoms, (at_wide + 1) * atoms)
+            near = value_z[:, lanes]
+            left = jnp.concatenate(
+                [near * charged[c : c + 1, lanes] for c in range(2 * fine)], axis=0
+            )
+            across = weights[at_narrow, :, lanes]
+            total = lax.dot_general(
+                jnp.concatenate(split(left), axis=1),
+                jnp.concatenate([across, across], axis=1),
+                NT,
+                preferred_element_type=jnp.float32,
+            )
+            total = total[:, 0:128] + total[:, 128:256]
+            start = at_wide // copies * 128
+            for c in range(2 * fine):
+                spot = slice(c % 2 * GRID_X + start, c % 2 * GRID_X + start + 128)
+                k = at_wide % copies
+                part = total[c * window : (c + 1) * window]
+                grid[k, c // 2, pl.ds(first, HALO_Z), spot] += part[:HALO_Z]
+                grid[k, c // 2, pl.ds(first + HALO_Z, cells_z), spot] = part[HALO_Z:]
+
+    in_pairs(narrow_count, spread)
+
+
+def joined(grid, j, lanes, cells_x):
+    total = None
+    for k in range(grid.shape[0]):
+        moved = pltpu.roll(grid[k, j, :, lanes], (k * cells_x - HALO_X) % GRID_X, 1)
+        total = moved if total is None else total + moved
+    plane = total[HALO_Z:]
+    rest = plane[: GRID_Z - HALO_Z]
+    return jnp.concatenate([rest, plane[GRID_Z - HALO_Z :] + total[:HALO_Z]], axis=0)
+
+
+HALVES = (slice(0, GRID_X), slice(GRID_X, 2 * GRID_X))
+
+
+def atoms_kernel(table, phase, planes, weights, weights_z, waves, wave_slopes, grid):
+    cells_x = GRID_X // table.shape[0]
+    spread_sites(table, None, phase, grid, weights, weights_z, waves, wave_slopes)
+    for j in range(grid.shape[1]):
+        for lanes in HALVES:
+            planes[j, :, lanes] = joined(grid, j, lanes, cells_x)
+
+
 def mesh_kernel(
     table,
     shifts,
@@ -386,31 +517,28 @@
     fold_low,
     unfold_high,
     unfold_low,
+    planes,
+    atom_weights,
+    atom_weights_z,
+    atom_waves,
+    atom_wave_slopes,
     out_ref,
     grid,
-    planes,
     weights,
-    slopes,
     weights_z,
     waves,
     wave_slopes,
+    slopes,
 ):
     wide_count, narrow_count, _, atoms = table.shape
     cells_x = GRID_X // wide_count
     cells_z = GRID_Z // narrow_count
     window = cells_z + HALO_Z
-    reach = cells_x + HALO_X
-    pair = 2 * atoms
-    length = wide_count * pair
-    copies = grid.shape[0]
-    fine = grid.shape[1]
+    copies, fine = grid.shape[:2]
     channels = 2 * fine
-    rows = phase.shape[0]
-    half_x = GRID_X // 2
-    half_z = GRID_Z // 2
     piece = lax.axis_index("wide") * narrow_count + lax.axis_index("narrow")
-    lane_zero = lax.broadcasted_iota(jnp.int32, (1, half_x), 1) == 0
-    row_zero = lax.broadcasted_iota(jnp.int32, (half_z, 1), 0) == 0
+    lane_zero = lax.broadcasted_iota(jnp.int32, (1, GRID_X // 2), 1) == 0
+    row_zero = lax.broadcasted_iota(jnp.int32, (GRID_Z // 2, 1), 0) == 0
 
     def fold():
         return (fold_high[...], fold_low[...])
@@ -418,108 +546,11 @@
     def unfold():
         return (unfold_high[...], unfold_low[...])
 
-    def sites(at_wide, at_narrow):
-        atom = table[at_wide, at_narrow]
-        moved = shifts[at_wide, at_narrow]
-        found = []
-        for component, extent in enumerate((cells_x, GRID_Y, cells_z)):
-            start = atom[component : component + 1] * float(extent)
-            found.append(jnp.concatenate([start, start + moved[component : component + 1]], axis=1))
-        oxygen = 1.0 - atom[3:4]
-        found.append(jnp.concatenate([6.0 * oxygen + atom[3:4], -8.0 * oxygen], axis=1))
-        return found
-
-    def line(at_narrow):
-        groups = [sites(at_wide, at_narrow) for at_wide in range(wide_count)]
-        return [jnp.concatenate([g[k] for g in groups], axis=1) for k in range(4)]
-
-    def splines_z(row):
-        counter = lax.broadcasted_iota(jnp.int32, (window, 1), 0).astype(jnp.float32)
-        return spline_pair(row - (counter - float(HALO_Z)))
-
-    def fill_x(row, targets):
-        counter = lax.broadcasted_iota(jnp.int32, (reach, 1), 0).astype(jnp.float32)
-        both = spline_pair(row - (counter - float(HALO_X)))
-        rest = jnp.zeros((128 - reach, length), jnp.bfloat16)
-        for values, ref in zip(both, targets):
-            if ref is not None:
-                high, low = split(values)
-                ref[0:reach, :] = high
-                ref[reach:128, :] = rest
-                ref[128 : 128 + reach, :] = low
-                ref[128 + reach : 256, :] = rest
-
-    grid[:, :, 0:HALO_Z, :] = jnp.zeros((copies, fine, HALO_Z, 2 * GRID_X), jnp.float32)
-
-    def spread(at_narrow):
-        row_x, row_y, row_z, charge = line(at_narrow)
-        lower = jnp.floor(row_y)
-        back = lax.broadcasted_iota(jnp.int32, (8, 1), 0)
-        value_y, slope_y = spline_pair((row_y - lower) + back.astype(jnp.float32))
-        cell = lax.rem(lower.astype(jnp.int32) - back + GRID_Y, GRID_Y)
-        wave_blocks = []
-        slope_blocks = []
-        for block in range(length // 128):
-            lanes = slice(block * 128, (block + 1) * 128)
-            wave = jnp.zeros((rows, 128), jnp.float32)
-            wave_slope = jnp.zeros((rows, 128), jnp.float32)
-            for k in range(4):
-                spot = jnp.broadcast_to(cell[k : k + 1, lanes], (rows, 128))
-                found = lookup(phase[...], spot)
-                wave = wave + value_y[k : k + 1, lanes] * found
-                wave_slope = wave_slope + slope_y[k : k + 1, lanes] * found
-            wave_blocks.append(wave)
-            slope_blocks.append(wave_slope)
-        wave = jnp.concatenate(wave_blocks, axis=1)
-        waves[at_narrow] = wave
-        wave_slopes[at_narrow] = jnp.concatenate(slope_blocks, axis=1)
-        fill_x(row_x, (weights.at[at_narrow], None))
-        value_z, _ = splines_z(row_z)
-        weights_z[at_narrow] = value_z
-        charged = wave * charge
-        first = pl.multiple_of(at_narrow * cells_z, HALO_Z)
-        for at_wide in range(wide_count):
-            lanes = slice(at_wide * pair, (at_wide + 1) * pair)
-            near = value_z[:, lanes]
-            left = jnp.concatenate(
-                [near * charged[c : c + 1, lanes] for c in range(channels)], axis=0
-            )
-            high, low = split(left)
-            across = weights[at_narrow, :, lanes]
-            total = lax.dot_general(high, across, NT, preferred_element_type=jnp.float32)
-            total = total[:, 0:128] + (
-                total[:, 128:256]
-                + lax.dot_general(low, across[0:128], NT, preferred_element_type=jnp.float32)
-            )
-            start = at_wide // copies * 128
-            for c in range(channels):
-                spot = slice(c % 2 * GRID_X + start, c % 2 * GRID_X + start + 128)
-                k = at_wide % copies
-                part = total[c * window : (c + 1) * window]
-                grid[k, c // 2, pl.ds(first, HALO_Z), spot] += part[:HALO_Z]
-                grid[k, c // 2, pl.ds(first + HALO_Z, cells_z), spot] = part[HALO_Z:]
-
-    def in_pairs(step):
-        def both(index, carry):
-            step(2 * index, 0)
-            step(2 * index + 1, 1)
-            return carry
-
-        lax.fori_loop(0, narrow_count // 2, both, 0)
-
-    in_pairs(lambda at_narrow, _: spread(at_narrow))
-
-    def gather(j, carry):
-        for lanes in (slice(0, GRID_X), slice(GRID_X, 2 * GRID_X)):
-            total = None
-            for k in range(copies):
-                moved = pltpu.roll(grid[k, j, :, lanes], (k * cells_x - HALO_X) % GRID_X, 1)
-                total = moved if total is None else total + moved
-            planes[j, :, lanes] = total[HALO_Z:]
-            planes[j, GRID_Z - HALO_Z :, lanes] += total[:HALO_Z]
-        return carry
-
-    lax.fori_loop(0, fine, gather, 0)
+    spread_sites(table, shifts, phase, grid, weights, weights_z, waves, wave_slopes)
+
+    def whole(j):
+        return [planes[j, :, lanes] + joined(grid, j, lanes, cells_x) for lanes in HALVES]
+
     is_first = piece == 0
 
     def paired(real, imag, zero, axis):
@@ -573,13 +604,14 @@
         part = jnp.sum(green * (real * real + imag * imag), axis=0, keepdims=True)
         return green * real, green * imag, share * part
 
-    second_plane = jnp.where(is_first, planes[0, :, GRID_X:], 0.0)
-    last_real, last_imag, energy = to_modes(second_plane, None, fine)
+    first_real, first_imag = whole(0)
+    last_real, last_imag, energy = to_modes(jnp.where(is_first, first_imag, 0.0), None, fine)
     for j in range(fine):
-        imag = planes[j, :, GRID_X:]
         if j == 0:
-            imag = jnp.where(is_first, 0.0, imag)
-        real, imag, part = to_modes(planes[j, :, 0:GRID_X], imag, j)
+            real, imag = first_real, jnp.where(is_first, 0.0, first_imag)
+        else:
+            real, imag = whole(j)
+        real, imag, part = to_modes(real, imag, j)
         energy = energy + part
         if j == 0:
             real, imag = real - last_imag, imag + last_real
@@ -588,7 +620,7 @@
         imag = multiply(fold(), split(imag))
         real, imag = merged(real, imag, lane_zero, 1)
         scale = jnp.where(piece * fine + j == 0, 1.0, 2.0)
-        for part, lanes in ((real, slice(0, GRID_X)), (imag, slice(GRID_X, 2 * GRID_X))):
+        for part, lanes in zip((real, imag), HALVES):
             part = multiply(split(part * scale), unfold())
             for k in range(copies):
                 moved = pltpu.roll(part, (HALO_X - k * cells_x) % GRID_X, 1)
@@ -597,25 +629,28 @@
     energy = jnp.broadcast_to(jnp.sum(energy, axis=1, keepdims=True), (1, 128))
 
     def collect(at_narrow, buffer):
-        row_x, _, row_z, _ = line(at_narrow)
-        fill_x(row_x, (None, slopes.at[buffer]))
-        value_z = weights_z[at_narrow]
-        _, slope_z = splines_z(row_z)
+        kinds = (
+            (None, atom_weights, atom_weights_z, atom_waves, atom_wave_slopes),
+            (shifts, weights, weights_z, waves, wave_slopes),
+        )
+        slopes_z = []
+        for kind, given in enumerate(kinds):
+            row_x, _, row_z, _ = site_rows(table, given[0], at_narrow)
+            splines_x(row_x, cells_x + HALO_X, None, slopes.at[buffer, kind])
+            slopes_z.append(splines_z(row_z, window)[1])
         first = pl.multiple_of(at_narrow * cells_z, HALO_Z)
         lefts = []
         for k in range(copies):
             left = jnp.concatenate(
                 [
-                    grid[k, c // 2, pl.ds(first, window), c % 2 * GRID_X : (c % 2 + 1) * GRID_X]
+                    grid[k, c // 2, pl.ds(first, window), HALVES[c % 2]]
                     for c in range(channels)
                 ],
                 axis=0,
             )
             lefts.append(split(left))
-        wave = waves[at_narrow]
-        wave_slope = wave_slopes[at_narrow]
         for at_wide in range(wide_count):
-            lanes = slice(at_wide * pair, (at_wide + 1) * pair)
+            lanes = slice(at_wide * atoms, (at_wide + 1) * atoms)
             start = at_wide // copies * 128
             high = lefts[at_wide % copies][0][:, start : start + 128]
             low = lefts[at_wide % copies][1][:, start : start + 128]
@@ -626,18 +661,25 @@
                     twice, right, NN, preferred_element_type=jnp.float32
                 ) + lax.dot_general(low, right[0:128], NN, preferred_element_type=jnp.float32)
 
-            value = across(weights[at_narrow, :, lanes])
-            slope = across(slopes[buffer, :, lanes])
-            plain = jnp.zeros((window, pair), jnp.float32)
+            def both(index):
+                return jnp.concatenate([given[index][at_narrow, :, lanes] for given in kinds], axis=1)
+
+            value = across(both(1))
+            slope = across(
+                jnp.concatenate([slopes[buffer, kind, :, lanes] for kind in range(2)], axis=1)
+            )
+            near = both(2)
+            near_slope = jnp.concatenate([row[:, lanes] for row in slopes_z], axis=1)
+            wave = both(3)
+            wave_slope = both(4)
+            plain = jnp.zeros((window, 2 * atoms), jnp.float32)
             along_x = plain
             along_y = plain
             for c in range(channels):
                 block = slice(c * window, (c + 1) * window)
-                plain = plain + value[block] * wave[c : c + 1, lanes]
-                along_x = along_x + slope[block] * wave[c : c + 1, lanes]
-                along_y = along_y + value[block] * wave_slope[c : c + 1, lanes]
-            near = value_z[:, lanes]
-            near_slope = slope_z[:, lanes]
+                plain = plain + value[block] * wave[c : c + 1]
+                along_x = along_x + slope[block] * wave[c : c + 1]
+                along_y = along_y + value[block] * wave_slope[c : c + 1]
             results = [
                 jnp.sum(near * plain, axis=0, keepdims=True),
                 -jnp.sum(near * along_x, axis=0, keepdims=True),
@@ -645,10 +687,10 @@
                 -jnp.sum(near_slope * plain, axis=0, keepdims=True),
             ]
             for k, row in enumerate(results):
-                out_ref[at_wide, at_narrow, :, k * pair : (k + 1) * pair] = row
-            out_ref[at_wide, at_narrow, :, 4 * pair :] = energy
-
-    in_pairs(collect)
+                out_ref[at_wide, at_narrow, :, 2 * k * atoms : 2 * (k + 1) * atoms] = row
+            out_ref[at_wide, at_narrow, :, 8 * atoms :] = energy
+
+    in_pairs(narrow_count, collect)
 
 
 def finish_kernel(arrived, species, atom_ref, centroid_ref, energy_ref):
@@ -820,32 +862,43 @@
     shifts = lax.all_to_all(shifts, axes, 0, 0, tiled=True)
     shifts = shifts.reshape(wide_count, narrow_count, 4, atoms)
 
-    cells_x = GRID_X // wide_count
-    copies = 128 // cells_x
-    length = wide_count * 2 * atoms
+    copies = 128 // (GRID_X // wide_count)
+    window = GRID_Z // narrow_count + HALO_Z
+    length = wide_count * atoms
+    grid = pltpu.VMEM((copies, fine, HALO_Z + GRID_Z, 2 * GRID_X), jnp.float32)
+    kept = (
+        shaped((narrow_count, 256, length), bf16),
+        shaped((narrow_count, window, length)),
+        shaped((narrow_count, wave_rows, length)),
+        shaped((narrow_count, wave_rows, length)),
+    )
+    spread_atoms = pl.pallas_call(
+        atoms_kernel,
+        out_shape=(shaped((fine, GRID_Z, 2 * GRID_X)),) + kept,
+        in_specs=vmem(2),
+        out_specs=tuple(vmem(5)),
+        scratch_shapes=[grid],
+        compiler_params=limits(24),
+        cost_estimate=pl.CostEstimate(
+            flops=2 * 3 * pieces * atoms * 2 * fine * window * 128,
+            bytes_accessed=8 * 1024 * 1024,
+            transcendentals=0,
+        ),
+        name="atoms",
+    )(table, phase)
     out_width = 8 * atoms + 128
+    tables = halves(fold_table(GRID_X)) + halves(fold_table(GRID_X).T)
     partial = pl.pallas_call(
         mesh_kernel,
         out_shape=shaped((wide_count, narrow_count, 1, out_width)),
-        in_specs=vmem(8),
+        in_specs=vmem(13),
         out_specs=vmem(1)[0],
-        scratch_shapes=[
-            pltpu.VMEM((copies, fine, HALO_Z + GRID_Z, 2 * GRID_X), jnp.float32),
-            pltpu.VMEM((fine + 1, GRID_Z, 2 * GRID_X), jnp.float32),
-        ]
-        + [pltpu.VMEM((narrow_count, 256, length), bf16), pltpu.VMEM((2, 256, length), bf16)]
-        + [pltpu.VMEM((narrow_count, GRID_Z // narrow_count + HALO_Z, length), jnp.float32)]
-        + [pltpu.VMEM((narrow_count, wave_rows, length), jnp.float32)] * 2,
-        compiler_params=limits(48),
+        scratch_shapes=[grid]
+        + [pltpu.VMEM(array.shape, array.dtype) for array in kept]
+        + [pltpu.VMEM((2, 2, 256, length), bf16)],
+        compiler_params=limits(36),
         name="mesh",
-    )(
-        table,
-        shifts,
-        phase,
-        green,
-        *[jnp.asarray(half) for half in halves(fold_table(GRID_X))],
-        *[jnp.asarray(half) for half in halves(fold_table(GRID_X).T)],
-    )
+    )(table, shifts, phase, green, *[jnp.asarray(half) for half in tables], *spread_atoms)
     arrived = lax.all_to_all(partial.reshape(pieces, 1, out_width), axes, 0, 0, tiled=True)
     atom_field, centroid_field, energy = pl.pallas_call(
         finish_kernel,

time: 71.6 us -> 81.2 us (1.13)
  local copies, waits for them, and re-layouts: 1.5 us -> 13.1 us
  blocking collectives: 20.1 us -> 13.4 us
  starting transfers between devices: 7.3 us -> 10.2 us
  Pallas kernels: 38.3 us -> 40 us
    unnamed x16 -> x34, local copies, waits for them, and re-layouts: 1.5 us -> 13.1 us
    all_to_all x1 -> x0, blocking collectives: 9.89 us -> none  [local(): shifts = lax.all_to_all(shifts, axes, 0, 0, tiled=True)]
    pallas_call x0 -> x1, Pallas kernels: none -> 5.02 us  [local(): pl.pallas_call(atoms_kernel, out_shape=(shaped((fine, GRID_Z, 2 * GRID_X)...]
    all_to_all x1, blocking collectives: 10.2 us -> 13.4 us  [local(): lax.all_to_all(partial.reshape(pieces, 1, out_width), axes, 0, 0, tiled=T...]
    all_to_all x0 -> x1, starting transfers between devices: none -> 2.88 us  [local(): shifts = lax.all_to_all(shifts, axes, 0, 0, tiled=True)]
    pallas_call x1, Pallas kernels: 20.6 us -> 18.3 us  [local(): pl.pallas_call(mesh_kernel, out_shape=shaped((wide_count, narrow_count, 1...]
    pallas_call x1, Pallas kernels: 10.9 us -> 9.86 us  [local(): pl.pallas_call(centroid_kernel, out_shape=(shaped((3, 1, atoms)), shaped(...]
  transfers between devices with their start and end apart: 1 -> 2, of which waited for: 1 -> 1; matrix products, arithmetic and copies ran while one was open for 0% -> 0% of each run, Pallas kernels for 6% -> 11%
where the time goes in v5:
time: 81.2 us; the launch traced here: 80.7 us
  Pallas kernels  40 us (49%)
  blocking collectives  13.4 us (17%)
  local copies, waits for them, and re-layouts  13.1 us (16%)
  starting transfers between devices  10.2 us (13%)
  waiting for transfers between devices  3.33 us (4%)
    pallas_call x1, Pallas kernels, local(): pl.pallas_call(mesh_kernel, out_shape=shaped((wide_count, narrow_count, 1...  18.3 us
    all_to_all x1, blocking collectives, local(): lax.all_to_all(partial.reshape(pieces, 1, out_width), axes, 0, 0, tiled=T...  13.4 us
    unnamed x34, local copies, waits for them, and re-layouts  13.1 us
    pallas_call x1, Pallas kernels, local(): pl.pallas_call(centroid_kernel, out_shape=(shaped((3, 1, atoms)), shaped(...  9.86 us
    all_to_all x1, starting transfers between devices, local(): table = lax.all_to_all(packed, axes, 0, 0, tiled=True)  7.3 us
    pallas_call x1, Pallas kernels, local(): pl.pallas_call(atoms_kernel, out_shape=(shaped((fine, GRID_Z, 2 * GRID_X)...  5.02 us
    pallas_call x1, Pallas kernels, local(): pl.pallas_call(prepare_kernel, out_shape=(shaped((listed, atoms), jnp.int...  3.93 us
    all_to_all x1, waiting for transfers between devices, local(): table = lax.all_to_all(packed, axes, 0, 0, tiled=True)  3.33 us
  transfers between devices with their start and end apart: 2, of which 1 were waited for; matrix products, arithmetic and copies ran while one was open for 0% of the time, Pallas kernels for 11%

profile of v5, /device:TPU:0, one launch (start us, length us, event | category | flops | bytes accessed | tf_op | source)
XLA Modules:
  0.0 80.7 jit_solution(13759781328302995506)
XLA Ops:
  0.6 1.3 %pack.1 = f32[32,4,128]{2,1,0:T(4,128)} custom-call(f32[3,1,128]{2,1,0:T(1,128)} %bitcast.34, s32[1,128]{1,0:T(1,128)} %bitcast.32), custom_call_target="tpu_custom_call" | custom-call | tf_op jit(solution)/shard_map/pack/pallas_call | solution.py:780
  1.9 7.3 %all-to-all-start = ((f32[32,4,128]{2,1,0:T(4,128)}), f32[32,4,128]{2,1,0:T(4,128)S(1)}, u32[]{:S(2)}, u32[]{:S(2)}) async-start(f32[32,4,128]{2,1,0:T(4,128)} %pack.1), calls=%async_computation | async-start | bytes 131072 | tf_op jit(solution)/shard_map/all_to_all | solution.py:787
  9.2 3.9 %prepare.1 = (s32[128,128]{1,0:T(8,128)}, f32[256,16]{1,0:T(8,128)}, bf16[64,96]{1,0:T(8,128)(2,1)}, bf16[128,192]{1,0:T(8,128)(2,1)}, bf16[240,1600]{1,0:T(8,12...) custom-call(s32[128,128]{1,0:T(8,128)} %bitcast.31, ...), custom_call_target="tpu_custom_call" | custom-call | flops 1000000 | bytes 3072000 | tf_op jit(solution)/shard_map/prepare/pallas_call | solution.py:820
  13.2 0.0 copy-start.16
  13.2 3.3 %all-to-all-done = f32[32,4,128]{2,1,0:T(4,128)S(1)} async-done(((f32[32,4,128]{2,1,0:T(4,128)}), f32[32,4,128]{2,1,0:T(4,128)S(1)}, u32[]{:S(2)}, u32[]{:S(2)}) %all-to-all-start) | async-done | bytes 65568 | tf_op jit(solution)/shard_map/all_to_all | solution.py:787
  16.5 0.6 copy-done.5
  17.2 9.9 %centroids.1 = (f32[3,1,128]{2,1,0:T(1,128)}, f32[32,4,128]{2,1,0:T(4,128)}) custom-call(f32[4,8,4,128]{3,2,1,0:T(4,128)} %bitcast.24, s32[128,128]{1,0:T(8,128)} %get-tuple-element.26.codes, f32[256,16]{1,0:T(8,128)} %get-tuple-element.27.columns, bf16[64,96]{1,0:T(8,128)(2,1)} %get-tuple-element.28.second, bf16[128,192]{1,0:T(8,128)(2,1)} %get-tuple-element.29.third, ...), custom_call_target="tpu_custom_call" | custom-call | tf_op jit(solution)/shard_map/centroids/pallas_call | solution.py:848
  27.0 0.0 copy-start.2
  27.0 2.9 %all-to-all-start.1 = ((f32[32,4,128]{2,1,0:T(4,128)}), f32[32,4,128]{2,1,0:T(4,128)S(1)}, u32[]{:S(2)}, u32[]{:S(2)}) async-start(f32[32,4,128]{2,1,0:T(4,128)} %get-tuple-element.37), calls=%async_computation.1 | async-start | bytes 131072 | tf_op jit(solution)/shard_map/all_to_all | solution.py:862
  29.9 0.0 copy-done.16
  29.9 0.0 copy-start.6
  29.9 0.8 %copy-done.6 = f32[32,4,128]{2,1,0:T(4,128)S(1)} copy-done((f32[32,4,128]{2,1,0:T(4,128)S(1)}, f32[32,4,128]{2,1,0:T(4,128)}, u32[]{:S(2)}) %copy-start.6) | copy-done | bytes 65560
  30.8 5.0 %atoms.1 = (f32[4,256,512]{2,1,0:T(8,128)S(1)}, bf16[8,256,512]{2,1,0:T(8,128)(2,1)S(1)}, f32[8,40,512]{2,1,0:T(8,128)S(1)}, f32[8,8,512]{2,1,0:T(8,128)S(1)}, f32[8,8,512]{2,1,0:T(8,128)S(1)}) custom-call(f32[4,8,4,128]{3,2,1,0:T(4,128)S(1)} %bitcast.25, f32[8,256]{1,0:T(8,128)S(1)} %copy-done.16), custom_call_target="tpu_custom_call" | custom-call | flops 1006632960 | bytes 8388608 | tf_op jit(solution)/shard_map/atoms/pallas_call | solution.py:875
  35.8 0.0 copy-start
  35.8 1.3 %copy-done = bf16[8,256,512]{2,1,0:T(8,128)(2,1)} copy-done((bf16[8,256,512]{2,1,0:T(8,128)(2,1)}, bf16[8,256,512]{2,1,0:T(8,128)(2,1)S(1)}, u32[]{:S(2)}) %copy-start) | copy-done | bytes 2097176
  37.2 0.8 %copy-done.3 = f32[8,40,512]{2,1,0:T(8,128)} copy-done((f32[8,40,512]{2,1,0:T(8,128)}, f32[8,40,512]{2,1,0:T(8,128)S(1)}, u32[]{:S(2)}) %copy-start.3) | copy-done | bytes 655384
  38.0 0.7 copy-done.12
  38.7 0.7 copy-done.14
  39.3 0.0 all-to-all-done.1
  39.3 0.0 copy-done.2
  39.3 0.0 copy-done.7
  39.3 1.6 %copy-done.1 = bf16[8,256,512]{2,1,0:T(8,128)(2,1)S(1)} copy-done((bf16[8,256,512]{2,1,0:T(8,128)(2,1)S(1)}, bf16[8,256,512]{2,1,0:T(8,128)(2,1)}, u32[]{:S(2)}) %copy-start.1) | copy-done | bytes 2097176
  40.9 1.1 %copy-done.4 = f32[8,40,512]{2,1,0:T(8,128)S(1)} copy-done((f32[8,40,512]{2,1,0:T(8,128)S(1)}, f32[8,40,512]{2,1,0:T(8,128)}, u32[]{:S(2)}) %copy-start.4) | copy-done | bytes 655384
  42.0 0.9 %copy-done.8 = bf16[256,256]{1,0:T(8,128)(2,1)S(1)} copy-done((bf16[256,256]{1,0:T(8,128)(2,1)S(1)}, bf16[256,256]{1,0:T(8,128)(2,1)}, u32[]{:S(2)}) %copy-start.8) | copy-done | bytes 131096
  42.9 0.9 %copy-done.9 = bf16[256,256]{1,0:T(8,128)(2,1)S(1)} copy-done((bf16[256,256]{1,0:T(8,128)(2,1)S(1)}, bf16[256,256]{1,0:T(8,128)(2,1)}, u32[]{:S(2)}) %copy-start.9) | copy-done | bytes 131096
  43.8 0.9 %copy-done.10 = bf16[256,256]{1,0:T(8,128)(2,1)S(1)} copy-done((bf16[256,256]{1,0:T(8,128)(2,1)S(1)}, bf16[256,256]{1,0:T(8,128)(2,1)}, u32[]{:S(2)}) %copy-start.10) | copy-done | bytes 131096
  44.7 0.9 %copy-done.11 = bf16[256,256]{1,0:T(8,128)(2,1)S(1)} copy-done((bf16[256,256]{1,0:T(8,128)(2,1)S(1)}, bf16[256,256]{1,0:T(8,128)(2,1)}, u32[]{:S(2)}) %copy-start.11) | copy-done | bytes 131096
  45.6 0.9 %copy-done.13 = f32[8,8,512]{2,1,0:T(8,128)S(1)} copy-done((f32[8,8,512]{2,1,0:T(8,128)S(1)}, f32[8,8,512]{2,1,0:T(8,128)}, u32[]{:S(2)}) %copy-start.13) | copy-done | bytes 131096
  46.5 0.9 %copy-done.15 = f32[8,8,512]{2,1,0:T(8,128)S(1)} copy-done((f32[8,8,512]{2,1,0:T(8,128)S(1)}, f32[8,8,512]{2,1,0:T(8,128)}, u32[]{:S(2)}) %copy-start.15) | copy-done | bytes 131096
  47.4 18.3 %mesh.1 = f32[4,8,1,1152]{3,2,1,0:T(1,128)S(1)} custom-call(f32[4,8,4,128]{3,2,1,0:T(4,128)S(1)} %bitcast.26, f32[4,8,4,128]{3,2,1,0:T(4,128)S(1)} %bitcast.28, f32[8,256]{1,0:T(8,128)S(1)} %copy-done.16, f32[5,256,256]{2,1,0:T(8,128)S(1)} %copy-done.2, bf16[256,256]{1,0:T(8,128)(2,1)S(1)} %copy-done.11, bf16[256,256]{1,0:T(8,128)(2,1)S(1)} %copy-done.10, ...), custom_call_target="tpu_custom_call" | custom-call | tf_op jit(solution)/shard_map/mesh/pallas_call | solution.py:891
  65.8 13.4 %all_to_all.15.arrived = f32[32,1,1152]{2,1,0:T(1,128)} all-to-all(f32[32,1,1152]{2,1,0:T(1,128)S(1)} %bitcast.27), channel_id=1, replica_groups=mesh['wide'=4,'narrow'=8] {'wide','narrow'}, dimensions={0} | all-to-all | bytes 294912 | tf_op jit(solution)/shard_map/all_to_all | solution.py:902
  79.2 1.5 %finish.1 = (f32[4,1,128]{2,1,0:T(1,128)}, f32[4,1,128]{2,1,0:T(1,128)}, f32[1,128]{1,0:T(1,128)}) custom-call(f32[32,1,1152]{2,1,0:T(1,128)} %all_to_all.15.arrived, s32[1,128]{1,0:T(1,128)} %bitcast.33), custom_call_target="tpu_custom_call" | custom-call | tf_op jit(solution)/shard_map/finish/pallas_call | solution.py:903
  (13 shorter events, 0.0 us)
Async XLA Ops:
  1.9 14.6 %all-to-all-start = ((f32[32,4,128]{2,1,0:T(4,128)}), f32[32,4,128]{2,1,0:T(4,128)S(1)}, u32[]{:S(2)}, u32[]{:S(2)}) async-start(f32[32,4,128]{2,1,0:T(4,128)} %pack.1), calls=%async_computation | async-start | bytes 131072 | tf_op jit(solution)/shard_map/all_to_all | solution.py:787
  13.2 16.7 %copy-start.16 = (f32[8,256]{1,0:T(8,128)S(1)}, f32[8,256]{1,0:T(8,128)}, u32[]{:S(2)}) copy-start(f32[8,256]{1,0:T(8,128)} %get-tuple-element.38.phase) | copy-start | bytes 24580
  16.5 0.6 copy-start.5
  27.0 12.3 %copy-start.2 = (f32[5,256,256]{2,1,0:T(8,128)S(1)}, f32[5,256,256]{2,1,0:T(8,128)}, u32[]{:S(2)}) copy-start(f32[5,256,256]{2,1,0:T(8,128)} %get-tuple-element.39.green_ref) | copy-start | bytes 3932164
  27.0 12.3 %all-to-all-start.1 = ((f32[32,4,128]{2,1,0:T(4,128)}), f32[32,4,128]{2,1,0:T(4,128)S(1)}, u32[]{:S(2)}, u32[]{:S(2)}) async-start(f32[32,4,128]{2,1,0:T(4,128)} %get-tuple-element.37), calls=%async_computation.1 | async-start | bytes 131072 | tf_op jit(solution)/shard_map/all_to_all | solution.py:862
  29.9 0.8 %copy-start.6 = (f32[32,4,128]{2,1,0:T(4,128)S(1)}, f32[32,4,128]{2,1,0:T(4,128)}, u32[]{:S(2)}) copy-start(f32[32,4,128]{2,1,0:T(4,128)} %copy-done.5) | copy-start | bytes 196612
  30.8 8.5 %copy-start.7 = (f32[32,4,128]{2,1,0:T(4,128)S(1)}, f32[32,4,128]{2,1,0:T(4,128)}, u32[]{:S(2)}) copy-start(f32[32,4,128]{2,1,0:T(4,128)} %copy-done.5) | copy-start | bytes 196612
  35.8 1.3 %copy-start = (bf16[8,256,512]{2,1,0:T(8,128)(2,1)}, bf16[8,256,512]{2,1,0:T(8,128)(2,1)S(1)}, u32[]{:S(2)}) copy-start(bf16[8,256,512]{2,1,0:T(8,128)(2,1)S(1)} %get-tuple-element.41.atom_weights) | copy-start | bytes 6291460
  37.1 0.8 %copy-start.3 = (f32[8,40,512]{2,1,0:T(8,128)}, f32[8,40,512]{2,1,0:T(8,128)S(1)}, u32[]{:S(2)}) copy-start(f32[8,40,512]{2,1,0:T(8,128)S(1)} %get-tuple-element.42.atom_weights_z) | copy-start | bytes 1966084
  38.0 0.7 copy-start.12
  38.7 0.7 copy-start.14
  39.3 1.6 %copy-start.1 = (bf16[8,256,512]{2,1,0:T(8,128)(2,1)S(1)}, bf16[8,256,512]{2,1,0:T(8,128)(2,1)}, u32[]{:S(2)}) copy-start(bf16[8,256,512]{2,1,0:T(8,128)(2,1)} %copy-done) | copy-start | bytes 6291460
  40.9 1.1 %copy-start.4 = (f32[8,40,512]{2,1,0:T(8,128)S(1)}, f32[8,40,512]{2,1,0:T(8,128)}, u32[]{:S(2)}) copy-start(f32[8,40,512]{2,1,0:T(8,128)} %copy-done.3) | copy-start | bytes 1966084
  42.0 0.9 %copy-start.8 = (bf16[256,256]{1,0:T(8,128)(2,1)S(1)}, bf16[256,256]{1,0:T(8,128)(2,1)}, u32[]{:S(2)}) copy-start(bf16[256,256]{1,0:T(8,128)(2,1)} %constant.14.clone.unfold_low) | copy-start | bytes 393220
  42.9 0.9 %copy-start.9 = (bf16[256,256]{1,0:T(8,128)(2,1)S(1)}, bf16[256,256]{1,0:T(8,128)(2,1)}, u32[]{:S(2)}) copy-start(bf16[256,256]{1,0:T(8,128)(2,1)} %constant.13.clone.unfold_high) | copy-start | bytes 393220
  43.8 0.9 %copy-start.10 = (bf16[256,256]{1,0:T(8,128)(2,1)S(1)}, bf16[256,256]{1,0:T(8,128)(2,1)}, u32[]{:S(2)}) copy-start(bf16[256,256]{1,0:T(8,128)(2,1)} %constant.12.clone.fold_low) | copy-start | bytes 393220
  44.7 0.9 %copy-start.11 = (bf16[256,256]{1,0:T(8,128)(2,1)S(1)}, bf16[256,256]{1,0:T(8,128)(2,1)}, u32[]{:S(2)}) copy-start(bf16[256,256]{1,0:T(8,128)(2,1)} %constant.11.clone.fold_high) | copy-start | bytes 393220
  45.6 0.9 %copy-start.13 = (f32[8,8,512]{2,1,0:T(8,128)S(1)}, f32[8,8,512]{2,1,0:T(8,128)}, u32[]{:S(2)}) copy-start(f32[8,8,512]{2,1,0:T(8,128)} %copy-done.12) | copy-start | bytes 393220
  46.5 0.9 %copy-start.15 = (f32[8,8,512]{2,1,0:T(8,128)S(1)}, f32[8,8,512]{2,1,0:T(8,128)}, u32[]{:S(2)}) copy-start(f32[8,8,512]{2,1,0:T(8,128)} %copy-done.14) | copy-start | bytes 393220

commit v6 on v4

--- a/solution.py
+++ b/solution.py
@@ -38,6 +38,20 @@
         return lax.dot_general(a, b, dims, preferred_element_type=jnp.float32)
 
     return one(left[0], right[0]) + (one(left[1], right[0]) + one(left[0], right[1]))
+
+
+def product(left, right, dims=NN):
+    return lax.dot_general(left, right, dims, preferred_element_type=jnp.float32)
+
+
+def as_left(value):
+    high, low = split(value)
+    return jnp.concatenate([high, low, high], axis=1)
+
+
+def as_right(value):
+    high, low = split(value)
+    return jnp.concatenate([high, high, low], axis=0)
 
 
 def spline_pair(offset):
@@ -155,12 +169,8 @@
     for kind in range(2):
         rows[kind : kind + 1, 0:width_one] = embed_one_w[kind : kind + 1, :]
         rows[2 + kind : 3 + kind, 0:width_one] = embed_one_b[kind : kind + 1, :]
-    for row, source, groups in ((4, embed_two_b, 2), (5, embed_three_b, 4)):
-        for k in range(groups):
-            rows[row : row + 1, k * ROW_PAD : k * ROW_PAD + width_one] = source[
-                :, k * width_one : (k + 1) * width_one
-            ]
-    for row, source in ((6, fit_one_b), (7, fit_two_b), (8, fit_three_b)):
+        rows[2 + kind : 3 + kind, width_one : width_one + 1] = jnp.full((1, 1), 40.0, jnp.float32)
+    for row, source in ((4, fit_one_b), (5, fit_two_b), (6, fit_three_b)):
         rows[row : row + 1, 0:hidden] = source[...]
     columns_ref[...] = jnp.transpose(rows[...])
 
@@ -169,6 +179,9 @@
         square[0:width_one, k * ROW_PAD : k * ROW_PAD + width_one] = embed_two_w[
             :, k * width_one : (k + 1) * width_one
         ]
+        square[
+            width_one : width_one + 1, k * ROW_PAD : k * ROW_PAD + width_one
+        ] = embed_two_b[:, k * width_one : (k + 1) * width_one]
     high, low = split(jnp.transpose(square[0:128, 0:128])[0 : 2 * ROW_PAD, 0:ROW_PAD])
     second_ref[...] = jnp.concatenate([high, high, low], axis=1)
     square[0:128, 0:128] = jnp.zeros((128, 128), jnp.float32)
@@ -179,6 +192,10 @@
             ] = embed_three_w[
                 g * width_one : (g + 1) * width_one, k * width_one : (k + 1) * width_one
             ]
+    for k in range(4):
+        square[
+            width_one : width_one + 1, k * ROW_PAD : k * ROW_PAD + width_one
+        ] = embed_three_b[:, k * width_one : (k + 1) * width_one]
     high, low = split(jnp.transpose(square[0:128, 0:128])[:, 0 : 2 * ROW_PAD])
     third_ref[...] = jnp.concatenate([high, high, low], axis=1)
     for copy in copies[11:13]:
@@ -238,14 +255,18 @@
     arrivals,
     *held,
 ):
-    sources = (one_high, one_low, two_high, two_low, three_high, three_low, fit_out_w)
+    sources = (table, codes, columns, second, third)
+    sources += (one_high, one_low, two_high, two_low, three_high, three_low, fit_out_w)
     copies = [
         pltpu.make_async_copy(source, target, arrivals.at[k])
         for k, (source, target) in enumerate(zip(sources, held))
     ]
     for copy in copies:
         copy.start()
-    one_high, one_low, two_high, two_low, three_high, three_low, fit_out_w = held
+    table, codes, columns, second, third = held[:5]
+    one_high, one_low, two_high, two_low, three_high, three_low, fit_out_w = held[5:]
+    for copy in copies[:5]:
+        copy.wait()
     wide_count, narrow_count, _, atoms = table.shape
     listed = codes.shape[0]
     width_three = fit_out_w.shape[0]
@@ -267,12 +288,9 @@
     weight_hydrogen = jnp.broadcast_to(columns[0:ROW_PAD, 1:2], (ROW_PAD, atoms))
     bias_oxygen = jnp.broadcast_to(columns[0:ROW_PAD, 2:3], (ROW_PAD, atoms))
     bias_hydrogen = jnp.broadcast_to(columns[0:ROW_PAD, 3:4], (ROW_PAD, atoms))
-    second_bias = columns[0 : 2 * ROW_PAD, 4:5]
-    third_bias = columns[0 : 4 * ROW_PAD, 5:6]
     matrix[...] = jnp.zeros_like(matrix)
 
-    def chunk(index, carry):
-        first = pl.multiple_of(index * SLOT_CHUNK, SLOT_CHUNK)
+    def chunk(first):
         code = codes[pl.ds(first, SLOT_CHUNK), :]
         offset = code // atoms
         slot = code - offset * atoms
@@ -318,7 +336,7 @@
             NN,
             preferred_element_type=jnp.float32,
         )
-        layer_two = jnp.tanh(layer_two + second_bias) + jnp.concatenate(
+        layer_two = jnp.tanh(layer_two) + jnp.concatenate(
             [layer_one, layer_one], axis=0
         )
         high, low = split(layer_two)
@@ -328,7 +346,7 @@
             NN,
             preferred_element_type=jnp.float32,
         )
-        layer_three = jnp.tanh(layer_three + third_bias) + jnp.concatenate(
+        layer_three = jnp.tanh(layer_three) + jnp.concatenate(
             [layer_two, layer_two], axis=0
         )
         for part in range(4):
@@ -336,9 +354,14 @@
             for k in range(SLOT_CHUNK):
                 total = total + layer_three[:, k * atoms : (k + 1) * atoms] * radial[part][k : k + 1]
             matrix[part] = total
+
+    def two_chunks(index, carry):
+        first = pl.multiple_of(index * (2 * SLOT_CHUNK), 2 * SLOT_CHUNK)
+        chunk(first)
+        chunk(pl.multiple_of(first + SLOT_CHUNK, SLOT_CHUNK))
         return carry
 
-    lax.fori_loop(0, listed // SLOT_CHUNK, chunk, 0)
+    lax.fori_loop(0, listed // (2 * SLOT_CHUNK), two_chunks, 0)
 
     parts = []
     for part in range(4):
@@ -354,16 +377,16 @@
         for part in range(1, 4):
             total = total + parts[part][row : row + 1] * leading[part]
         descriptor[row * AXIS_COLUMNS : (row + 1) * AXIS_COLUMNS, :] = total
-    for copy in copies:
+    for copy in copies[5:]:
         copy.wait()
 
     def layer(high_ref, low_ref, given, column):
         weights = (high_ref[...], low_ref[...])
         return jnp.tanh(multiply(weights, split(given)) + columns[0:hidden_width, column : column + 1])
 
-    hidden = layer(one_high, one_low, descriptor[...], 6)
-    hidden = hidden + layer(two_high, two_low, hidden, 7)
-    hidden = hidden + layer(three_high, three_low, hidden, 8)
+    hidden = layer(one_high, one_low, descriptor[...], 4)
+    hidden = hidden + layer(two_high, two_low, hidden, 5)
+    hidden = hidden + layer(three_high, three_low, hidden, 6)
     coeffs = multiply(split(fit_out_w[...]), split(hidden))
     vector = jnp.concatenate(
         [jnp.sum(coeffs * parts[1 + c], axis=0, keepdims=True) for c in range(3)], axis=0
@@ -382,10 +405,10 @@
     shifts,
     phase,
     green_ref,
-    fold_high,
-    fold_low,
-    unfold_high,
-    unfold_low,
+    fold_left,
+    fold_right,
+    unfold_left,
+    unfold_right,
     out_ref,
     grid,
     planes,
@@ -411,12 +434,6 @@
     piece = lax.axis_index("wide") * narrow_count + lax.axis_index("narrow")
     lane_zero = lax.broadcasted_iota(jnp.int32, (1, half_x), 1) == 0
     row_zero = lax.broadcasted_iota(jnp.int32, (half_z, 1), 0) == 0
-
-    def fold():
-        return (fold_high[...], fold_low[...])
-
-    def unfold():
-        return (unfold_high[...], unfold_low[...])
 
     def sites(at_wide, at_narrow):
         atom = table[at_wide, at_narrow]
@@ -486,11 +503,10 @@
             )
             high, low = split(left)
             across = weights[at_narrow, :, lanes]
-            total = lax.dot_general(high, across, NT, preferred_element_type=jnp.float32)
-            total = total[:, 0:128] + (
-                total[:, 128:256]
-                + lax.dot_general(low, across[0:128], NT, preferred_element_type=jnp.float32)
+            total = product(
+                jnp.concatenate([high, low], axis=1), jnp.concatenate([across, across], axis=1), NT
             )
+            total = total[:, 0:128] + total[:, 128:256]
             start = at_wide // copies * 128
             for c in range(channels):
                 spot = slice(c % 2 * GRID_X + start, c % 2 * GRID_X + start + 128)
@@ -560,12 +576,12 @@
         return jnp.concatenate(real, axis=axis), jnp.concatenate(imag, axis=axis)
 
     def to_modes(real, imag, j):
-        real = multiply(split(real), fold())
+        real = product(as_left(real), fold_right[...])
         if imag is not None:
-            imag = multiply(split(imag), fold())
+            imag = product(as_left(imag), fold_right[...])
         real, imag = paired(real, imag, lane_zero, 1)
-        real = multiply(unfold(), split(real))
-        imag = multiply(unfold(), split(imag))
+        real = product(unfold_left[...], as_right(real))
+        imag = product(unfold_left[...], as_right(imag))
         real, imag = paired(real, imag, row_zero, 0)
         green = green_ref[j]
         mode = GRID_Y // 2 if j == fine else piece * fine + j
@@ -584,12 +600,12 @@
         if j == 0:
             real, imag = real - last_imag, imag + last_real
         real, imag = merged(real, imag, row_zero, 0)
-        real = multiply(fold(), split(real))
-        imag = multiply(fold(), split(imag))
+        real = product(fold_left[...], as_right(real))
+        imag = product(fold_left[...], as_right(imag))
         real, imag = merged(real, imag, lane_zero, 1)
         scale = jnp.where(piece * fine + j == 0, 1.0, 2.0)
         for part, lanes in ((real, slice(0, GRID_X)), (imag, slice(GRID_X, 2 * GRID_X))):
-            part = multiply(split(part * scale), unfold())
+            part = product(as_left(part * scale), unfold_right[...])
             for k in range(copies):
                 moved = pltpu.roll(part, (HALO_X - k * cells_x) % GRID_X, 1)
                 grid[k, j, HALO_Z:, lanes] = moved
@@ -619,12 +635,10 @@
             start = at_wide // copies * 128
             high = lefts[at_wide % copies][0][:, start : start + 128]
             low = lefts[at_wide % copies][1][:, start : start + 128]
-            twice = jnp.concatenate([high, high], axis=1)
+            thrice = jnp.concatenate([high, high, low], axis=1)
 
             def across(right):
-                return lax.dot_general(
-                    twice, right, NN, preferred_element_type=jnp.float32
-                ) + lax.dot_general(low, right[0:128], NN, preferred_element_type=jnp.float32)
+                return product(thrice, jnp.concatenate([right, right[0:128]], axis=0))
 
             value = across(weights[at_narrow, :, lanes])
             slope = across(slopes[buffer, :, lanes])
@@ -684,10 +698,10 @@
     return np.concatenate([np.cos(turns), sines], axis=1)
 
 
-def halves(table):
+def sides(table):
     high = table.astype(jnp.bfloat16)
     low = (table - high.astype(np.float64)).astype(jnp.bfloat16)
-    return high, low
+    return np.concatenate([high, low, high], axis=1), np.concatenate([high, high, low], axis=0)
 
 
 def vmem(count):
@@ -802,11 +816,11 @@
         name="prepare",
     )(*arguments)
     phase, green = prepared[10:]
-    fitted = (*prepared[4:10], fit_out_w.T)
+    fitted = (table, *prepared[:10], fit_out_w.T)
     dipole, shifts = pl.pallas_call(
         centroid_kernel,
         out_shape=(shaped((3, 1, atoms)), shaped((pieces, 4, atoms))),
-        in_specs=vmem(5) + hbm(7),
+        in_specs=hbm(12),
         out_specs=tuple(vmem(2)),
         scratch_shapes=[
             pltpu.VMEM((4, tall, atoms), jnp.float32),
@@ -816,7 +830,7 @@
         + [pltpu.VMEM(array.shape, array.dtype) for array in fitted],
         compiler_params=limits(62),
         name="centroids",
-    )(table, *prepared[:4], *fitted)
+    )(*fitted)
     shifts = lax.all_to_all(shifts, axes, 0, 0, tiled=True)
     shifts = shifts.reshape(wide_count, narrow_count, 4, atoms)
 
@@ -843,8 +857,8 @@
         shifts,
         phase,
         green,
-        *[jnp.asarray(half) for half in halves(fold_table(GRID_X))],
-        *[jnp.asarray(half) for half in halves(fold_table(GRID_X).T)],
+        *[jnp.asarray(side) for side in sides(fold_table(GRID_X))],
+        *[jnp.asarray(side) for side in sides(fold_table(GRID_X).T)],
     )
     arrived = lax.all_to_all(partial.reshape(pieces, 1, out_width), axes, 0, 0, tiled=True)
     atom_field, centroid_field, energy = pl.pallas_call(

time: 71.6 us -> 74.5 us (1.041)
  local copies, waits for them, and re-layouts: 1.5 us -> 4.46 us
    unnamed x16, local copies, waits for them, and re-layouts: 1.5 us -> 4.46 us
    pallas_call x1, Pallas kernels: 10.9 us -> 9.87 us  [local(): pl.pallas_call(centroid_kernel, out_shape=(shaped((3, 1, atoms)), shaped(...]
    pallas_call x1, Pallas kernels: 20.6 us -> 21.6 us  [local(): pl.pallas_call(mesh_kernel, out_shape=shaped((wide_count, narrow_count, 1...]
  transfers between devices with their start and end apart: 1 -> 1, of which waited for: 1 -> 1; matrix products, arithmetic and copies ran while one was open for 0% -> 0% of each run, Pallas kernels for 6% -> 5%
where the time goes in v6:
time: 74.5 us; the launch traced here: 74.1 us
  Pallas kernels  38.2 us (51%)
  blocking collectives  20.1 us (27%)
  starting transfers between devices  7.3 us (10%)
  local copies, waits for them, and re-layouts  4.46 us (6%)
  waiting for transfers between devices  3.29 us (4%)
    pallas_call x1, Pallas kernels, local(): pl.pallas_call(mesh_kernel, out_shape=shaped((wide_count, narrow_count, 1...  21.6 us
    all_to_all x1, blocking collectives, local(): lax.all_to_all(partial.reshape(pieces, 1, out_width), axes, 0, 0, tiled=T...  10.2 us
    pallas_call x1, Pallas kernels, local(): pl.pallas_call(centroid_kernel, out_shape=(shaped((3, 1, atoms)), shaped(...  9.87 us
    all_to_all x1, blocking collectives, local(): shifts = lax.all_to_all(shifts, axes, 0, 0, tiled=True)  9.86 us
    all_to_all x1, starting transfers between devices, local(): table = lax.all_to_all(packed, axes, 0, 0, tiled=True)  7.3 us
    unnamed x16, local copies, waits for them, and re-layouts  4.46 us
    pallas_call x1, Pallas kernels, local(): pl.pallas_call(prepare_kernel, out_shape=(shaped((listed, atoms), jnp.int...  3.95 us
    all_to_all x1, waiting for transfers between devices, local(): table = lax.all_to_all(packed, axes, 0, 0, tiled=True)  3.29 us
  transfers between devices with their start and end apart: 1, of which 1 were waited for; matrix products, arithmetic and copies ran while one was open for 0% of the time, Pallas kernels for 5%

profile of v6, /device:TPU:0, one launch (start us, length us, event | category | flops | bytes accessed | tf_op | source)
XLA Modules:
  0.0 74.1 jit_solution(1948546182287372771)
XLA Ops:
  0.6 1.3 %pack.1 = f32[32,4,128]{2,1,0:T(4,128)} custom-call(f32[3,1,128]{2,1,0:T(1,128)} %bitcast.33, s32[1,128]{1,0:T(1,128)} %bitcast.31), custom_call_target="tpu_custom_call" | custom-call | tf_op jit(solution)/shard_map/pack/pallas_call | solution.py:752
  2.0 7.3 %all-to-all-start = ((f32[32,4,128]{2,1,0:T(4,128)}), f32[32,4,128]{2,1,0:T(4,128)S(1)}, u32[]{:S(2)}, u32[]{:S(2)}) async-start(f32[32,4,128]{2,1,0:T(4,128)} %pack.1), calls=%async_computation | async-start | bytes 131072 | tf_op jit(solution)/shard_map/all_to_all | solution.py:759
  9.3 3.9 %prepare.1 = (s32[128,128]{1,0:T(8,128)}, f32[256,16]{1,0:T(8,128)}, bf16[64,96]{1,0:T(8,128)(2,1)}, bf16[128,192]{1,0:T(8,128)(2,1)}, bf16[240,1600]{1,0:T(8,12...) custom-call(s32[128,128]{1,0:T(8,128)} %bitcast.30, ...), custom_call_target="tpu_custom_call" | custom-call | flops 1000000 | bytes 3072000 | tf_op jit(solution)/shard_map/prepare/pallas_call | solution.py:792
  13.2 0.0 copy-start
  13.2 0.0 copy-start.3
  13.2 0.0 copy-start.7
  13.2 3.3 %all-to-all-done = f32[32,4,128]{2,1,0:T(4,128)S(1)} async-done(((f32[32,4,128]{2,1,0:T(4,128)}), f32[32,4,128]{2,1,0:T(4,128)S(1)}, u32[]{:S(2)}, u32[]{:S(2)}) %all-to-all-start) | async-done | bytes 65568 | tf_op jit(solution)/shard_map/all_to_all | solution.py:759
  16.5 0.0 copy-start.1
  16.5 0.6 copy-done.1
  17.2 9.9 %centroids.1 = (f32[3,1,128]{2,1,0:T(1,128)}, f32[32,4,128]{2,1,0:T(4,128)}) custom-call(f32[4,8,4,128]{3,2,1,0:T(4,128)} %bitcast.25, s32[128,128]{1,0:T(8,128)} %get-tuple-element.21.codes, f32[256,16]{1,0:T(8,128)} %get-tuple-element.22.columns, bf16[64,96]{1,0:T(8,128)(2,1)} %get-tuple-element.23.second, bf16[128,192]{1,0:T(8,128)(2,1)} %get-tuple-element.24.third, ...), custom_call_target="tpu_custom_call" | custom-call | tf_op jit(solution)/shard_map/centroids/pallas_call | solution.py:820
  27.1 9.9 %all_to_all.15 = f32[32,4,128]{2,1,0:T(4,128)S(1)} all-to-all(f32[32,4,128]{2,1,0:T(4,128)} %get-tuple-element.32), channel_id=1, replica_groups=mesh['wide'=4,'narrow'=8] {'wide','narrow'}, dimensions={0} | all-to-all | bytes 131072 | tf_op jit(solution)/shard_map/all_to_all | solution.py:834
  36.9 0.0 copy-done
  36.9 0.0 copy-done.3
  36.9 0.0 copy-done.7
  36.9 0.0 copy-start.2
  36.9 0.8 %copy-done.2 = f32[32,4,128]{2,1,0:T(4,128)S(1)} copy-done((f32[32,4,128]{2,1,0:T(4,128)S(1)}, f32[32,4,128]{2,1,0:T(4,128)}, u32[]{:S(2)}) %copy-start.2) | copy-done | bytes 65560
  37.8 0.0 copy-start.4
  37.8 1.0 %copy-done.4 = bf16[256,768]{1,0:T(8,128)(2,1)S(1)} copy-done((bf16[256,768]{1,0:T(8,128)(2,1)S(1)}, bf16[256,768]{1,0:T(8,128)(2,1)}, u32[]{:S(2)}) %copy-start.4) | copy-done | bytes 393240
  38.8 0.0 copy-start.5
  38.8 1.0 %copy-done.5 = bf16[768,256]{1,0:T(8,128)(2,1)S(1)} copy-done((bf16[768,256]{1,0:T(8,128)(2,1)S(1)}, bf16[768,256]{1,0:T(8,128)(2,1)}, u32[]{:S(2)}) %copy-start.5) | copy-done | bytes 393240
  39.8 0.0 copy-start.6
  39.8 1.0 %copy-done.6 = bf16[256,768]{1,0:T(8,128)(2,1)S(1)} copy-done((bf16[256,768]{1,0:T(8,128)(2,1)S(1)}, bf16[256,768]{1,0:T(8,128)(2,1)}, u32[]{:S(2)}) %copy-start.6) | copy-done | bytes 393240
  40.8 21.6 %mesh.1 = f32[4,8,1,1152]{3,2,1,0:T(1,128)S(1)} custom-call(f32[4,8,4,128]{3,2,1,0:T(4,128)S(1)} %bitcast.26, f32[4,8,4,128]{3,2,1,0:T(4,128)S(1)} %bitcast.27, f32[8,256]{1,0:T(8,128)S(1)} %copy-done.7, f32[5,256,256]{2,1,0:T(8,128)S(1)} %copy-done, bf16[256,768]{1,0:T(8,128)(2,1)S(1)} %copy-done.6, bf16[768,256]{1,0:T(8,128)(2,1)S(1)} %copy-done.5, ...), custom_call_target="tpu_custom_call" | custom-call | tf_op jit(solution)/shard_map/mesh/pallas_call | solution.py:841
  62.3 10.2 %all_to_all.16.arrived = f32[32,1,1152]{2,1,0:T(1,128)} all-to-all(f32[32,1,1152]{2,1,0:T(1,128)S(1)} %bitcast.24), channel_id=1, replica_groups=mesh['wide'=4,'narrow'=8] {'wide','narrow'}, dimensions={0} | all-to-all | bytes 294912 | tf_op jit(solution)/shard_map/all_to_all | solution.py:863
  72.5 1.5 %finish.1 = (f32[4,1,128]{2,1,0:T(1,128)}, f32[4,1,128]{2,1,0:T(1,128)}, f32[1,128]{1,0:T(1,128)}) custom-call(f32[32,1,1152]{2,1,0:T(1,128)} %all_to_all.16.arrived, s32[1,128]{1,0:T(1,128)} %bitcast.32), custom_call_target="tpu_custom_call" | custom-call | tf_op jit(solution)/shard_map/finish/pallas_call | solution.py:864
Async XLA Ops:
  2.0 14.6 %all-to-all-start = ((f32[32,4,128]{2,1,0:T(4,128)}), f32[32,4,128]{2,1,0:T(4,128)S(1)}, u32[]{:S(2)}, u32[]{:S(2)}) async-start(f32[32,4,128]{2,1,0:T(4,128)} %pack.1), calls=%async_computation | async-start | bytes 131072 | tf_op jit(solution)/shard_map/all_to_all | solution.py:759
  13.2 23.7 %copy-start = (f32[5,256,256]{2,1,0:T(8,128)S(1)}, f32[5,256,256]{2,1,0:T(8,128)}, u32[]{:S(2)}) copy-start(f32[5,256,256]{2,1,0:T(8,128)} %get-tuple-element.34.green_ref) | copy-start | bytes 3932164
  13.2 23.7 %copy-start.3 = (bf16[768,256]{1,0:T(8,128)(2,1)S(1)}, bf16[768,256]{1,0:T(8,128)(2,1)}, u32[]{:S(2)}) copy-start(bf16[768,256]{1,0:T(8,128)(2,1)} %constant.14.clone.unfold_right) | copy-start | bytes 1179652
  13.2 23.7 %copy-start.7 = (f32[8,256]{1,0:T(8,128)S(1)}, f32[8,256]{1,0:T(8,128)}, u32[]{:S(2)}) copy-start(f32[8,256]{1,0:T(8,128)} %get-tuple-element.33.phase) | copy-start | bytes 24580
  16.5 0.6 copy-start.1
  36.9 0.8 %copy-start.2 = (f32[32,4,128]{2,1,0:T(4,128)S(1)}, f32[32,4,128]{2,1,0:T(4,128)}, u32[]{:S(2)}) copy-start(f32[32,4,128]{2,1,0:T(4,128)} %copy-done.1) | copy-start | bytes 196612
  37.8 1.0 %copy-start.4 = (bf16[256,768]{1,0:T(8,128)(2,1)S(1)}, bf16[256,768]{1,0:T(8,128)(2,1)}, u32[]{:S(2)}) copy-start(bf16[256,768]{1,0:T(8,128)(2,1)} %constant.13.clone.unfold_left) | copy-start | bytes 1179652
  38.8 1.0 %copy-start.5 = (bf16[768,256]{1,0:T(8,128)(2,1)S(1)}, bf16[768,256]{1,0:T(8,128)(2,1)}, u32[]{:S(2)}) copy-start(bf16[768,256]{1,0:T(8,128)(2,1)} %constant.12.clone.fold_right) | copy-start | bytes 1179652
  39.8 1.0 %copy-start.6 = (bf16[256,768]{1,0:T(8,128)(2,1)S(1)}, bf16[256,768]{1,0:T(8,128)(2,1)}, u32[]{:S(2)}) copy-start(bf16[256,768]{1,0:T(8,128)(2,1)} %constant.11.clone.fold_left) | copy-start | bytes 1179652

commit v7 on v6

--- a/solution.py
+++ b/solution.py
@@ -22,6 +22,7 @@
 SLOT_CHUNK = 16
 HALO_X = 16
 HALO_Z = 8
+HALO_BITS = 16
 
 NN = (((1,), (0,)), ((), ()))
 NT = (((1,), (1,)), ((), ()))
@@ -38,20 +39,6 @@
         return lax.dot_general(a, b, dims, preferred_element_type=jnp.float32)
 
     return one(left[0], right[0]) + (one(left[1], right[0]) + one(left[0], right[1]))
-
-
-def product(left, right, dims=NN):
-    return lax.dot_general(left, right, dims, preferred_element_type=jnp.float32)
-
-
-def as_left(value):
-    high, low = split(value)
-    return jnp.concatenate([high, low, high], axis=1)
-
-
-def as_right(value):
-    high, low = split(value)
-    return jnp.concatenate([high, high, low], axis=0)
 
 
 def spline_pair(offset):
@@ -81,8 +68,10 @@
 
 
 def pack_kernel(positions, species, out_ref):
+    kinds = species[...]
     rows = [positions[component] for component in range(3)]
-    rows.append(species[...].astype(jnp.float32))
+    rows[0] = jnp.where(kinds > 0, -rows[0], rows[0])
+    rows.append(kinds.astype(jnp.float32))
     rows = jnp.concatenate(rows, axis=0)
     for target in range(out_ref.shape[0]):
         out_ref[target] = rows
@@ -275,7 +264,7 @@
     cells = (GRID_X // wide_count, GRID_Y, GRID_Z // narrow_count)
     at_wide = lax.axis_index("wide")
     at_narrow = lax.axis_index("narrow")
-    own = table[at_wide, at_narrow]
+    own = jnp.abs(table[at_wide, at_narrow])
     nearby = []
     for step in range(9):
         wide_at = lax.rem(at_wide + (step // 3 - 1) + wide_count, wide_count)
@@ -300,7 +289,7 @@
         step_y = rest - 3 * step_z
         brick = step_x * 3 + step_z
         found = []
-        for component in range(4):
+        for component in range(3):
             picked = jnp.zeros((SLOT_CHUNK, atoms), jnp.float32)
             for step in range(9):
                 row = jnp.broadcast_to(
@@ -309,6 +298,8 @@
                 here = jnp.take_along_axis(row, slot, axis=1, mode="promise_in_bounds")
                 picked = jnp.where(brick == step, here, picked)
             found.append(picked)
+        hydrogen = found[0] < 0.0
+        found[0] = jnp.abs(found[0])
         scaled = []
         for component, step in enumerate((step_x, step_y, step_z)):
             extent = float(cells[component])
@@ -320,7 +311,6 @@
             1.0 + (scaled[0] * scaled[0] + scaled[1] * scaled[1] + scaled[2] * scaled[2])
         )
         radial = [smooth] + [smooth * part for part in scaled]
-        hydrogen = found[3] > 0.5
         first_layers = []
         for k in range(SLOT_CHUNK):
             row = smooth[k : k + 1]
@@ -405,13 +395,14 @@
     shifts,
     phase,
     green_ref,
-    fold_left,
-    fold_right,
-    unfold_left,
-    unfold_right,
+    fold_high,
+    fold_low,
+    unfold_high,
+    unfold_low,
     out_ref,
     grid,
     planes,
+    packed,
     weights,
     slopes,
     weights_z,
@@ -435,8 +426,14 @@
     lane_zero = lax.broadcasted_iota(jnp.int32, (1, half_x), 1) == 0
     row_zero = lax.broadcasted_iota(jnp.int32, (half_z, 1), 0) == 0
 
+    def fold():
+        return (fold_high[...], fold_low[...])
+
+    def unfold():
+        return (unfold_high[...], unfold_low[...])
+
     def sites(at_wide, at_narrow):
-        atom = table[at_wide, at_narrow]
+        atom = jnp.abs(table[at_wide, at_narrow])
         moved = shifts[at_wide, at_narrow]
         found = []
         for component, extent in enumerate((cells_x, GRID_Y, cells_z)):
@@ -503,10 +500,11 @@
             )
             high, low = split(left)
             across = weights[at_narrow, :, lanes]
-            total = product(
-                jnp.concatenate([high, low], axis=1), jnp.concatenate([across, across], axis=1), NT
+            total = lax.dot_general(high, across, NT, preferred_element_type=jnp.float32)
+            total = total[:, 0:128] + (
+                total[:, 128:256]
+                + lax.dot_general(low, across[0:128], NT, preferred_element_type=jnp.float32)
             )
-            total = total[:, 0:128] + total[:, 128:256]
             start = at_wide // copies * 128
             for c in range(channels):
                 spot = slice(c % 2 * GRID_X + start, c % 2 * GRID_X + start + 128)
@@ -576,12 +574,12 @@
         return jnp.concatenate(real, axis=axis), jnp.concatenate(imag, axis=axis)
 
     def to_modes(real, imag, j):
-        real = product(as_left(real), fold_right[...])
+        real = multiply(split(real), fold())
         if imag is not None:
-            imag = product(as_left(imag), fold_right[...])
+            imag = multiply(split(imag), fold())
         real, imag = paired(real, imag, lane_zero, 1)
-        real = product(unfold_left[...], as_right(real))
-        imag = product(unfold_left[...], as_right(imag))
+        real = multiply(unfold(), split(real))
+        imag = multiply(unfold(), split(imag))
         real, imag = paired(real, imag, row_zero, 0)
         green = green_ref[j]
         mode = GRID_Y // 2 if j == fine else piece * fine + j
@@ -600,16 +598,28 @@
         if j == 0:
             real, imag = real - last_imag, imag + last_real
         real, imag = merged(real, imag, row_zero, 0)
-        real = product(fold_left[...], as_right(real))
-        imag = product(fold_left[...], as_right(imag))
+        real = multiply(fold(), split(real))
+        imag = multiply(fold(), split(imag))
         real, imag = merged(real, imag, lane_zero, 1)
         scale = jnp.where(piece * fine + j == 0, 1.0, 2.0)
         for part, lanes in ((real, slice(0, GRID_X)), (imag, slice(GRID_X, 2 * GRID_X))):
-            part = product(as_left(part * scale), unfold_right[...])
-            for k in range(copies):
-                moved = pltpu.roll(part, (HALO_X - k * cells_x) % GRID_X, 1)
-                grid[k, j, HALO_Z:, lanes] = moved
-                grid[k, j, 0:HALO_Z, lanes] = moved[GRID_Z - HALO_Z :]
+            part = multiply(split(part * scale), unfold())
+            channel = 2 * j + (0 if lanes.start == 0 else 1)
+            for at_wide in range(wide_count):
+                moved = pltpu.roll(part, (HALO_X - at_wide * cells_x) % GRID_X, 1)[:, 0:128]
+                high = moved.astype(jnp.bfloat16).astype(jnp.float32)
+                again = pltpu.roll(high, reach % 128, 1)
+                low = pltpu.roll(moved - high, 2 * reach % 128, 1)
+                sides = []
+                for side in range(2):
+                    lane = lax.broadcasted_iota(jnp.int32, (1, 128), 1) + side * 128
+                    value = jnp.where(lane < 2 * reach, again, low)
+                    if side == 0:
+                        value = jnp.where(lane < reach, high, value)
+                    sides.append(value.astype(jnp.bfloat16))
+                block = jnp.concatenate(sides, axis=1)
+                packed[at_wide, channel, HALO_BITS:, :] = block
+                packed[at_wide, channel, 0:HALO_BITS, :] = block[GRID_Z - HALO_BITS :]
     energy = jnp.broadcast_to(jnp.sum(energy, axis=1, keepdims=True), (1, 128))
 
     def collect(at_narrow, buffer):
@@ -617,28 +627,21 @@
         fill_x(row_x, (None, slopes.at[buffer]))
         value_z = weights_z[at_narrow]
         _, slope_z = splines_z(row_z)
-        first = pl.multiple_of(at_narrow * cells_z, HALO_Z)
-        lefts = []
-        for k in range(copies):
-            left = jnp.concatenate(
-                [
-                    grid[k, c // 2, pl.ds(first, window), c % 2 * GRID_X : (c % 2 + 1) * GRID_X]
-                    for c in range(channels)
-                ],
-                axis=0,
-            )
-            lefts.append(split(left))
+        first = pl.multiple_of(at_narrow * cells_z, HALO_BITS)
         wave = waves[at_narrow]
         wave_slope = wave_slopes[at_narrow]
         for at_wide in range(wide_count):
             lanes = slice(at_wide * pair, (at_wide + 1) * pair)
-            start = at_wide // copies * 128
-            high = lefts[at_wide % copies][0][:, start : start + 128]
-            low = lefts[at_wide % copies][1][:, start : start + 128]
-            thrice = jnp.concatenate([high, high, low], axis=1)
+            tall = cells_z + HALO_BITS
+            left = jnp.concatenate(
+                [packed[at_wide, c, pl.ds(first, tall), :] for c in range(channels)], axis=0
+            )
 
             def across(right):
-                return product(thrice, jnp.concatenate([right, right[0:128]], axis=0))
+                high = right[0:reach]
+                rest = jnp.zeros((256 - 3 * reach, pair), jnp.bfloat16)
+                right = jnp.concatenate([high, right[128 : 128 + reach], high, rest], axis=0)
+                return lax.dot_general(left, right, NN, preferred_element_type=jnp.float32)
 
             value = across(weights[at_narrow, :, lanes])
             slope = across(slopes[buffer, :, lanes])
@@ -646,7 +649,7 @@
             along_x = plain
             along_y = plain
             for c in range(channels):
-                block = slice(c * window, (c + 1) * window)
+                block = slice((c + 1) * tall - window, (c + 1) * tall)
                 plain = plain + value[block] * wave[c : c + 1, lanes]
                 along_x = along_x + slope[block] * wave[c : c + 1, lanes]
                 along_y = along_y + value[block] * wave_slope[c : c + 1, lanes]
@@ -698,10 +701,10 @@
     return np.concatenate([np.cos(turns), sines], axis=1)
 
 
-def sides(table):
+def halves(table):
     high = table.astype(jnp.bfloat16)
     low = (table - high.astype(np.float64)).astype(jnp.bfloat16)
-    return np.concatenate([high, low, high], axis=1), np.concatenate([high, high, low], axis=0)
+    return high, low
 
 
 def vmem(count):
@@ -845,7 +848,8 @@
         out_specs=vmem(1)[0],
         scratch_shapes=[
             pltpu.VMEM((copies, fine, HALO_Z + GRID_Z, 2 * GRID_X), jnp.float32),
-            pltpu.VMEM((fine + 1, GRID_Z, 2 * GRID_X), jnp.float32),
+            pltpu.VMEM((fine, GRID_Z, 2 * GRID_X), jnp.float32),
+            pltpu.VMEM((wide_count, 2 * fine, HALO_BITS + GRID_Z, 256), bf16),
         ]
         + [pltpu.VMEM((narrow_count, 256, length), bf16), pltpu.VMEM((2, 256, length), bf16)]
         + [pltpu.VMEM((narrow_count, GRID_Z // narrow_count + HALO_Z, length), jnp.float32)]
@@ -857,8 +861,8 @@
         shifts,
         phase,
         green,
-        *[jnp.asarray(side) for side in sides(fold_table(GRID_X))],
-        *[jnp.asarray(side) for side in sides(fold_table(GRID_X).T)],
+        *[jnp.asarray(half) for half in halves(fold_table(GRID_X))],
+        *[jnp.asarray(half) for half in halves(fold_table(GRID_X).T)],
     )
     arrived = lax.all_to_all(partial.reshape(pieces, 1, out_width), axes, 0, 0, tiled=True)
     atom_field, centroid_field, energy = pl.pallas_call(

time: 74.5 us -> 70.4 us (0.945)
  local copies, waits for them, and re-layouts: 4.46 us -> 1.5 us
  Pallas kernels: 38.2 us -> 37.1 us
    unnamed x16, local copies, waits for them, and re-layouts: 4.46 us -> 1.5 us
    pallas_call x1, Pallas kernels: 21.6 us -> 20.4 us  [local(): pl.pallas_call(mesh_kernel, out_shape=shaped((wide_count, narrow_count, 1...]
  transfers between devices with their start and end apart: 1 -> 1, of which waited for: 1 -> 1; matrix products, arithmetic and copies ran while one was open for 0% -> 0% of each run, Pallas kernels for 5% -> 6%
where the time goes in v7:
time: 70.4 us; the launch traced here: 70 us
  Pallas kernels  37.1 us (53%)
  blocking collectives  20.1 us (29%)
  starting transfers between devices  7.3 us (10%)
  waiting for transfers between devices  3.25 us (5%)
  local copies, waits for them, and re-layouts  1.5 us (2%)
  between operations  0.75 us (1%)
    pallas_call x1, Pallas kernels, local(): pl.pallas_call(mesh_kernel, out_shape=shaped((wide_count, narrow_count, 1...  20.4 us
    all_to_all x1, blocking collectives, local(): lax.all_to_all(partial.reshape(pieces, 1, out_width), axes, 0, 0, tiled=T...  10.2 us
    pallas_call x1, Pallas kernels, local(): pl.pallas_call(centroid_kernel, out_shape=(shaped((3, 1, atoms)), shaped(...  9.95 us
    all_to_all x1, blocking collectives, local(): shifts = lax.all_to_all(shifts, axes, 0, 0, tiled=True)  9.89 us
    all_to_all x1, starting transfers between devices, local(): table = lax.all_to_all(packed, axes, 0, 0, tiled=True)  7.3 us
    pallas_call x1, Pallas kernels, local(): pl.pallas_call(prepare_kernel, out_shape=(shaped((listed, atoms), jnp.int...  3.95 us
    all_to_all x1, waiting for transfers between devices, local(): table = lax.all_to_all(packed, axes, 0, 0, tiled=True)  3.25 us
    pallas_call x1, Pallas kernels, local(): pl.pallas_call(finish_kernel, out_shape=(shaped((4, 1, atoms)), shaped((4...  1.53 us
  transfers between devices with their start and end apart: 1, of which 1 were waited for; matrix products, arithmetic and copies ran while one was open for 0% of the time, Pallas kernels for 6%

profile of v7, /device:TPU:0, one launch (start us, length us, event | category | flops | bytes accessed | tf_op | source)
XLA Modules:
  0.0 70.0 jit_solution(16989197631788360991)
XLA Ops:
  0.6 1.3 %pack.1 = f32[32,4,128]{2,1,0:T(4,128)} custom-call(f32[3,1,128]{2,1,0:T(1,128)} %bitcast.33, s32[1,128]{1,0:T(1,128)} %bitcast.31), custom_call_target="tpu_custom_call" | custom-call | tf_op jit(solution)/shard_map/pack/pallas_call | solution.py:755
  2.0 7.3 %all-to-all-start = ((f32[32,4,128]{2,1,0:T(4,128)}), f32[32,4,128]{2,1,0:T(4,128)S(1)}, u32[]{:S(2)}, u32[]{:S(2)}) async-start(f32[32,4,128]{2,1,0:T(4,128)} %pack.1), calls=%async_computation | async-start | bytes 131072 | tf_op jit(solution)/shard_map/all_to_all | solution.py:762
  9.3 3.9 %prepare.1 = (s32[128,128]{1,0:T(8,128)}, f32[256,16]{1,0:T(8,128)}, bf16[64,96]{1,0:T(8,128)(2,1)}, bf16[128,192]{1,0:T(8,128)(2,1)}, bf16[240,1600]{1,0:T(8,12...) custom-call(s32[128,128]{1,0:T(8,128)} %bitcast.30, ...), custom_call_target="tpu_custom_call" | custom-call | flops 1000000 | bytes 3072000 | tf_op jit(solution)/shard_map/prepare/pallas_call | solution.py:795
  13.2 0.0 copy-start
  13.2 0.0 copy-start.3
  13.2 0.0 copy-start.4
  13.3 0.0 copy-start.5
  13.3 0.0 copy-start.6
  13.3 0.0 copy-start.7
  13.3 3.3 %all-to-all-done = f32[32,4,128]{2,1,0:T(4,128)S(1)} async-done(((f32[32,4,128]{2,1,0:T(4,128)}), f32[32,4,128]{2,1,0:T(4,128)S(1)}, u32[]{:S(2)}, u32[]{:S(2)}) %all-to-all-start) | async-done | bytes 65568 | tf_op jit(solution)/shard_map/all_to_all | solution.py:762
  16.5 0.0 copy-start.1
  16.5 0.6 copy-done.1
  17.2 9.9 %centroids.1 = (f32[3,1,128]{2,1,0:T(1,128)}, f32[32,4,128]{2,1,0:T(4,128)}) custom-call(f32[4,8,4,128]{3,2,1,0:T(4,128)} %bitcast.25, s32[128,128]{1,0:T(8,128)} %get-tuple-element.21.codes, f32[256,16]{1,0:T(8,128)} %get-tuple-element.22.columns, bf16[64,96]{1,0:T(8,128)(2,1)} %get-tuple-element.23.second, bf16[128,192]{1,0:T(8,128)(2,1)} %get-tuple-element.24.third, ...), custom_call_target="tpu_custom_call" | custom-call | tf_op jit(solution)/shard_map/centroids/pallas_call | solution.py:823
  27.1 9.9 %all_to_all.15 = f32[32,4,128]{2,1,0:T(4,128)S(1)} all-to-all(f32[32,4,128]{2,1,0:T(4,128)} %get-tuple-element.32), channel_id=1, replica_groups=mesh['wide'=4,'narrow'=8] {'wide','narrow'}, dimensions={0} | all-to-all | bytes 131072 | tf_op jit(solution)/shard_map/all_to_all | solution.py:837
  37.0 0.0 copy-done
  37.0 0.0 copy-done.3
  37.0 0.0 copy-done.4
  37.0 0.0 copy-done.5
  37.0 0.0 copy-done.6
  37.0 0.0 copy-done.7
  37.1 0.0 copy-start.2
  37.1 0.8 %copy-done.2 = f32[32,4,128]{2,1,0:T(4,128)S(1)} copy-done((f32[32,4,128]{2,1,0:T(4,128)S(1)}, f32[32,4,128]{2,1,0:T(4,128)}, u32[]{:S(2)}) %copy-start.2) | copy-done | bytes 65560
  37.9 20.4 %mesh.1 = f32[4,8,1,1152]{3,2,1,0:T(1,128)S(1)} custom-call(f32[4,8,4,128]{3,2,1,0:T(4,128)S(1)} %bitcast.26, f32[4,8,4,128]{3,2,1,0:T(4,128)S(1)} %bitcast.27, f32[8,256]{1,0:T(8,128)S(1)} %copy-done.7, f32[5,256,256]{2,1,0:T(8,128)S(1)} %copy-done, bf16[256,256]{1,0:T(8,128)(2,1)S(1)} %copy-done.6, bf16[256,256]{1,0:T(8,128)(2,1)S(1)} %copy-done.5, ...), custom_call_target="tpu_custom_call" | custom-call | tf_op jit(solution)/shard_map/mesh/pallas_call | solution.py:844
  58.3 10.2 %all_to_all.16.arrived = f32[32,1,1152]{2,1,0:T(1,128)} all-to-all(f32[32,1,1152]{2,1,0:T(1,128)S(1)} %bitcast.24), channel_id=1, replica_groups=mesh['wide'=4,'narrow'=8] {'wide','narrow'}, dimensions={0} | all-to-all | bytes 294912 | tf_op jit(solution)/shard_map/all_to_all | solution.py:867
  68.5 1.5 %finish.1 = (f32[4,1,128]{2,1,0:T(1,128)}, f32[4,1,128]{2,1,0:T(1,128)}, f32[1,128]{1,0:T(1,128)}) custom-call(f32[32,1,1152]{2,1,0:T(1,128)} %all_to_all.16.arrived, s32[1,128]{1,0:T(1,128)} %bitcast.32), custom_call_target="tpu_custom_call" | custom-call | tf_op jit(solution)/shard_map/finish/pallas_call | solution.py:868
Async XLA Ops:
  2.0 14.6 %all-to-all-start = ((f32[32,4,128]{2,1,0:T(4,128)}), f32[32,4,128]{2,1,0:T(4,128)S(1)}, u32[]{:S(2)}, u32[]{:S(2)}) async-start(f32[32,4,128]{2,1,0:T(4,128)} %pack.1), calls=%async_computation | async-start | bytes 131072 | tf_op jit(solution)/shard_map/all_to_all | solution.py:762
  13.2 23.8 %copy-start = (f32[5,256,256]{2,1,0:T(8,128)S(1)}, f32[5,256,256]{2,1,0:T(8,128)}, u32[]{:S(2)}) copy-start(f32[5,256,256]{2,1,0:T(8,128)} %get-tuple-element.34.green_ref) | copy-start | bytes 3932164
  13.2 23.8 %copy-start.3 = (bf16[256,256]{1,0:T(8,128)(2,1)S(1)}, bf16[256,256]{1,0:T(8,128)(2,1)}, u32[]{:S(2)}) copy-start(bf16[256,256]{1,0:T(8,128)(2,1)} %constant.14.clone.unfold_low) | copy-start | bytes 393220
  13.2 23.8 %copy-start.4 = (bf16[256,256]{1,0:T(8,128)(2,1)S(1)}, bf16[256,256]{1,0:T(8,128)(2,1)}, u32[]{:S(2)}) copy-start(bf16[256,256]{1,0:T(8,128)(2,1)} %constant.13.clone.unfold_high) | copy-start | bytes 393220
  13.3 23.8 %copy-start.5 = (bf16[256,256]{1,0:T(8,128)(2,1)S(1)}, bf16[256,256]{1,0:T(8,128)(2,1)}, u32[]{:S(2)}) copy-start(bf16[256,256]{1,0:T(8,128)(2,1)} %constant.12.clone.fold_low) | copy-start | bytes 393220
  13.3 23.8 %copy-start.6 = (bf16[256,256]{1,0:T(8,128)(2,1)S(1)}, bf16[256,256]{1,0:T(8,128)(2,1)}, u32[]{:S(2)}) copy-start(bf16[256,256]{1,0:T(8,128)(2,1)} %constant.11.clone.fold_high) | copy-start | bytes 393220
  13.3 23.8 %copy-start.7 = (f32[8,256]{1,0:T(8,128)S(1)}, f32[8,256]{1,0:T(8,128)}, u32[]{:S(2)}) copy-start(f32[8,256]{1,0:T(8,128)} %get-tuple-element.33.phase) | copy-start | bytes 24580
  16.5 0.6 copy-start.1
  37.1 0.8 %copy-start.2 = (f32[32,4,128]{2,1,0:T(4,128)S(1)}, f32[32,4,128]{2,1,0:T(4,128)}, u32[]{:S(2)}) copy-start(f32[32,4,128]{2,1,0:T(4,128)} %copy-done.1) | copy-start | bytes 196612

commit v8 on v7

--- a/solution.py
+++ b/solution.py
@@ -403,7 +403,8 @@
     grid,
     planes,
     packed,
-    weights,
+    weights_even,
+    weights_odd,
     slopes,
     weights_z,
     waves,
@@ -465,7 +466,10 @@
 
     grid[:, :, 0:HALO_Z, :] = jnp.zeros((copies, fine, HALO_Z, 2 * GRID_X), jnp.float32)
 
-    def spread(at_narrow):
+    weights = (weights_even, weights_odd)
+
+    def spread(index, odd):
+        at_narrow = 2 * index + odd
         row_x, row_y, row_z, charge = line(at_narrow)
         lower = jnp.floor(row_y)
         back = lax.broadcasted_iota(jnp.int32, (8, 1), 0)
@@ -487,7 +491,7 @@
         wave = jnp.concatenate(wave_blocks, axis=1)
         waves[at_narrow] = wave
         wave_slopes[at_narrow] = jnp.concatenate(slope_blocks, axis=1)
-        fill_x(row_x, (weights.at[at_narrow], None))
+        fill_x(row_x, (weights[odd].at[index], None))
         value_z, _ = splines_z(row_z)
         weights_z[at_narrow] = value_z
         charged = wave * charge
@@ -499,7 +503,7 @@
                 [near * charged[c : c + 1, lanes] for c in range(channels)], axis=0
             )
             high, low = split(left)
-            across = weights[at_narrow, :, lanes]
+            across = weights[odd][index, :, lanes]
             total = lax.dot_general(high, across, NT, preferred_element_type=jnp.float32)
             total = total[:, 0:128] + (
                 total[:, 128:256]
@@ -515,13 +519,13 @@
 
     def in_pairs(step):
         def both(index, carry):
-            step(2 * index, 0)
-            step(2 * index + 1, 1)
+            step(index, 0)
+            step(index, 1)
             return carry
 
         lax.fori_loop(0, narrow_count // 2, both, 0)
 
-    in_pairs(lambda at_narrow, _: spread(at_narrow))
+    in_pairs(spread)
 
     def gather(j, carry):
         for lanes in (slice(0, GRID_X), slice(GRID_X, 2 * GRID_X)):
@@ -573,38 +577,51 @@
         ]
         return jnp.concatenate(real, axis=axis), jnp.concatenate(imag, axis=axis)
 
-    def to_modes(real, imag, j):
-        real = multiply(split(real), fold())
-        if imag is not None:
-            imag = multiply(split(imag), fold())
+    modes = {}
+    parts = []
+
+    def slot(j):
+        first_imag = planes[0, :, GRID_X:]
+        if j == fine:
+            real, imag = jnp.where(is_first, first_imag, 0.0), None
+        else:
+            real, imag = planes[j, :, 0:GRID_X], planes[j, :, GRID_X:]
+            if j == 0:
+                imag = jnp.where(is_first, 0.0, imag)
+        real = split(real)
+        imag = None if imag is None else split(imag)
+        yield
+        real = multiply(real, fold())
+        imag = None if imag is None else multiply(imag, fold())
+        yield
         real, imag = paired(real, imag, lane_zero, 1)
-        real = multiply(unfold(), split(real))
-        imag = multiply(unfold(), split(imag))
+        real, imag = split(real), split(imag)
+        yield
+        real, imag = multiply(unfold(), real), multiply(unfold(), imag)
+        yield
         real, imag = paired(real, imag, row_zero, 0)
         green = green_ref[j]
         mode = GRID_Y // 2 if j == fine else piece * fine + j
         share = jnp.where((mode == 0) | (mode == GRID_Y // 2), 0.5, 1.0)
-        part = jnp.sum(green * (real * real + imag * imag), axis=0, keepdims=True)
-        return green * real, green * imag, share * part
-
-    second_plane = jnp.where(is_first, planes[0, :, GRID_X:], 0.0)
-    last_real, last_imag, energy = to_modes(second_plane, None, fine)
-    for j in range(fine):
-        imag = planes[j, :, GRID_X:]
+        parts.append(share * jnp.sum(green * (real * real + imag * imag), axis=0, keepdims=True))
+        real, imag = green * real, green * imag
+        if j == fine:
+            modes[j] = (real, imag)
+            return
         if j == 0:
-            imag = jnp.where(is_first, 0.0, imag)
-        real, imag, part = to_modes(planes[j, :, 0:GRID_X], imag, j)
-        energy = energy + part
-        if j == 0:
-            real, imag = real - last_imag, imag + last_real
+            real, imag = real - modes[fine][1], imag + modes[fine][0]
         real, imag = merged(real, imag, row_zero, 0)
-        real = multiply(fold(), split(real))
-        imag = multiply(fold(), split(imag))
+        real, imag = split(real), split(imag)
+        yield
+        real, imag = multiply(fold(), real), multiply(fold(), imag)
+        yield
         real, imag = merged(real, imag, lane_zero, 1)
         scale = jnp.where(piece * fine + j == 0, 1.0, 2.0)
-        for part, lanes in ((real, slice(0, GRID_X)), (imag, slice(GRID_X, 2 * GRID_X))):
-            part = multiply(split(part * scale), unfold())
-            channel = 2 * j + (0 if lanes.start == 0 else 1)
+        real, imag = split(real * scale), split(imag * scale)
+        yield
+        real, imag = multiply(real, unfold()), multiply(imag, unfold())
+        yield
+        for k, part in enumerate((real, imag)):
             for at_wide in range(wide_count):
                 moved = pltpu.roll(part, (HALO_X - at_wide * cells_x) % GRID_X, 1)[:, 0:128]
                 high = moved.astype(jnp.bfloat16).astype(jnp.float32)
@@ -618,13 +635,22 @@
                         value = jnp.where(lane < reach, high, value)
                     sides.append(value.astype(jnp.bfloat16))
                 block = jnp.concatenate(sides, axis=1)
-                packed[at_wide, channel, HALO_BITS:, :] = block
-                packed[at_wide, channel, 0:HALO_BITS, :] = block[GRID_Z - HALO_BITS :]
+                packed[at_wide, 2 * j + k, HALO_BITS:, :] = block
+                packed[at_wide, 2 * j + k, 0:HALO_BITS, :] = block[GRID_Z - HALO_BITS :]
+
+    waiting = [slot(j) for j in [fine, *range(fine)]]
+    running = []
+    while waiting or running:
+        if waiting:
+            running.append(waiting.pop(0))
+        running = [one for one in running if next(one, running) is not running]
+    energy = sum(parts[1:], parts[0])
     energy = jnp.broadcast_to(jnp.sum(energy, axis=1, keepdims=True), (1, 128))
 
-    def collect(at_narrow, buffer):
+    def collect(index, odd):
+        at_narrow = 2 * index + odd
         row_x, _, row_z, _ = line(at_narrow)
-        fill_x(row_x, (None, slopes.at[buffer]))
+        fill_x(row_x, (None, slopes.at[odd]))
         value_z = weights_z[at_narrow]
         _, slope_z = splines_z(row_z)
         first = pl.multiple_of(at_narrow * cells_z, HALO_BITS)
@@ -643,8 +669,8 @@
                 right = jnp.concatenate([high, right[128 : 128 + reach], high, rest], axis=0)
                 return lax.dot_general(left, right, NN, preferred_element_type=jnp.float32)
 
-            value = across(weights[at_narrow, :, lanes])
-            slope = across(slopes[buffer, :, lanes])
+            value = across(weights[odd][index, :, lanes])
+            slope = across(slopes[odd, :, lanes])
             plain = jnp.zeros((window, pair), jnp.float32)
             along_x = plain
             along_y = plain
@@ -851,7 +877,8 @@
             pltpu.VMEM((fine, GRID_Z, 2 * GRID_X), jnp.float32),
             pltpu.VMEM((wide_count, 2 * fine, HALO_BITS + GRID_Z, 256), bf16),
         ]
-        + [pltpu.VMEM((narrow_count, 256, length), bf16), pltpu.VMEM((2, 256, length), bf16)]
+        + [pltpu.VMEM((narrow_count // 2, 256, length), bf16)] * 2
+        + [pltpu.VMEM((2, 256, length), bf16)]
         + [pltpu.VMEM((narrow_count, GRID_Z // narrow_count + HALO_Z, length), jnp.float32)]
         + [pltpu.VMEM((narrow_count, wave_rows, length), jnp.float32)] * 2,
         compiler_params=limits(48),

time: 70.4 us -> 69.1 us (0.982)
  Pallas kernels: 37.1 us -> 35.8 us
    pallas_call x1, Pallas kernels: 20.4 us -> 19.1 us  [local(): pl.pallas_call(mesh_kernel, out_shape=shaped((wide_count, narrow_count, 1...]
where the time goes in v8:
time: 69.1 us; the launch traced here: 68.7 us
  Pallas kernels  35.8 us (52%)
  blocking collectives  20.1 us (29%)
  starting transfers between devices  7.3 us (11%)
  waiting for transfers between devices  3.25 us (5%)
  local copies, waits for them, and re-layouts  1.5 us (2%)
  between operations  0.75 us (1%)
    pallas_call x1, Pallas kernels, local(): pl.pallas_call(mesh_kernel, out_shape=shaped((wide_count, narrow_count, 1...  19.1 us
    all_to_all x1, blocking collectives, local(): lax.all_to_all(partial.reshape(pieces, 1, out_width), axes, 0, 0, tiled=T...  10.2 us
    pallas_call x1, Pallas kernels, local(): pl.pallas_call(centroid_kernel, out_shape=(shaped((3, 1, atoms)), shaped(...  9.95 us
    all_to_all x1, blocking collectives, local(): shifts = lax.all_to_all(shifts, axes, 0, 0, tiled=True)  9.89 us
    all_to_all x1, starting transfers between devices, local(): table = lax.all_to_all(packed, axes, 0, 0, tiled=True)  7.3 us
    pallas_call x1, Pallas kernels, local(): pl.pallas_call(prepare_kernel, out_shape=(shaped((listed, atoms), jnp.int...  3.95 us
    all_to_all x1, waiting for transfers between devices, local(): table = lax.all_to_all(packed, axes, 0, 0, tiled=True)  3.25 us
    pallas_call x1, Pallas kernels, local(): pl.pallas_call(finish_kernel, out_shape=(shaped((4, 1, atoms)), shaped((4...  1.53 us
  transfers between devices with their start and end apart: 1, of which 1 were waited for; matrix products, arithmetic and copies ran while one was open for 0% of the time, Pallas kernels for 6%

profile of v8, /device:TPU:0, one launch (start us, length us, event | category | flops | bytes accessed | tf_op | source)
XLA Modules:
  0.0 68.7 jit_solution(16574910632594971931)
XLA Ops:
  0.6 1.3 %pack.1 = f32[32,4,128]{2,1,0:T(4,128)} custom-call(f32[3,1,128]{2,1,0:T(1,128)} %bitcast.33, s32[1,128]{1,0:T(1,128)} %bitcast.31), custom_call_target="tpu_custom_call" | custom-call | tf_op jit(solution)/shard_map/pack/pallas_call | solution.py:781
  2.0 7.3 %all-to-all-start = ((f32[32,4,128]{2,1,0:T(4,128)}), f32[32,4,128]{2,1,0:T(4,128)S(1)}, u32[]{:S(2)}, u32[]{:S(2)}) async-start(f32[32,4,128]{2,1,0:T(4,128)} %pack.1), calls=%async_computation | async-start | bytes 131072 | tf_op jit(solution)/shard_map/all_to_all | solution.py:788
  9.3 3.9 %prepare.1 = (s32[128,128]{1,0:T(8,128)}, f32[256,16]{1,0:T(8,128)}, bf16[64,96]{1,0:T(8,128)(2,1)}, bf16[128,192]{1,0:T(8,128)(2,1)}, bf16[240,1600]{1,0:T(8,12...) custom-call(s32[128,128]{1,0:T(8,128)} %bitcast.30, ...), custom_call_target="tpu_custom_call" | custom-call | flops 1000000 | bytes 3072000 | tf_op jit(solution)/shard_map/prepare/pallas_call | solution.py:821
  13.2 0.0 copy-start
  13.2 0.0 copy-start.3
  13.2 0.0 copy-start.4
  13.3 0.0 copy-start.5
  13.3 0.0 copy-start.6
  13.3 0.0 copy-start.7
  13.3 3.3 %all-to-all-done = f32[32,4,128]{2,1,0:T(4,128)S(1)} async-done(((f32[32,4,128]{2,1,0:T(4,128)}), f32[32,4,128]{2,1,0:T(4,128)S(1)}, u32[]{:S(2)}, u32[]{:S(2)}) %all-to-all-start) | async-done | bytes 65568 | tf_op jit(solution)/shard_map/all_to_all | solution.py:788
  16.5 0.0 copy-start.1
  16.5 0.6 copy-done.1
  17.2 9.9 %centroids.1 = (f32[3,1,128]{2,1,0:T(1,128)}, f32[32,4,128]{2,1,0:T(4,128)}) custom-call(f32[4,8,4,128]{3,2,1,0:T(4,128)} %bitcast.25, s32[128,128]{1,0:T(8,128)} %get-tuple-element.21.codes, f32[256,16]{1,0:T(8,128)} %get-tuple-element.22.columns, bf16[64,96]{1,0:T(8,128)(2,1)} %get-tuple-element.23.second, bf16[128,192]{1,0:T(8,128)(2,1)} %get-tuple-element.24.third, ...), custom_call_target="tpu_custom_call" | custom-call | tf_op jit(solution)/shard_map/centroids/pallas_call | solution.py:849
  27.1 9.9 %all_to_all.15 = f32[32,4,128]{2,1,0:T(4,128)S(1)} all-to-all(f32[32,4,128]{2,1,0:T(4,128)} %get-tuple-element.32), channel_id=1, replica_groups=mesh['wide'=4,'narrow'=8] {'wide','narrow'}, dimensions={0} | all-to-all | bytes 131072 | tf_op jit(solution)/shard_map/all_to_all | solution.py:863
  37.0 0.0 copy-done
  37.0 0.0 copy-done.3
  37.0 0.0 copy-done.4
  37.0 0.0 copy-done.5
  37.0 0.0 copy-done.6
  37.0 0.0 copy-done.7
  37.1 0.0 copy-start.2
  37.1 0.8 %copy-done.2 = f32[32,4,128]{2,1,0:T(4,128)S(1)} copy-done((f32[32,4,128]{2,1,0:T(4,128)S(1)}, f32[32,4,128]{2,1,0:T(4,128)}, u32[]{:S(2)}) %copy-start.2) | copy-done | bytes 65560
  37.9 19.1 %mesh.1 = f32[4,8,1,1152]{3,2,1,0:T(1,128)S(1)} custom-call(f32[4,8,4,128]{3,2,1,0:T(4,128)S(1)} %bitcast.26, f32[4,8,4,128]{3,2,1,0:T(4,128)S(1)} %bitcast.27, f32[8,256]{1,0:T(8,128)S(1)} %copy-done.7, f32[5,256,256]{2,1,0:T(8,128)S(1)} %copy-done, bf16[256,256]{1,0:T(8,128)(2,1)S(1)} %copy-done.6, bf16[256,256]{1,0:T(8,128)(2,1)S(1)} %copy-done.5, ...), custom_call_target="tpu_custom_call" | custom-call | tf_op jit(solution)/shard_map/mesh/pallas_call | solution.py:870
  57.0 10.2 %all_to_all.16.arrived = f32[32,1,1152]{2,1,0:T(1,128)} all-to-all(f32[32,1,1152]{2,1,0:T(1,128)S(1)} %bitcast.24), channel_id=1, replica_groups=mesh['wide'=4,'narrow'=8] {'wide','narrow'}, dimensions={0} | all-to-all | bytes 294912 | tf_op jit(solution)/shard_map/all_to_all | solution.py:894
  67.2 1.5 %finish.1 = (f32[4,1,128]{2,1,0:T(1,128)}, f32[4,1,128]{2,1,0:T(1,128)}, f32[1,128]{1,0:T(1,128)}) custom-call(f32[32,1,1152]{2,1,0:T(1,128)} %all_to_all.16.arrived, s32[1,128]{1,0:T(1,128)} %bitcast.32), custom_call_target="tpu_custom_call" | custom-call | tf_op jit(solution)/shard_map/finish/pallas_call | solution.py:895
Async XLA Ops:
  2.0 14.6 %all-to-all-start = ((f32[32,4,128]{2,1,0:T(4,128)}), f32[32,4,128]{2,1,0:T(4,128)S(1)}, u32[]{:S(2)}, u32[]{:S(2)}) async-start(f32[32,4,128]{2,1,0:T(4,128)} %pack.1), calls=%async_computation | async-start | bytes 131072 | tf_op jit(solution)/shard_map/all_to_all | solution.py:788
  13.2 23.8 %copy-start = (f32[5,256,256]{2,1,0:T(8,128)S(1)}, f32[5,256,256]{2,1,0:T(8,128)}, u32[]{:S(2)}) copy-start(f32[5,256,256]{2,1,0:T(8,128)} %get-tuple-element.34.green_ref) | copy-start | bytes 3932164
  13.2 23.8 %copy-start.3 = (bf16[256,256]{1,0:T(8,128)(2,1)S(1)}, bf16[256,256]{1,0:T(8,128)(2,1)}, u32[]{:S(2)}) copy-start(bf16[256,256]{1,0:T(8,128)(2,1)} %constant.14.clone.unfold_low) | copy-start | bytes 393220
  13.2 23.8 %copy-start.4 = (bf16[256,256]{1,0:T(8,128)(2,1)S(1)}, bf16[256,256]{1,0:T(8,128)(2,1)}, u32[]{:S(2)}) copy-start(bf16[256,256]{1,0:T(8,128)(2,1)} %constant.13.clone.unfold_high) | copy-start | bytes 393220
  13.3 23.8 %copy-start.5 = (bf16[256,256]{1,0:T(8,128)(2,1)S(1)}, bf16[256,256]{1,0:T(8,128)(2,1)}, u32[]{:S(2)}) copy-start(bf16[256,256]{1,0:T(8,128)(2,1)} %constant.12.clone.fold_low) | copy-start | bytes 393220
  13.3 23.8 %copy-start.6 = (bf16[256,256]{1,0:T(8,128)(2,1)S(1)}, bf16[256,256]{1,0:T(8,128)(2,1)}, u32[]{:S(2)}) copy-start(bf16[256,256]{1,0:T(8,128)(2,1)} %constant.11.clone.fold_high) | copy-start | bytes 393220
  13.3 23.8 %copy-start.7 = (f32[8,256]{1,0:T(8,128)S(1)}, f32[8,256]{1,0:T(8,128)}, u32[]{:S(2)}) copy-start(f32[8,256]{1,0:T(8,128)} %get-tuple-element.33.phase) | copy-start | bytes 24580
  16.5 0.6 copy-start.1
  37.1 0.8 %copy-start.2 = (f32[32,4,128]{2,1,0:T(4,128)S(1)}, f32[32,4,128]{2,1,0:T(4,128)}, u32[]{:S(2)}) copy-start(f32[32,4,128]{2,1,0:T(4,128)} %copy-done.1) | copy-start | bytes 196612

commit v9 on v5

--- a/solution.py
+++ b/solution.py
@@ -22,6 +22,7 @@
 SLOT_CHUNK = 16
 HALO_X = 16
 HALO_Z = 8
+HALO_BITS = 16
 
 NN = (((1,), (0,)), ((), ()))
 NT = (((1,), (1,)), ((), ()))
@@ -38,6 +39,14 @@
         return lax.dot_general(a, b, dims, preferred_element_type=jnp.float32)
 
     return one(left[0], right[0]) + (one(left[1], right[0]) + one(left[0], right[1]))
+
+
+def skewed(waiting):
+    running = []
+    while waiting or running:
+        if waiting:
+            running.append(waiting.pop(0))
+        running = [one for one in running if next(one, running) is not running]
 
 
 def spline_pair(offset):
@@ -67,8 +76,10 @@
 
 
 def pack_kernel(positions, species, out_ref):
+    kinds = species[...]
     rows = [positions[component] for component in range(3)]
-    rows.append(species[...].astype(jnp.float32))
+    rows[0] = jnp.where(kinds > 0, -rows[0], rows[0])
+    rows.append(kinds.astype(jnp.float32))
     rows = jnp.concatenate(rows, axis=0)
     for target in range(out_ref.shape[0]):
         out_ref[target] = rows
@@ -238,17 +249,23 @@
     shift_ref,
     matrix,
     descriptor,
+    embedded_even,
+    embedded_odd,
     arrivals,
     *held,
 ):
-    sources = (one_high, one_low, two_high, two_low, three_high, three_low, fit_out_w)
+    sources = (table, codes, columns, second, third)
+    sources += (one_high, one_low, two_high, two_low, three_high, three_low, fit_out_w)
     copies = [
         pltpu.make_async_copy(source, target, arrivals.at[k])
         for k, (source, target) in enumerate(zip(sources, held))
     ]
     for copy in copies:
         copy.start()
-    one_high, one_low, two_high, two_low, three_high, three_low, fit_out_w = held
+    table, codes, columns, second, third = held[:5]
+    one_high, one_low, two_high, two_low, three_high, three_low, fit_out_w = held[5:]
+    for copy in copies[:5]:
+        copy.wait()
     wide_count, narrow_count, _, atoms = table.shape
     listed = codes.shape[0]
     width_three = fit_out_w.shape[0]
@@ -257,7 +274,7 @@
     cells = (GRID_X // wide_count, GRID_Y, GRID_Z // narrow_count)
     at_wide = lax.axis_index("wide")
     at_narrow = lax.axis_index("narrow")
-    own = table[at_wide, at_narrow]
+    own = jnp.abs(table[at_wide, at_narrow])
     nearby = []
     for step in range(9):
         wide_at = lax.rem(at_wide + (step // 3 - 1) + wide_count, wide_count)
@@ -272,7 +289,7 @@
     bias_hydrogen = jnp.broadcast_to(columns[0:ROW_PAD, 3:4], (ROW_PAD, atoms))
     matrix[...] = jnp.zeros_like(matrix)
 
-    def chunk(first):
+    def chunk(first, embedded):
         code = codes[pl.ds(first, SLOT_CHUNK), :]
         offset = code // atoms
         slot = code - offset * atoms
@@ -282,7 +299,7 @@
         step_y = rest - 3 * step_z
         brick = step_x * 3 + step_z
         found = []
-        for component in range(4):
+        for component in range(3):
             picked = jnp.zeros((SLOT_CHUNK, atoms), jnp.float32)
             for step in range(9):
                 row = jnp.broadcast_to(
@@ -291,6 +308,8 @@
                 here = jnp.take_along_axis(row, slot, axis=1, mode="promise_in_bounds")
                 picked = jnp.where(brick == step, here, picked)
             found.append(picked)
+        hydrogen = found[0] < 0.0
+        found[0] = jnp.abs(found[0])
         scaled = []
         for component, step in enumerate((step_x, step_y, step_z)):
             extent = float(cells[component])
@@ -302,45 +321,53 @@
             1.0 + (scaled[0] * scaled[0] + scaled[1] * scaled[1] + scaled[2] * scaled[2])
         )
         radial = [smooth] + [smooth * part for part in scaled]
-        hydrogen = found[3] > 0.5
-        first_layers = []
-        for k in range(SLOT_CHUNK):
-            row = smooth[k : k + 1]
-            kind = hydrogen[k : k + 1]
-            weight = jnp.where(kind, weight_hydrogen, weight_oxygen)
-            bias = jnp.where(kind, bias_hydrogen, bias_oxygen)
-            first_layers.append(jnp.tanh(weight * row + bias))
-        layer_one = jnp.concatenate(first_layers, axis=1)
-        high, low = split(layer_one)
-        layer_two = lax.dot_general(
-            second_all,
-            jnp.concatenate([high, low, high], axis=0),
-            NN,
-            preferred_element_type=jnp.float32,
-        )
-        layer_two = jnp.tanh(layer_two) + jnp.concatenate(
-            [layer_one, layer_one], axis=0
-        )
-        high, low = split(layer_two)
-        layer_three = lax.dot_general(
-            third_all,
-            jnp.concatenate([high, low, high], axis=0),
-            NN,
-            preferred_element_type=jnp.float32,
-        )
-        layer_three = jnp.tanh(layer_three) + jnp.concatenate(
-            [layer_two, layer_two], axis=0
-        )
-        for part in range(4):
-            total = matrix[part]
+        def slot_pair(k):
+            layers = []
+            for slot_at in (k, k + 1):
+                row = smooth[slot_at : slot_at + 1]
+                kind = hydrogen[slot_at : slot_at + 1]
+                weight = jnp.where(kind, weight_hydrogen, weight_oxygen)
+                bias = jnp.where(kind, bias_hydrogen, bias_oxygen)
+                layers.append(jnp.tanh(weight * row + bias))
+            layer = jnp.concatenate(layers, axis=1)
+            high, low = split(layer)
+            yield
+            given = lax.dot_general(
+                second_all,
+                jnp.concatenate([high, low, high], axis=0),
+                NN,
+                preferred_element_type=jnp.float32,
+            )
+            yield
+            layer = jnp.tanh(given) + jnp.concatenate([layer, layer], axis=0)
+            high, low = split(layer)
+            yield
+            given = lax.dot_general(
+                third_all,
+                jnp.concatenate([high, low, high], axis=0),
+                NN,
+                preferred_element_type=jnp.float32,
+            )
+            yield
+            embedded[:, k * atoms : (k + 2) * atoms] = jnp.tanh(given) + jnp.concatenate(
+                [layer, layer], axis=0
+            )
+
+        skewed([slot_pair(k) for k in range(0, SLOT_CHUNK, 2)])
+        for block in range(4):
+            lines = slice(block * ROW_PAD, (block + 1) * ROW_PAD)
+            totals = [matrix[part, lines, :] for part in range(4)]
             for k in range(SLOT_CHUNK):
-                total = total + layer_three[:, k * atoms : (k + 1) * atoms] * radial[part][k : k + 1]
-            matrix[part] = total
+                value = embedded[lines, k * atoms : (k + 1) * atoms]
+                for part in range(4):
+                    totals[part] = totals[part] + value * radial[part][k : k + 1]
+            for part in range(4):
+                matrix[part, lines, :] = totals[part]
 
     def two_chunks(index, carry):
         first = pl.multiple_of(index * (2 * SLOT_CHUNK), 2 * SLOT_CHUNK)
-        chunk(first)
-        chunk(pl.multiple_of(first + SLOT_CHUNK, SLOT_CHUNK))
+        chunk(first, embedded_even)
+        chunk(pl.multiple_of(first + SLOT_CHUNK, SLOT_CHUNK), embedded_odd)
         return carry
 
     lax.fori_loop(0, listed // (2 * SLOT_CHUNK), two_chunks, 0)
@@ -359,7 +386,7 @@
         for part in range(1, 4):
             total = total + parts[part][row : row + 1] * leading[part]
         descriptor[row * AXIS_COLUMNS : (row + 1) * AXIS_COLUMNS, :] = total
-    for copy in copies:
+    for copy in copies[5:]:
         copy.wait()
 
     def layer(high_ref, low_ref, given, column):
@@ -402,8 +429,8 @@
 
 def in_pairs(count, step):
     def both(index, carry):
-        step(2 * index, 0)
-        step(2 * index + 1, 1)
+        step(index, 0)
+        step(index, 1)
         return carry
 
     lax.fori_loop(0, count // 2, both, 0)
@@ -414,7 +441,7 @@
     extents = (GRID_X // wide_count, GRID_Y, GRID_Z // narrow_count)
     rows = [[], [], [], []]
     for at_wide in range(wide_count):
-        atom = table[at_wide, at_narrow]
+        atom = jnp.abs(table[at_wide, at_narrow])
         for component, extent in enumerate(extents):
             row = atom[component : component + 1] * float(extent)
             if shifts is not None:
@@ -435,7 +462,8 @@
     rows = phase.shape[0]
     grid[:, :, 0:HALO_Z, :] = jnp.zeros((copies, fine, HALO_Z, 2 * GRID_X), jnp.float32)
 
-    def spread(at_narrow, _):
+    def spread(index, odd):
+        at_narrow = 2 * index + odd
         row_x, row_y, row_z, charge = site_rows(table, shifts, at_narrow)
         lower = jnp.floor(row_y)
         back = lax.broadcasted_iota(jnp.int32, (8, 1), 0)
@@ -457,7 +485,7 @@
         wave = jnp.concatenate(wave_blocks, axis=1)
         waves[at_narrow] = wave
         wave_slopes[at_narrow] = jnp.concatenate(slope_blocks, axis=1)
-        splines_x(row_x, cells_x + HALO_X, weights.at[at_narrow], None)
+        splines_x(row_x, cells_x + HALO_X, weights[odd].at[index], None)
         value_z, _ = splines_z(row_z, window)
         weights_z[at_narrow] = value_z
         charged = wave * charge
@@ -468,7 +496,7 @@
             left = jnp.concatenate(
                 [near * charged[c : c + 1, lanes] for c in range(2 * fine)], axis=0
             )
-            across = weights[at_narrow, :, lanes]
+            across = weights[odd][index, :, lanes]
             total = lax.dot_general(
                 jnp.concatenate(split(left), axis=1),
                 jnp.concatenate([across, across], axis=1),
@@ -500,42 +528,52 @@
 HALVES = (slice(0, GRID_X), slice(GRID_X, 2 * GRID_X))
 
 
-def atoms_kernel(table, phase, planes, weights, weights_z, waves, wave_slopes, grid):
+def start_all(sources, targets, arrivals):
+    copies = [
+        pltpu.make_async_copy(source, target, arrivals.at[k])
+        for k, (source, target) in enumerate(zip(sources, targets))
+    ]
+    for copy in copies:
+        copy.start()
+    return copies
+
+
+def atoms_kernel(table, phase, *refs):
+    outs, (grid, leaving, planes_leaving), kept = refs[:6], refs[6:9], refs[9:]
+    planes, weights_even, weights_odd, weights_z, waves, wave_slopes = kept
     cells_x = GRID_X // table.shape[0]
-    spread_sites(table, None, phase, grid, weights, weights_z, waves, wave_slopes)
+    spread_sites(
+        table, None, phase, grid, (weights_even, weights_odd), weights_z, waves, wave_slopes
+    )
+    copies = start_all(kept[1:], outs[1:], leaving)
     for j in range(grid.shape[1]):
         for lanes in HALVES:
             planes[j, :, lanes] = joined(grid, j, lanes, cells_x)
-
-
-def mesh_kernel(
-    table,
-    shifts,
-    phase,
-    green_ref,
-    fold_high,
-    fold_low,
-    unfold_high,
-    unfold_low,
-    planes,
-    atom_weights,
-    atom_weights_z,
-    atom_waves,
-    atom_wave_slopes,
-    out_ref,
-    grid,
-    weights,
-    weights_z,
-    waves,
-    wave_slopes,
-    slopes,
-):
+        out = pltpu.make_async_copy(planes.at[j], outs[0].at[j], planes_leaving.at[j])
+        out.start()
+        copies.append(out)
+    for copy in copies:
+        copy.wait()
+
+
+def mesh_kernel(*refs):
+    sources, out_ref, refs = refs[:14], refs[14], refs[15:]
+    grid, packed, weights_even, weights_odd, weights_z, waves, wave_slopes = refs[:7]
+    slopes, arrivals = refs[7:9]
+    held = refs[9:]
+    arriving = start_all(sources, held, arrivals)
+    table, shifts, phase, planes, green_ref = held[:5]
+    fold_high, fold_low, unfold_high, unfold_low = held[5:9]
+    atom_weights = held[9:11]
+    atom_weights_z, atom_waves, atom_wave_slopes = held[11:]
+    weights = (weights_even, weights_odd)
     wide_count, narrow_count, _, atoms = table.shape
     cells_x = GRID_X // wide_count
     cells_z = GRID_Z // narrow_count
     window = cells_z + HALO_Z
     copies, fine = grid.shape[:2]
     channels = 2 * fine
+    reach = cells_x + HALO_X
     piece = lax.axis_index("wide") * narrow_count + lax.axis_index("narrow")
     lane_zero = lax.broadcasted_iota(jnp.int32, (1, GRID_X // 2), 1) == 0
     row_zero = lax.broadcasted_iota(jnp.int32, (GRID_Z // 2, 1), 0) == 0
@@ -546,10 +584,15 @@
     def unfold():
         return (unfold_high[...], unfold_low[...])
 
+    for copy in arriving[:3]:
+        copy.wait()
     spread_sites(table, shifts, phase, grid, weights, weights_z, waves, wave_slopes)
-
-    def whole(j):
-        return [planes[j, :, lanes] + joined(grid, j, lanes, cells_x) for lanes in HALVES]
+    for copy in arriving[3:9]:
+        copy.wait()
+
+    for j in range(fine):
+        for lanes in HALVES:
+            planes[j, :, lanes] += joined(grid, j, lanes, cells_x)
 
     is_first = piece == 0
 
@@ -590,45 +633,76 @@
         ]
         return jnp.concatenate(real, axis=axis), jnp.concatenate(imag, axis=axis)
 
-    def to_modes(real, imag, j):
-        real = multiply(split(real), fold())
-        if imag is not None:
-            imag = multiply(split(imag), fold())
+    modes = {}
+    parts = []
+
+    def slot(j):
+        first_imag = planes[0, :, GRID_X:]
+        if j == fine:
+            real, imag = jnp.where(is_first, first_imag, 0.0), None
+        else:
+            real, imag = planes[j, :, 0:GRID_X], planes[j, :, GRID_X:]
+            if j == 0:
+                imag = jnp.where(is_first, 0.0, imag)
+        real = split(real)
+        imag = None if imag is None else split(imag)
+        yield
+        real = multiply(real, fold())
+        imag = None if imag is None else multiply(imag, fold())
+        yield
         real, imag = paired(real, imag, lane_zero, 1)
-        real = multiply(unfold(), split(real))
-        imag = multiply(unfold(), split(imag))
+        real, imag = split(real), split(imag)
+        yield
+        real, imag = multiply(unfold(), real), multiply(unfold(), imag)
+        yield
         real, imag = paired(real, imag, row_zero, 0)
         green = green_ref[j]
         mode = GRID_Y // 2 if j == fine else piece * fine + j
         share = jnp.where((mode == 0) | (mode == GRID_Y // 2), 0.5, 1.0)
-        part = jnp.sum(green * (real * real + imag * imag), axis=0, keepdims=True)
-        return green * real, green * imag, share * part
-
-    first_real, first_imag = whole(0)
-    last_real, last_imag, energy = to_modes(jnp.where(is_first, first_imag, 0.0), None, fine)
-    for j in range(fine):
+        parts.append(share * jnp.sum(green * (real * real + imag * imag), axis=0, keepdims=True))
+        real, imag = green * real, green * imag
+        if j == fine:
+            modes[j] = (real, imag)
+            return
         if j == 0:
-            real, imag = first_real, jnp.where(is_first, 0.0, first_imag)
-        else:
-            real, imag = whole(j)
-        real, imag, part = to_modes(real, imag, j)
-        energy = energy + part
-        if j == 0:
-            real, imag = real - last_imag, imag + last_real
+            real, imag = real - modes[fine][1], imag + modes[fine][0]
         real, imag = merged(real, imag, row_zero, 0)
-        real = multiply(fold(), split(real))
-        imag = multiply(fold(), split(imag))
+        real, imag = split(real), split(imag)
+        yield
+        real, imag = multiply(fold(), real), multiply(fold(), imag)
+        yield
         real, imag = merged(real, imag, lane_zero, 1)
         scale = jnp.where(piece * fine + j == 0, 1.0, 2.0)
-        for part, lanes in zip((real, imag), HALVES):
-            part = multiply(split(part * scale), unfold())
-            for k in range(copies):
-                moved = pltpu.roll(part, (HALO_X - k * cells_x) % GRID_X, 1)
-                grid[k, j, HALO_Z:, lanes] = moved
-                grid[k, j, 0:HALO_Z, lanes] = moved[GRID_Z - HALO_Z :]
+        real, imag = split(real * scale), split(imag * scale)
+        yield
+        real, imag = multiply(real, unfold()), multiply(imag, unfold())
+        yield
+        for k, part in enumerate((real, imag)):
+            for at_wide in range(wide_count):
+                moved = pltpu.roll(part, (HALO_X - at_wide * cells_x) % GRID_X, 1)[:, 0:128]
+                high = moved.astype(jnp.bfloat16).astype(jnp.float32)
+                again = pltpu.roll(high, reach % 128, 1)
+                low = pltpu.roll(moved - high, 2 * reach % 128, 1)
+                sides = []
+                for side in range(2):
+                    lane = lax.broadcasted_iota(jnp.int32, (1, 128), 1) + side * 128
+                    value = jnp.where(lane < 2 * reach, again, low)
+                    if side == 0:
+                        value = jnp.where(lane < reach, high, value)
+                    sides.append(value.astype(jnp.bfloat16))
+                block = jnp.concatenate(sides, axis=1)
+                packed[at_wide, 2 * j + k, HALO_BITS:, :] = block
+                packed[at_wide, 2 * j + k, 0:HALO_BITS, :] = block[GRID_Z - HALO_BITS :]
+
+    skewed([slot(j) for j in [fine, *range(fine)]])
+    energy = sum(parts[1:], parts[0])
     energy = jnp.broadcast_to(jnp.sum(energy, axis=1, keepdims=True), (1, 128))
 
-    def collect(at_narrow, buffer):
+    for copy in arriving[9:]:
+        copy.wait()
+
+    def collect(index, odd):
+        at_narrow = 2 * index + odd
         kinds = (
             (None, atom_weights, atom_weights_z, atom_waves, atom_wave_slopes),
             (shifts, weights, weights_z, waves, wave_slopes),
@@ -636,37 +710,30 @@
         slopes_z = []
         for kind, given in enumerate(kinds):
             row_x, _, row_z, _ = site_rows(table, given[0], at_narrow)
-            splines_x(row_x, cells_x + HALO_X, None, slopes.at[buffer, kind])
+            splines_x(row_x, cells_x + HALO_X, None, slopes.at[odd, kind])
             slopes_z.append(splines_z(row_z, window)[1])
-        first = pl.multiple_of(at_narrow * cells_z, HALO_Z)
-        lefts = []
-        for k in range(copies):
-            left = jnp.concatenate(
-                [
-                    grid[k, c // 2, pl.ds(first, window), HALVES[c % 2]]
-                    for c in range(channels)
-                ],
-                axis=0,
-            )
-            lefts.append(split(left))
+        first = pl.multiple_of(at_narrow * cells_z, HALO_BITS)
+        tall = cells_z + HALO_BITS
         for at_wide in range(wide_count):
             lanes = slice(at_wide * atoms, (at_wide + 1) * atoms)
-            start = at_wide // copies * 128
-            high = lefts[at_wide % copies][0][:, start : start + 128]
-            low = lefts[at_wide % copies][1][:, start : start + 128]
-            twice = jnp.concatenate([high, high], axis=1)
+            left = jnp.concatenate(
+                [packed[at_wide, c, pl.ds(first, tall), :] for c in range(channels)], axis=0
+            )
 
             def across(right):
-                return lax.dot_general(
-                    twice, right, NN, preferred_element_type=jnp.float32
-                ) + lax.dot_general(low, right[0:128], NN, preferred_element_type=jnp.float32)
-
-            def both(index):
-                return jnp.concatenate([given[index][at_narrow, :, lanes] for given in kinds], axis=1)
-
-            value = across(both(1))
+                high = right[0:reach]
+                rest = jnp.zeros((256 - 3 * reach, 2 * atoms), jnp.bfloat16)
+                right = jnp.concatenate([high, right[128 : 128 + reach], high, rest], axis=0)
+                return lax.dot_general(left, right, NN, preferred_element_type=jnp.float32)
+
+            def both(which):
+                return jnp.concatenate([given[which][at_narrow, :, lanes] for given in kinds], axis=1)
+
+            value = across(
+                jnp.concatenate([given[1][odd][index, :, lanes] for given in kinds], axis=1)
+            )
             slope = across(
-                jnp.concatenate([slopes[buffer, kind, :, lanes] for kind in range(2)], axis=1)
+                jnp.concatenate([slopes[odd, kind, :, lanes] for kind in range(2)], axis=1)
             )
             near = both(2)
             near_slope = jnp.concatenate([row[:, lanes] for row in slopes_z], axis=1)
@@ -676,7 +743,7 @@
             along_x = plain
             along_y = plain
             for c in range(channels):
-                block = slice(c * window, (c + 1) * window)
+                block = slice((c + 1) * tall - window, (c + 1) * tall)
                 plain = plain + value[block] * wave[c : c + 1]
                 along_x = along_x + slope[block] * wave[c : c + 1]
                 along_y = along_y + value[block] * wave_slope[c : c + 1]
@@ -844,21 +911,23 @@
         name="prepare",
     )(*arguments)
     phase, green = prepared[10:]
-    fitted = (*prepared[4:10], fit_out_w.T)
+    fitted = (table, *prepared[:10], fit_out_w.T)
     dipole, shifts = pl.pallas_call(
         centroid_kernel,
         out_shape=(shaped((3, 1, atoms)), shaped((pieces, 4, atoms))),
-        in_specs=vmem(5) + hbm(7),
+        in_specs=hbm(12),
         out_specs=tuple(vmem(2)),
         scratch_shapes=[
             pltpu.VMEM((4, tall, atoms), jnp.float32),
             pltpu.VMEM((width_three * AXIS_COLUMNS, atoms), jnp.float32),
+            pltpu.VMEM((tall, SLOT_CHUNK * atoms), jnp.float32),
+            pltpu.VMEM((tall, SLOT_CHUNK * atoms), jnp.float32),
             pltpu.SemaphoreType.DMA((len(fitted),)),
         ]
         + [pltpu.VMEM(array.shape, array.dtype) for array in fitted],
         compiler_params=limits(62),
         name="centroids",
-    )(table, *prepared[:4], *fitted)
+    )(*fitted)
     shifts = lax.all_to_all(shifts, axes, 0, 0, tiled=True)
     shifts = shifts.reshape(wide_count, narrow_count, 4, atoms)
 
@@ -866,19 +935,26 @@
     window = GRID_Z // narrow_count + HALO_Z
     length = wide_count * atoms
     grid = pltpu.VMEM((copies, fine, HALO_Z + GRID_Z, 2 * GRID_X), jnp.float32)
+    planes = shaped((fine, GRID_Z, 2 * GRID_X))
     kept = (
-        shaped((narrow_count, 256, length), bf16),
+        shaped((narrow_count // 2, 256, length), bf16),
+        shaped((narrow_count // 2, 256, length), bf16),
         shaped((narrow_count, window, length)),
         shaped((narrow_count, wave_rows, length)),
         shaped((narrow_count, wave_rows, length)),
     )
     spread_atoms = pl.pallas_call(
         atoms_kernel,
-        out_shape=(shaped((fine, GRID_Z, 2 * GRID_X)),) + kept,
+        out_shape=(planes,) + kept,
         in_specs=vmem(2),
-        out_specs=tuple(vmem(5)),
-        scratch_shapes=[grid],
-        compiler_params=limits(24),
+        out_specs=tuple(hbm(6)),
+        scratch_shapes=[
+            grid,
+            pltpu.SemaphoreType.DMA((len(kept),)),
+            pltpu.SemaphoreType.DMA((fine,)),
+        ]
+        + [pltpu.VMEM(array.shape, array.dtype) for array in (planes,) + kept],
+        compiler_params=limits(62),
         cost_estimate=pl.CostEstimate(
             flops=2 * 3 * pieces * atoms * 2 * fine * window * 128,
             bytes_accessed=8 * 1024 * 1024,
@@ -888,17 +964,23 @@
     )(table, phase)
     out_width = 8 * atoms + 128
     tables = halves(fold_table(GRID_X)) + halves(fold_table(GRID_X).T)
+    tables = [jnp.asarray(half) for half in tables]
+    given = (table, shifts, phase, spread_atoms[0], green, *tables, *spread_atoms[1:])
     partial = pl.pallas_call(
         mesh_kernel,
         out_shape=shaped((wide_count, narrow_count, 1, out_width)),
-        in_specs=vmem(13),
+        in_specs=hbm(len(given)),
         out_specs=vmem(1)[0],
-        scratch_shapes=[grid]
+        scratch_shapes=[
+            grid,
+            pltpu.VMEM((wide_count, 2 * fine, HALO_BITS + GRID_Z, 256), bf16),
+        ]
         + [pltpu.VMEM(array.shape, array.dtype) for array in kept]
-        + [pltpu.VMEM((2, 2, 256, length), bf16)],
-        compiler_params=limits(36),
+        + [pltpu.VMEM((2, 2, 256, length), bf16), pltpu.SemaphoreType.DMA((len(given),))]
+        + [pltpu.VMEM(array.shape, array.dtype) for array in given],
+        compiler_params=limits(62),
         name="mesh",
-    )(table, shifts, phase, green, *[jnp.asarray(half) for half in tables], *spread_atoms)
+    )(*given)
     arrived = lax.all_to_all(partial.reshape(pieces, 1, out_width), axes, 0, 0, tiled=True)
     atom_field, centroid_field, energy = pl.pallas_call(
         finish_kernel,

time: 81.2 us -> 71.4 us (0.88)
  local copies, waits for them, and re-layouts: 13.1 us -> 1.24 us
  Pallas kernels: 40 us -> 42.1 us
    unnamed x34 -> x4, local copies, waits for them, and re-layouts: 13.1 us -> 1.24 us
    pallas_call x1, Pallas kernels: 5.02 us -> 6.94 us  [local(): pl.pallas_call(atoms_kernel, out_shape=(planes,) + kept, in_specs=vmem(2)...]
    pallas_call x1, Pallas kernels: 9.86 us -> 10.9 us  [local(): pl.pallas_call(centroid_kernel, out_shape=(shaped((3, 1, atoms)), shaped(...]
    pallas_call x1, Pallas kernels: 18.3 us -> 17.5 us  [local(): pl.pallas_call(mesh_kernel, out_shape=shaped((wide_count, narrow_count, 1...]
  transfers between devices with their start and end apart: 2 -> 2, of which waited for: 1 -> 2; matrix products, arithmetic and copies ran while one was open for 0% -> 0% of each run, Pallas kernels for 11% -> 15%
where the time goes in v9:
time: 71.4 us; the launch traced here: 71 us
  Pallas kernels  42.1 us (59%)
  blocking collectives  13.5 us (19%)
  starting transfers between devices  10 us (14%)
  waiting for transfers between devices  3.52 us (5%)
  local copies, waits for them, and re-layouts  1.24 us (2%)
    pallas_call x1, Pallas kernels, local(): pl.pallas_call(mesh_kernel, out_shape=shaped((wide_count, narrow_count, 1...  17.5 us
    all_to_all x1, blocking collectives, local(): lax.all_to_all(partial.reshape(pieces, 1, out_width), axes, 0, 0, tiled=T...  13.5 us
    pallas_call x1, Pallas kernels, local(): pl.pallas_call(centroid_kernel, out_shape=(shaped((3, 1, atoms)), shaped(...  10.9 us
    all_to_all x1, starting transfers between devices, local(): table = lax.all_to_all(packed, axes, 0, 0, tiled=True)  7.3 us
    pallas_call x1, Pallas kernels, local(): pl.pallas_call(atoms_kernel, out_shape=(planes,) + kept, in_specs=vmem(2)...  6.94 us
    pallas_call x1, Pallas kernels, local(): pl.pallas_call(prepare_kernel, out_shape=(shaped((listed, atoms), jnp.int...  3.89 us
    all_to_all x1, waiting for transfers between devices, local(): table = lax.all_to_all(packed, axes, 0, 0, tiled=True)  3.37 us
    all_to_all x1, starting transfers between devices, local(): shifts = lax.all_to_all(shifts, axes, 0, 0, tiled=True)  2.75 us
  transfers between devices with their start and end apart: 2, of which 2 were waited for; matrix products, arithmetic and copies ran while one was open for 0% of the time, Pallas kernels for 15%

profile of v9, /device:TPU:0, one launch (start us, length us, event | category | flops | bytes accessed | tf_op | source)
XLA Modules:
  0.0 71.0 jit_solution(5344416544236621283)
XLA Ops:
  0.6 1.3 %pack.1 = f32[32,4,128]{2,1,0:T(4,128)} custom-call(f32[3,1,128]{2,1,0:T(1,128)} %bitcast.34, s32[1,128]{1,0:T(1,128)} %bitcast.32), custom_call_target="tpu_custom_call" | custom-call | tf_op jit(solution)/shard_map/pack/pallas_call | solution.py:847
  1.9 7.3 %all-to-all-start = ((f32[32,4,128]{2,1,0:T(4,128)}), f32[32,4,128]{2,1,0:T(4,128)S(1)}, u32[]{:S(2)}, u32[]{:S(2)}) async-start(f32[32,4,128]{2,1,0:T(4,128)} %pack.1), calls=%async_computation | async-start | bytes 131072 | tf_op jit(solution)/shard_map/all_to_all | solution.py:854
  9.3 3.9 %prepare.1 = (s32[128,128]{1,0:T(8,128)}, f32[256,16]{1,0:T(8,128)}, bf16[64,96]{1,0:T(8,128)(2,1)}, bf16[128,192]{1,0:T(8,128)(2,1)}, bf16[240,1600]{1,0:T(8,12...) custom-call(s32[128,128]{1,0:T(8,128)} %bitcast.31, ...), custom_call_target="tpu_custom_call" | custom-call | flops 1000000 | bytes 3072000 | tf_op jit(solution)/shard_map/prepare/pallas_call | solution.py:887
  13.2 3.4 %all-to-all-done = f32[32,4,128]{2,1,0:T(4,128)S(1)} async-done(((f32[32,4,128]{2,1,0:T(4,128)}), f32[32,4,128]{2,1,0:T(4,128)S(1)}, u32[]{:S(2)}, u32[]{:S(2)}) %all-to-all-start) | async-done | bytes 65568 | tf_op jit(solution)/shard_map/all_to_all | solution.py:854
  16.5 0.0 copy-start
  16.5 0.6 copy-done
  17.2 10.9 %centroids.1 = (f32[3,1,128]{2,1,0:T(1,128)}, f32[32,4,128]{2,1,0:T(4,128)}) custom-call(f32[4,8,4,128]{3,2,1,0:T(4,128)} %bitcast.25, s32[128,128]{1,0:T(8,128)} %get-tuple-element.27.codes, f32[256,16]{1,0:T(8,128)} %get-tuple-element.28.columns, bf16[64,96]{1,0:T(8,128)(2,1)} %get-tuple-element.29.second, bf16[128,192]{1,0:T(8,128)(2,1)} %get-tuple-element.30.third, ...), custom_call_target="tpu_custom_call" | custom-call | tf_op jit(solution)/shard_map/centroids/pallas_call | solution.py:915
  28.1 2.8 %all-to-all-start.1 = ((f32[32,4,128]{2,1,0:T(4,128)}), f32[32,4,128]{2,1,0:T(4,128)S(1)}, u32[]{:S(2)}, u32[]{:S(2)}) async-start(f32[32,4,128]{2,1,0:T(4,128)} %get-tuple-element.38), calls=%async_computation.1 | async-start | bytes 131072 | tf_op jit(solution)/shard_map/all_to_all | solution.py:931
  30.8 6.9 %atoms.1 = (f32[4,256,512]{2,1,0:T(8,128)}, bf16[4,256,512]{2,1,0:T(8,128)(2,1)}, bf16[4,256,512]{2,1,0:T(8,128)(2,1)}, f32[8,40,512]{2,1,0:T(8,128)}, f32[8,8,512]{2,1,0:T(8,128)}, /*index=5*/f32[8,8,512]{2,1,0:T(8,128)}) custom-call(f32[4,8,4,128]{3,2,1,0:T(4,128)} %bitcast.26, f32[8,256]{1,0:T(8,128)} %get-tuple-element.39.phase.refs_2_), custom_call_target="tpu_custom_call" | custom-call | flops 1006632960 | bytes 8388608 | tf_op jit(solution)/shard_map/atoms/pallas_call | solution.py:946
  37.8 0.1 all-to-all-done.1
  37.9 0.0 copy-start.1
  37.9 0.6 copy-done.1
  38.5 17.5 %mesh.1 = f32[4,8,1,1152]{3,2,1,0:T(1,128)} custom-call(f32[4,8,4,128]{3,2,1,0:T(4,128)} %bitcast.27, f32[4,8,4,128]{3,2,1,0:T(4,128)} %bitcast.29, f32[8,256]{1,0:T(8,128)} %get-tuple-element.39.phase.refs_2_, f32[4,256,512]{2,1,0:T(8,128)} %get-tuple-element.40.refs_3_, f32[5,256,256]{2,1,0:T(8,128)} %get-tuple-element.41.refs_4_, ...), custom_call_target="tpu_custom_call" | custom-call | tf_op jit(solution)/shard_map/mesh/pallas_call | solution.py:969
  56.0 13.5 %all_to_all.15.arrived = f32[32,1,1152]{2,1,0:T(1,128)} all-to-all(f32[32,1,1152]{2,1,0:T(1,128)} %bitcast.28), channel_id=1, replica_groups=mesh['wide'=4,'narrow'=8] {'wide','narrow'}, dimensions={0} | all-to-all | bytes 294912 | tf_op jit(solution)/shard_map/all_to_all | solution.py:984
  69.5 1.5 %finish.1 = (f32[4,1,128]{2,1,0:T(1,128)}, f32[4,1,128]{2,1,0:T(1,128)}, f32[1,128]{1,0:T(1,128)}) custom-call(f32[32,1,1152]{2,1,0:T(1,128)} %all_to_all.15.arrived, s32[1,128]{1,0:T(1,128)} %bitcast.33), custom_call_target="tpu_custom_call" | custom-call | tf_op jit(solution)/shard_map/finish/pallas_call | solution.py:985
Async XLA Ops:
  1.9 14.6 %all-to-all-start = ((f32[32,4,128]{2,1,0:T(4,128)}), f32[32,4,128]{2,1,0:T(4,128)S(1)}, u32[]{:S(2)}, u32[]{:S(2)}) async-start(f32[32,4,128]{2,1,0:T(4,128)} %pack.1), calls=%async_computation | async-start | bytes 131072 | tf_op jit(solution)/shard_map/all_to_all | solution.py:854
  16.5 0.6 copy-start
  28.1 9.9 %all-to-all-start.1 = ((f32[32,4,128]{2,1,0:T(4,128)}), f32[32,4,128]{2,1,0:T(4,128)S(1)}, u32[]{:S(2)}, u32[]{:S(2)}) async-start(f32[32,4,128]{2,1,0:T(4,128)} %get-tuple-element.38), calls=%async_computation.1 | async-start | bytes 131072 | tf_op jit(solution)/shard_map/all_to_all | solution.py:931
  37.9 0.6 copy-start.1

commit v10 on v8

--- a/solution.py
+++ b/solution.py
@@ -39,6 +39,22 @@
         return lax.dot_general(a, b, dims, preferred_element_type=jnp.float32)
 
     return one(left[0], right[0]) + (one(left[1], right[0]) + one(left[0], right[1]))
+
+
+def by_right(left, right):
+    rows = left[0].shape[0]
+    both = lax.dot_general(
+        jnp.concatenate(left, axis=0), right[0], NN, preferred_element_type=jnp.float32
+    )
+    rest = lax.dot_general(left[0], right[1], NN, preferred_element_type=jnp.float32)
+    return both[:rows] + (both[rows:] + rest)
+
+
+def by_left(left, right):
+    rows = left.shape[0] // 2
+    both = lax.dot_general(left, right[0], NN, preferred_element_type=jnp.float32)
+    rest = lax.dot_general(left[:rows], right[1], NN, preferred_element_type=jnp.float32)
+    return both[:rows] + (both[rows:] + rest)
 
 
 def spline_pair(offset):
@@ -395,18 +411,18 @@
     shifts,
     phase,
     green_ref,
-    fold_high,
-    fold_low,
-    unfold_high,
-    unfold_low,
+    fold_stack,
+    unfold_stack,
     out_ref,
     grid,
     planes,
     packed,
     weights_even,
     weights_odd,
-    slopes,
+    slopes_even,
+    slopes_odd,
     weights_z,
+    slopes_z,
     waves,
     wave_slopes,
 ):
@@ -428,10 +444,10 @@
     row_zero = lax.broadcasted_iota(jnp.int32, (half_z, 1), 0) == 0
 
     def fold():
-        return (fold_high[...], fold_low[...])
+        return (fold_stack[0:GRID_X, :], fold_stack[GRID_X:, :])
 
     def unfold():
-        return (unfold_high[...], unfold_low[...])
+        return (unfold_stack[0:GRID_X, :], unfold_stack[GRID_X:, :])
 
     def sites(at_wide, at_narrow):
         atom = jnp.abs(table[at_wide, at_narrow])
@@ -457,16 +473,16 @@
         both = spline_pair(row - (counter - float(HALO_X)))
         rest = jnp.zeros((128 - reach, length), jnp.bfloat16)
         for values, ref in zip(both, targets):
-            if ref is not None:
-                high, low = split(values)
-                ref[0:reach, :] = high
-                ref[reach:128, :] = rest
-                ref[128 : 128 + reach, :] = low
-                ref[128 + reach : 256, :] = rest
+            high, low = split(values)
+            ref[0:reach, :] = high
+            ref[reach:128, :] = rest
+            ref[128 : 128 + reach, :] = low
+            ref[128 + reach : 256, :] = rest
 
     grid[:, :, 0:HALO_Z, :] = jnp.zeros((copies, fine, HALO_Z, 2 * GRID_X), jnp.float32)
 
     weights = (weights_even, weights_odd)
+    slopes = (slopes_even, slopes_odd)
 
     def spread(index, odd):
         at_narrow = 2 * index + odd
@@ -491,9 +507,10 @@
         wave = jnp.concatenate(wave_blocks, axis=1)
         waves[at_narrow] = wave
         wave_slopes[at_narrow] = jnp.concatenate(slope_blocks, axis=1)
-        fill_x(row_x, (weights[odd].at[index], None))
-        value_z, _ = splines_z(row_z)
+        fill_x(row_x, (weights[odd].at[index], slopes[odd].at[index]))
+        value_z, slope_z = splines_z(row_z)
         weights_z[at_narrow] = value_z
+        slopes_z[at_narrow] = slope_z
         charged = wave * charge
         first = pl.multiple_of(at_narrow * cells_z, HALO_Z)
         for at_wide in range(wide_count):
@@ -502,13 +519,14 @@
             left = jnp.concatenate(
                 [near * charged[c : c + 1, lanes] for c in range(channels)], axis=0
             )
-            high, low = split(left)
-            across = weights[odd][index, :, lanes]
-            total = lax.dot_general(high, across, NT, preferred_element_type=jnp.float32)
-            total = total[:, 0:128] + (
-                total[:, 128:256]
-                + lax.dot_general(low, across[0:128], NT, preferred_element_type=jnp.float32)
+            total = lax.dot_general(
+                jnp.concatenate(split(left), axis=0),
+                weights[odd][index, :, lanes],
+                NT,
+                preferred_element_type=jnp.float32,
             )
+            tall = channels * window
+            total = total[:tall, 0:128] + (total[:tall, 128:256] + total[tall:, 0:128])
             start = at_wide // copies * 128
             for c in range(channels):
                 spot = slice(c % 2 * GRID_X + start, c % 2 * GRID_X + start + 128)
@@ -591,13 +609,13 @@
         real = split(real)
         imag = None if imag is None else split(imag)
         yield
-        real = multiply(real, fold())
-        imag = None if imag is None else multiply(imag, fold())
+        real = by_right(real, fold())
+        imag = None if imag is None else by_right(imag, fold())
         yield
         real, imag = paired(real, imag, lane_zero, 1)
         real, imag = split(real), split(imag)
         yield
-        real, imag = multiply(unfold(), real), multiply(unfold(), imag)
+        real, imag = by_left(unfold_stack[...], real), by_left(unfold_stack[...], imag)
         yield
         real, imag = paired(real, imag, row_zero, 0)
         green = green_ref[j]
@@ -613,13 +631,13 @@
         real, imag = merged(real, imag, row_zero, 0)
         real, imag = split(real), split(imag)
         yield
-        real, imag = multiply(fold(), real), multiply(fold(), imag)
+        real, imag = by_left(fold_stack[...], real), by_left(fold_stack[...], imag)
         yield
         real, imag = merged(real, imag, lane_zero, 1)
         scale = jnp.where(piece * fine + j == 0, 1.0, 2.0)
         real, imag = split(real * scale), split(imag * scale)
         yield
-        real, imag = multiply(real, unfold()), multiply(imag, unfold())
+        real, imag = by_right(real, unfold()), by_right(imag, unfold())
         yield
         for k, part in enumerate((real, imag)):
             for at_wide in range(wide_count):
@@ -649,10 +667,8 @@
 
     def collect(index, odd):
         at_narrow = 2 * index + odd
-        row_x, _, row_z, _ = line(at_narrow)
-        fill_x(row_x, (None, slopes.at[odd]))
         value_z = weights_z[at_narrow]
-        _, slope_z = splines_z(row_z)
+        slope_z = slopes_z[at_narrow]
         first = pl.multiple_of(at_narrow * cells_z, HALO_BITS)
         wave = waves[at_narrow]
         wave_slope = wave_slopes[at_narrow]
@@ -670,7 +686,7 @@
                 return lax.dot_general(left, right, NN, preferred_element_type=jnp.float32)
 
             value = across(weights[odd][index, :, lanes])
-            slope = across(slopes[odd, :, lanes])
+            slope = across(slopes[odd][index, :, lanes])
             plain = jnp.zeros((window, pair), jnp.float32)
             along_x = plain
             along_y = plain
@@ -870,16 +886,15 @@
     partial = pl.pallas_call(
         mesh_kernel,
         out_shape=shaped((wide_count, narrow_count, 1, out_width)),
-        in_specs=vmem(8),
+        in_specs=vmem(6),
         out_specs=vmem(1)[0],
         scratch_shapes=[
             pltpu.VMEM((copies, fine, HALO_Z + GRID_Z, 2 * GRID_X), jnp.float32),
             pltpu.VMEM((fine, GRID_Z, 2 * GRID_X), jnp.float32),
             pltpu.VMEM((wide_count, 2 * fine, HALO_BITS + GRID_Z, 256), bf16),
         ]
-        + [pltpu.VMEM((narrow_count // 2, 256, length), bf16)] * 2
-        + [pltpu.VMEM((2, 256, length), bf16)]
-        + [pltpu.VMEM((narrow_count, GRID_Z // narrow_count + HALO_Z, length), jnp.float32)]
+        + [pltpu.VMEM((narrow_count // 2, 256, length), bf16)] * 4
+        + [pltpu.VMEM((narrow_count, GRID_Z // narrow_count + HALO_Z, length), jnp.float32)] * 2
         + [pltpu.VMEM((narrow_count, wave_rows, length), jnp.float32)] * 2,
         compiler_params=limits(48),
         name="mesh",
@@ -888,8 +903,8 @@
         shifts,
         phase,
         green,
-        *[jnp.asarray(half) for half in halves(fold_table(GRID_X))],
-        *[jnp.asarray(half) for half in halves(fold_table(GRID_X).T)],
+        jnp.asarray(np.concatenate(halves(fold_table(GRID_X)))),
+        jnp.asarray(np.concatenate(halves(fold_table(GRID_X).T))),
     )
     arrived = lax.all_to_all(partial.reshape(pieces, 1, out_width), axes, 0, 0, tiled=True)
     atom_field, centroid_field, energy = pl.pallas_call(

time: 69.1 us -> 69.1 us (level)
    unnamed x16 -> x12, local copies, waits for them, and re-layouts: 1.5 us -> 1.47 us
where the time goes in v10:
time: 69.1 us; the launch traced here: 68.7 us
  Pallas kernels  35.9 us (52%)
  blocking collectives  20.1 us (29%)
  starting transfers between devices  7.3 us (11%)
  waiting for transfers between devices  3.29 us (5%)
  local copies, waits for them, and re-layouts  1.47 us (2%)
  between operations  0.72 us (1%)
    pallas_call x1, Pallas kernels, local(): pl.pallas_call(mesh_kernel, out_shape=shaped((wide_count, narrow_count, 1...  19.1 us
    all_to_all x1, blocking collectives, local(): lax.all_to_all(partial.reshape(pieces, 1, out_width), axes, 0, 0, tiled=T...  10.2 us
    pallas_call x1, Pallas kernels, local(): pl.pallas_call(centroid_kernel, out_shape=(shaped((3, 1, atoms)), shaped(...  9.96 us
    all_to_all x1, blocking collectives, local(): shifts = lax.all_to_all(shifts, axes, 0, 0, tiled=True)  9.85 us
    all_to_all x1, starting transfers between devices, local(): table = lax.all_to_all(packed, axes, 0, 0, tiled=True)  7.3 us
    pallas_call x1, Pallas kernels, local(): pl.pallas_call(prepare_kernel, out_shape=(shaped((listed, atoms), jnp.int...  3.94 us
    all_to_all x1, waiting for transfers between devices, local(): table = lax.all_to_all(packed, axes, 0, 0, tiled=True)  3.29 us
    pallas_call x1, Pallas kernels, local(): pl.pallas_call(finish_kernel, out_shape=(shaped((4, 1, atoms)), shaped((4...  1.53 us
  transfers between devices with their start and end apart: 1, of which 1 were waited for; matrix products, arithmetic and copies ran while one was open for 0% of the time, Pallas kernels for 6%

profile of v10, /device:TPU:0, one launch (start us, length us, event | category | flops | bytes accessed | tf_op | source)
XLA Modules:
  0.0 68.7 jit_solution(15776817404294264292)
XLA Ops:
  0.6 1.3 %pack.1 = f32[32,4,128]{2,1,0:T(4,128)} custom-call(f32[3,1,128]{2,1,0:T(1,128)} %bitcast.33, s32[1,128]{1,0:T(1,128)} %bitcast.31), custom_call_target="tpu_custom_call" | custom-call | tf_op jit(solution)/shard_map/pack/pallas_call | solution.py:797
  1.9 7.3 %all-to-all-start = ((f32[32,4,128]{2,1,0:T(4,128)}), f32[32,4,128]{2,1,0:T(4,128)S(1)}, u32[]{:S(2)}, u32[]{:S(2)}) async-start(f32[32,4,128]{2,1,0:T(4,128)} %pack.1), calls=%async_computation | async-start | bytes 131072 | tf_op jit(solution)/shard_map/all_to_all | solution.py:804
  9.3 3.9 %prepare.1 = (s32[128,128]{1,0:T(8,128)}, f32[256,16]{1,0:T(8,128)}, bf16[64,96]{1,0:T(8,128)(2,1)}, bf16[128,192]{1,0:T(8,128)(2,1)}, bf16[240,1600]{1,0:T(8,12...) custom-call(s32[128,128]{1,0:T(8,128)} %bitcast.30, ...), custom_call_target="tpu_custom_call" | custom-call | flops 1000000 | bytes 3072000 | tf_op jit(solution)/shard_map/prepare/pallas_call | solution.py:837
  13.2 0.0 copy-start
  13.2 0.0 copy-start.3
  13.2 0.0 copy-start.4
  13.2 0.0 copy-start.5
  13.2 3.3 %all-to-all-done = f32[32,4,128]{2,1,0:T(4,128)S(1)} async-done(((f32[32,4,128]{2,1,0:T(4,128)}), f32[32,4,128]{2,1,0:T(4,128)S(1)}, u32[]{:S(2)}, u32[]{:S(2)}) %all-to-all-start) | async-done | bytes 65568 | tf_op jit(solution)/shard_map/all_to_all | solution.py:804
  16.5 0.0 copy-start.1
  16.5 0.6 copy-done.1
  17.1 10.0 %centroids.1 = (f32[3,1,128]{2,1,0:T(1,128)}, f32[32,4,128]{2,1,0:T(4,128)}) custom-call(f32[4,8,4,128]{3,2,1,0:T(4,128)} %bitcast.25, s32[128,128]{1,0:T(8,128)} %get-tuple-element.21.codes, f32[256,16]{1,0:T(8,128)} %get-tuple-element.22.columns, bf16[64,96]{1,0:T(8,128)(2,1)} %get-tuple-element.23.second, bf16[128,192]{1,0:T(8,128)(2,1)} %get-tuple-element.24.third, ...), custom_call_target="tpu_custom_call" | custom-call | tf_op jit(solution)/shard_map/centroids/pallas_call | solution.py:865
  27.1 9.9 %all_to_all.15 = f32[32,4,128]{2,1,0:T(4,128)S(1)} all-to-all(f32[32,4,128]{2,1,0:T(4,128)} %get-tuple-element.32), channel_id=1, replica_groups=mesh['wide'=4,'narrow'=8] {'wide','narrow'}, dimensions={0} | all-to-all | bytes 131072 | tf_op jit(solution)/shard_map/all_to_all | solution.py:879
  37.0 0.0 copy-done
  37.0 0.0 copy-done.3
  37.0 0.0 copy-done.4
  37.0 0.0 copy-done.5
  37.0 0.0 copy-start.2
  37.0 0.8 %copy-done.2 = f32[32,4,128]{2,1,0:T(4,128)S(1)} copy-done((f32[32,4,128]{2,1,0:T(4,128)S(1)}, f32[32,4,128]{2,1,0:T(4,128)}, u32[]{:S(2)}) %copy-start.2) | copy-done | bytes 65560
  37.8 19.1 %mesh.1 = f32[4,8,1,1152]{3,2,1,0:T(1,128)S(1)} custom-call(f32[4,8,4,128]{3,2,1,0:T(4,128)S(1)} %bitcast.26, f32[4,8,4,128]{3,2,1,0:T(4,128)S(1)} %bitcast.27, f32[8,256]{1,0:T(8,128)S(1)} %copy-done.5, f32[5,256,256]{2,1,0:T(8,128)S(1)} %copy-done, bf16[512,256]{1,0:T(8,128)(2,1)S(1)} %copy-done.4, bf16[512,256]{1,0:T(8,128)(2,1)S(1)} %copy-done.3), custom_call_target="tpu_custom_call" | custom-call | tf_op jit(solution)/shard_map/mesh/pallas_call | solution.py:886
  57.0 10.2 %all_to_all.16.arrived = f32[32,1,1152]{2,1,0:T(1,128)} all-to-all(f32[32,1,1152]{2,1,0:T(1,128)S(1)} %bitcast.24), channel_id=1, replica_groups=mesh['wide'=4,'narrow'=8] {'wide','narrow'}, dimensions={0} | all-to-all | bytes 294912 | tf_op jit(solution)/shard_map/all_to_all | solution.py:909
  67.2 1.5 %finish.1 = (f32[4,1,128]{2,1,0:T(1,128)}, f32[4,1,128]{2,1,0:T(1,128)}, f32[1,128]{1,0:T(1,128)}) custom-call(f32[32,1,1152]{2,1,0:T(1,128)} %all_to_all.16.arrived, s32[1,128]{1,0:T(1,128)} %bitcast.32), custom_call_target="tpu_custom_call" | custom-call | tf_op jit(solution)/shard_map/finish/pallas_call | solution.py:910
Async XLA Ops:
  1.9 14.6 %all-to-all-start = ((f32[32,4,128]{2,1,0:T(4,128)}), f32[32,4,128]{2,1,0:T(4,128)S(1)}, u32[]{:S(2)}, u32[]{:S(2)}) async-start(f32[32,4,128]{2,1,0:T(4,128)} %pack.1), calls=%async_computation | async-start | bytes 131072 | tf_op jit(solution)/shard_map/all_to_all | solution.py:804
  13.2 23.8 %copy-start = (f32[5,256,256]{2,1,0:T(8,128)S(1)}, f32[5,256,256]{2,1,0:T(8,128)}, u32[]{:S(2)}) copy-start(f32[5,256,256]{2,1,0:T(8,128)} %get-tuple-element.34.green_ref) | copy-start | bytes 3932164
  13.2 23.8 %copy-start.3 = (bf16[512,256]{1,0:T(8,128)(2,1)S(1)}, bf16[512,256]{1,0:T(8,128)(2,1)}, u32[]{:S(2)}) copy-start(bf16[512,256]{1,0:T(8,128)(2,1)} %constant.8.clone.unfold_stack) | copy-start | bytes 786436
  13.2 23.8 %copy-start.4 = (bf16[512,256]{1,0:T(8,128)(2,1)S(1)}, bf16[512,256]{1,0:T(8,128)(2,1)}, u32[]{:S(2)}) copy-start(bf16[512,256]{1,0:T(8,128)(2,1)} %constant.7.clone.fold_stack) | copy-start | bytes 786436
  13.2 23.7 %copy-start.5 = (f32[8,256]{1,0:T(8,128)S(1)}, f32[8,256]{1,0:T(8,128)}, u32[]{:S(2)}) copy-start(f32[8,256]{1,0:T(8,128)} %get-tuple-element.33.phase) | copy-start | bytes 24580
  16.5 0.6 copy-start.1
  37.0 0.8 %copy-start.2 = (f32[32,4,128]{2,1,0:T(4,128)S(1)}, f32[32,4,128]{2,1,0:T(4,128)}, u32[]{:S(2)}) copy-start(f32[32,4,128]{2,1,0:T(4,128)} %copy-done.1) | copy-start | bytes 196612

commit v11 on v10

--- a/solution.py
+++ b/solution.py
@@ -41,20 +41,27 @@
     return one(left[0], right[0]) + (one(left[1], right[0]) + one(left[0], right[1]))
 
 
-def by_right(left, right):
-    rows = left[0].shape[0]
-    both = lax.dot_general(
-        jnp.concatenate(left, axis=0), right[0], NN, preferred_element_type=jnp.float32
-    )
-    rest = lax.dot_general(left[0], right[1], NN, preferred_element_type=jnp.float32)
-    return both[:rows] + (both[rows:] + rest)
-
-
-def by_left(left, right):
+def by_right(lefts, right):
+    rows = lefts[0][0].shape[0]
+    width = right.shape[1] // 2
+    stacked = jnp.concatenate([half for left in lefts for half in left], axis=0)
+    both = lax.dot_general(stacked, right, NN, preferred_element_type=jnp.float32)
+    results = []
+    for k in range(len(lefts)):
+        high = both[2 * k * rows : (2 * k + 1) * rows]
+        low = both[(2 * k + 1) * rows : (2 * k + 2) * rows]
+        results.append(high[:, :width] + (high[:, width:] + low[:, :width]))
+    return results
+
+
+def by_left(left, rights):
     rows = left.shape[0] // 2
-    both = lax.dot_general(left, right[0], NN, preferred_element_type=jnp.float32)
-    rest = lax.dot_general(left[:rows], right[1], NN, preferred_element_type=jnp.float32)
-    return both[:rows] + (both[rows:] + rest)
+    width = rights[0][0].shape[1]
+    highs, lows = (jnp.concatenate(half, axis=1) for half in zip(*rights))
+    both = lax.dot_general(left, highs, NN, preferred_element_type=jnp.float32)
+    rest = lax.dot_general(left[:rows], lows, NN, preferred_element_type=jnp.float32)
+    total = both[:rows] + (both[rows:] + rest)
+    return total[:, :width], total[:, width:]
 
 
 def spline_pair(offset):
@@ -413,6 +420,8 @@
     green_ref,
     fold_stack,
     unfold_stack,
+    fold_wide,
+    unfold_wide,
     out_ref,
     grid,
     planes,
@@ -442,12 +451,6 @@
     piece = lax.axis_index("wide") * narrow_count + lax.axis_index("narrow")
     lane_zero = lax.broadcasted_iota(jnp.int32, (1, half_x), 1) == 0
     row_zero = lax.broadcasted_iota(jnp.int32, (half_z, 1), 0) == 0
-
-    def fold():
-        return (fold_stack[0:GRID_X, :], fold_stack[GRID_X:, :])
-
-    def unfold():
-        return (unfold_stack[0:GRID_X, :], unfold_stack[GRID_X:, :])
 
     def sites(at_wide, at_narrow):
         atom = jnp.abs(table[at_wide, at_narrow])
@@ -609,13 +612,15 @@
         real = split(real)
         imag = None if imag is None else split(imag)
         yield
-        real = by_right(real, fold())
-        imag = None if imag is None else by_right(imag, fold())
+        if imag is None:
+            (real,) = by_right([real], fold_wide[...])
+        else:
+            real, imag = by_right([real, imag], fold_wide[...])
         yield
         real, imag = paired(real, imag, lane_zero, 1)
         real, imag = split(real), split(imag)
         yield
-        real, imag = by_left(unfold_stack[...], real), by_left(unfold_stack[...], imag)
+        real, imag = by_left(unfold_stack[...], [real, imag])
         yield
         real, imag = paired(real, imag, row_zero, 0)
         green = green_ref[j]
@@ -631,13 +636,13 @@
         real, imag = merged(real, imag, row_zero, 0)
         real, imag = split(real), split(imag)
         yield
-        real, imag = by_left(fold_stack[...], real), by_left(fold_stack[...], imag)
+        real, imag = by_left(fold_stack[...], [real, imag])
         yield
         real, imag = merged(real, imag, lane_zero, 1)
         scale = jnp.where(piece * fine + j == 0, 1.0, 2.0)
         real, imag = split(real * scale), split(imag * scale)
         yield
-        real, imag = by_right(real, unfold()), by_right(imag, unfold())
+        real, imag = by_right([real, imag], unfold_wide[...])
         yield
         for k, part in enumerate((real, imag)):
             for at_wide in range(wide_count):
@@ -679,14 +684,15 @@
                 [packed[at_wide, c, pl.ds(first, tall), :] for c in range(channels)], axis=0
             )
 
-            def across(right):
-                high = right[0:reach]
-                rest = jnp.zeros((256 - 3 * reach, pair), jnp.bfloat16)
-                right = jnp.concatenate([high, right[128 : 128 + reach], high, rest], axis=0)
-                return lax.dot_general(left, right, NN, preferred_element_type=jnp.float32)
-
-            value = across(weights[odd][index, :, lanes])
-            slope = across(slopes[odd][index, :, lanes])
+            right = jnp.concatenate(
+                [weights[odd][index, :, lanes], slopes[odd][index, :, lanes]], axis=1
+            )
+            high = right[0:reach]
+            rest = jnp.zeros((256 - 3 * reach, 2 * pair), jnp.bfloat16)
+            right = jnp.concatenate([high, right[128 : 128 + reach], high, rest], axis=0)
+            both = lax.dot_general(left, right, NN, preferred_element_type=jnp.float32)
+            value = both[:, 0:pair]
+            slope = both[:, pair:]
             plain = jnp.zeros((window, pair), jnp.float32)
             along_x = plain
             along_y = plain
@@ -886,7 +892,7 @@
     partial = pl.pallas_call(
         mesh_kernel,
         out_shape=shaped((wide_count, narrow_count, 1, out_width)),
-        in_specs=vmem(6),
+        in_specs=vmem(8),
         out_specs=vmem(1)[0],
         scratch_shapes=[
             pltpu.VMEM((copies, fine, HALO_Z + GRID_Z, 2 * GRID_X), jnp.float32),
@@ -903,8 +909,11 @@
         shifts,
         phase,
         green,
-        jnp.asarray(np.concatenate(halves(fold_table(GRID_X)))),
-        jnp.asarray(np.concatenate(halves(fold_table(GRID_X).T))),
+        *[
+            jnp.asarray(np.concatenate(halves(table_of), axis=axis))
+            for axis in range(2)
+            for table_of in (fold_table(GRID_X), fold_table(GRID_X).T)
+        ],
     )
     arrived = lax.all_to_all(partial.reshape(pieces, 1, out_width), axes, 0, 0, tiled=True)
     atom_field, centroid_field, energy = pl.pallas_call(

time: 69.1 us -> 71.4 us (1.033)
  local copies, waits for them, and re-layouts: 1.47 us -> 3.38 us
    unnamed x12 -> x16, local copies, waits for them, and re-layouts: 1.47 us -> 3.38 us
where the time goes in v11:
time: 71.4 us; the launch traced here: 71 us
  Pallas kernels  36.2 us (51%)
  blocking collectives  20.1 us (28%)
  starting transfers between devices  7.3 us (10%)
  local copies, waits for them, and re-layouts  3.38 us (5%)
  waiting for transfers between devices  3.28 us (5%)
  between operations  0.72 us (1%)
    pallas_call x1, Pallas kernels, local(): pl.pallas_call(mesh_kernel, out_shape=shaped((wide_count, narrow_count, 1...  19.4 us
    all_to_all x1, blocking collectives, local(): lax.all_to_all(partial.reshape(pieces, 1, out_width), axes, 0, 0, tiled=T...  10.2 us
    pallas_call x1, Pallas kernels, local(): pl.pallas_call(centroid_kernel, out_shape=(shaped((3, 1, atoms)), shaped(...  9.95 us
    all_to_all x1, blocking collectives, local(): shifts = lax.all_to_all(shifts, axes, 0, 0, tiled=True)  9.87 us
    all_to_all x1, starting transfers between devices, local(): table = lax.all_to_all(packed, axes, 0, 0, tiled=True)  7.3 us
    pallas_call x1, Pallas kernels, local(): pl.pallas_call(prepare_kernel, out_shape=(shaped((listed, atoms), jnp.int...  3.95 us
    unnamed x16, local copies, waits for them, and re-layouts  3.38 us
    all_to_all x1, waiting for transfers between devices, local(): table = lax.all_to_all(packed, axes, 0, 0, tiled=True)  3.28 us
  transfers between devices with their start and end apart: 1, of which 1 were waited for; matrix products, arithmetic and copies ran while one was open for 0% of the time, Pallas kernels for 6%

profile of v11, /device:TPU:0, one launch (start us, length us, event | category | flops | bytes accessed | tf_op | source)
XLA Modules:
  0.0 71.0 jit_solution(9884361280379945359)
XLA Ops:
  0.6 1.3 %pack.1 = f32[32,4,128]{2,1,0:T(4,128)} custom-call(f32[3,1,128]{2,1,0:T(1,128)} %bitcast.33, s32[1,128]{1,0:T(1,128)} %bitcast.31), custom_call_target="tpu_custom_call" | custom-call | tf_op jit(solution)/shard_map/pack/pallas_call | solution.py:803
  2.0 7.3 %all-to-all-start = ((f32[32,4,128]{2,1,0:T(4,128)}), f32[32,4,128]{2,1,0:T(4,128)S(1)}, u32[]{:S(2)}, u32[]{:S(2)}) async-start(f32[32,4,128]{2,1,0:T(4,128)} %pack.1), calls=%async_computation | async-start | bytes 131072 | tf_op jit(solution)/shard_map/all_to_all | solution.py:810
  9.3 3.9 %prepare.1 = (s32[128,128]{1,0:T(8,128)}, f32[256,16]{1,0:T(8,128)}, bf16[64,96]{1,0:T(8,128)(2,1)}, bf16[128,192]{1,0:T(8,128)(2,1)}, bf16[240,1600]{1,0:T(8,12...) custom-call(s32[128,128]{1,0:T(8,128)} %bitcast.30, ...), custom_call_target="tpu_custom_call" | custom-call | flops 1000000 | bytes 3072000 | tf_op jit(solution)/shard_map/prepare/pallas_call | solution.py:843
  13.2 0.0 copy-start
  13.2 0.0 copy-start.3
  13.2 0.0 copy-start.4
  13.3 0.0 copy-start.7
  13.3 3.3 %all-to-all-done = f32[32,4,128]{2,1,0:T(4,128)S(1)} async-done(((f32[32,4,128]{2,1,0:T(4,128)}), f32[32,4,128]{2,1,0:T(4,128)S(1)}, u32[]{:S(2)}, u32[]{:S(2)}) %all-to-all-start) | async-done | bytes 65568 | tf_op jit(solution)/shard_map/all_to_all | solution.py:810
  16.5 0.0 copy-start.1
  16.5 0.6 copy-done.1
  17.2 9.9 %centroids.1 = (f32[3,1,128]{2,1,0:T(1,128)}, f32[32,4,128]{2,1,0:T(4,128)}) custom-call(f32[4,8,4,128]{3,2,1,0:T(4,128)} %bitcast.25, s32[128,128]{1,0:T(8,128)} %get-tuple-element.21.codes, f32[256,16]{1,0:T(8,128)} %get-tuple-element.22.columns, bf16[64,96]{1,0:T(8,128)(2,1)} %get-tuple-element.23.second, bf16[128,192]{1,0:T(8,128)(2,1)} %get-tuple-element.24.third, ...), custom_call_target="tpu_custom_call" | custom-call | tf_op jit(solution)/shard_map/centroids/pallas_call | solution.py:871
  27.1 9.9 %all_to_all.15 = f32[32,4,128]{2,1,0:T(4,128)S(1)} all-to-all(f32[32,4,128]{2,1,0:T(4,128)} %get-tuple-element.32), channel_id=1, replica_groups=mesh['wide'=4,'narrow'=8] {'wide','narrow'}, dimensions={0} | all-to-all | bytes 131072 | tf_op jit(solution)/shard_map/all_to_all | solution.py:885
  37.0 0.0 copy-done
  37.0 0.0 copy-done.3
  37.0 0.0 copy-done.4
  37.0 0.0 copy-done.7
  37.0 0.0 copy-start.2
  37.0 0.8 %copy-done.2 = f32[32,4,128]{2,1,0:T(4,128)S(1)} copy-done((f32[32,4,128]{2,1,0:T(4,128)S(1)}, f32[32,4,128]{2,1,0:T(4,128)}, u32[]{:S(2)}) %copy-start.2) | copy-done | bytes 65560
  37.9 0.0 copy-start.5
  37.9 0.9 %copy-done.5 = bf16[512,256]{1,0:T(8,128)(2,1)S(1)} copy-done((bf16[512,256]{1,0:T(8,128)(2,1)S(1)}, bf16[512,256]{1,0:T(8,128)(2,1)}, u32[]{:S(2)}) %copy-start.5) | copy-done | bytes 262168
  38.8 0.0 copy-start.6
  38.8 0.9 %copy-done.6 = bf16[512,256]{1,0:T(8,128)(2,1)S(1)} copy-done((bf16[512,256]{1,0:T(8,128)(2,1)S(1)}, bf16[512,256]{1,0:T(8,128)(2,1)}, u32[]{:S(2)}) %copy-start.6) | copy-done | bytes 262168
  39.8 19.4 %mesh.1 = f32[4,8,1,1152]{3,2,1,0:T(1,128)S(1)} custom-call(f32[4,8,4,128]{3,2,1,0:T(4,128)S(1)} %bitcast.26, f32[4,8,4,128]{3,2,1,0:T(4,128)S(1)} %bitcast.27, f32[8,256]{1,0:T(8,128)S(1)} %copy-done.7, f32[5,256,256]{2,1,0:T(8,128)S(1)} %copy-done, bf16[512,256]{1,0:T(8,128)(2,1)S(1)} %copy-done.6, bf16[512,256]{1,0:T(8,128)(2,1)S(1)} %copy-done.5, ...), custom_call_target="tpu_custom_call" | custom-call | tf_op jit(solution)/shard_map/mesh/pallas_call | solution.py:892
  59.2 10.2 %all_to_all.16.arrived = f32[32,1,1152]{2,1,0:T(1,128)} all-to-all(f32[32,1,1152]{2,1,0:T(1,128)S(1)} %bitcast.24), channel_id=1, replica_groups=mesh['wide'=4,'narrow'=8] {'wide','narrow'}, dimensions={0} | all-to-all | bytes 294912 | tf_op jit(solution)/shard_map/all_to_all | solution.py:918
  69.4 1.5 %finish.1 = (f32[4,1,128]{2,1,0:T(1,128)}, f32[4,1,128]{2,1,0:T(1,128)}, f32[1,128]{1,0:T(1,128)}) custom-call(f32[32,1,1152]{2,1,0:T(1,128)} %all_to_all.16.arrived, s32[1,128]{1,0:T(1,128)} %bitcast.32), custom_call_target="tpu_custom_call" | custom-call | tf_op jit(solution)/shard_map/finish/pallas_call | solution.py:919
Async XLA Ops:
  2.0 14.6 %all-to-all-start = ((f32[32,4,128]{2,1,0:T(4,128)}), f32[32,4,128]{2,1,0:T(4,128)S(1)}, u32[]{:S(2)}, u32[]{:S(2)}) async-start(f32[32,4,128]{2,1,0:T(4,128)} %pack.1), calls=%async_computation | async-start | bytes 131072 | tf_op jit(solution)/shard_map/all_to_all | solution.py:810
  13.2 23.8 %copy-start = (f32[5,256,256]{2,1,0:T(8,128)S(1)}, f32[5,256,256]{2,1,0:T(8,128)}, u32[]{:S(2)}) copy-start(f32[5,256,256]{2,1,0:T(8,128)} %get-tuple-element.34.green_ref) | copy-start | bytes 3932164
  13.2 23.8 %copy-start.3 = (bf16[256,512]{1,0:T(8,128)(2,1)S(1)}, bf16[256,512]{1,0:T(8,128)(2,1)}, u32[]{:S(2)}) copy-start(bf16[256,512]{1,0:T(8,128)(2,1)} %constant.14.clone.unfold_wide) | copy-start | bytes 786436
  13.2 23.8 %copy-start.4 = (bf16[256,512]{1,0:T(8,128)(2,1)S(1)}, bf16[256,512]{1,0:T(8,128)(2,1)}, u32[]{:S(2)}) copy-start(bf16[256,512]{1,0:T(8,128)(2,1)} %constant.13.clone.fold_wide) | copy-start | bytes 786436
  13.3 23.8 %copy-start.7 = (f32[8,256]{1,0:T(8,128)S(1)}, f32[8,256]{1,0:T(8,128)}, u32[]{:S(2)}) copy-start(f32[8,256]{1,0:T(8,128)} %get-tuple-element.33.phase) | copy-start | bytes 24580
  16.5 0.6 copy-start.1
  37.0 0.8 %copy-start.2 = (f32[32,4,128]{2,1,0:T(4,128)S(1)}, f32[32,4,128]{2,1,0:T(4,128)}, u32[]{:S(2)}) copy-start(f32[32,4,128]{2,1,0:T(4,128)} %copy-done.1) | copy-start | bytes 196612
  37.9 0.9 %copy-start.5 = (bf16[512,256]{1,0:T(8,128)(2,1)S(1)}, bf16[512,256]{1,0:T(8,128)(2,1)}, u32[]{:S(2)}) copy-start(bf16[512,256]{1,0:T(8,128)(2,1)} %constant.12.clone.unfold_stack) | copy-start | bytes 786436
  38.8 0.9 %copy-start.6 = (bf16[512,256]{1,0:T(8,128)(2,1)S(1)}, bf16[512,256]{1,0:T(8,128)(2,1)}, u32[]{:S(2)}) copy-start(bf16[512,256]{1,0:T(8,128)(2,1)} %constant.11.clone.fold_stack) | copy-start | bytes 786436

commit v12 on v10

--- a/solution.py
+++ b/solution.py
@@ -69,13 +69,21 @@
     return value, slope
 
 
+def wrapped(value, length):
+    if length & (length - 1) == 0:
+        return jnp.bitwise_and(value, length - 1)
+    return lax.rem(value, length)
+
+
 def lookup(row_table, spot):
     found = None
+    lane = jnp.bitwise_and(spot, 127)
+    block = lax.shift_right_logical(spot, 7)
     for part in range(row_table.shape[1] // 128):
-        inside = spot // 128 == part
+        inside = block == part
         here = jnp.take_along_axis(
             jnp.broadcast_to(row_table[:, part * 128 : (part + 1) * 128], spot.shape),
-            lax.rem(spot, 128),
+            lane,
             axis=1,
             mode="promise_in_bounds",
         )
@@ -179,30 +187,21 @@
         rows[row : row + 1, 0:hidden] = source[...]
     columns_ref[...] = jnp.transpose(rows[...])
 
+    row = lax.broadcasted_iota(jnp.int32, square.shape, 0)
+    lane = lax.broadcasted_iota(jnp.int32, square.shape, 1)
+    for width, weight, bias, target in (
+        (width_one, embed_two_w, embed_two_b, second_ref),
+        (2 * width_one, embed_three_w, embed_three_b, third_ref),
+    ):
+        tall, deep = target.shape[0] // 2, target.shape[1] // 3
+        again = (lane - tall == row) | (lane - tall == row + width)
+        again = (again & (row < width)) | ((lane - tall == 2 * width) & (row == width))
+        square[...] = jnp.where(again, 1.0, 0.0)
+        square[0:width, 0 : 2 * width] = weight[...]
+        square[width : width + 1, 0 : 2 * width] = bias[...]
+        high, low = split(jnp.transpose(square[...])[0 : 2 * tall, 0:deep])
+        target[...] = jnp.concatenate([high, high, low], axis=1)
     square[...] = jnp.zeros_like(square)
-    for k in range(2):
-        square[0:width_one, k * ROW_PAD : k * ROW_PAD + width_one] = embed_two_w[
-            :, k * width_one : (k + 1) * width_one
-        ]
-        square[
-            width_one : width_one + 1, k * ROW_PAD : k * ROW_PAD + width_one
-        ] = embed_two_b[:, k * width_one : (k + 1) * width_one]
-    high, low = split(jnp.transpose(square[0:128, 0:128])[0 : 2 * ROW_PAD, 0:ROW_PAD])
-    second_ref[...] = jnp.concatenate([high, high, low], axis=1)
-    square[0:128, 0:128] = jnp.zeros((128, 128), jnp.float32)
-    for g in range(2):
-        for k in range(4):
-            square[
-                g * ROW_PAD : g * ROW_PAD + width_one, k * ROW_PAD : k * ROW_PAD + width_one
-            ] = embed_three_w[
-                g * width_one : (g + 1) * width_one, k * width_one : (k + 1) * width_one
-            ]
-    for k in range(4):
-        square[
-            width_one : width_one + 1, k * ROW_PAD : k * ROW_PAD + width_one
-        ] = embed_three_b[:, k * width_one : (k + 1) * width_one]
-    high, low = split(jnp.transpose(square[0:128, 0:128])[:, 0 : 2 * ROW_PAD])
-    third_ref[...] = jnp.concatenate([high, high, low], axis=1)
     for copy in copies[11:13]:
         copy.wait()
     for source, high_ref, low_ref in (
@@ -218,7 +217,7 @@
     mode = piece * fine + row // 2
     for part in range(GRID_Y // 128):
         cell = lax.broadcasted_iota(jnp.int32, shape, 1) + part * 128
-        spot = lax.rem(mode * cell, GRID_Y)
+        spot = wrapped(mode * cell, GRID_Y)
         cosine = lookup(constants[0:1, :], spot)
         sine = lookup(constants[1:2, :], spot)
         alternate = (1 - 2 * lax.rem(cell, 2)).astype(jnp.float32)
@@ -297,8 +296,11 @@
 
     def chunk(first):
         code = codes[pl.ds(first, SLOT_CHUNK), :]
-        offset = code // atoms
-        slot = code - offset * atoms
+        slot = wrapped(code, atoms)
+        if atoms & (atoms - 1) == 0:
+            offset = lax.shift_right_logical(code, atoms.bit_length() - 1)
+        else:
+            offset = code // atoms
         step_x = jnp.where(offset >= 9, 1, 0) + jnp.where(offset >= 18, 1, 0)
         rest = offset - 9 * step_x
         step_z = jnp.where(rest >= 3, 1, 0) + jnp.where(rest >= 6, 1, 0)
@@ -336,25 +338,25 @@
             first_layers.append(jnp.tanh(weight * row + bias))
         layer_one = jnp.concatenate(first_layers, axis=1)
         high, low = split(layer_one)
-        layer_two = lax.dot_general(
+        both = lax.dot_general(
             second_all,
             jnp.concatenate([high, low, high], axis=0),
             NN,
             preferred_element_type=jnp.float32,
         )
-        layer_two = jnp.tanh(layer_two) + jnp.concatenate(
-            [layer_one, layer_one], axis=0
-        )
-        high, low = split(layer_two)
-        layer_three = lax.dot_general(
+        tall = both.shape[0] // 2
+        layer_two = jnp.tanh(both[:tall]) + both[tall:]
+        deep = third_all.shape[1] // 3
+        rest = jnp.zeros((deep - tall, layer_two.shape[1]), jnp.float32)
+        high, low = split(jnp.concatenate([layer_two, rest], axis=0))
+        both = lax.dot_general(
             third_all,
             jnp.concatenate([high, low, high], axis=0),
             NN,
             preferred_element_type=jnp.float32,
         )
-        layer_three = jnp.tanh(layer_three) + jnp.concatenate(
-            [layer_two, layer_two], axis=0
-        )
+        tall = both.shape[0] // 2
+        layer_three = jnp.tanh(both[:tall]) + both[tall:]
         for part in range(4):
             total = matrix[part]
             for k in range(SLOT_CHUNK):
@@ -371,12 +373,7 @@
 
     parts = []
     for part in range(4):
-        padded = matrix[part] * (1.0 / listed)
-        parts.append(
-            jnp.concatenate(
-                [padded[k * ROW_PAD : k * ROW_PAD + width_one] for k in range(4)], axis=0
-            )
-        )
+        parts.append(matrix[part, 0:width_three, :] * (1.0 / listed))
     leading = [part[0:AXIS_COLUMNS] for part in parts]
     for row in range(width_three):
         total = parts[0][row : row + 1] * leading[0]
@@ -490,7 +487,7 @@
         lower = jnp.floor(row_y)
         back = lax.broadcasted_iota(jnp.int32, (8, 1), 0)
         value_y, slope_y = spline_pair((row_y - lower) + back.astype(jnp.float32))
-        cell = lax.rem(lower.astype(jnp.int32) - back + GRID_Y, GRID_Y)
+        cell = wrapped(lower.astype(jnp.int32) - back + GRID_Y, GRID_Y)
         wave_blocks = []
         slope_blocks = []
         for block in range(length // 128):
@@ -640,8 +637,13 @@
         real, imag = by_right(real, unfold()), by_right(imag, unfold())
         yield
         for k, part in enumerate((real, imag)):
+            turned = [
+                pltpu.roll(part, (HALO_X - at_wide * cells_x) % GRID_X, 1)
+                for at_wide in range(copies)
+            ]
             for at_wide in range(wide_count):
-                moved = pltpu.roll(part, (HALO_X - at_wide * cells_x) % GRID_X, 1)[:, 0:128]
+                start = at_wide // copies * 128
+                moved = turned[at_wide % copies][:, start : start + 128]
                 high = moved.astype(jnp.bfloat16).astype(jnp.float32)
                 again = pltpu.roll(high, reach % 128, 1)
                 low = pltpu.roll(moved - high, 2 * reach % 128, 1)
@@ -804,7 +806,8 @@
     table = lax.all_to_all(packed, axes, 0, 0, tiled=True)
     table = table.reshape(wide_count, narrow_count, 4, atoms)
 
-    tall = 4 * ROW_PAD
+    tall_two = -(-(width_three // 2 + 1) // 8) * 8
+    tall_three = -(-width_three // 8) * 8
     bf16 = jnp.bfloat16
     wave_rows = -(-2 * fine // 8) * 8
     angle = np.arange(GRID_Y) * (2.0 * math.pi / GRID_Y)
@@ -839,8 +842,8 @@
         out_shape=(
             shaped((listed, atoms), jnp.int32),
             shaped((256, 16)),
-            shaped((2 * ROW_PAD, 3 * ROW_PAD), bf16),
-            shaped((tall, 6 * ROW_PAD), bf16),
+            shaped((2 * tall_two, 3 * ROW_PAD), bf16),
+            shaped((2 * tall_three, 6 * ROW_PAD), bf16),
             shaped((hidden, entries), bf16),
             shaped((hidden, entries), bf16),
         )
@@ -868,7 +871,7 @@
         in_specs=hbm(12),
         out_specs=tuple(vmem(2)),
         scratch_shapes=[
-            pltpu.VMEM((4, tall, atoms), jnp.float32),
+            pltpu.VMEM((4, tall_three, atoms), jnp.float32),
             pltpu.VMEM((width_three * AXIS_COLUMNS, atoms), jnp.float32),
             pltpu.SemaphoreType.DMA((len(fitted),)),
         ]

time: 69.1 us -> 68 us (0.984)
  Pallas kernels: 35.9 us -> 34.8 us
    pallas_call x1, Pallas kernels: 19.1 us -> 18.4 us  [local(): pl.pallas_call(mesh_kernel, out_shape=shaped((wide_count, narrow_count, 1...]
where the time goes in v12:
time: 68 us; the launch traced here: 67.6 us
  Pallas kernels  34.8 us (51%)
  blocking collectives  20.1 us (30%)
  starting transfers between devices  7.3 us (11%)
  waiting for transfers between devices  3.28 us (5%)
  local copies, waits for them, and re-layouts  1.47 us (2%)
  between operations  0.72 us (1%)
    pallas_call x1, Pallas kernels, local(): pl.pallas_call(mesh_kernel, out_shape=shaped((wide_count, narrow_count, 1...  18.4 us
    all_to_all x1, blocking collectives, local(): lax.all_to_all(partial.reshape(pieces, 1, out_width), axes, 0, 0, tiled=T...  10.2 us
    all_to_all x1, blocking collectives, local(): shifts = lax.all_to_all(shifts, axes, 0, 0, tiled=True)  9.87 us
    pallas_call x1, Pallas kernels, local(): pl.pallas_call(centroid_kernel, out_shape=(shaped((3, 1, atoms)), shaped(...  9.55 us
    all_to_all x1, starting transfers between devices, local(): table = lax.all_to_all(packed, axes, 0, 0, tiled=True)  7.3 us
    pallas_call x1, Pallas kernels, local(): pl.pallas_call(prepare_kernel, out_shape=(shaped((listed, atoms), jnp.int...  3.95 us
    all_to_all x1, waiting for transfers between devices, local(): table = lax.all_to_all(packed, axes, 0, 0, tiled=True)  3.28 us
    pallas_call x1, Pallas kernels, local(): pl.pallas_call(finish_kernel, out_shape=(shaped((4, 1, atoms)), shaped((4...  1.53 us
  transfers between devices with their start and end apart: 1, of which 1 were waited for; matrix products, arithmetic and copies ran while one was open for 0% of the time, Pallas kernels for 6%

profile of v12, /device:TPU:0, one launch (start us, length us, event | category | flops | bytes accessed | tf_op | source)
XLA Modules:
  0.0 67.6 jit_solution(5155552682195289705)
XLA Ops:
  0.6 1.3 %pack.1 = f32[32,4,128]{2,1,0:T(4,128)} custom-call(f32[3,1,128]{2,1,0:T(1,128)} %bitcast.33, s32[1,128]{1,0:T(1,128)} %bitcast.31), custom_call_target="tpu_custom_call" | custom-call | tf_op jit(solution)/shard_map/pack/pallas_call | solution.py:799
  1.9 7.3 %all-to-all-start = ((f32[32,4,128]{2,1,0:T(4,128)}), f32[32,4,128]{2,1,0:T(4,128)S(1)}, u32[]{:S(2)}, u32[]{:S(2)}) async-start(f32[32,4,128]{2,1,0:T(4,128)} %pack.1), calls=%async_computation | async-start | bytes 131072 | tf_op jit(solution)/shard_map/all_to_all | solution.py:806
  9.2 3.9 %prepare.1 = (s32[128,128]{1,0:T(8,128)}, f32[256,16]{1,0:T(8,128)}, bf16[112,96]{1,0:T(8,128)(2,1)}, bf16[208,192]{1,0:T(8,128)(2,1)}, bf16[240,1600]{1,0:T(8,1...) custom-call(s32[128,128]{1,0:T(8,128)} %bitcast.30, ...), custom_call_target="tpu_custom_call" | custom-call | flops 1000000 | bytes 3072000 | tf_op jit(solution)/shard_map/prepare/pallas_call | solution.py:840
  13.2 0.0 copy-start
  13.2 0.0 copy-start.3
  13.2 0.0 copy-start.4
  13.2 0.0 copy-start.5
  13.2 3.3 %all-to-all-done = f32[32,4,128]{2,1,0:T(4,128)S(1)} async-done(((f32[32,4,128]{2,1,0:T(4,128)}), f32[32,4,128]{2,1,0:T(4,128)S(1)}, u32[]{:S(2)}, u32[]{:S(2)}) %all-to-all-start) | async-done | bytes 65568 | tf_op jit(solution)/shard_map/all_to_all | solution.py:806
  16.5 0.0 copy-start.1
  16.5 0.6 copy-done.1
  17.1 9.5 %centroids.1 = (f32[3,1,128]{2,1,0:T(1,128)}, f32[32,4,128]{2,1,0:T(4,128)}) custom-call(f32[4,8,4,128]{3,2,1,0:T(4,128)} %bitcast.25, s32[128,128]{1,0:T(8,128)} %get-tuple-element.21.codes, f32[256,16]{1,0:T(8,128)} %get-tuple-element.22.columns, bf16[112,96]{1,0:T(8,128)(2,1)} %get-tuple-element.23.second, bf16[208,192]{1,0:T(8,128)(2,1)} %get-tuple-element.24.third, ...), custom_call_target="tpu_custom_call" | custom-call | tf_op jit(solution)/shard_map/centroids/pallas_call | solution.py:868
  26.7 9.9 %all_to_all.15 = f32[32,4,128]{2,1,0:T(4,128)S(1)} all-to-all(f32[32,4,128]{2,1,0:T(4,128)} %get-tuple-element.32), channel_id=1, replica_groups=mesh['wide'=4,'narrow'=8] {'wide','narrow'}, dimensions={0} | all-to-all | bytes 131072 | tf_op jit(solution)/shard_map/all_to_all | solution.py:882
  36.6 0.0 copy-done
  36.6 0.0 copy-done.3
  36.6 0.0 copy-done.4
  36.6 0.0 copy-done.5
  36.6 0.0 copy-start.2
  36.6 0.8 %copy-done.2 = f32[32,4,128]{2,1,0:T(4,128)S(1)} copy-done((f32[32,4,128]{2,1,0:T(4,128)S(1)}, f32[32,4,128]{2,1,0:T(4,128)}, u32[]{:S(2)}) %copy-start.2) | copy-done | bytes 65560
  37.4 18.4 %mesh.1 = f32[4,8,1,1152]{3,2,1,0:T(1,128)S(1)} custom-call(f32[4,8,4,128]{3,2,1,0:T(4,128)S(1)} %bitcast.26, f32[4,8,4,128]{3,2,1,0:T(4,128)S(1)} %bitcast.27, f32[8,256]{1,0:T(8,128)S(1)} %copy-done.5, f32[5,256,256]{2,1,0:T(8,128)S(1)} %copy-done, bf16[512,256]{1,0:T(8,128)(2,1)S(1)} %copy-done.4, bf16[512,256]{1,0:T(8,128)(2,1)S(1)} %copy-done.3), custom_call_target="tpu_custom_call" | custom-call | tf_op jit(solution)/shard_map/mesh/pallas_call | solution.py:889
  55.9 10.2 %all_to_all.16.arrived = f32[32,1,1152]{2,1,0:T(1,128)} all-to-all(f32[32,1,1152]{2,1,0:T(1,128)S(1)} %bitcast.24), channel_id=1, replica_groups=mesh['wide'=4,'narrow'=8] {'wide','narrow'}, dimensions={0} | all-to-all | bytes 294912 | tf_op jit(solution)/shard_map/all_to_all | solution.py:912
  66.1 1.5 %finish.1 = (f32[4,1,128]{2,1,0:T(1,128)}, f32[4,1,128]{2,1,0:T(1,128)}, f32[1,128]{1,0:T(1,128)}) custom-call(f32[32,1,1152]{2,1,0:T(1,128)} %all_to_all.16.arrived, s32[1,128]{1,0:T(1,128)} %bitcast.32), custom_call_target="tpu_custom_call" | custom-call | tf_op jit(solution)/shard_map/finish/pallas_call | solution.py:913
Async XLA Ops:
  1.9 14.6 %all-to-all-start = ((f32[32,4,128]{2,1,0:T(4,128)}), f32[32,4,128]{2,1,0:T(4,128)S(1)}, u32[]{:S(2)}, u32[]{:S(2)}) async-start(f32[32,4,128]{2,1,0:T(4,128)} %pack.1), calls=%async_computation | async-start | bytes 131072 | tf_op jit(solution)/shard_map/all_to_all | solution.py:806
  13.2 23.4 %copy-start = (f32[5,256,256]{2,1,0:T(8,128)S(1)}, f32[5,256,256]{2,1,0:T(8,128)}, u32[]{:S(2)}) copy-start(f32[5,256,256]{2,1,0:T(8,128)} %get-tuple-element.34.green_ref) | copy-start | bytes 3932164
  13.2 23.4 %copy-start.3 = (bf16[512,256]{1,0:T(8,128)(2,1)S(1)}, bf16[512,256]{1,0:T(8,128)(2,1)}, u32[]{:S(2)}) copy-start(bf16[512,256]{1,0:T(8,128)(2,1)} %constant.8.clone.unfold_stack) | copy-start | bytes 786436
  13.2 23.3 %copy-start.4 = (bf16[512,256]{1,0:T(8,128)(2,1)S(1)}, bf16[512,256]{1,0:T(8,128)(2,1)}, u32[]{:S(2)}) copy-start(bf16[512,256]{1,0:T(8,128)(2,1)} %constant.7.clone.fold_stack) | copy-start | bytes 786436
  13.2 23.3 %copy-start.5 = (f32[8,256]{1,0:T(8,128)S(1)}, f32[8,256]{1,0:T(8,128)}, u32[]{:S(2)}) copy-start(f32[8,256]{1,0:T(8,128)} %get-tuple-element.33.phase) | copy-start | bytes 24580
  16.5 0.6 copy-start.1
  36.6 0.8 %copy-start.2 = (f32[32,4,128]{2,1,0:T(4,128)S(1)}, f32[32,4,128]{2,1,0:T(4,128)}, u32[]{:S(2)}) copy-start(f32[32,4,128]{2,1,0:T(4,128)} %copy-done.1) | copy-start | bytes 196612

commit v13 on v12

--- a/solution.py
+++ b/solution.py
@@ -19,6 +19,7 @@
 coulomb = 0.25
 
 ROW_PAD = 32
+LOOP_BODY = 4
 SLOT_CHUNK = 16
 HALO_X = 16
 HALO_Z = 8
@@ -254,6 +255,7 @@
     fit_out_w,
     dipole_ref,
     shift_ref,
+    table_ref,
     matrix,
     descriptor,
     arrivals,
@@ -271,6 +273,8 @@
     one_high, one_low, two_high, two_low, three_high, three_low, fit_out_w = held[5:]
     for copy in copies[:5]:
         copy.wait()
+    handing_on = pltpu.make_async_copy(table, table_ref, arrivals.at[len(copies)])
+    handing_on.start()
     wide_count, narrow_count, _, atoms = table.shape
     listed = codes.shape[0]
     width_three = fit_out_w.shape[0]
@@ -363,13 +367,12 @@
                 total = total + layer_three[:, k * atoms : (k + 1) * atoms] * radial[part][k : k + 1]
             matrix[part] = total
 
-    def two_chunks(index, carry):
-        first = pl.multiple_of(index * (2 * SLOT_CHUNK), 2 * SLOT_CHUNK)
-        chunk(first)
-        chunk(pl.multiple_of(first + SLOT_CHUNK, SLOT_CHUNK))
+    def chunks(index, carry):
+        for step in range(LOOP_BODY):
+            chunk(pl.multiple_of((index * LOOP_BODY + step) * SLOT_CHUNK, SLOT_CHUNK))
         return carry
 
-    lax.fori_loop(0, listed // (2 * SLOT_CHUNK), two_chunks, 0)
+    lax.fori_loop(0, listed // (LOOP_BODY * SLOT_CHUNK), chunks, 0)
 
     parts = []
     for part in range(4):
@@ -401,6 +404,7 @@
     moved = jnp.concatenate([moved, jnp.zeros((1, atoms), jnp.float32)], axis=0)
     for target in range(shift_ref.shape[0]):
         shift_ref[target] = moved
+    handing_on.wait()
 
 
 def mesh_kernel(
@@ -414,14 +418,11 @@
     grid,
     planes,
     packed,
-    weights_even,
-    weights_odd,
-    slopes_even,
-    slopes_odd,
     weights_z,
     slopes_z,
     waves,
     wave_slopes,
+    *across_refs,
 ):
     wide_count, narrow_count, _, atoms = table.shape
     cells_x = GRID_X // wide_count
@@ -478,11 +479,11 @@
 
     grid[:, :, 0:HALO_Z, :] = jnp.zeros((copies, fine, HALO_Z, 2 * GRID_X), jnp.float32)
 
-    weights = (weights_even, weights_odd)
-    slopes = (slopes_even, slopes_odd)
+    weights = across_refs[:LOOP_BODY]
+    slopes = across_refs[LOOP_BODY:]
 
     def spread(index, odd):
-        at_narrow = 2 * index + odd
+        at_narrow = LOOP_BODY * index + odd
         row_x, row_y, row_z, charge = line(at_narrow)
         lower = jnp.floor(row_y)
         back = lax.broadcasted_iota(jnp.int32, (8, 1), 0)
@@ -516,14 +517,11 @@
             left = jnp.concatenate(
                 [near * charged[c : c + 1, lanes] for c in range(channels)], axis=0
             )
-            total = lax.dot_general(
-                jnp.concatenate(split(left), axis=0),
-                weights[odd][index, :, lanes],
-                NT,
-                preferred_element_type=jnp.float32,
-            )
-            tall = channels * window
-            total = total[:tall, 0:128] + (total[:tall, 128:256] + total[tall:, 0:128])
+            high, low = split(left)
+            across = weights[odd][index, :, lanes]
+            total = lax.dot_general(high, across, NT, preferred_element_type=jnp.float32)
+            rest = lax.dot_general(low, across[0:128], NT, preferred_element_type=jnp.float32)
+            total = total[:, 0:128] + (total[:, 128:256] + rest)
             start = at_wide // copies * 128
             for c in range(channels):
                 spot = slice(c % 2 * GRID_X + start, c % 2 * GRID_X + start + 128)
@@ -532,15 +530,15 @@
                 grid[k, c // 2, pl.ds(first, HALO_Z), spot] += part[:HALO_Z]
                 grid[k, c // 2, pl.ds(first + HALO_Z, cells_z), spot] = part[HALO_Z:]
 
-    def in_pairs(step):
-        def both(index, carry):
-            step(index, 0)
-            step(index, 1)
+    def in_groups(step):
+        def body(index, carry):
+            for odd in range(LOOP_BODY):
+                step(index, odd)
             return carry
 
-        lax.fori_loop(0, narrow_count // 2, both, 0)
-
-    in_pairs(spread)
+        lax.fori_loop(0, narrow_count // LOOP_BODY, body, 0)
+
+    in_groups(spread)
 
     def gather(j, carry):
         for lanes in (slice(0, GRID_X), slice(GRID_X, 2 * GRID_X)):
@@ -668,7 +666,7 @@
     energy = jnp.broadcast_to(jnp.sum(energy, axis=1, keepdims=True), (1, 128))
 
     def collect(index, odd):
-        at_narrow = 2 * index + odd
+        at_narrow = LOOP_BODY * index + odd
         value_z = weights_z[at_narrow]
         slope_z = slopes_z[at_narrow]
         first = pl.multiple_of(at_narrow * cells_z, HALO_BITS)
@@ -709,7 +707,7 @@
                 out_ref[at_wide, at_narrow, :, k * pair : (k + 1) * pair] = row
             out_ref[at_wide, at_narrow, :, 4 * pair :] = energy
 
-    in_pairs(collect)
+    in_groups(collect)
 
 
 def finish_kernel(arrived, species, atom_ref, centroid_ref, energy_ref):
@@ -865,15 +863,15 @@
     )(*arguments)
     phase, green = prepared[10:]
     fitted = (table, *prepared[:10], fit_out_w.T)
-    dipole, shifts = pl.pallas_call(
+    dipole, shifts, table = pl.pallas_call(
         centroid_kernel,
-        out_shape=(shaped((3, 1, atoms)), shaped((pieces, 4, atoms))),
+        out_shape=(shaped((3, 1, atoms)), shaped((pieces, 4, atoms)), shaped(table.shape)),
         in_specs=hbm(12),
-        out_specs=tuple(vmem(2)),
+        out_specs=tuple(vmem(2) + hbm(1)),
         scratch_shapes=[
             pltpu.VMEM((4, tall_three, atoms), jnp.float32),
             pltpu.VMEM((width_three * AXIS_COLUMNS, atoms), jnp.float32),
-            pltpu.SemaphoreType.DMA((len(fitted),)),
+            pltpu.SemaphoreType.DMA((len(fitted) + 1,)),
         ]
         + [pltpu.VMEM(array.shape, array.dtype) for array in fitted],
         compiler_params=limits(62),
@@ -896,9 +894,9 @@
             pltpu.VMEM((fine, GRID_Z, 2 * GRID_X), jnp.float32),
             pltpu.VMEM((wide_count, 2 * fine, HALO_BITS + GRID_Z, 256), bf16),
         ]
-        + [pltpu.VMEM((narrow_count // 2, 256, length), bf16)] * 4
         + [pltpu.VMEM((narrow_count, GRID_Z // narrow_count + HALO_Z, length), jnp.float32)] * 2
-        + [pltpu.VMEM((narrow_count, wave_rows, length), jnp.float32)] * 2,
+        + [pltpu.VMEM((narrow_count, wave_rows, length), jnp.float32)] * 2
+        + [pltpu.VMEM((narrow_count // LOOP_BODY, 256, length), bf16)] * (2 * LOOP_BODY),
         compiler_params=limits(48),
         name="mesh",
     )(

time: 68 us -> 67 us (0.985)
  Pallas kernels: 34.8 us -> 33.8 us
    pallas_call x1, Pallas kernels: 18.4 us -> 17.7 us  [local(): pl.pallas_call(mesh_kernel, out_shape=shaped((wide_count, narrow_count, 1...]
where the time goes in v13:
time: 67 us; the launch traced here: 66.6 us
  Pallas kernels  33.8 us (50%)
  blocking collectives  20.1 us (30%)
  starting transfers between devices  7.3 us (11%)
  waiting for transfers between devices  3.28 us (5%)
  local copies, waits for them, and re-layouts  1.47 us (2%)
  between operations  0.72 us (1%)
    pallas_call x1, Pallas kernels, local(): pl.pallas_call(mesh_kernel, out_shape=shaped((wide_count, narrow_count, 1...  17.7 us
    all_to_all x1, blocking collectives, local(): lax.all_to_all(partial.reshape(pieces, 1, out_width), axes, 0, 0, tiled=T...  10.2 us
    all_to_all x1, blocking collectives, local(): shifts = lax.all_to_all(shifts, axes, 0, 0, tiled=True)  9.87 us
    pallas_call x1, Pallas kernels, local(): pl.pallas_call(centroid_kernel, out_shape=(shaped((3, 1, atoms)), shaped(...  9.28 us
    all_to_all x1, starting transfers between devices, local(): table = lax.all_to_all(packed, axes, 0, 0, tiled=True)  7.3 us
    pallas_call x1, Pallas kernels, local(): pl.pallas_call(prepare_kernel, out_shape=(shaped((listed, atoms), jnp.int...  3.95 us
    all_to_all x1, waiting for transfers between devices, local(): table = lax.all_to_all(packed, axes, 0, 0, tiled=True)  3.28 us
    pallas_call x1, Pallas kernels, local(): pl.pallas_call(finish_kernel, out_shape=(shaped((4, 1, atoms)), shaped((4...  1.53 us
  transfers between devices with their start and end apart: 1, of which 1 were waited for; matrix products, arithmetic and copies ran while one was open for 0% of the time, Pallas kernels for 6%

profile of v13, /device:TPU:0, one launch (start us, length us, event | category | flops | bytes accessed | tf_op | source)
XLA Modules:
  0.0 66.6 jit_solution(8182927433678585181)
XLA Ops:
  0.6 1.3 %pack.1 = f32[32,4,128]{2,1,0:T(4,128)} custom-call(f32[3,1,128]{2,1,0:T(1,128)} %bitcast.32, s32[1,128]{1,0:T(1,128)} %bitcast.30), custom_call_target="tpu_custom_call" | custom-call | tf_op jit(solution)/shard_map/pack/pallas_call | solution.py:797
  1.9 7.3 %all-to-all-start = ((f32[32,4,128]{2,1,0:T(4,128)}), f32[32,4,128]{2,1,0:T(4,128)S(1)}, u32[]{:S(2)}, u32[]{:S(2)}) async-start(f32[32,4,128]{2,1,0:T(4,128)} %pack.1), calls=%async_computation | async-start | bytes 131072 | tf_op jit(solution)/shard_map/all_to_all | solution.py:804
  9.2 3.9 %prepare.1 = (s32[128,128]{1,0:T(8,128)}, f32[256,16]{1,0:T(8,128)}, bf16[112,96]{1,0:T(8,128)(2,1)}, bf16[208,192]{1,0:T(8,128)(2,1)}, bf16[240,1600]{1,0:T(8,1...) custom-call(s32[128,128]{1,0:T(8,128)} %bitcast.29, ...), custom_call_target="tpu_custom_call" | custom-call | flops 1000000 | bytes 3072000 | tf_op jit(solution)/shard_map/prepare/pallas_call | solution.py:838
  13.2 0.0 copy-start
  13.2 0.0 copy-start.1
  13.2 0.0 copy-start.2
  13.2 0.0 copy-start.4
  13.2 3.3 %all-to-all-done = f32[32,4,128]{2,1,0:T(4,128)S(1)} async-done(((f32[32,4,128]{2,1,0:T(4,128)}), f32[32,4,128]{2,1,0:T(4,128)S(1)}, u32[]{:S(2)}, u32[]{:S(2)}) %all-to-all-start) | async-done | bytes 65568 | tf_op jit(solution)/shard_map/all_to_all | solution.py:804
  16.5 0.0 copy-start.5
  16.5 0.6 copy-done.5
  17.1 9.3 %centroids.1 = (f32[3,1,128]{2,1,0:T(1,128)}, f32[32,4,128]{2,1,0:T(4,128)}, f32[4,8,4,128]{3,2,1,0:T(4,128)}) custom-call(f32[4,8,4,128]{3,2,1,0:T(4,128)} %bitcast.27, s32[128,128]{1,0:T(8,128)} %get-tuple-element.22.codes, f32[256,16]{1,0:T(8,128)} %get-tuple-element.23.columns, bf16[112,96]{1,0:T(8,128)(2,1)} %get-tuple-element.24.second, ...), custom_call_target="tpu_custom_call" | custom-call | tf_op jit(solution)/shard_map/centroids/pallas_call | solution.py:866
  26.4 9.9 %all_to_all.15 = f32[32,4,128]{2,1,0:T(4,128)S(1)} all-to-all(f32[32,4,128]{2,1,0:T(4,128)} %get-tuple-element.34), channel_id=1, replica_groups=mesh['wide'=4,'narrow'=8] {'wide','narrow'}, dimensions={0} | all-to-all | bytes 131072 | tf_op jit(solution)/shard_map/all_to_all | solution.py:880
  36.3 0.0 copy-done
  36.3 0.0 copy-done.1
  36.3 0.0 copy-done.2
  36.3 0.0 copy-done.4
  36.3 0.0 copy-start.3
  36.3 0.8 %copy-done.3 = f32[4,8,4,128]{3,2,1,0:T(4,128)S(1)} copy-done((f32[4,8,4,128]{3,2,1,0:T(4,128)S(1)}, f32[4,8,4,128]{3,2,1,0:T(4,128)}, u32[]{:S(2)}) %copy-start.3) | copy-done | bytes 65560
  37.2 17.7 %mesh.1 = f32[4,8,1,1152]{3,2,1,0:T(1,128)S(1)} custom-call(f32[4,8,4,128]{3,2,1,0:T(4,128)S(1)} %copy-done.3, f32[4,8,4,128]{3,2,1,0:T(4,128)S(1)} %bitcast.25, f32[8,256]{1,0:T(8,128)S(1)} %copy-done.4, f32[5,256,256]{2,1,0:T(8,128)S(1)} %copy-done, bf16[512,256]{1,0:T(8,128)(2,1)S(1)} %copy-done.2, bf16[512,256]{1,0:T(8,128)(2,1)S(1)} %copy-done.1), custom_call_target="tpu_custom_call" | custom-call | tf_op jit(solution)/shard_map/mesh/pallas_call | solution.py:887
  54.9 10.2 %all_to_all.16.arrived = f32[32,1,1152]{2,1,0:T(1,128)} all-to-all(f32[32,1,1152]{2,1,0:T(1,128)S(1)} %bitcast.24), channel_id=1, replica_groups=mesh['wide'=4,'narrow'=8] {'wide','narrow'}, dimensions={0} | all-to-all | bytes 294912 | tf_op jit(solution)/shard_map/all_to_all | solution.py:910
  65.1 1.5 %finish.1 = (f32[4,1,128]{2,1,0:T(1,128)}, f32[4,1,128]{2,1,0:T(1,128)}, f32[1,128]{1,0:T(1,128)}) custom-call(f32[32,1,1152]{2,1,0:T(1,128)} %all_to_all.16.arrived, s32[1,128]{1,0:T(1,128)} %bitcast.31), custom_call_target="tpu_custom_call" | custom-call | tf_op jit(solution)/shard_map/finish/pallas_call | solution.py:911
Async XLA Ops:
  1.9 14.6 %all-to-all-start = ((f32[32,4,128]{2,1,0:T(4,128)}), f32[32,4,128]{2,1,0:T(4,128)S(1)}, u32[]{:S(2)}, u32[]{:S(2)}) async-start(f32[32,4,128]{2,1,0:T(4,128)} %pack.1), calls=%async_computation | async-start | bytes 131072 | tf_op jit(solution)/shard_map/all_to_all | solution.py:804
  13.2 23.1 %copy-start = (f32[5,256,256]{2,1,0:T(8,128)S(1)}, f32[5,256,256]{2,1,0:T(8,128)}, u32[]{:S(2)}) copy-start(f32[5,256,256]{2,1,0:T(8,128)} %get-tuple-element.36.green_ref) | copy-start | bytes 3932164
  13.2 23.1 %copy-start.1 = (bf16[512,256]{1,0:T(8,128)(2,1)S(1)}, bf16[512,256]{1,0:T(8,128)(2,1)}, u32[]{:S(2)}) copy-start(bf16[512,256]{1,0:T(8,128)(2,1)} %constant.8.clone.unfold_stack) | copy-start | bytes 786436
  13.2 23.1 %copy-start.2 = (bf16[512,256]{1,0:T(8,128)(2,1)S(1)}, bf16[512,256]{1,0:T(8,128)(2,1)}, u32[]{:S(2)}) copy-start(bf16[512,256]{1,0:T(8,128)(2,1)} %constant.7.clone.fold_stack) | copy-start | bytes 786436
  13.2 23.1 %copy-start.4 = (f32[8,256]{1,0:T(8,128)S(1)}, f32[8,256]{1,0:T(8,128)}, u32[]{:S(2)}) copy-start(f32[8,256]{1,0:T(8,128)} %get-tuple-element.35.phase) | copy-start | bytes 24580
  16.5 0.6 copy-start.5
  36.3 0.8 %copy-start.3 = (f32[4,8,4,128]{3,2,1,0:T(4,128)S(1)}, f32[4,8,4,128]{3,2,1,0:T(4,128)}, u32[]{:S(2)}) copy-start(f32[4,8,4,128]{3,2,1,0:T(4,128)} %get-tuple-element.33.table) | copy-start | bytes 196612

commit v14 on v13

--- a/solution.py
+++ b/solution.py
@@ -19,7 +19,7 @@
 coulomb = 0.25
 
 ROW_PAD = 32
-LOOP_BODY = 4
+LOOP_BODY = 8
 SLOT_CHUNK = 16
 HALO_X = 16
 HALO_Z = 8
@@ -408,7 +408,7 @@
 
 
 def mesh_kernel(
-    table,
+    cells,
     shifts,
     phase,
     green_ref,
@@ -424,7 +424,7 @@
     wave_slopes,
     *across_refs,
 ):
-    wide_count, narrow_count, _, atoms = table.shape
+    wide_count, narrow_count, _, atoms = cells.shape
     cells_x = GRID_X // wide_count
     cells_z = GRID_Z // narrow_count
     window = cells_z + HALO_Z
@@ -448,11 +448,11 @@
         return (unfold_stack[0:GRID_X, :], unfold_stack[GRID_X:, :])
 
     def sites(at_wide, at_narrow):
-        atom = jnp.abs(table[at_wide, at_narrow])
+        atom = cells[at_wide, at_narrow]
         moved = shifts[at_wide, at_narrow]
         found = []
-        for component, extent in enumerate((cells_x, GRID_Y, cells_z)):
-            start = atom[component : component + 1] * float(extent)
+        for component in range(3):
+            start = atom[component : component + 1]
             found.append(jnp.concatenate([start, start + moved[component : component + 1]], axis=1))
         oxygen = 1.0 - atom[3:4]
         found.append(jnp.concatenate([6.0 * oxygen + atom[3:4], -8.0 * oxygen], axis=1))
@@ -882,6 +882,11 @@
 
     cells_x = GRID_X // wide_count
     copies = 128 // cells_x
+    component = lax.broadcasted_iota(jnp.int32, table.shape, 2)
+    extents = (cells_x, GRID_Y, GRID_Z // narrow_count)
+    cells = jnp.abs(table)
+    for k, extent in enumerate(extents):
+        cells = jnp.where(component == k, cells * float(extent), cells)
     length = wide_count * 2 * atoms
     out_width = 8 * atoms + 128
     partial = pl.pallas_call(
@@ -900,7 +905,7 @@
         compiler_params=limits(48),
         name="mesh",
     )(
-        table,
+        cells,
         shifts,
         phase,
         green,

time: 67 us -> 66 us (0.985)
  blocking collectives: 20.1 us -> 10.2 us
  waiting for transfers between devices: 3.28 us -> 9.4 us
  starting transfers between devices: 7.3 us -> 10.1 us
  other arithmetic: 0 us -> 0.95 us
  local copies, waits for them, and re-layouts: 1.47 us -> 0.63 us
    all_to_all x1 -> x0, blocking collectives: 9.87 us -> none  [local(): shifts = lax.all_to_all(shifts, axes, 0, 0, tiled=True)]
    all_to_all x0 -> x1, waiting for transfers between devices: none -> 6.16 us  [local(): shifts = lax.all_to_all(shifts, axes, 0, 0, tiled=True)]
    all_to_all x0 -> x1, starting transfers between devices: none -> 2.78 us  [local(): shifts = lax.all_to_all(shifts, axes, 0, 0, tiled=True)]
    select_n x0 -> x1, other arithmetic: none -> 0.94 us  [local(): cells = jnp.where(component == k, cells * float(extent), cells)]
    pallas_call x1, Pallas kernels: 9.28 us -> 8.4 us  [local(): pl.pallas_call(centroid_kernel, out_shape=(shaped((3, 1, atoms)), shaped(...]
    unnamed x12 -> x10, local copies, waits for them, and re-layouts: 1.47 us -> 0.63 us
    pallas_call x1, Pallas kernels: 17.7 us -> 18.4 us  [local(): pl.pallas_call(mesh_kernel, out_shape=shaped((wide_count, narrow_count, 1...]
  transfers between devices with their start and end apart: 1 -> 2, of which waited for: 1 -> 2; matrix products, arithmetic and copies ran while one was open for 0% -> 1% of each run, Pallas kernels for 6% -> 6%
where the time goes in v14:
time: 66 us; the launch traced here: 65.6 us
  Pallas kernels  33.6 us (51%)
  blocking collectives  10.2 us (15%)
  starting transfers between devices  10.1 us (15%)
  waiting for transfers between devices  9.4 us (14%)
  other arithmetic  0.95 us (1%)
  between operations  0.73 us (1%)
    pallas_call x1, Pallas kernels, local(): pl.pallas_call(mesh_kernel, out_shape=shaped((wide_count, narrow_count, 1...  18.4 us
    all_to_all x1, blocking collectives, local(): lax.all_to_all(partial.reshape(pieces, 1, out_width), axes, 0, 0, tiled=T...  10.2 us
    pallas_call x1, Pallas kernels, local(): pl.pallas_call(centroid_kernel, out_shape=(shaped((3, 1, atoms)), shaped(...  8.4 us
    all_to_all x1, starting transfers between devices, local(): table = lax.all_to_all(packed, axes, 0, 0, tiled=True)  7.3 us
    all_to_all x1, waiting for transfers between devices, local(): shifts = lax.all_to_all(shifts, axes, 0, 0, tiled=True)  6.16 us
    pallas_call x1, Pallas kernels, local(): pl.pallas_call(prepare_kernel, out_shape=(shaped((listed, atoms), jnp.int...  3.95 us
    all_to_all x1, waiting for transfers between devices, local(): table = lax.all_to_all(packed, axes, 0, 0, tiled=True)  3.24 us
    all_to_all x1, starting transfers between devices, local(): shifts = lax.all_to_all(shifts, axes, 0, 0, tiled=True)  2.78 us
  transfers between devices with their start and end apart: 2, of which 2 were waited for; matrix products, arithmetic and copies ran while one was open for 1% of the time, Pallas kernels for 6%

profile of v14, /device:TPU:0, one launch (start us, length us, event | category | flops | bytes accessed | tf_op | source)
XLA Modules:
  0.0 65.6 jit_solution(4010721599534837367)
XLA Ops:
  0.6 1.3 %pack.1 = f32[32,4,128]{2,1,0:T(4,128)} custom-call(f32[3,1,128]{2,1,0:T(1,128)} %bitcast.32, s32[1,128]{1,0:T(1,128)} %bitcast.30), custom_call_target="tpu_custom_call" | custom-call | tf_op jit(solution)/shard_map/pack/pallas_call | solution.py:797
  1.9 7.3 %all-to-all-start = ((f32[32,4,128]{2,1,0:T(4,128)}), f32[32,4,128]{2,1,0:T(4,128)S(1)}, u32[]{:S(2)}, u32[]{:S(2)}) async-start(f32[32,4,128]{2,1,0:T(4,128)} %pack.1), calls=%async_computation | async-start | bytes 131072 | tf_op jit(solution)/shard_map/all_to_all | solution.py:804
  9.3 4.0 %prepare.1 = (s32[128,128]{1,0:T(8,128)}, f32[256,16]{1,0:T(8,128)}, bf16[112,96]{1,0:T(8,128)(2,1)}, bf16[208,192]{1,0:T(8,128)(2,1)}, bf16[240,1600]{1,0:T(8,1...) custom-call(s32[128,128]{1,0:T(8,128)} %bitcast.29, ...), custom_call_target="tpu_custom_call" | custom-call | flops 1000000 | bytes 3072000 | tf_op jit(solution)/shard_map/prepare/pallas_call | solution.py:838
  13.2 0.0 copy-start
  13.2 0.0 copy-start.1
  13.2 0.0 copy-start.2
  13.3 0.0 copy-start.3
  13.3 3.2 %all-to-all-done = f32[32,4,128]{2,1,0:T(4,128)S(1)} async-done(((f32[32,4,128]{2,1,0:T(4,128)}), f32[32,4,128]{2,1,0:T(4,128)S(1)}, u32[]{:S(2)}, u32[]{:S(2)}) %all-to-all-start) | async-done | bytes 65568 | tf_op jit(solution)/shard_map/all_to_all | solution.py:804
  16.5 0.0 copy-start.4
  16.5 0.6 copy-done.4
  17.1 8.4 %centroids.1 = (f32[3,1,128]{2,1,0:T(1,128)}, f32[32,4,128]{2,1,0:T(4,128)}, f32[4,8,4,128]{3,2,1,0:T(4,128)}) custom-call(f32[4,8,4,128]{3,2,1,0:T(4,128)} %bitcast.27, s32[128,128]{1,0:T(8,128)} %get-tuple-element.22.codes, f32[256,16]{1,0:T(8,128)} %get-tuple-element.23.columns, bf16[112,96]{1,0:T(8,128)(2,1)} %get-tuple-element.24.second, ...), custom_call_target="tpu_custom_call" | custom-call | tf_op jit(solution)/shard_map/centroids/pallas_call | solution.py:866
  25.5 2.8 %all-to-all-start.1 = ((f32[32,4,128]{2,1,0:T(4,128)}), f32[32,4,128]{2,1,0:T(4,128)S(1)}, u32[]{:S(2)}, u32[]{:S(2)}) async-start(f32[32,4,128]{2,1,0:T(4,128)} %get-tuple-element.34), calls=%async_computation.1 | async-start | bytes 131072 | tf_op jit(solution)/shard_map/all_to_all | solution.py:880
  28.3 0.9 %multiply_select_fusion.cells = f32[4,8,4,128]{3,2,1,0:T(4,128)S(1)} fusion(f32[4,8,4,128]{3,2,1,0:T(4,128)} %get-tuple-element.33, pred[4]{0:T(512)(128)(4,1)S(1)} %get-tuple-element.44, pred[4]{0:T(512)(128)(4,1)S(1)} %get-tuple-element.45, pred[4]{0:T(512)(128)(4,1)S(1)} %iota_compare_fusion.2), kind=kLoop, calls=%fused_computation | loop fusion | flops 114688 | bytes 131084 | tf_op jit(solution)/shard_map/jit(_where)/select_n | solution.py:889
  29.3 6.2 %all-to-all-done.1 = f32[32,4,128]{2,1,0:T(4,128)S(1)} async-done(((f32[32,4,128]{2,1,0:T(4,128)}), f32[32,4,128]{2,1,0:T(4,128)S(1)}, u32[]{:S(2)}, u32[]{:S(2)}) %all-to-all-start.1) | async-done | bytes 65568 | tf_op jit(solution)/shard_map/all_to_all | solution.py:880
  35.4 0.0 copy-done
  35.4 0.0 copy-done.1
  35.4 0.0 copy-done.2
  35.4 0.0 copy-done.3
  35.5 18.4 %mesh.1 = f32[4,8,1,1152]{3,2,1,0:T(1,128)S(1)} custom-call(f32[4,8,4,128]{3,2,1,0:T(4,128)S(1)} %multiply_select_fusion.cells, f32[4,8,4,128]{3,2,1,0:T(4,128)S(1)} %bitcast.25, f32[8,256]{1,0:T(8,128)S(1)} %copy-done.3, f32[5,256,256]{2,1,0:T(8,128)S(1)} %copy-done, bf16[512,256]{1,0:T(8,128)(2,1)S(1)} %copy-done.1, bf16[512,256]{1,0:T(8,128)(2,1)S(1)} %copy-done.2), custom_call_target="tpu_custom_call" | custom-call | tf_op jit(solution)/shard_map/mesh/pallas_call | solution.py:892
  53.9 10.2 %all_to_all.15.arrived = f32[32,1,1152]{2,1,0:T(1,128)} all-to-all(f32[32,1,1152]{2,1,0:T(1,128)S(1)} %bitcast.24), channel_id=1, replica_groups=mesh['wide'=4,'narrow'=8] {'wide','narrow'}, dimensions={0} | all-to-all | bytes 294912 | tf_op jit(solution)/shard_map/all_to_all | solution.py:915
  64.1 1.5 %finish.1 = (f32[4,1,128]{2,1,0:T(1,128)}, f32[4,1,128]{2,1,0:T(1,128)}, f32[1,128]{1,0:T(1,128)}) custom-call(f32[32,1,1152]{2,1,0:T(1,128)} %all_to_all.15.arrived, s32[1,128]{1,0:T(1,128)} %bitcast.31), custom_call_target="tpu_custom_call" | custom-call | tf_op jit(solution)/shard_map/finish/pallas_call | solution.py:916
  (2 shorter events, 0.0 us)
Async XLA Ops:
  1.9 14.6 %all-to-all-start = ((f32[32,4,128]{2,1,0:T(4,128)}), f32[32,4,128]{2,1,0:T(4,128)S(1)}, u32[]{:S(2)}, u32[]{:S(2)}) async-start(f32[32,4,128]{2,1,0:T(4,128)} %pack.1), calls=%async_computation | async-start | bytes 131072 | tf_op jit(solution)/shard_map/all_to_all | solution.py:804
  13.2 22.2 %copy-start = (f32[5,256,256]{2,1,0:T(8,128)S(1)}, f32[5,256,256]{2,1,0:T(8,128)}, u32[]{:S(2)}) copy-start(f32[5,256,256]{2,1,0:T(8,128)} %get-tuple-element.36.green_ref) | copy-start | bytes 3932164
  13.2 22.2 %copy-start.1 = (bf16[512,256]{1,0:T(8,128)(2,1)S(1)}, bf16[512,256]{1,0:T(8,128)(2,1)}, u32[]{:S(2)}) copy-start(bf16[512,256]{1,0:T(8,128)(2,1)} %constant.19.clone.fold_stack) | copy-start | bytes 786436
  13.2 22.2 %copy-start.2 = (bf16[512,256]{1,0:T(8,128)(2,1)S(1)}, bf16[512,256]{1,0:T(8,128)(2,1)}, u32[]{:S(2)}) copy-start(bf16[512,256]{1,0:T(8,128)(2,1)} %constant.20.clone.unfold_stack) | copy-start | bytes 786436
  13.3 22.2 %copy-start.3 = (f32[8,256]{1,0:T(8,128)S(1)}, f32[8,256]{1,0:T(8,128)}, u32[]{:S(2)}) copy-start(f32[8,256]{1,0:T(8,128)} %get-tuple-element.35.phase) | copy-start | bytes 24580
  16.5 0.6 copy-start.4
  25.5 9.9 %all-to-all-start.1 = ((f32[32,4,128]{2,1,0:T(4,128)}), f32[32,4,128]{2,1,0:T(4,128)S(1)}, u32[]{:S(2)}, u32[]{:S(2)}) async-start(f32[32,4,128]{2,1,0:T(4,128)} %get-tuple-element.34), calls=%async_computation.1 | async-start | bytes 131072 | tf_op jit(solution)/shard_map/all_to_all | solution.py:880

commit v15 on v14

--- a/solution.py
+++ b/solution.py
@@ -19,7 +19,8 @@
 coulomb = 0.25
 
 ROW_PAD = 32
-LOOP_BODY = 8
+LOOP_BODY = 4
+CHUNK_BODY = 8
 SLOT_CHUNK = 16
 HALO_X = 16
 HALO_Z = 8
@@ -368,11 +369,11 @@
             matrix[part] = total
 
     def chunks(index, carry):
-        for step in range(LOOP_BODY):
-            chunk(pl.multiple_of((index * LOOP_BODY + step) * SLOT_CHUNK, SLOT_CHUNK))
+        for step in range(CHUNK_BODY):
+            chunk(pl.multiple_of((index * CHUNK_BODY + step) * SLOT_CHUNK, SLOT_CHUNK))
         return carry
 
-    lax.fori_loop(0, listed // (LOOP_BODY * SLOT_CHUNK), chunks, 0)
+    lax.fori_loop(0, listed // (CHUNK_BODY * SLOT_CHUNK), chunks, 0)
 
     parts = []
     for part in range(4):

time: 66 us -> 65.3 us (0.989)
  Pallas kernels: 33.6 us -> 32.9 us
    pallas_call x1, Pallas kernels: 18.4 us -> 17.8 us  [local(): pl.pallas_call(mesh_kernel, out_shape=shaped((wide_count, narrow_count, 1...]
where the time goes in v15:
time: 65.3 us; the launch traced here: 65 us
  Pallas kernels  32.9 us (50%)
  blocking collectives  10.2 us (16%)
  starting transfers between devices  10.1 us (15%)
  waiting for transfers between devices  9.4 us (14%)
  other arithmetic  0.95 us (1%)
  between operations  0.73 us (1%)
    pallas_call x1, Pallas kernels, local(): pl.pallas_call(mesh_kernel, out_shape=shaped((wide_count, narrow_count, 1...  17.8 us
    all_to_all x1, blocking collectives, local(): lax.all_to_all(partial.reshape(pieces, 1, out_width), axes, 0, 0, tiled=T...  10.2 us
    pallas_call x1, Pallas kernels, local(): pl.pallas_call(centroid_kernel, out_shape=(shaped((3, 1, atoms)), shaped(...  8.4 us
    all_to_all x1, starting transfers between devices, local(): table = lax.all_to_all(packed, axes, 0, 0, tiled=True)  7.3 us
    all_to_all x1, waiting for transfers between devices, local(): shifts = lax.all_to_all(shifts, axes, 0, 0, tiled=True)  6.16 us
    pallas_call x1, Pallas kernels, local(): pl.pallas_call(prepare_kernel, out_shape=(shaped((listed, atoms), jnp.int...  3.95 us
    all_to_all x1, waiting for transfers between devices, local(): table = lax.all_to_all(packed, axes, 0, 0, tiled=True)  3.24 us
    all_to_all x1, starting transfers between devices, local(): shifts = lax.all_to_all(shifts, axes, 0, 0, tiled=True)  2.78 us
  transfers between devices with their start and end apart: 2, of which 2 were waited for; matrix products, arithmetic and copies ran while one was open for 1% of the time, Pallas kernels for 6%

profile of v15, /device:TPU:0, one launch (start us, length us, event | category | flops | bytes accessed | tf_op | source)
XLA Modules:
  0.0 65.0 jit_solution(2632988409775949267)
XLA Ops:
  0.6 1.3 %pack.1 = f32[32,4,128]{2,1,0:T(4,128)} custom-call(f32[3,1,128]{2,1,0:T(1,128)} %bitcast.32, s32[1,128]{1,0:T(1,128)} %bitcast.30), custom_call_target="tpu_custom_call" | custom-call | tf_op jit(solution)/shard_map/pack/pallas_call | solution.py:798
  1.9 7.3 %all-to-all-start = ((f32[32,4,128]{2,1,0:T(4,128)}), f32[32,4,128]{2,1,0:T(4,128)S(1)}, u32[]{:S(2)}, u32[]{:S(2)}) async-start(f32[32,4,128]{2,1,0:T(4,128)} %pack.1), calls=%async_computation | async-start | bytes 131072 | tf_op jit(solution)/shard_map/all_to_all | solution.py:805
  9.3 4.0 %prepare.1 = (s32[128,128]{1,0:T(8,128)}, f32[256,16]{1,0:T(8,128)}, bf16[112,96]{1,0:T(8,128)(2,1)}, bf16[208,192]{1,0:T(8,128)(2,1)}, bf16[240,1600]{1,0:T(8,1...) custom-call(s32[128,128]{1,0:T(8,128)} %bitcast.29, ...), custom_call_target="tpu_custom_call" | custom-call | flops 1000000 | bytes 3072000 | tf_op jit(solution)/shard_map/prepare/pallas_call | solution.py:839
  13.2 0.0 copy-start
  13.2 0.0 copy-start.1
  13.2 0.0 copy-start.2
  13.3 0.0 copy-start.3
  13.3 3.2 %all-to-all-done = f32[32,4,128]{2,1,0:T(4,128)S(1)} async-done(((f32[32,4,128]{2,1,0:T(4,128)}), f32[32,4,128]{2,1,0:T(4,128)S(1)}, u32[]{:S(2)}, u32[]{:S(2)}) %all-to-all-start) | async-done | bytes 65568 | tf_op jit(solution)/shard_map/all_to_all | solution.py:805
  16.5 0.0 copy-start.4
  16.5 0.6 copy-done.4
  17.1 8.4 %centroids.1 = (f32[3,1,128]{2,1,0:T(1,128)}, f32[32,4,128]{2,1,0:T(4,128)}, f32[4,8,4,128]{3,2,1,0:T(4,128)}) custom-call(f32[4,8,4,128]{3,2,1,0:T(4,128)} %bitcast.27, s32[128,128]{1,0:T(8,128)} %get-tuple-element.22.codes, f32[256,16]{1,0:T(8,128)} %get-tuple-element.23.columns, bf16[112,96]{1,0:T(8,128)(2,1)} %get-tuple-element.24.second, ...), custom_call_target="tpu_custom_call" | custom-call | tf_op jit(solution)/shard_map/centroids/pallas_call | solution.py:867
  25.5 2.8 %all-to-all-start.1 = ((f32[32,4,128]{2,1,0:T(4,128)}), f32[32,4,128]{2,1,0:T(4,128)S(1)}, u32[]{:S(2)}, u32[]{:S(2)}) async-start(f32[32,4,128]{2,1,0:T(4,128)} %get-tuple-element.34), calls=%async_computation.1 | async-start | bytes 131072 | tf_op jit(solution)/shard_map/all_to_all | solution.py:881
  28.3 0.9 %multiply_select_fusion.cells = f32[4,8,4,128]{3,2,1,0:T(4,128)S(1)} fusion(f32[4,8,4,128]{3,2,1,0:T(4,128)} %get-tuple-element.33, pred[4]{0:T(512)(128)(4,1)S(1)} %get-tuple-element.44, pred[4]{0:T(512)(128)(4,1)S(1)} %get-tuple-element.45, pred[4]{0:T(512)(128)(4,1)S(1)} %iota_compare_fusion.2), kind=kLoop, calls=%fused_computation | loop fusion | flops 114688 | bytes 131084 | tf_op jit(solution)/shard_map/jit(_where)/select_n | solution.py:890
  29.3 6.2 %all-to-all-done.1 = f32[32,4,128]{2,1,0:T(4,128)S(1)} async-done(((f32[32,4,128]{2,1,0:T(4,128)}), f32[32,4,128]{2,1,0:T(4,128)S(1)}, u32[]{:S(2)}, u32[]{:S(2)}) %all-to-all-start.1) | async-done | bytes 65568 | tf_op jit(solution)/shard_map/all_to_all | solution.py:881
  35.4 0.0 copy-done
  35.4 0.0 copy-done.1
  35.4 0.0 copy-done.2
  35.4 0.0 copy-done.3
  35.5 17.8 %mesh.1 = f32[4,8,1,1152]{3,2,1,0:T(1,128)S(1)} custom-call(f32[4,8,4,128]{3,2,1,0:T(4,128)S(1)} %multiply_select_fusion.cells, f32[4,8,4,128]{3,2,1,0:T(4,128)S(1)} %bitcast.25, f32[8,256]{1,0:T(8,128)S(1)} %copy-done.3, f32[5,256,256]{2,1,0:T(8,128)S(1)} %copy-done, bf16[512,256]{1,0:T(8,128)(2,1)S(1)} %copy-done.1, bf16[512,256]{1,0:T(8,128)(2,1)S(1)} %copy-done.2), custom_call_target="tpu_custom_call" | custom-call | tf_op jit(solution)/shard_map/mesh/pallas_call | solution.py:893
  53.2 10.2 %all_to_all.15.arrived = f32[32,1,1152]{2,1,0:T(1,128)} all-to-all(f32[32,1,1152]{2,1,0:T(1,128)S(1)} %bitcast.24), channel_id=1, replica_groups=mesh['wide'=4,'narrow'=8] {'wide','narrow'}, dimensions={0} | all-to-all | bytes 294912 | tf_op jit(solution)/shard_map/all_to_all | solution.py:916
  63.4 1.5 %finish.1 = (f32[4,1,128]{2,1,0:T(1,128)}, f32[4,1,128]{2,1,0:T(1,128)}, f32[1,128]{1,0:T(1,128)}) custom-call(f32[32,1,1152]{2,1,0:T(1,128)} %all_to_all.15.arrived, s32[1,128]{1,0:T(1,128)} %bitcast.31), custom_call_target="tpu_custom_call" | custom-call | tf_op jit(solution)/shard_map/finish/pallas_call | solution.py:917
  (2 shorter events, 0.0 us)
Async XLA Ops:
  1.9 14.6 %all-to-all-start = ((f32[32,4,128]{2,1,0:T(4,128)}), f32[32,4,128]{2,1,0:T(4,128)S(1)}, u32[]{:S(2)}, u32[]{:S(2)}) async-start(f32[32,4,128]{2,1,0:T(4,128)} %pack.1), calls=%async_computation | async-start | bytes 131072 | tf_op jit(solution)/shard_map/all_to_all | solution.py:805
  13.2 22.2 %copy-start = (f32[5,256,256]{2,1,0:T(8,128)S(1)}, f32[5,256,256]{2,1,0:T(8,128)}, u32[]{:S(2)}) copy-start(f32[5,256,256]{2,1,0:T(8,128)} %get-tuple-element.36.green_ref) | copy-start | bytes 3932164
  13.2 22.2 %copy-start.1 = (bf16[512,256]{1,0:T(8,128)(2,1)S(1)}, bf16[512,256]{1,0:T(8,128)(2,1)}, u32[]{:S(2)}) copy-start(bf16[512,256]{1,0:T(8,128)(2,1)} %constant.19.clone.fold_stack) | copy-start | bytes 786436
  13.2 22.2 %copy-start.2 = (bf16[512,256]{1,0:T(8,128)(2,1)S(1)}, bf16[512,256]{1,0:T(8,128)(2,1)}, u32[]{:S(2)}) copy-start(bf16[512,256]{1,0:T(8,128)(2,1)} %constant.20.clone.unfold_stack) | copy-start | bytes 786436
  13.3 22.2 %copy-start.3 = (f32[8,256]{1,0:T(8,128)S(1)}, f32[8,256]{1,0:T(8,128)}, u32[]{:S(2)}) copy-start(f32[8,256]{1,0:T(8,128)} %get-tuple-element.35.phase) | copy-start | bytes 24580
  16.5 0.6 copy-start.4
  25.5 9.9 %all-to-all-start.1 = ((f32[32,4,128]{2,1,0:T(4,128)}), f32[32,4,128]{2,1,0:T(4,128)S(1)}, u32[]{:S(2)}, u32[]{:S(2)}) async-start(f32[32,4,128]{2,1,0:T(4,128)} %get-tuple-element.34), calls=%async_computation.1 | async-start | bytes 131072 | tf_op jit(solution)/shard_map/all_to_all | solution.py:881

commit v16 on v15

--- a/solution.py
+++ b/solution.py
@@ -20,8 +20,8 @@
 
 ROW_PAD = 32
 LOOP_BODY = 4
-CHUNK_BODY = 8
-SLOT_CHUNK = 16
+CHUNK_BODY = 4
+SLOT_CHUNK = 32
 HALO_X = 16
 HALO_Z = 8
 HALO_BITS = 16

time: 65.3 us -> 65.7 us (level)
  no operation moved by 1% of the time
where the time goes in v16:
time: 65.7 us; the launch traced here: 65.4 us
  Pallas kernels  33.4 us (51%)
  blocking collectives  10.2 us (16%)
  starting transfers between devices  10.1 us (15%)
  waiting for transfers between devices  9.4 us (14%)
  other arithmetic  0.95 us (1%)
  between operations  0.73 us (1%)
    pallas_call x1, Pallas kernels, local(): pl.pallas_call(mesh_kernel, out_shape=shaped((wide_count, narrow_count, 1...  17.8 us
    all_to_all x1, blocking collectives, local(): lax.all_to_all(partial.reshape(pieces, 1, out_width), axes, 0, 0, tiled=T...  10.2 us
    pallas_call x1, Pallas kernels, local(): pl.pallas_call(centroid_kernel, out_shape=(shaped((3, 1, atoms)), shaped(...  8.83 us
    all_to_all x1, starting transfers between devices, local(): table = lax.all_to_all(packed, axes, 0, 0, tiled=True)  7.3 us
    all_to_all x1, waiting for transfers between devices, local(): shifts = lax.all_to_all(shifts, axes, 0, 0, tiled=True)  6.16 us
    pallas_call x1, Pallas kernels, local(): pl.pallas_call(prepare_kernel, out_shape=(shaped((listed, atoms), jnp.int...  3.95 us
    all_to_all x1, waiting for transfers between devices, local(): table = lax.all_to_all(packed, axes, 0, 0, tiled=True)  3.24 us
    all_to_all x1, starting transfers between devices, local(): shifts = lax.all_to_all(shifts, axes, 0, 0, tiled=True)  2.79 us
  transfers between devices with their start and end apart: 2, of which 2 were waited for; matrix products, arithmetic and copies ran while one was open for 1% of the time, Pallas kernels for 6%

profile of v16, /device:TPU:0, one launch (start us, length us, event | category | flops | bytes accessed | tf_op | source)
XLA Modules:
  0.0 65.4 jit_solution(4256527723387219777)
XLA Ops:
  0.6 1.3 %pack.1 = f32[32,4,128]{2,1,0:T(4,128)} custom-call(f32[3,1,128]{2,1,0:T(1,128)} %bitcast.32, s32[1,128]{1,0:T(1,128)} %bitcast.30), custom_call_target="tpu_custom_call" | custom-call | tf_op jit(solution)/shard_map/pack/pallas_call | solution.py:798
  1.9 7.3 %all-to-all-start = ((f32[32,4,128]{2,1,0:T(4,128)}), f32[32,4,128]{2,1,0:T(4,128)S(1)}, u32[]{:S(2)}, u32[]{:S(2)}) async-start(f32[32,4,128]{2,1,0:T(4,128)} %pack.1), calls=%async_computation | async-start | bytes 131072 | tf_op jit(solution)/shard_map/all_to_all | solution.py:805
  9.3 4.0 %prepare.1 = (s32[128,128]{1,0:T(8,128)}, f32[256,16]{1,0:T(8,128)}, bf16[112,96]{1,0:T(8,128)(2,1)}, bf16[208,192]{1,0:T(8,128)(2,1)}, bf16[240,1600]{1,0:T(8,1...) custom-call(s32[128,128]{1,0:T(8,128)} %bitcast.29, ...), custom_call_target="tpu_custom_call" | custom-call | flops 1000000 | bytes 3072000 | tf_op jit(solution)/shard_map/prepare/pallas_call | solution.py:839
  13.2 0.0 copy-start
  13.2 0.0 copy-start.1
  13.2 0.0 copy-start.2
  13.3 0.0 copy-start.3
  13.3 3.2 %all-to-all-done = f32[32,4,128]{2,1,0:T(4,128)S(1)} async-done(((f32[32,4,128]{2,1,0:T(4,128)}), f32[32,4,128]{2,1,0:T(4,128)S(1)}, u32[]{:S(2)}, u32[]{:S(2)}) %all-to-all-start) | async-done | bytes 65568 | tf_op jit(solution)/shard_map/all_to_all | solution.py:805
  16.5 0.0 copy-start.4
  16.5 0.6 copy-done.4
  17.1 8.8 %centroids.1 = (f32[3,1,128]{2,1,0:T(1,128)}, f32[32,4,128]{2,1,0:T(4,128)}, f32[4,8,4,128]{3,2,1,0:T(4,128)}) custom-call(f32[4,8,4,128]{3,2,1,0:T(4,128)} %bitcast.27, s32[128,128]{1,0:T(8,128)} %get-tuple-element.22.codes, f32[256,16]{1,0:T(8,128)} %get-tuple-element.23.columns, bf16[112,96]{1,0:T(8,128)(2,1)} %get-tuple-element.24.second, ...), custom_call_target="tpu_custom_call" | custom-call | tf_op jit(solution)/shard_map/centroids/pallas_call | solution.py:867
  26.0 2.8 %all-to-all-start.1 = ((f32[32,4,128]{2,1,0:T(4,128)}), f32[32,4,128]{2,1,0:T(4,128)S(1)}, u32[]{:S(2)}, u32[]{:S(2)}) async-start(f32[32,4,128]{2,1,0:T(4,128)} %get-tuple-element.34), calls=%async_computation.1 | async-start | bytes 131072 | tf_op jit(solution)/shard_map/all_to_all | solution.py:881
  28.8 0.9 %multiply_select_fusion.cells = f32[4,8,4,128]{3,2,1,0:T(4,128)S(1)} fusion(f32[4,8,4,128]{3,2,1,0:T(4,128)} %get-tuple-element.33, pred[4]{0:T(512)(128)(4,1)S(1)} %get-tuple-element.44, pred[4]{0:T(512)(128)(4,1)S(1)} %get-tuple-element.45, pred[4]{0:T(512)(128)(4,1)S(1)} %iota_compare_fusion.2), kind=kLoop, calls=%fused_computation | loop fusion | flops 114688 | bytes 131084 | tf_op jit(solution)/shard_map/jit(_where)/select_n | solution.py:890
  29.7 6.2 %all-to-all-done.1 = f32[32,4,128]{2,1,0:T(4,128)S(1)} async-done(((f32[32,4,128]{2,1,0:T(4,128)}), f32[32,4,128]{2,1,0:T(4,128)S(1)}, u32[]{:S(2)}, u32[]{:S(2)}) %all-to-all-start.1) | async-done | bytes 65568 | tf_op jit(solution)/shard_map/all_to_all | solution.py:881
  35.9 0.0 copy-done
  35.9 0.0 copy-done.1
  35.9 0.0 copy-done.2
  35.9 0.0 copy-done.3
  35.9 17.8 %mesh.1 = f32[4,8,1,1152]{3,2,1,0:T(1,128)S(1)} custom-call(f32[4,8,4,128]{3,2,1,0:T(4,128)S(1)} %multiply_select_fusion.cells, f32[4,8,4,128]{3,2,1,0:T(4,128)S(1)} %bitcast.25, f32[8,256]{1,0:T(8,128)S(1)} %copy-done.3, f32[5,256,256]{2,1,0:T(8,128)S(1)} %copy-done, bf16[512,256]{1,0:T(8,128)(2,1)S(1)} %copy-done.1, bf16[512,256]{1,0:T(8,128)(2,1)S(1)} %copy-done.2), custom_call_target="tpu_custom_call" | custom-call | tf_op jit(solution)/shard_map/mesh/pallas_call | solution.py:893
  53.6 10.2 %all_to_all.15.arrived = f32[32,1,1152]{2,1,0:T(1,128)} all-to-all(f32[32,1,1152]{2,1,0:T(1,128)S(1)} %bitcast.24), channel_id=1, replica_groups=mesh['wide'=4,'narrow'=8] {'wide','narrow'}, dimensions={0} | all-to-all | bytes 294912 | tf_op jit(solution)/shard_map/all_to_all | solution.py:916
  63.9 1.5 %finish.1 = (f32[4,1,128]{2,1,0:T(1,128)}, f32[4,1,128]{2,1,0:T(1,128)}, f32[1,128]{1,0:T(1,128)}) custom-call(f32[32,1,1152]{2,1,0:T(1,128)} %all_to_all.15.arrived, s32[1,128]{1,0:T(1,128)} %bitcast.31), custom_call_target="tpu_custom_call" | custom-call | tf_op jit(solution)/shard_map/finish/pallas_call | solution.py:917
  (2 shorter events, 0.0 us)
Async XLA Ops:
  1.9 14.6 %all-to-all-start = ((f32[32,4,128]{2,1,0:T(4,128)}), f32[32,4,128]{2,1,0:T(4,128)S(1)}, u32[]{:S(2)}, u32[]{:S(2)}) async-start(f32[32,4,128]{2,1,0:T(4,128)} %pack.1), calls=%async_computation | async-start | bytes 131072 | tf_op jit(solution)/shard_map/all_to_all | solution.py:805
  13.2 22.6 %copy-start = (f32[5,256,256]{2,1,0:T(8,128)S(1)}, f32[5,256,256]{2,1,0:T(8,128)}, u32[]{:S(2)}) copy-start(f32[5,256,256]{2,1,0:T(8,128)} %get-tuple-element.36.green_ref) | copy-start | bytes 3932164
  13.2 22.6 %copy-start.1 = (bf16[512,256]{1,0:T(8,128)(2,1)S(1)}, bf16[512,256]{1,0:T(8,128)(2,1)}, u32[]{:S(2)}) copy-start(bf16[512,256]{1,0:T(8,128)(2,1)} %constant.19.clone.fold_stack) | copy-start | bytes 786436
  13.2 22.6 %copy-start.2 = (bf16[512,256]{1,0:T(8,128)(2,1)S(1)}, bf16[512,256]{1,0:T(8,128)(2,1)}, u32[]{:S(2)}) copy-start(bf16[512,256]{1,0:T(8,128)(2,1)} %constant.20.clone.unfold_stack) | copy-start | bytes 786436
  13.3 22.6 %copy-start.3 = (f32[8,256]{1,0:T(8,128)S(1)}, f32[8,256]{1,0:T(8,128)}, u32[]{:S(2)}) copy-start(f32[8,256]{1,0:T(8,128)} %get-tuple-element.35.phase) | copy-start | bytes 24580
  16.5 0.6 copy-start.4
  26.0 9.9 %all-to-all-start.1 = ((f32[32,4,128]{2,1,0:T(4,128)}), f32[32,4,128]{2,1,0:T(4,128)S(1)}, u32[]{:S(2)}, u32[]{:S(2)}) async-start(f32[32,4,128]{2,1,0:T(4,128)} %get-tuple-element.34), calls=%async_computation.1 | async-start | bytes 131072 | tf_op jit(solution)/shard_map/all_to_all | solution.py:881
